TPU v7x, 32 devices: a whole 2x2x4 slice. The times are simulated.
32 devices in a mesh: grp: 2 (over x), lat: 16 (over z, y, core).
Axes of the slice: x: 2, y: 2, z: 4, core: 2. Of those that a mesh axis runs over, the one named last changes fastest.
Arguments:
- activations: bfloat16 [4096, 4096], P(('grp', 'lat')), parts along dimension 0, may hold values from -162 to 162
- block_ids: int32 [4096, 2], P(('grp', 'lat')), parts along dimension 0, may hold values from 0 to 63, all different within a row; in each aligned block of 128 rows (0 to 127, 128 to 255, ...) at most 6 rows name the same one
- enc_weight: bfloat16 [4096, 4096], P(None, 'lat'), may hold values from -0.09375 to 0.09375
- enc_bias: float32 [4096], P('lat'), may hold values from -3 to 3
- dec_weight: bfloat16 [4096, 4096], P('lat'), may hold values from -0.5 to 0.5
- dec_bias: float32 [4096], replicated, may hold values from -3 to 3
Outputs:
- rebuilt: bfloat16 [4096, 4096], P(('grp', 'lat')), parts along dimension 0
- enc_grad: bfloat16 [8192, 4096], P('grp', 'lat'), parts along dimension 0
- dec_grad: bfloat16 [8192, 4096], P(('grp', 'lat')), parts along dimension 0
- bias_grad: float32 [8192], P(('grp', 'lat')), parts along dimension 0
There are 2 independent parts, one for each index of `grp`. A program takes and returns all parts, laid end to end along the dimension named above; an argument that names none is the same for every part. Nothing has to cross between parts.
Inputs may be any that keep to these rules, and one draw needn't show every extreme that they name: `block_ids`: within each token's row the 2 blocks differ. Among the 128 tokens of one index of lat no block is named by more than 6 tokens, and some block is named by exactly 6.
All inputs are finite; a program needn't handle non-finite values.
Results may differ from a plain program's by a relative error of at most 0.0058.
Values may be sent and summed in bfloat16 or wider, within the bound.
No kernel may reach another device: no remote copies, remote signals or barrier semaphores. Data moves between devices by JAX's collectives and lax.ppermute only.
A program may use at most 128 MiB of HBM per device.

v0:
```python
import jax
import jax.numpy as jnp
from jax import lax
from jax.sharding import PartitionSpec as P

BLOCK = 64
LOSS_SCALE = 0.5
F32 = jnp.float32
BF16 = jnp.bfloat16


def activate(preact):
    inner_arg = 0.7978845608 * (preact + 0.044715 * preact * preact * preact)
    tangent = jnp.tanh(inner_arg)
    output = 0.5 * preact * (1.0 + tangent)
    slopes = 0.5 * (1.0 + tangent) + 0.5 * preact * (1.0 - tangent * tangent) * 0.7978845608 * (
        1.0 + 0.134145 * preact * preact
    )
    return (output, slopes)


def dot(left, right, left_dim, right_dim):
    dims = (((left_dim,), (right_dim,)), ((), ()))
    return lax.dot_general(left, right, dims, preferred_element_type=F32)


def exchange(rows):
    return lax.all_to_all(rows, "lat", split_axis=0, concat_axis=0, tiled=True)


def per_device(activations, block_ids, enc_weight, enc_bias, dec_weight, dec_bias):
    tok_rows, feature_dim = activations.shape
    active_count = block_ids.shape[1]
    lat_devices = lax.axis_size("lat")
    local_latents = enc_weight.shape[1]
    blocks_dev = local_latents // BLOCK
    nblocks = blocks_dev * lat_devices
    capacity = max(2, 3 * tok_rows * active_count // (2 * nblocks))
    slot_total = nblocks * capacity

    flat_ids = block_ids.reshape(-1)
    pairs = flat_ids.shape[0]
    order = jnp.arange(pairs, dtype=jnp.int32)
    same = (flat_ids[:, None] == flat_ids[None, :]) & (order[None, :] < order[:, None])
    slot_of = flat_ids * capacity + jnp.sum(same.astype(jnp.int32), axis=1)
    slot_of = slot_of.reshape(tok_rows, active_count)
    slots = jnp.arange(slot_total, dtype=jnp.int32)
    select = jnp.any(slots[:, None, None] == slot_of[None, :, :], axis=2).astype(BF16)

    squares = jnp.sum(jnp.square(activations.astype(F32)))
    squares = lax.all_gather(jnp.full((8, 128), squares, F32), "lat", axis=0, tiled=True)
    square_sum = jnp.sum(squares.reshape(lat_devices, 8, 128)[:, 0, 0])
    mean_square = square_sum / (tok_rows * lat_devices * feature_dim) + 1e-06
    scale = LOSS_SCALE / mean_square

    send_rows = dot(select, activations, 1, 0).astype(BF16)
    received = exchange(send_rows)
    row_block = (slots % (blocks_dev * capacity)) // capacity
    own = row_block[:, None] == (jnp.arange(local_latents, dtype=jnp.int32) // BLOCK)[None, :]
    preact = dot(received, enc_weight, 1, 0) + enc_bias[None, :]
    output, slopes = activate(preact)
    code_rows = jnp.where(own, output, 0.0).astype(BF16)
    slopes = jnp.where(own, slopes, 0.0)
    partial_value = dot(code_rows, dec_weight, 1, 0).astype(BF16)
    returned = exchange(partial_value)
    full = dec_bias[None, :] + dot(select, returned, 0, 0)
    errors = (full - activations.astype(F32)).astype(BF16)
    err_rows = dot(select, errors, 1, 0).astype(BF16)
    got_errors = exchange(err_rows)
    code_grad = dot(got_errors, dec_weight, 1, 1) * (slopes * scale)
    bias_grad = jnp.sum(code_grad, axis=0)
    enc_grad = dot(received, code_grad.astype(BF16), 0, 0).astype(BF16)
    dec_grad = (dot(code_rows, got_errors, 0, 0) * scale).astype(BF16)
    return (full.astype(BF16), enc_grad, dec_grad, bias_grad)


def solution(mesh):
    return jax.shard_map(
        per_device,
        mesh=mesh,
        in_specs=(
            P(("grp", "lat"), None),
            P(("grp", "lat"), None),
            P(None, "lat"),
            P("lat"),
            P("lat", None),
            P(),
        ),
        out_specs=(
            P(("grp", "lat"), None),
            P("grp", "lat"),
            P(("grp", "lat"), None),
            P(("grp", "lat")),
        ),
        check_vma=False,
    )
```

profile of v0, /device:TPU:13, one launch (start us, length us, event | category | flops | bytes accessed | tf_op | source)
XLA Modules:
  0.0 273.0 jit_solution(14206194479015500193)
XLA Ops:
  0.6 0.0 copy-start
  0.6 0.9 copy.18
  1.6 0.1 eq.50
  1.7 0.2 convert_reduce_fusion
  1.9 0.1 reduce_sum.39
  2.1 0.1 copy.19
  2.1 0.7 multiply_add_fusion.1
  2.9 3.9 %convolution_convert_fusion.2 = bf16[384,4096]{1,0:T(8,128)(2,1)} fusion(pred[384,128]{1,0:T(8,128)(4,1)S(1)} %fusion.11, bf16[128,4096]{1,0:T(8,128)(2,1)} %param.6), kind=kOutput, calls=%fused_computation.2 | convolution fusion | flops 404226048 | bytes 4243456 | tf_op jit(solution)/shard_map/dot_general | solution.py:24
  6.8 6.7 %all-to-all-start = ((bf16[16,24,4096]{2,1,0:T(8,128)(2,1)}), bf16[16,24,4096]{2,1,0:T(8,128)(2,1)}, u32[]{:S(2)}, u32[]{:S(2)}) async-start(bf16[16,24,4096]{2,1,0:T(8,128)(2,1)} %bitcast.22), calls=%async_computation | async-start | bytes 6291456 | tf_op jit(solution)/shard_map/all_to_all | solution.py:28
  13.5 70.0 %all-to-all-done = bf16[16,24,4096]{2,1,0:T(8,128)(2,1)} async-done(((bf16[16,24,4096]{2,1,0:T(8,128)(2,1)}), bf16[16,24,4096]{2,1,0:T(8,128)(2,1)}, u32[]{:S(2)}, u32[]{:S(2)}) %all-to-all-start) | async-done | bytes 3145760 | tf_op jit(solution)/shard_map/all_to_all | solution.py:28
  83.5 3.5 %convolution_add_fusion.1 = f32[384,256]{1,0:T(8,128)S(1)} fusion(bf16[384,4096]{1,0:T(8,128)(2,1)} %bitcast.1, bf16[4096,256]{1,0:T(8,128)(2,1)} %param.8, f32[256]{0:T(256)S(1)} %copy-done.5), kind=kOutput, calls=%fused_computation.12 | convolution fusion | flops 805404672 | bytes 5637120 | tf_op jit(solution)/shard_map/dot_general | solution.py:24
  87.0 1.1 convolution_convert_fusion
  88.1 74.5 %all_to_all.36 = bf16[16,24,4096]{2,1,0:T(8,128)(2,1)S(1)} all-to-all(bf16[16,24,4096]{2,1,0:T(8,128)(2,1)S(1)} %bitcast.23), channel_id=1, replica_groups=mesh['grp'=2,'lat'=16] {'lat'}, dimensions={0} | all-to-all | bytes 6291456 | tf_op jit(solution)/shard_map/all_to_all | solution.py:28
  162.6 1.7 fusion.20
  164.3 2.7 convolution_convert_fusion.1
  167.0 5.3 %all-to-all-start.2 = ((bf16[16,24,4096]{2,1,0:T(8,128)(2,1)}), bf16[16,24,4096]{2,1,0:T(8,128)(2,1)}, u32[]{:S(2)}, u32[]{:S(2)}) async-start(bf16[16,24,4096]{2,1,0:T(8,128)(2,1)} %bitcast.21), calls=%async_computation.2 | async-start | bytes 6291456 | tf_op jit(solution)/shard_map/all_to_all | solution.py:28
  172.4 0.6 dynamic-slice
  172.9 1.1 fusion.2
  174.1 1.4 dynamic-update-slice
  175.5 83.4 %all-reduce = f32[16]{0:T(128)S(1)} all-reduce(f32[16]{0:T(128)S(1)} %dynamic-update-slice), channel_id=2, replica_groups=mesh['grp'=2,'lat'=16] {'lat'}, use_global_device_ids=true, to_apply=%add | all-reduce | flops 16 | bytes 128
  258.9 0.6 reduce_sum.41
  260.2 3.6 %fusion.21 = (f32[256]{0:T(256)}, bf16[384,256]{1,0:T(8,128)(2,1)S(1)}) fusion(f32[]{:T(128)S(6)} %div.32, f32[384,256]{1,0:T(8,128)S(1)} %copy-done.3, s32[256]{0:T(256)S(1)} %and_select_fusion, s32[384]{0:T(512)S(1)} %add_select_fusion, bf16[384,4096]{1,0:T(8,128)(2,1)} %bitcast.5, bf16[256,4096]{1,0:T(8,128)(2,1)S(1)} %copy-done), kind=kOutput, calls=%fused_computation.45 | convolution fusion | flops 807567104 | bytes 5836292 | tf_op jit(solution)/shard_map/dot_general | solution.py:24
  263.8 4.6 %fusion = bf16[256,4096]{1,0:T(8,128)(2,1)} fusion(bf16[384,4096]{1,0:T(8,128)(2,1)} %bitcast.5, f32[]{:T(128)S(6)} %div.32, f32[384,256]{1,0:T(8,128)S(1)} %copy-done.3, s32[256]{0:T(256)S(1)} %and_select_fusion, s32[384]{0:T(512)S(1)} %add_select_fusion), kind=kOutput, calls=%fused_computation.4 | convolution fusion | flops 808484864 | bytes 5638660 | tf_op jit(solution)/shard_map/dot_general | solution.py:24
  268.4 4.5 %convolution_convert_fusion.3 = bf16[4096,256]{1,0:T(8,128)(2,1)} fusion(bf16[384,4096]{1,0:T(8,128)(2,1)} %bitcast.1, bf16[384,256]{1,0:T(8,128)(2,1)S(1)} %get-tuple-element.7), kind=kOutput, calls=%fused_computation.5 | convolution fusion | flops 806354944 | bytes 5439488 | tf_op jit(solution)/shard_map/dot_general | solution.py:24
  (18 shorter events, 0.1 us)
Async XLA Ops:
  0.6 86.4 %copy-start = (bf16[256,4096]{1,0:T(8,128)(2,1)S(1)}, bf16[256,4096]{1,0:T(8,128)(2,1)}, u32[]{:S(2)}) copy-start(bf16[256,4096]{1,0:T(8,128)(2,1)} %param.10) | copy-start | bytes 6291460
  6.8 76.7 %copy-start.5 = (f32[256]{0:T(256)S(1)}, f32[256]{0:T(256)}, u32[]{:S(2)}) copy-start(f32[256]{0:T(256)} %param.9) | copy-start | bytes 3076
  6.8 76.7 %all-to-all-start = ((bf16[16,24,4096]{2,1,0:T(8,128)(2,1)}), bf16[16,24,4096]{2,1,0:T(8,128)(2,1)}, u32[]{:S(2)}, u32[]{:S(2)}) async-start(bf16[16,24,4096]{2,1,0:T(8,128)(2,1)} %bitcast.22), calls=%async_computation | async-start | bytes 6291456 | tf_op jit(solution)/shard_map/all_to_all | solution.py:28
  87.0 1.1 copy-start.2
  88.1 74.5 %copy-start.4 = (f32[4096]{0:T(1024)S(1)}, f32[4096]{0:T(1024)}, u32[]{:S(2)}) copy-start(f32[4096]{0:T(1024)} %param.11) | copy-start | bytes 49156
  162.6 1.7 copy-start.1
  167.0 5.3 %copy-start.6 = (u32[32]{0:T(128)S(1)}, u32[32]{0:T(128)}, u32[]{:S(2)}) copy-start(u32[32]{0:T(128)} %constant.60) | copy-start | bytes 388
  167.0 93.2 %copy-start.3 = (f32[384,256]{1,0:T(8,128)S(1)}, f32[384,256]{1,0:T(8,128)}, u32[]{:S(2)}) copy-start(f32[384,256]{1,0:T(8,128)} %copy-done.2) | copy-start | bytes 1179652
  167.0 93.2 %all-to-all-start.2 = ((bf16[16,24,4096]{2,1,0:T(8,128)(2,1)}), bf16[16,24,4096]{2,1,0:T(8,128)(2,1)}, u32[]{:S(2)}, u32[]{:S(2)}) async-start(bf16[16,24,4096]{2,1,0:T(8,128)(2,1)} %bitcast.21), calls=%async_computation.2 | async-start | bytes 6291456 | tf_op jit(solution)/shard_map/all_to_all | solution.py:28
where the time goes:
time: 275 us; the launch traced here: 273 us
  blocking collectives  158 us (57%)
  waiting for transfers between devices  70 us (25%)
  matrix products  25.6 us (9%)
  starting transfers between devices  12 us (4%)
  local copies, waits for them, and re-layouts  3.3 us (1%)
    unnamed x1, blocking collectives  83.4 us
    all_to_all x1, blocking collectives, exchange(): return lax.all_to_all(rows, 'lat', split_axis=0, concat_axis=0, tiled=True)  74.5 us
    all_to_all x2, waiting for transfers between devices, exchange(): return lax.all_to_all(rows, 'lat', split_axis=0, concat_axis=0, tiled=True)  70 us
    dot_general x8, matrix products, dot(): return lax.dot_general(left, right, dims, preferred_element_type=F32)  25.6 us
    all_to_all x2, starting transfers between devices, exchange(): return lax.all_to_all(rows, 'lat', split_axis=0, concat_axis=0, tiled=True)  12 us
  transfers between devices with their start and end apart: 2, of which 1 were waited for; matrix products, arithmetic and copies ran while one was open for 1% of the time, Pallas kernels for 0%

commit v1 on v0

v1 whole, which is shorter than its diff:
```python
import jax
import jax.numpy as jnp
from jax import lax
from jax.sharding import PartitionSpec as P

BLOCK = 64
LOSS_SCALE = 0.5
CHUNKS = 2
F32 = jnp.float32
BF16 = jnp.bfloat16


def activate(preact):
    inner_arg = 0.7978845608 * (preact + 0.044715 * preact * preact * preact)
    tangent = jnp.tanh(inner_arg)
    output = 0.5 * preact * (1.0 + tangent)
    slopes = 0.5 * (1.0 + tangent) + 0.5 * preact * (1.0 - tangent * tangent) * 0.7978845608 * (
        1.0 + 0.134145 * preact * preact
    )
    return (output, slopes)


def dot(left, right, left_dim, right_dim):
    dims = (((left_dim,), (right_dim,)), ((), ()))
    return lax.dot_general(left, right, dims, preferred_element_type=F32)


def together(*values):
    return lax.optimization_barrier(values)


def per_device(activations, block_ids, enc_weight, enc_bias, dec_weight, dec_bias):
    tok_rows, feature_dim = activations.shape
    active_count = block_ids.shape[1]
    devices = lax.axis_size("lat")
    half = devices // 2
    local_latents = enc_weight.shape[1]
    blocks_dev = local_latents // BLOCK
    nblocks = blocks_dev * devices
    capacity = max(2, 3 * tok_rows * active_count // (2 * nblocks))
    half_slots = half * blocks_dev * capacity
    width = feature_dim // CHUNKS
    halves = [list(range(half)), list(range(half, devices))]

    def exchange(rows):
        return lax.all_to_all(
            rows, "lat", split_axis=0, concat_axis=0, axis_index_groups=halves, tiled=True
        )

    def swap(rows, step=half):
        return lax.ppermute(rows, "lat", [(i, i ^ step) for i in range(devices)])

    def cut(rows):
        return [rows[:, i * width : (i + 1) * width] for i in range(CHUNKS)]

    def pick(select, rows):
        return dot(select, rows, 1, 0).astype(BF16)

    flat_ids = block_ids.reshape(-1)
    pairs = flat_ids.shape[0]
    order = jnp.arange(pairs, dtype=jnp.int32)
    same = (flat_ids[:, None] == flat_ids[None, :]) & (order[None, :] < order[:, None])
    slot_of = flat_ids * capacity + jnp.sum(same.astype(jnp.int32), axis=1)
    slot_of = slot_of.reshape(tok_rows, active_count).T
    my_half = lax.axis_index("lat") // half
    slots = jnp.arange(half_slots, dtype=jnp.int32)

    def selection(slot):
        slot = slot - my_half * half_slots
        return jnp.any(slots[:, None, None] == slot[None, :, :], axis=1).astype(BF16)

    squares = jnp.full((8, 128), jnp.sum(jnp.square(activations.astype(F32))), F32)
    steps = [1 << i for i in range((devices - 1).bit_length())]

    def more(squares):
        return squares + swap(squares, steps.pop(0)) if steps else squares

    act_cut = cut(activations)
    slot_held = swap(slot_of)
    held_0 = swap(act_cut[0])
    sel_own = selection(slot_of)
    got_own = exchange(pick(sel_own, activations))
    held_0, slot_held, got_own, squares = together(held_0, slot_held, got_own, more(squares))
    sel_held = selection(slot_held)
    held_1 = swap(act_cut[1])
    got_0 = exchange(pick(sel_held, held_0))
    held_1, got_0, squares = together(held_1, got_0, more(squares))
    got_1 = exchange(pick(sel_held, held_1))
    got_1, squares = together(got_1, more(squares))
    got_held = [got_0, got_1]

    row_block = (slots % (blocks_dev * capacity)) // capacity
    own = row_block[:, None] == (jnp.arange(local_latents, dtype=jnp.int32) // BLOCK)[None, :]

    def encode(preact):
        output, slopes = activate(preact + enc_bias[None, :])
        return jnp.where(own, output, 0.0).astype(BF16), jnp.where(own, slopes, 0.0)

    enc_cut = [enc_weight[i * width : (i + 1) * width] for i in range(CHUNKS)]
    dec_cut = cut(dec_weight)
    code_own, slope_own = encode(dot(got_own, enc_weight, 1, 0))
    code_held, slope_held = encode(sum(dot(a, b, 1, 0) for a, b in zip(got_held, enc_cut)))

    back_0 = exchange(dot(code_held, dec_cut[0], 1, 0).astype(BF16))
    back_0, code_held, code_own, squares = together(back_0, code_held, code_own, more(squares))
    while steps:
        squares = more(squares)
    far_0 = swap(dot(sel_held, back_0, 0, 0).astype(BF16))
    back_1 = exchange(dot(code_held, dec_cut[1], 1, 0).astype(BF16))
    far_0, back_1, code_own = together(far_0, back_1, code_own)
    far_1 = swap(dot(sel_held, back_1, 0, 0).astype(BF16))
    back_own = exchange(dot(code_own, dec_weight, 1, 0).astype(BF16))
    far_1, back_own = together(far_1, back_own)

    full = dec_bias[None, :] + dot(sel_own, back_own, 0, 0)
    full = full + jnp.concatenate([far_0, far_1], axis=1).astype(F32)
    errors = (full - activations.astype(F32)).astype(BF16)
    err_cut = cut(errors)
    far_0 = swap(err_cut[0])
    err_own = exchange(pick(sel_own, errors))
    far_0, err_own = together(far_0, err_own)
    far_1 = swap(err_cut[1])
    err_0 = exchange(pick(sel_held, far_0))
    far_1, err_0 = together(far_1, err_0)
    err_1 = exchange(pick(sel_held, far_1))
    err_held = [err_0, err_1]
    mean_square = squares[0, 0] / (tok_rows * devices * feature_dim) + 1e-06
    scale = LOSS_SCALE / mean_square

    grad_own = dot(err_own, dec_weight, 1, 1) * (slope_own * scale)
    grad_held = sum(dot(a, b, 1, 1) for a, b in zip(err_held, dec_cut)) * (slope_held * scale)
    bias_grad = jnp.sum(grad_own, axis=0) + jnp.sum(grad_held, axis=0)
    grad_own, grad_held = grad_own.astype(BF16), grad_held.astype(BF16)
    enc_grad = [
        (dot(a[:, i * width : (i + 1) * width], grad_own, 0, 0) + dot(b, grad_held, 0, 0)).astype(BF16)
        for i, (a, b) in enumerate(zip([got_own] * CHUNKS, got_held))
    ]
    dec_grad = [
        ((dot(code_own, a, 0, 0) + dot(code_held, b, 0, 0)) * scale).astype(BF16)
        for a, b in zip(cut(err_own), err_held)
    ]
    return (
        full.astype(BF16),
        jnp.concatenate(enc_grad, axis=0),
        jnp.concatenate(dec_grad, axis=1),
        bias_grad,
    )


def solution(mesh):
    return jax.shard_map(
        per_device,
        mesh=mesh,
        in_specs=(
            P(("grp", "lat"), None),
            P(("grp", "lat"), None),
            P(None, "lat"),
            P("lat"),
            P("lat", None),
            P(),
        ),
        out_specs=(
            P(("grp", "lat"), None),
            P("grp", "lat"),
            P(("grp", "lat"), None),
            P(("grp", "lat")),
        ),
        check_vma=False,
    )
```

time: 275 us -> 290 us (1.055)
  blocking collectives: 158 us -> 0 us
  waiting for transfers between devices: 70 us -> 171 us
  starting transfers between devices: 12 us -> 62.7 us
  matrix products: 25.6 us -> 38.4 us
  other arithmetic: 2.7 us -> 6.28 us
  local copies, waits for them, and re-layouts: 3.3 us -> 6.7 us
    ppermute x0 -> x11, waiting for transfers between devices: none -> 166 us  [swap(): return lax.ppermute(rows, 'lat', [(i, i ^ step) for i in range(devices)])]
    unnamed x1 -> x0, blocking collectives: 83.4 us -> none
    all_to_all x1 -> x0, blocking collectives: 74.5 us -> none  [exchange(): return lax.all_to_all(rows, 'lat', split_axis=0, concat_axis=0, tiled=True)]
    all_to_all x2 -> x9, waiting for transfers between devices: 70 us -> 4.17 us  [exchange(): lax.all_to_all(rows, 'lat', split_axis=0, concat_axis=0, axis_index_group...]
    all_to_all x2 -> x9, starting transfers between devices: 12 us -> 53.8 us  [exchange(): lax.all_to_all(rows, 'lat', split_axis=0, concat_axis=0, axis_index_group...]
    dot_general x8 -> x26, matrix products: 25.6 us -> 38.4 us  [dot(): return lax.dot_general(left, right, dims, preferred_element_type=F32)]
    ppermute x0 -> x11, starting transfers between devices: none -> 8.86 us  [swap(): return lax.ppermute(rows, 'lat', [(i, i ^ step) for i in range(devices)])]
    concatenate x0 -> x2, other arithmetic: none -> 2.95 us  [the longest x1 1.5 us: per_device(): jnp.concatenate(dec_grad, axis=1)]
  transfers between devices with their start and end apart: 2 -> 20, of which waited for: 1 -> 11; matrix products, arithmetic and copies ran while one was open for 1% -> 4% of each run, Pallas kernels for 0% -> 0%
where the time goes in v1:
time: 290 us; the launch traced here: 286 us
  waiting for transfers between devices  171 us (59%)
  starting transfers between devices  62.7 us (22%)
  matrix products  38.4 us (13%)
  local copies, waits for them, and re-layouts  6.7 us (2%)
  other arithmetic  6.28 us (2%)
    ppermute x11, waiting for transfers between devices, swap(): return lax.ppermute(rows, 'lat', [(i, i ^ step) for i in range(devices)])  166 us
    all_to_all x9, starting transfers between devices, exchange(): lax.all_to_all(rows, 'lat', split_axis=0, concat_axis=0, axis_index_group...  53.8 us
    dot_general x26, matrix products, dot(): return lax.dot_general(left, right, dims, preferred_element_type=F32)  38.4 us
    ppermute x11, starting transfers between devices, swap(): return lax.ppermute(rows, 'lat', [(i, i ^ step) for i in range(devices)])  8.86 us
  transfers between devices with their start and end apart: 20, of which 11 were waited for; matrix products, arithmetic and copies ran while one was open for 4% of the time, Pallas kernels for 0%

profile of v1, /device:TPU:13, one launch (start us, length us, event | category | flops | bytes accessed | tf_op | source)
XLA Modules:
  0.0 286.2 jit_solution(16080242402782566399)
XLA Ops:
  2.7 2.9 %convolution_convert_fusion.2 = bf16[192,4096]{1,0:T(8,128)(2,1)} fusion(pred[192,128]{1,0:T(8,128)(4,1)S(1)} %fusion.38, bf16[128,4096]{1,0:T(8,128)(2,1)} %param.6), kind=kOutput, calls=%fused_computation.2 | convolution fusion | flops 202113024 | bytes 2646016 | tf_op jit(solution)/shard_map/dot_general | solution.py:25
  5.6 4.6 %all-to-all-start = ((bf16[8,24,4096]{2,1,0:T(8,128)(2,1)}), bf16[8,24,4096]{2,1,0:T(8,128)(2,1)S(1)}, u32[]{:S(2)}, u32[]{:S(2)}) async-start(bf16[8,24,4096]{2,1,0:T(8,128)(2,1)} %bitcast.1), calls=%async_computation | async-start | bytes 3145728 | tf_op jit(solution)/shard_map/all_to_all | solution.py:46
  11.2 2.3 collective-permute-start
  17.5 24.2 %collective-permute-done.1 = s32[2,128]{1,0:T(2,128)S(1)} collective-permute-done((s32[2,128]{1,0:T(2,128)S(1)}, s32[2,128]{1,0:T(2,128)S(1)}, u32[]{:S(2)}, u32[]{:S(2)}) %collective-permute-start.1) | collective-permute-done | bytes 1056 | tf_op jit(solution)/shard_map/ppermute | solution.py:51
  43.1 4.8 %all-to-all-start.1 = ((bf16[8,24,2048]{2,1,0:T(8,128)(2,1)}), bf16[8,24,2048]{2,1,0:T(8,128)(2,1)S(1)}, u32[]{:S(2)}, u32[]{:S(2)}) async-start(bf16[8,24,2048]{2,1,0:T(8,128)(2,1)} %bitcast.77), calls=%async_computation.1 | async-start | bytes 1572864 | tf_op jit(solution)/shard_map/all_to_all | solution.py:46
  48.3 9.4 %collective-permute-done.4 = f32[8,128]{1,0:T(8,128)S(1)} collective-permute-done((f32[8,128]{1,0:T(8,128)S(1)}, f32[8,128]{1,0:T(8,128)S(1)}, u32[]{:S(2)}, u32[]{:S(2)}) %collective-permute-start.4) | collective-permute-done | bytes 4128 | tf_op jit(solution)/shard_map/ppermute | solution.py:51
  57.8 12.8 %collective-permute-done.3 = bf16[128,2048]{1,0:T(8,128)(2,1)} collective-permute-done((bf16[128,2048]{1,0:T(8,128)(2,1)}, bf16[128,2048]{1,0:T(8,128)(2,1)}, u32[]{:S(2)}, u32[]{:S(2)}) %collective-permute-start.3) | collective-permute-done | bytes 524320 | tf_op jit(solution)/shard_map/ppermute | solution.py:51
  70.6 2.6 convolution_convert_fusion.7
  73.2 7.7 %all-to-all-start.2 = ((bf16[8,24,2048]{2,1,0:T(8,128)(2,1)}), bf16[8,24,2048]{2,1,0:T(8,128)(2,1)S(1)}, u32[]{:S(2)}, u32[]{:S(2)}) async-start(bf16[8,24,2048]{2,1,0:T(8,128)(2,1)} %bitcast.78), calls=%async_computation.2 | async-start | bytes 1572864 | tf_op jit(solution)/shard_map/all_to_all | solution.py:46
  81.2 9.4 %collective-permute-done.5 = f32[8,128]{1,0:T(8,128)S(1)} collective-permute-done((f32[8,128]{1,0:T(8,128)S(1)}, f32[8,128]{1,0:T(8,128)S(1)}, u32[]{:S(2)}, u32[]{:S(2)}) %collective-permute-start.5) | collective-permute-done | bytes 4128 | tf_op jit(solution)/shard_map/ppermute | solution.py:51
  96.2 6.1 %all-to-all-start.3 = ((bf16[8,24,2048]{2,1,0:T(8,128)(2,1)}), bf16[8,24,2048]{2,1,0:T(8,128)(2,1)}, u32[]{:S(2)}, u32[]{:S(2)}) async-start(bf16[8,24,2048]{2,1,0:T(8,128)(2,1)} %bitcast.79), calls=%async_computation.3 | async-start | bytes 1572864 | tf_op jit(solution)/shard_map/all_to_all | solution.py:46
  103.0 9.2 %collective-permute-done.6 = f32[8,128]{1,0:T(8,128)S(1)} collective-permute-done((f32[8,128]{1,0:T(8,128)S(1)}, f32[8,128]{1,0:T(8,128)S(1)}, u32[]{:S(2)}, u32[]{:S(2)}) %collective-permute-start.6) | collective-permute-done | bytes 4128 | tf_op jit(solution)/shard_map/ppermute | solution.py:51
  113.4 6.1 %all-to-all-start.4 = ((bf16[8,24,2048]{2,1,0:T(8,128)(2,1)}), bf16[8,24,2048]{2,1,0:T(8,128)(2,1)}, u32[]{:S(2)}, u32[]{:S(2)}) async-start(bf16[8,24,2048]{2,1,0:T(8,128)(2,1)} %bitcast.80), calls=%async_computation.4 | async-start | bytes 1572864 | tf_op jit(solution)/shard_map/all_to_all | solution.py:46
  122.0 22.2 %collective-permute-done.7 = bf16[128,2048]{1,0:T(8,128)(2,1)} collective-permute-done((bf16[128,2048]{1,0:T(8,128)(2,1)S(1)}, bf16[128,2048]{1,0:T(8,128)(2,1)}, u32[]{:S(2)}, u32[]{:S(2)}) %collective-permute-start.7) | collective-permute-done | bytes 524320 | tf_op jit(solution)/shard_map/ppermute | solution.py:51
  146.0 7.1 %all-to-all-start.5 = ((bf16[8,24,4096]{2,1,0:T(8,128)(2,1)}), bf16[8,24,4096]{2,1,0:T(8,128)(2,1)S(1)}, u32[]{:S(2)}, u32[]{:S(2)}) async-start(bf16[8,24,4096]{2,1,0:T(8,128)(2,1)} %bitcast.65), calls=%async_computation.5 | async-start | bytes 3145728 | tf_op jit(solution)/shard_map/all_to_all | solution.py:46
  155.9 27.6 %collective-permute-done.8 = bf16[128,2048]{1,0:T(8,128)(2,1)} collective-permute-done((bf16[128,2048]{1,0:T(8,128)(2,1)S(1)}, bf16[128,2048]{1,0:T(8,128)(2,1)}, u32[]{:S(2)}, u32[]{:S(2)}) %collective-permute-start.8) | collective-permute-done | bytes 524320 | tf_op jit(solution)/shard_map/ppermute | solution.py:51
  184.7 3.4 %fusion.8 = (bf16[128,4096]{1,0:T(8,128)(2,1)S(1)}, bf16[128,4096]{1,0:T(8,128)(2,1)}) fusion(bf16[128,4096]{1,0:T(8,128)(2,1)S(1)} %copy-done, bf16[128,2048]{1,0:T(8,128)(2,1)} %collective-permute-done.8, bf16[128,2048]{1,0:T(8,128)(2,1)} %collective-permute-done.7, pred[192,128]{1,0:T(8,128)(4,1)S(1)} %fusion.38, bf16[192,4096]{1,0:T(8,128)(2,1)} %bitcast.66, ...), kind=kOutput, calls=%fused_computation.26 | convolution fusion | flops 206569472 | bytes 5808128 | tf_op jit(solution)/shard_map/dot_general | solution.py:25
  189.8 5.1 %all-to-all-start.6 = ((bf16[8,24,4096]{2,1,0:T(8,128)(2,1)}), bf16[8,24,4096]{2,1,0:T(8,128)(2,1)}, u32[]{:S(2)}, u32[]{:S(2)}) async-start(bf16[8,24,4096]{2,1,0:T(8,128)(2,1)} %bitcast.64), calls=%async_computation.6 | async-start | bytes 3145728 | tf_op jit(solution)/shard_map/all_to_all | solution.py:46
  196.8 28.2 %collective-permute-done.9 = bf16[128,2048]{1,0:T(8,128)(2,1)S(1)} collective-permute-done((bf16[128,2048]{1,0:T(8,128)(2,1)S(1)}, bf16[128,2048]{1,0:T(8,128)(2,1)S(1)}, u32[]{:S(2)}, u32[]{:S(2)}) %collective-permute-start.9) | collective-permute-done | bytes 524320 | tf_op jit(solution)/shard_map/ppermute | solution.py:51
  226.2 4.8 %all-to-all-start.7 = ((bf16[8,24,2048]{2,1,0:T(8,128)(2,1)}), bf16[8,24,2048]{2,1,0:T(8,128)(2,1)S(1)}, u32[]{:S(2)}, u32[]{:S(2)}) async-start(bf16[8,24,2048]{2,1,0:T(8,128)(2,1)} %bitcast.81), calls=%async_computation.7 | async-start | bytes 1572864 | tf_op jit(solution)/shard_map/all_to_all | solution.py:46
  232.0 22.5 %collective-permute-done.10 = bf16[128,2048]{1,0:T(8,128)(2,1)} collective-permute-done((bf16[128,2048]{1,0:T(8,128)(2,1)}, bf16[128,2048]{1,0:T(8,128)(2,1)}, u32[]{:S(2)}, u32[]{:S(2)}) %collective-permute-start.10) | collective-permute-done | bytes 524320 | tf_op jit(solution)/shard_map/ppermute | solution.py:51
  254.5 2.6 convolution_convert_fusion.3
  257.1 7.5 %all-to-all-start.8 = ((bf16[8,24,2048]{2,1,0:T(8,128)(2,1)}), bf16[8,24,2048]{2,1,0:T(8,128)(2,1)}, u32[]{:S(2)}, u32[]{:S(2)}) async-start(bf16[8,24,2048]{2,1,0:T(8,128)(2,1)} %bitcast.76), calls=%async_computation.8 | async-start | bytes 1572864 | tf_op jit(solution)/shard_map/all_to_all | solution.py:46
  270.2 4.2 %all-to-all-done.8 = bf16[8,24,2048]{2,1,0:T(8,128)(2,1)} async-done(((bf16[8,24,2048]{2,1,0:T(8,128)(2,1)}), bf16[8,24,2048]{2,1,0:T(8,128)(2,1)}, u32[]{:S(2)}, u32[]{:S(2)}) %all-to-all-start.8) | async-done | bytes 786464 | tf_op jit(solution)/shard_map/all_to_all | solution.py:46
  (103 shorter events, 47.3 us)
Async XLA Ops:
  5.6 36.0 %all-to-all-start = ((bf16[8,24,4096]{2,1,0:T(8,128)(2,1)}), bf16[8,24,4096]{2,1,0:T(8,128)(2,1)S(1)}, u32[]{:S(2)}, u32[]{:S(2)}) async-start(bf16[8,24,4096]{2,1,0:T(8,128)(2,1)} %bitcast.1), calls=%async_computation | async-start | bytes 3145728 | tf_op jit(solution)/shard_map/all_to_all | solution.py:46
  11.2 30.5 %collective-permute-start = (bf16[128,2048]{1,0:T(8,128)(2,1)S(1)}, bf16[128,2048]{1,0:T(8,128)(2,1)S(1)}, u32[]{:S(2)}, u32[]{:S(2)}) collective-permute-start(bf16[128,2048]{1,0:T(8,128)(2,1)S(1)} %get-tuple-element.55), channel_id=1, source_target_pairs={{0,8},{1,9},{2,10},{3,11},{4,12},{5,13},{6,14},{7,15},{8,0},{9,1},... | collective-permute-start | bytes 1572872 | tf_op jit(solution)/shard_map/ppermute | solution.py:51
  15.3 1.5 collective-permute-start.2
  16.0 25.7 %collective-permute-start.1 = (s32[2,128]{1,0:T(2,128)S(1)}, s32[2,128]{1,0:T(2,128)S(1)}, u32[]{:S(2)}, u32[]{:S(2)}) collective-permute-start(s32[2,128]{1,0:T(2,128)S(1)} %get-tuple-element.49), channel_id=1, source_target_pairs={{0,8},{1,9},{2,10},{3,11},{4,12},{5,13},{6,14},{7,15},{8,0},{9,1},... | collective-permute-start | bytes 3080 | tf_op jit(solution)/shard_map/ppermute | solution.py:51
  41.7 31.5 %copy-start.4 = (bf16[8,24,4096]{2,1,0:T(8,128)(2,1)}, bf16[8,24,4096]{2,1,0:T(8,128)(2,1)S(1)}, u32[]{:S(2)}) copy-start(bf16[8,24,4096]{2,1,0:T(8,128)(2,1)S(1)} %all-to-all-done) | copy-start | bytes 4718596
  43.1 27.5 %all-to-all-start.1 = ((bf16[8,24,2048]{2,1,0:T(8,128)(2,1)}), bf16[8,24,2048]{2,1,0:T(8,128)(2,1)S(1)}, u32[]{:S(2)}, u32[]{:S(2)}) async-start(bf16[8,24,2048]{2,1,0:T(8,128)(2,1)} %bitcast.77), calls=%async_computation.1 | async-start | bytes 1572864 | tf_op jit(solution)/shard_map/all_to_all | solution.py:46
  47.8 22.8 %collective-permute-start.3 = (bf16[128,2048]{1,0:T(8,128)(2,1)}, bf16[128,2048]{1,0:T(8,128)(2,1)}, u32[]{:S(2)}, u32[]{:S(2)}) collective-permute-start(bf16[128,2048]{1,0:T(8,128)(2,1)} %get-tuple-element.54), channel_id=1, source_target_pairs={{0,8},{1,9},{2,10},{3,11},{4,12},{5,13},{6,14},{7,15},{8,0},{9,1},... | collective-permute-start | bytes 1572872 | tf_op jit(solution)/shard_map/ppermute | solution.py:51
  48.1 9.7 %collective-permute-start.4 = (f32[8,128]{1,0:T(8,128)S(1)}, f32[8,128]{1,0:T(8,128)S(1)}, u32[]{:S(2)}, u32[]{:S(2)}) collective-permute-start(f32[8,128]{1,0:T(8,128)S(1)} %broadcast_add_fusion), channel_id=1, source_target_pairs={{0,2},{1,3},{2,0},{3,1},{4,6},{5,7},{6,4},{7,5},{8,10},{9,11},{10,... | collective-permute-start | bytes 12296 | tf_op jit(solution)/shard_map/ppermute | solution.py:51
  73.2 17.4 %all-to-all-start.2 = ((bf16[8,24,2048]{2,1,0:T(8,128)(2,1)}), bf16[8,24,2048]{2,1,0:T(8,128)(2,1)S(1)}, u32[]{:S(2)}, u32[]{:S(2)}) async-start(bf16[8,24,2048]{2,1,0:T(8,128)(2,1)} %bitcast.78), calls=%async_computation.2 | async-start | bytes 1572864 | tf_op jit(solution)/shard_map/all_to_all | solution.py:46
  80.9 9.7 %collective-permute-start.5 = (f32[8,128]{1,0:T(8,128)S(1)}, f32[8,128]{1,0:T(8,128)S(1)}, u32[]{:S(2)}, u32[]{:S(2)}) collective-permute-start(f32[8,128]{1,0:T(8,128)S(1)} %add.123), channel_id=1, source_target_pairs={{0,4},{1,5},{2,6},{3,7},{4,0},{5,1},{6,2},{7,3},{8,12},{9,13},{10,... | collective-permute-start | bytes 12296 | tf_op jit(solution)/shard_map/ppermute | solution.py:51
  96.2 15.9 %all-to-all-start.3 = ((bf16[8,24,2048]{2,1,0:T(8,128)(2,1)}), bf16[8,24,2048]{2,1,0:T(8,128)(2,1)}, u32[]{:S(2)}, u32[]{:S(2)}) async-start(bf16[8,24,2048]{2,1,0:T(8,128)(2,1)} %bitcast.79), calls=%async_computation.3 | async-start | bytes 1572864 | tf_op jit(solution)/shard_map/all_to_all | solution.py:46
  102.4 9.8 %collective-permute-start.6 = (f32[8,128]{1,0:T(8,128)S(1)}, f32[8,128]{1,0:T(8,128)S(1)}, u32[]{:S(2)}, u32[]{:S(2)}) collective-permute-start(f32[8,128]{1,0:T(8,128)S(1)} %add.124), channel_id=1, source_target_pairs={{0,8},{1,9},{2,10},{3,11},{4,12},{5,13},{6,14},{7,15},{8,0},{9,1},... | collective-permute-start | bytes 12296 | tf_op jit(solution)/shard_map/ppermute | solution.py:51
  113.4 30.8 %all-to-all-start.4 = ((bf16[8,24,2048]{2,1,0:T(8,128)(2,1)}), bf16[8,24,2048]{2,1,0:T(8,128)(2,1)}, u32[]{:S(2)}, u32[]{:S(2)}) async-start(bf16[8,24,2048]{2,1,0:T(8,128)(2,1)} %bitcast.80), calls=%async_computation.4 | async-start | bytes 1572864 | tf_op jit(solution)/shard_map/all_to_all | solution.py:46
  121.1 23.2 %collective-permute-start.7 = (bf16[128,2048]{1,0:T(8,128)(2,1)S(1)}, bf16[128,2048]{1,0:T(8,128)(2,1)}, u32[]{:S(2)}, u32[]{:S(2)}) collective-permute-start(bf16[128,2048]{1,0:T(8,128)(2,1)S(1)} %convolution_convert_fusion.10), channel_id=1, source_target_pairs={{0,8},{1,9},{2,10},{3,11},{4,12},{5,13},{6,14},{7,15},{8,0},{9,1},... | collective-permute-start | bytes 1572872 | tf_op jit(solution)/shard_map/ppermute | solution.py:51
  146.0 38.7 %copy-start.13 = (f32[4096]{0:T(1024)S(1)}, f32[4096]{0:T(1024)}, u32[]{:S(2)}) copy-start(f32[4096]{0:T(1024)} %param.11) | copy-start | bytes 49156
  146.0 37.5 %all-to-all-start.5 = ((bf16[8,24,4096]{2,1,0:T(8,128)(2,1)}), bf16[8,24,4096]{2,1,0:T(8,128)(2,1)S(1)}, u32[]{:S(2)}, u32[]{:S(2)}) async-start(bf16[8,24,4096]{2,1,0:T(8,128)(2,1)} %bitcast.65), calls=%async_computation.5 | async-start | bytes 3145728 | tf_op jit(solution)/shard_map/all_to_all | solution.py:46
  154.6 29.0 %collective-permute-start.8 = (bf16[128,2048]{1,0:T(8,128)(2,1)S(1)}, bf16[128,2048]{1,0:T(8,128)(2,1)}, u32[]{:S(2)}, u32[]{:S(2)}) collective-permute-start(bf16[128,2048]{1,0:T(8,128)(2,1)S(1)} %convolution_convert_fusion.9), channel_id=1, source_target_pairs={{0,8},{1,9},{2,10},{3,11},{4,12},{5,13},{6,14},{7,15},{8,0},{9,1},... | collective-permute-start | bytes 1572872 | tf_op jit(solution)/shard_map/ppermute | solution.py:51
  189.8 35.2 %all-to-all-start.6 = ((bf16[8,24,4096]{2,1,0:T(8,128)(2,1)}), bf16[8,24,4096]{2,1,0:T(8,128)(2,1)}, u32[]{:S(2)}, u32[]{:S(2)}) async-start(bf16[8,24,4096]{2,1,0:T(8,128)(2,1)} %bitcast.64), calls=%async_computation.6 | async-start | bytes 3145728 | tf_op jit(solution)/shard_map/all_to_all | solution.py:46
  195.7 29.3 %collective-permute-start.9 = (bf16[128,2048]{1,0:T(8,128)(2,1)S(1)}, bf16[128,2048]{1,0:T(8,128)(2,1)S(1)}, u32[]{:S(2)}, u32[]{:S(2)}) collective-permute-start(bf16[128,2048]{1,0:T(8,128)(2,1)S(1)} %get-tuple-element.52), channel_id=1, source_target_pairs={{0,8},{1,9},{2,10},{3,11},{4,12},{5,13},{6,14},{7,15},{8,0},{9,1},... | collective-permute-start | bytes 1572872 | tf_op jit(solution)/shard_map/ppermute | solution.py:51
  226.2 39.6 %copy-start.2 = (bf16[256,4096]{1,0:T(8,128)(2,1)S(1)}, bf16[256,4096]{1,0:T(8,128)(2,1)}, u32[]{:S(2)}) copy-start(bf16[256,4096]{1,0:T(8,128)(2,1)} %param.10) | copy-start | bytes 6291460
  226.2 39.6 %copy-start.18 = (f32[192,256]{1,0:T(8,128)S(1)}, f32[192,256]{1,0:T(8,128)}, u32[]{:S(2)}) copy-start(f32[192,256]{1,0:T(8,128)} %get-tuple-element.58) | copy-start | bytes 589828
  226.2 28.3 %all-to-all-start.7 = ((bf16[8,24,2048]{2,1,0:T(8,128)(2,1)}), bf16[8,24,2048]{2,1,0:T(8,128)(2,1)S(1)}, u32[]{:S(2)}, u32[]{:S(2)}) async-start(bf16[8,24,2048]{2,1,0:T(8,128)(2,1)} %bitcast.81), calls=%async_computation.7 | async-start | bytes 1572864 | tf_op jit(solution)/shard_map/all_to_all | solution.py:46
  231.1 23.4 %collective-permute-start.10 = (bf16[128,2048]{1,0:T(8,128)(2,1)}, bf16[128,2048]{1,0:T(8,128)(2,1)}, u32[]{:S(2)}, u32[]{:S(2)}) collective-permute-start(bf16[128,2048]{1,0:T(8,128)(2,1)} %get-tuple-element.53), channel_id=1, source_target_pairs={{0,8},{1,9},{2,10},{3,11},{4,12},{5,13},{6,14},{7,15},{8,0},{9,1},... | collective-permute-start | bytes 1572872 | tf_op jit(solution)/shard_map/ppermute | solution.py:51
  257.1 17.3 %all-to-all-start.8 = ((bf16[8,24,2048]{2,1,0:T(8,128)(2,1)}), bf16[8,24,2048]{2,1,0:T(8,128)(2,1)}, u32[]{:S(2)}, u32[]{:S(2)}) async-start(bf16[8,24,2048]{2,1,0:T(8,128)(2,1)} %bitcast.76), calls=%async_computation.8 | async-start | bytes 1572864 | tf_op jit(solution)/shard_map/all_to_all | solution.py:46
  (15 other events, 78.1 us)

commit v2 on v0

v2 whole, which is shorter than its diff:
```python
import jax
import jax.numpy as jnp
from jax import lax
from jax.experimental import pallas as pl
from jax.experimental.pallas import tpu as pltpu
from jax.sharding import PartitionSpec as P

BLOCK = 64
LOSS_SCALE = 0.5
F32 = jnp.float32
BF16 = jnp.bfloat16


def activate(preact):
    inner_arg = 0.7978845608 * (preact + 0.044715 * preact * preact * preact)
    tangent = jnp.tanh(inner_arg)
    output = 0.5 * preact * (1.0 + tangent)
    slopes = 0.5 * (1.0 + tangent) + 0.5 * preact * (1.0 - tangent * tangent) * 0.7978845608 * (
        1.0 + 0.134145 * preact * preact
    )
    return (output, slopes)


def dot(left, right, left_dim, right_dim):
    dims = (((left_dim,), (right_dim,)), ((), ()))
    return lax.dot_general(left, right, dims, preferred_element_type=F32)


def together(*values):
    return lax.optimization_barrier(values)


def squares_kernel(rows_ref, total_ref):
    total = jnp.zeros((8, 128), F32)
    rows, columns = rows_ref.shape
    for i in range(0, columns, 128):
        part = rows_ref[:, i : i + 128].astype(F32)
        total = total + jnp.sum((part * part).reshape(rows // 8, 8, 128), axis=0)
    total_ref[...] = jnp.full((8, 128), jnp.sum(total), F32)


def sum_of_squares(rows):
    return pl.pallas_call(
        squares_kernel,
        out_shape=jax.ShapeDtypeStruct((8, 128), F32),
        in_specs=[pl.BlockSpec(memory_space=pltpu.VMEM)],
        out_specs=pl.BlockSpec(memory_space=pltpu.VMEM),
        cost_estimate=pl.CostEstimate(
            flops=50_000_000_000, bytes_accessed=rows.size * 2, transcendentals=0
        ),
        name="squares",
    )(rows)


def per_device(activations, block_ids, enc_weight, enc_bias, dec_weight, dec_bias):
    tok_rows, feature_dim = activations.shape
    active_count = block_ids.shape[1]
    devices = lax.axis_size("lat")
    half = devices // 2
    local_latents = enc_weight.shape[1]
    blocks_dev = local_latents // BLOCK
    nblocks = blocks_dev * devices
    capacity = max(2, 3 * tok_rows * active_count // (2 * nblocks))
    dev_slots = blocks_dev * capacity
    half_slots = half * dev_slots
    halves = [list(range(half)), list(range(half, devices))]

    def exchange(rows, groups=None):
        return lax.all_to_all(
            rows, "lat", split_axis=0, concat_axis=0, axis_index_groups=groups, tiled=True
        )

    def swap(rows, step=half):
        return lax.ppermute(rows, "lat", [(i, i ^ step) for i in range(devices)])

    def pick(select, rows):
        return dot(select, rows, 1, 0).astype(BF16)

    held = swap(activations)
    squares = sum_of_squares(activations)

    flat_ids = block_ids.reshape(-1)
    pairs = flat_ids.shape[0]
    order = jnp.arange(pairs, dtype=jnp.int32)
    same = (flat_ids[:, None] == flat_ids[None, :]) & (order[None, :] < order[:, None])
    slot_of = flat_ids * capacity + jnp.sum(same.astype(jnp.int32), axis=1)
    slot_of = slot_of.reshape(tok_rows, active_count).T
    slot_held = swap(slot_of)
    lower = lax.axis_index("lat") < half
    slots = jnp.arange(2 * half_slots, dtype=jnp.int32)

    def selection(slot, names):
        return jnp.any(names[:, None, None] == slot[None, :, :], axis=1).astype(BF16)

    select = selection(slot_of, slots)
    names = slots[:half_slots] + jnp.where(lower, 0, half_slots)

    got_own = exchange(pick(selection(slot_of, names), activations), halves)
    held, slot_held, got_own, squares = together(held, slot_held, got_own, squares)
    got_held = exchange(pick(selection(slot_held, names), held), halves)

    row_block = (slots[:half_slots] % dev_slots) // capacity
    own = row_block[:, None] == (jnp.arange(local_latents, dtype=jnp.int32) // BLOCK)[None, :]

    def encode(rows):
        output, slopes = activate(dot(rows, enc_weight, 1, 0) + enc_bias[None, :])
        return jnp.where(own, output, 0.0).astype(BF16), jnp.where(own, slopes, 0.0)

    def ordered(own_part, held_part):
        first = jnp.where(lower, own_part, held_part)
        second = jnp.where(lower, held_part, own_part)
        return jnp.concatenate([first, second], axis=0)

    code_own, slope_own = encode(got_own)
    code_held, slope_held = encode(got_held)
    code_rows, slopes = ordered(code_own, code_held), ordered(slope_own, slope_held)

    returned = exchange(dot(code_rows, dec_weight, 1, 0).astype(BF16))
    step = 1
    while step < devices:
        squares = squares + swap(squares, step)
        step *= 2
    returned, squares = together(returned, squares)
    full = dec_bias[None, :] + dot(select, returned, 0, 0)
    errors = (full - activations.astype(F32)).astype(BF16)
    got_errors = exchange(pick(select, errors))

    mean_square = squares[0, 0] / (tok_rows * devices * feature_dim) + 1e-06
    scale = LOSS_SCALE / mean_square
    code_grad = dot(got_errors, dec_weight, 1, 1) * (slopes * scale)
    bias_grad = jnp.sum(code_grad, axis=0)
    code_grad = code_grad.astype(BF16)
    lower_grad, upper_grad = code_grad[:half_slots], code_grad[half_slots:]
    grad_own = jnp.where(lower, lower_grad, upper_grad)
    grad_held = jnp.where(lower, upper_grad, lower_grad)
    enc_grad = (dot(got_own, grad_own, 0, 0) + dot(got_held, grad_held, 0, 0)).astype(BF16)
    dec_grad = (dot(code_rows, got_errors, 0, 0) * scale).astype(BF16)
    return (full.astype(BF16), enc_grad, dec_grad, bias_grad)


def solution(mesh):
    return jax.shard_map(
        per_device,
        mesh=mesh,
        in_specs=(
            P(("grp", "lat"), None),
            P(("grp", "lat"), None),
            P(None, "lat"),
            P("lat"),
            P("lat", None),
            P(),
        ),
        out_specs=(
            P(("grp", "lat"), None),
            P("grp", "lat"),
            P(("grp", "lat"), None),
            P(("grp", "lat")),
        ),
        check_vma=False,
    )
```

time: 275 us -> 258 us (0.938)
  blocking collectives: 158 us -> 0 us
  waiting for transfers between devices: 70 us -> 188 us
  starting transfers between devices: 12 us -> 29.9 us
  matrix products: 25.6 us -> 32.8 us
    ppermute x0 -> x6, waiting for transfers between devices: none -> 102 us  [swap(): return lax.ppermute(rows, 'lat', [(i, i ^ step) for i in range(devices)])]
    unnamed x1 -> x0, blocking collectives: 83.4 us -> none
    all_to_all x1 -> x0, blocking collectives: 74.5 us -> none  [exchange(): return lax.all_to_all(rows, 'lat', split_axis=0, concat_axis=0, tiled=True)]
    all_to_all x2 -> x4, waiting for transfers between devices: 70 us -> 86.3 us  [exchange(): lax.all_to_all(rows, 'lat', split_axis=0, concat_axis=0, axis_index_group...]
    all_to_all x2 -> x4, starting transfers between devices: 12 us -> 26.4 us  [exchange(): lax.all_to_all(rows, 'lat', split_axis=0, concat_axis=0, axis_index_group...]
    dot_general x8 -> x11, matrix products: 25.6 us -> 32.8 us  [dot(): return lax.dot_general(left, right, dims, preferred_element_type=F32)]
    ppermute x0 -> x6, starting transfers between devices: none -> 3.52 us  [swap(): return lax.ppermute(rows, 'lat', [(i, i ^ step) for i in range(devices)])]
  transfers between devices with their start and end apart: 2 -> 10, of which waited for: 1 -> 8; matrix products, arithmetic and copies ran while one was open for 1% -> 3% of each run, Pallas kernels for 0% -> 1%
where the time goes in v2:
time: 258 us
  waiting for transfers between devices  188 us (73%)
  matrix products  32.8 us (13%)
  starting transfers between devices  29.9 us (12%)
    ppermute x6, waiting for transfers between devices, swap(): return lax.ppermute(rows, 'lat', [(i, i ^ step) for i in range(devices)])  102 us
    all_to_all x4, waiting for transfers between devices, exchange(): lax.all_to_all(rows, 'lat', split_axis=0, concat_axis=0, axis_index_group...  86.3 us
    dot_general x11, matrix products, dot(): return lax.dot_general(left, right, dims, preferred_element_type=F32)  32.8 us
    all_to_all x4, starting transfers between devices, exchange(): lax.all_to_all(rows, 'lat', split_axis=0, concat_axis=0, axis_index_group...  26.4 us
  transfers between devices with their start and end apart: 10, of which 8 were waited for; matrix products, arithmetic and copies ran while one was open for 3% of the time, Pallas kernels for 1%

profile of v2, /device:TPU:13, one launch (start us, length us, event | category | flops | bytes accessed | tf_op | source)
XLA Modules:
  0.0 257.7 jit_solution(15510324101077227481)
XLA Ops:
  2.8 2.3 collective-permute-start.1
  5.3 2.9 %convolution_convert_fusion.3 = bf16[192,4096]{1,0:T(8,128)(2,1)} fusion(pred[192,128]{1,0:T(8,128)(4,1)S(1)} %compare_reduce_fusion.1, bf16[128,4096]{1,0:T(8,128)(2,1)} %rows_ref.1), kind=kOutput, calls=%fused_computation.7 | convolution fusion | flops 202113024 | bytes 2646016 | tf_op jit(solution)/shard_map/dot_general | solution.py:26
  8.3 5.2 %all-to-all-start = ((bf16[8,24,4096]{2,1,0:T(8,128)(2,1)}), bf16[8,24,4096]{2,1,0:T(8,128)(2,1)}, u32[]{:S(2)}, u32[]{:S(2)}) async-start(bf16[8,24,4096]{2,1,0:T(8,128)(2,1)} %bitcast.30), calls=%async_computation | async-start | bytes 3145728 | tf_op jit(solution)/shard_map/all_to_all | solution.py:69
  13.4 2.1 squares.1
  15.6 35.3 %collective-permute-done = bf16[128,4096]{1,0:T(8,128)(2,1)S(1)} collective-permute-done((bf16[128,4096]{1,0:T(8,128)(2,1)}, bf16[128,4096]{1,0:T(8,128)(2,1)S(1)}, u32[]{:S(2)}, u32[]{:S(2)}) %collective-permute-start) | collective-permute-done | bytes 1048608 | tf_op jit(solution)/shard_map/ppermute | solution.py:74
  50.9 1.7 convolution_convert_fusion.2
  52.6 8.5 %all-to-all-start.1 = ((bf16[8,24,4096]{2,1,0:T(8,128)(2,1)}), bf16[8,24,4096]{2,1,0:T(8,128)(2,1)}, u32[]{:S(2)}, u32[]{:S(2)}) async-start(bf16[8,24,4096]{2,1,0:T(8,128)(2,1)} %bitcast.31), calls=%async_computation.1 | async-start | bytes 3145728 | tf_op jit(solution)/shard_map/all_to_all | solution.py:69
  61.1 2.7 %convolution_add_fusion.3 = f32[192,256]{1,0:T(8,128)S(1)} fusion(bf16[192,4096]{1,0:T(8,128)(2,1)} %bitcast.2, bf16[4096,256]{1,0:T(8,128)(2,1)} %param.8, f32[256]{0:T(256)S(1)} %copy-done.4), kind=kOutput, calls=%fused_computation.12 | convolution fusion | flops 402702336 | bytes 3867648 | tf_op jit(solution)/shard_map/dot_general | solution.py:26
  63.8 15.5 %all-to-all-done.1 = bf16[8,24,4096]{2,1,0:T(8,128)(2,1)} async-done(((bf16[8,24,4096]{2,1,0:T(8,128)(2,1)}), bf16[8,24,4096]{2,1,0:T(8,128)(2,1)}, u32[]{:S(2)}, u32[]{:S(2)}) %all-to-all-start.1) | async-done | bytes 1572896 | tf_op jit(solution)/shard_map/all_to_all | solution.py:69
  79.3 2.7 %broadcast_select_fusion.3 = (bf16[192,256]{1,0:T(8,128)(2,1)S(1)}, bf16[192,256]{1,0:T(8,128)(2,1)S(1)}, f32[192,256]{1,0:T(8,128)S(1)}) fusion(pred[]{:T(512)S(6)} %lt.31, s32[256]{0:T(256)S(1)} %and_select_fusion, s32[192]{0:T(256)S(1)} %get-tuple-element.22, f32[192,256]{1,0:T(8,128)S(1)} %convolution_add_fusion.3, f32[256]{0:T(256)S(1)} %copy-done.4, ...), kind=kOutput, calls=%fused_computation.50 | convolution fusion | flops 403832832 | bytes 4262657 | tf_op jit(solution)/shard_map/dot_general | solution.py:26
  82.0 2.7 %convolution_convert_fusion = bf16[384,4096]{1,0:T(8,128)(2,1)} fusion(bf16[256,4096]{1,0:T(8,128)(2,1)S(1)} %copy-done, bf16[192,256]{1,0:T(8,128)(2,1)S(1)} %get-tuple-element.19, bf16[192,256]{1,0:T(8,128)(2,1)S(1)} %get-tuple-element.18), kind=kOutput, calls=%fused_computation | convolution fusion | flops 807272448 | bytes 5439488 | tf_op jit(solution)/shard_map/dot_general | solution.py:26
  84.7 6.7 %all-to-all-start.2 = ((bf16[16,24,4096]{2,1,0:T(8,128)(2,1)}), bf16[16,24,4096]{2,1,0:T(8,128)(2,1)}, u32[]{:S(2)}, u32[]{:S(2)}) async-start(bf16[16,24,4096]{2,1,0:T(8,128)(2,1)} %bitcast.29), calls=%async_computation.2 | async-start | bytes 6291456 | tf_op jit(solution)/shard_map/all_to_all | solution.py:69
  93.0 12.5 %collective-permute-done.3 = f32[8,128]{1,0:T(8,128)S(1)} collective-permute-done((f32[8,128]{1,0:T(8,128)S(1)}, f32[8,128]{1,0:T(8,128)S(1)}, u32[]{:S(2)}, u32[]{:S(2)}) %collective-permute-start.3) | collective-permute-done | bytes 4128 | tf_op jit(solution)/shard_map/ppermute | solution.py:74
  105.9 38.7 %collective-permute-done.4 = f32[8,128]{1,0:T(8,128)S(1)} collective-permute-done((f32[8,128]{1,0:T(8,128)S(1)}, f32[8,128]{1,0:T(8,128)S(1)}, u32[]{:S(2)}, u32[]{:S(2)}) %collective-permute-start.4) | collective-permute-done | bytes 4128 | tf_op jit(solution)/shard_map/ppermute | solution.py:74
  144.8 14.6 %collective-permute-done.5 = f32[8,128]{1,0:T(8,128)S(1)} collective-permute-done((f32[8,128]{1,0:T(8,128)S(1)}, f32[8,128]{1,0:T(8,128)S(1)}, u32[]{:S(2)}, u32[]{:S(2)}) %collective-permute-start.5) | collective-permute-done | bytes 4128 | tf_op jit(solution)/shard_map/ppermute | solution.py:74
  159.3 2.2 all-to-all-done.2
  161.6 3.7 %fusion.28 = (bf16[128,4096]{1,0:T(8,128)(2,1)}, f32[128,4096]{1,0:T(8,128)S(1)}) fusion(pred[384,128]{1,0:T(8,128)(4,1)S(1)} %fusion.2, bf16[384,4096]{1,0:T(8,128)(2,1)} %bitcast.6, f32[4096]{0:T(1024)S(1)} %copy-done.2), kind=kOutput, calls=%fused_computation.66 | convolution fusion | flops 403701760 | bytes 6356992 | tf_op jit(solution)/shard_map/dot_general | solution.py:26
  165.3 2.7 %convolution_convert_fusion.1 = bf16[384,4096]{1,0:T(8,128)(2,1)} fusion(pred[384,128]{1,0:T(8,128)(4,1)S(1)} %fusion.2, f32[128,4096]{1,0:T(8,128)S(1)} %get-tuple-element.26, bf16[128,4096]{1,0:T(8,128)(2,1)S(1)} %copy-done.1), kind=kOutput, calls=%fused_computation.1 | convolution fusion | flops 405798912 | bytes 6340608 | tf_op jit(solution)/shard_map/dot_general | solution.py:26
  168.0 6.0 %all-to-all-start.3 = ((bf16[16,24,4096]{2,1,0:T(8,128)(2,1)}), bf16[16,24,4096]{2,1,0:T(8,128)(2,1)}, u32[]{:S(2)}, u32[]{:S(2)}) async-start(bf16[16,24,4096]{2,1,0:T(8,128)(2,1)} %bitcast.28), calls=%async_computation.3 | async-start | bytes 6291456 | tf_op jit(solution)/shard_map/all_to_all | solution.py:69
  175.4 68.5 %all-to-all-done.3 = bf16[16,24,4096]{2,1,0:T(8,128)(2,1)} async-done(((bf16[16,24,4096]{2,1,0:T(8,128)(2,1)}), bf16[16,24,4096]{2,1,0:T(8,128)(2,1)}, u32[]{:S(2)}, u32[]{:S(2)}) %all-to-all-start.3) | async-done | bytes 3145760 | tf_op jit(solution)/shard_map/all_to_all | solution.py:69
  244.0 4.5 %fusion.1 = bf16[256,4096]{1,0:T(8,128)(2,1)} fusion(bf16[384,4096]{1,0:T(8,128)(2,1)} %bitcast.8, f32[]{:T(128)} %bitcast.9, bf16[192,256]{1,0:T(8,128)(2,1)S(1)} %get-tuple-element.19, bf16[192,256]{1,0:T(8,128)(2,1)S(1)} %get-tuple-element.18), kind=kOutput, calls=%fused_computation.5 | convolution fusion | flops 807796736 | bytes 5439492 | tf_op jit(solution)/shard_map/dot_general | solution.py:26
  248.5 3.5 %fusion.27 = (f32[256]{0:T(256)}, bf16[384,256]{1,0:T(8,128)(2,1)S(1)}) fusion(f32[]{:T(128)} %bitcast.9, f32[192,256]{1,0:T(8,128)S(1)} %get-tuple-element.17, f32[192,256]{1,0:T(8,128)S(1)} %get-tuple-element.16, bf16[384,4096]{1,0:T(8,128)(2,1)} %bitcast.8, bf16[256,4096]{1,0:T(8,128)(2,1)S(1)} %copy-done), kind=kOutput, calls=%fused_computation.65 | convolution fusion | flops 805797632 | bytes 5833732 | tf_op jit(solution)/shard_map/dot_general | solution.py:26
  251.9 2.2 fusion.16
  254.1 3.6 %fusion = bf16[4096,256]{1,0:T(8,128)(2,1)} fusion(f32[4096,256]{1,0:T(8,128)S(1)} %fusion.16, bf16[192,4096]{1,0:T(8,128)(2,1)} %bitcast.2, pred[]{:T(512)S(6)} %lt.31, bf16[384,256]{1,0:T(8,128)(2,1)S(1)} %get-tuple-element.21), kind=kOutput, calls=%fused_computation.4 | convolution fusion | flops 404799488 | bytes 8060929 | tf_op jit(solution)/shard_map/dot_general | solution.py:26
  (36 shorter events, 5.3 us)
Async XLA Ops:
  0.6 81.4 %copy-start = (bf16[256,4096]{1,0:T(8,128)(2,1)S(1)}, bf16[256,4096]{1,0:T(8,128)(2,1)}, u32[]{:S(2)}) copy-start(bf16[256,4096]{1,0:T(8,128)(2,1)} %param.10) | copy-start | bytes 6291460
  2.8 12.7 %collective-permute-start.1 = (s32[2,128]{1,0:T(2,128)S(1)}, s32[2,128]{1,0:T(2,128)S(1)}, u32[]{:S(2)}, u32[]{:S(2)}) collective-permute-start(s32[2,128]{1,0:T(2,128)S(1)} %add_bitcast_fusion), channel_id=1, source_target_pairs={{0,8},{1,9},{2,10},{3,11},{4,12},{5,13},{6,14},{7,15},{8,0},{9,1},... | collective-permute-start | bytes 3080 | tf_op jit(solution)/shard_map/ppermute | solution.py:74
  5.1 45.7 %collective-permute-start = (bf16[128,4096]{1,0:T(8,128)(2,1)}, bf16[128,4096]{1,0:T(8,128)(2,1)S(1)}, u32[]{:S(2)}, u32[]{:S(2)}) collective-permute-start(bf16[128,4096]{1,0:T(8,128)(2,1)} %rows_ref.1), channel_id=1, source_target_pairs={{0,8},{1,9},{2,10},{3,11},{4,12},{5,13},{6,14},{7,15},{8,0},{9,1},... | collective-permute-start | bytes 3145736 | tf_op jit(solution)/shard_map/ppermute | solution.py:74
  8.3 42.6 %all-to-all-start = ((bf16[8,24,4096]{2,1,0:T(8,128)(2,1)}), bf16[8,24,4096]{2,1,0:T(8,128)(2,1)}, u32[]{:S(2)}, u32[]{:S(2)}) async-start(bf16[8,24,4096]{2,1,0:T(8,128)(2,1)} %bitcast.30), calls=%async_computation | async-start | bytes 3145728 | tf_op jit(solution)/shard_map/all_to_all | solution.py:69
  52.6 8.5 %copy-start.4 = (f32[256]{0:T(256)S(1)}, f32[256]{0:T(256)}, u32[]{:S(2)}) copy-start(f32[256]{0:T(256)} %param.9) | copy-start | bytes 3076
  52.6 26.6 %all-to-all-start.1 = ((bf16[8,24,4096]{2,1,0:T(8,128)(2,1)}), bf16[8,24,4096]{2,1,0:T(8,128)(2,1)}, u32[]{:S(2)}, u32[]{:S(2)}) async-start(bf16[8,24,4096]{2,1,0:T(8,128)(2,1)} %bitcast.31), calls=%async_computation.1 | async-start | bytes 3145728 | tf_op jit(solution)/shard_map/all_to_all | solution.py:69
  84.7 6.8 %copy-start.3 = (f32[8,128]{1,0:T(8,128)S(1)}, f32[8,128]{1,0:T(8,128)}, u32[]{:S(2)}) copy-start(f32[8,128]{1,0:T(8,128)} %squares.1) | copy-start | bytes 12292
  84.7 76.9 %copy-start.2 = (f32[4096]{0:T(1024)S(1)}, f32[4096]{0:T(1024)}, u32[]{:S(2)}) copy-start(f32[4096]{0:T(1024)} %param.11) | copy-start | bytes 49156
  84.7 76.9 %all-to-all-start.2 = ((bf16[16,24,4096]{2,1,0:T(8,128)(2,1)}), bf16[16,24,4096]{2,1,0:T(8,128)(2,1)}, u32[]{:S(2)}, u32[]{:S(2)}) async-start(bf16[16,24,4096]{2,1,0:T(8,128)(2,1)} %bitcast.29), calls=%async_computation.2 | async-start | bytes 6291456 | tf_op jit(solution)/shard_map/all_to_all | solution.py:69
  91.5 1.3 collective-permute-start.2
  92.8 12.8 %collective-permute-start.3 = (f32[8,128]{1,0:T(8,128)S(1)}, f32[8,128]{1,0:T(8,128)S(1)}, u32[]{:S(2)}, u32[]{:S(2)}) collective-permute-start(f32[8,128]{1,0:T(8,128)S(1)} %add.107), channel_id=1, source_target_pairs={{0,2},{1,3},{2,0},{3,1},{4,6},{5,7},{6,4},{7,5},{8,10},{9,11},{10,... | collective-permute-start | bytes 12296 | tf_op jit(solution)/shard_map/ppermute | solution.py:74
  105.5 39.0 %collective-permute-start.4 = (f32[8,128]{1,0:T(8,128)S(1)}, f32[8,128]{1,0:T(8,128)S(1)}, u32[]{:S(2)}, u32[]{:S(2)}) collective-permute-start(f32[8,128]{1,0:T(8,128)S(1)} %add.108), channel_id=1, source_target_pairs={{0,4},{1,5},{2,6},{3,7},{4,0},{5,1},{6,2},{7,3},{8,12},{9,13},{10,... | collective-permute-start | bytes 12296 | tf_op jit(solution)/shard_map/ppermute | solution.py:74
  144.6 14.7 %collective-permute-start.5 = (f32[8,128]{1,0:T(8,128)S(1)}, f32[8,128]{1,0:T(8,128)S(1)}, u32[]{:S(2)}, u32[]{:S(2)}) collective-permute-start(f32[8,128]{1,0:T(8,128)S(1)} %add.109), channel_id=1, source_target_pairs={{0,8},{1,9},{2,10},{3,11},{4,12},{5,13},{6,14},{7,15},{8,0},{9,1},... | collective-permute-start | bytes 12296 | tf_op jit(solution)/shard_map/ppermute | solution.py:74
  161.6 3.7 %copy-start.1 = (bf16[128,4096]{1,0:T(8,128)(2,1)S(1)}, bf16[128,4096]{1,0:T(8,128)(2,1)}, u32[]{:S(2)}) copy-start(bf16[128,4096]{1,0:T(8,128)(2,1)} %rows_ref.1) | copy-start | bytes 3145732
  168.0 76.0 %all-to-all-start.3 = ((bf16[16,24,4096]{2,1,0:T(8,128)(2,1)}), bf16[16,24,4096]{2,1,0:T(8,128)(2,1)}, u32[]{:S(2)}, u32[]{:S(2)}) async-start(bf16[16,24,4096]{2,1,0:T(8,128)(2,1)} %bitcast.28), calls=%async_computation.3 | async-start | bytes 6291456 | tf_op jit(solution)/shard_map/all_to_all | solution.py:69

commit v3 on v2

--- a/solution.py
+++ b/solution.py
@@ -7,6 +7,8 @@
 
 BLOCK = 64
 LOSS_SCALE = 0.5
+PIECES = 4
+VMEM_LIMIT = 32 * 1024 * 1024
 F32 = jnp.float32
 BF16 = jnp.bfloat16
 
@@ -50,6 +52,149 @@
         ),
         name="squares",
     )(rows)
+
+
+def home_kernel(select_ref, select_t_ref, returned_ref, act_ref, bias_ref, full_ref, send_ref):
+    full = bias_ref[...] + dot(select_t_ref[...], returned_ref[...], 1, 0)
+    full_ref[...] = full.astype(BF16)
+    errors = (full - act_ref[...].astype(F32)).astype(BF16)
+    send_ref[...] = dot(select_ref[...], errors, 1, 0).astype(BF16)
+
+
+def rebuild(select, select_t, returned, activations, dec_bias):
+    slots, tokens = select.shape
+    features = activations.shape[1]
+    width = features // PIECES
+
+    def columns(rows):
+        return pl.BlockSpec((rows, width), lambda i: (0, i))
+
+    def whole(rows, cols):
+        return pl.BlockSpec((rows, cols), lambda i: (0, 0))
+
+    return pl.pallas_call(
+        home_kernel,
+        grid=(PIECES,),
+        out_shape=[
+            jax.ShapeDtypeStruct((tokens, features), BF16),
+            jax.ShapeDtypeStruct((slots, features), BF16),
+        ],
+        in_specs=[
+            whole(slots, tokens),
+            whole(tokens, slots),
+            columns(slots),
+            columns(tokens),
+            columns(1),
+        ],
+        out_specs=[columns(tokens), columns(slots)],
+        cost_estimate=pl.CostEstimate(
+            flops=4 * slots * tokens * features,
+            bytes_accessed=4 * (slots + tokens) * features,
+            transcendentals=0,
+        ),
+        compiler_params=pltpu.CompilerParams(vmem_limit_bytes=VMEM_LIMIT),
+        name="rebuild",
+    )(select, select_t, returned, activations, dec_bias)
+
+
+def grads_kernel(
+    count,
+    flag_ref,
+    squares_ref,
+    code_t_ref,
+    slopes_ref,
+    got_ref,
+    dec_ref,
+    own_ref,
+    held_ref,
+    dec_grad_ref,
+    enc_grad_ref,
+    bias_grad_ref,
+    total_ref,
+    code_grad_ref,
+):
+    step = pl.program_id(0)
+    scale = LOSS_SCALE / (squares_ref[0:1, 0:1] / count + 1e-06)
+
+    @pl.when(step < PIECES)
+    def _():
+        got = got_ref[...]
+        part = dot(got, dec_ref[...], 1, 1)
+        dec_grad_ref[...] = (dot(code_t_ref[...], got, 1, 0) * scale).astype(BF16)
+
+        @pl.when(step == 0)
+        def _():
+            total_ref[...] = part
+
+        @pl.when(step > 0)
+        def _():
+            total_ref[...] += part
+
+    @pl.when(step == PIECES - 1)
+    def _():
+        code_grad = total_ref[...] * (slopes_ref[...] * scale)
+        bias_grad_ref[...] = jnp.sum(code_grad, axis=0, keepdims=True)
+        code_grad_ref[...] = code_grad.astype(BF16)
+
+    @pl.when(step >= PIECES)
+    def _():
+        rows = own_ref.shape[0]
+        flag = flag_ref[0]
+        grad_own = code_grad_ref[pl.ds(pl.multiple_of(flag * rows, rows), rows), :]
+        grad_held = code_grad_ref[pl.ds(pl.multiple_of((1 - flag) * rows, rows), rows), :]
+        enc_grad = dot(own_ref[...], grad_own, 0, 0) + dot(held_ref[...], grad_held, 0, 0)
+        enc_grad_ref[...] = enc_grad.astype(BF16)
+
+
+def gradients(count, flag, squares, code_t, slopes, got_errors, dec_weight, own_rows, held_rows):
+    latents, slots = code_t.shape
+    features = dec_weight.shape[1]
+    width = features // PIECES
+    half_slots = own_rows.shape[0]
+
+    def early(rows):
+        return pl.BlockSpec((rows, width), lambda i, _: (0, jnp.minimum(i, PIECES - 1)))
+
+    def late(rows):
+        return pl.BlockSpec((rows, width), lambda i, _: (0, jnp.maximum(i - PIECES, 0)))
+
+    def whole(rows, cols):
+        return pl.BlockSpec((rows, cols), lambda i, _: (0, 0))
+
+    return pl.pallas_call(
+        lambda *refs: grads_kernel(count, *refs),
+        grid_spec=pltpu.PrefetchScalarGridSpec(
+            num_scalar_prefetch=1,
+            grid=(2 * PIECES,),
+            in_specs=[
+                whole(8, 128),
+                whole(latents, slots),
+                whole(slots, latents),
+                early(slots),
+                early(latents),
+                late(half_slots),
+                late(half_slots),
+            ],
+            out_specs=[
+                early(latents),
+                pl.BlockSpec((width, latents), lambda i, _: (jnp.maximum(i - PIECES, 0), 0)),
+                whole(1, latents),
+            ],
+            scratch_shapes=[pltpu.VMEM((slots, latents), F32), pltpu.VMEM((slots, latents), BF16)],
+        ),
+        out_shape=[
+            jax.ShapeDtypeStruct((latents, features), BF16),
+            jax.ShapeDtypeStruct((features, latents), BF16),
+            jax.ShapeDtypeStruct((1, latents), F32),
+        ],
+        cost_estimate=pl.CostEstimate(
+            flops=6 * slots * latents * features,
+            bytes_accessed=2 * features * (2 * slots + 3 * latents),
+            transcendentals=0,
+        ),
+        compiler_params=pltpu.CompilerParams(vmem_limit_bytes=VMEM_LIMIT),
+        name="gradients",
+    )(flag, squares, code_t, slopes, got_errors, dec_weight, own_rows, held_rows)
 
 
 def per_device(activations, block_ids, enc_weight, enc_bias, dec_weight, dec_bias):
@@ -93,6 +238,7 @@
         return jnp.any(names[:, None, None] == slot[None, :, :], axis=1).astype(BF16)
 
     select = selection(slot_of, slots)
+    select_t = jnp.any(slots[None, :, None] == slot_of.T[:, None, :], axis=2).astype(BF16)
     names = slots[:half_slots] + jnp.where(lower, 0, half_slots)
 
     got_own = exchange(pick(selection(slot_of, names), activations), halves)
@@ -121,21 +267,20 @@
         squares = squares + swap(squares, step)
         step *= 2
     returned, squares = together(returned, squares)
-    full = dec_bias[None, :] + dot(select, returned, 0, 0)
-    errors = (full - activations.astype(F32)).astype(BF16)
-    got_errors = exchange(pick(select, errors))
-
-    mean_square = squares[0, 0] / (tok_rows * devices * feature_dim) + 1e-06
-    scale = LOSS_SCALE / mean_square
-    code_grad = dot(got_errors, dec_weight, 1, 1) * (slopes * scale)
-    bias_grad = jnp.sum(code_grad, axis=0)
-    code_grad = code_grad.astype(BF16)
-    lower_grad, upper_grad = code_grad[:half_slots], code_grad[half_slots:]
-    grad_own = jnp.where(lower, lower_grad, upper_grad)
-    grad_held = jnp.where(lower, upper_grad, lower_grad)
-    enc_grad = (dot(got_own, grad_own, 0, 0) + dot(got_held, grad_held, 0, 0)).astype(BF16)
-    dec_grad = (dot(code_rows, got_errors, 0, 0) * scale).astype(BF16)
-    return (full.astype(BF16), enc_grad, dec_grad, bias_grad)
+    full, send_errors = rebuild(select, select_t, returned, activations, dec_bias[None, :])
+    got_errors = exchange(send_errors)
+    dec_grad, enc_grad, bias_grad = gradients(
+        tok_rows * devices * feature_dim,
+        jnp.where(lower, 0, 1).astype(jnp.int32).reshape(1),
+        squares,
+        code_rows.T,
+        slopes,
+        got_errors,
+        dec_weight,
+        got_own,
+        got_held,
+    )
+    return (full, enc_grad, dec_grad, bias_grad.reshape(local_latents))
 
 
 def solution(mesh):

time: 258 us -> 256 us (level)
  matrix products: 32.8 us -> 12.1 us
  Pallas kernels: 2.14 us -> 16.4 us
  local copies, waits for them, and re-layouts: 1.82 us -> 4.76 us
    dot_general x11 -> x5, matrix products: 32.8 us -> 12.1 us  [dot(): return lax.dot_general(left, right, dims, preferred_element_type=F32)]
    pallas_call x0 -> x2, Pallas kernels: none -> 14.3 us  [the longest x1 9.64 us: gradients(): pl.pallas_call(lambda *refs: grads_kernel(count, *refs), grid_spec=pltpu....]
    unnamed x11 -> x27, local copies, waits for them, and re-layouts: 0.96 us -> 4.26 us
  transfers between devices with their start and end apart: 10 -> 10, of which waited for: 8 -> 8; matrix products, arithmetic and copies ran while one was open for 3% -> 2% of each run, Pallas kernels for 1% -> 1%
where the time goes in v3:
time: 256 us; the launch traced here: 255 us
  waiting for transfers between devices  190 us (74%)
  starting transfers between devices  30.1 us (12%)
  Pallas kernels  16.4 us (6%)
  matrix products  12.1 us (5%)
  local copies, waits for them, and re-layouts  4.76 us (2%)
    ppermute x6, waiting for transfers between devices, swap(): return lax.ppermute(rows, 'lat', [(i, i ^ step) for i in range(devices)])  102 us
    all_to_all x4, waiting for transfers between devices, exchange(): lax.all_to_all(rows, 'lat', split_axis=0, concat_axis=0, axis_index_group...  87.9 us
    all_to_all x4, starting transfers between devices, exchange(): lax.all_to_all(rows, 'lat', split_axis=0, concat_axis=0, axis_index_group...  26.5 us
    dot_general x5, matrix products, dot(): return lax.dot_general(left, right, dims, preferred_element_type=F32)  12.1 us
    pallas_call x1, Pallas kernels, gradients(): pl.pallas_call(lambda *refs: grads_kernel(count, *refs), grid_spec=pltpu....  9.64 us
  transfers between devices with their start and end apart: 10, of which 8 were waited for; matrix products, arithmetic and copies ran while one was open for 2% of the time, Pallas kernels for 1%

profile of v3, /device:TPU:13, one launch (start us, length us, event | category | flops | bytes accessed | tf_op | source)
XLA Modules:
  0.0 255.5 jit_solution(9843007199598549095)
XLA Ops:
  0.6 0.9 copy.27
  2.8 2.3 collective-permute-start.1
  5.3 2.9 %convolution_convert_fusion.2 = bf16[192,4096]{1,0:T(8,128)(2,1)} fusion(pred[192,128]{1,0:T(8,128)(4,1)S(1)} %compare_reduce_fusion.1, bf16[128,4096]{1,0:T(8,128)(2,1)} %act_ref.1), kind=kOutput, calls=%fused_computation.2 | convolution fusion | flops 202113024 | bytes 2646016 | tf_op jit(solution)/shard_map/dot_general | solution.py:28
  8.3 5.2 %all-to-all-start = ((bf16[8,24,4096]{2,1,0:T(8,128)(2,1)}), bf16[8,24,4096]{2,1,0:T(8,128)(2,1)}, u32[]{:S(2)}, u32[]{:S(2)}) async-start(bf16[8,24,4096]{2,1,0:T(8,128)(2,1)} %bitcast.26), calls=%async_computation | async-start | bytes 3145728 | tf_op jit(solution)/shard_map/all_to_all | solution.py:214
  13.4 2.1 squares.1
  15.6 35.2 %collective-permute-done = bf16[128,4096]{1,0:T(8,128)(2,1)S(1)} collective-permute-done((bf16[128,4096]{1,0:T(8,128)(2,1)}, bf16[128,4096]{1,0:T(8,128)(2,1)S(1)}, u32[]{:S(2)}, u32[]{:S(2)}) %collective-permute-start) | collective-permute-done | bytes 1048608 | tf_op jit(solution)/shard_map/ppermute | solution.py:219
  50.9 1.7 convolution_convert_fusion.1
  52.6 8.5 %all-to-all-start.1 = ((bf16[8,24,4096]{2,1,0:T(8,128)(2,1)}), bf16[8,24,4096]{2,1,0:T(8,128)(2,1)}, u32[]{:S(2)}, u32[]{:S(2)}) async-start(bf16[8,24,4096]{2,1,0:T(8,128)(2,1)} %bitcast.27), calls=%async_computation.1 | async-start | bytes 3145728 | tf_op jit(solution)/shard_map/all_to_all | solution.py:214
  61.1 2.0 convolution_add_fusion.1
  63.1 16.2 %all-to-all-done.1 = bf16[8,24,4096]{2,1,0:T(8,128)(2,1)} async-done(((bf16[8,24,4096]{2,1,0:T(8,128)(2,1)}), bf16[8,24,4096]{2,1,0:T(8,128)(2,1)}, u32[]{:S(2)}, u32[]{:S(2)}) %all-to-all-start.1) | async-done | bytes 1572896 | tf_op jit(solution)/shard_map/all_to_all | solution.py:214
  79.3 2.8 %broadcast_select_fusion.3 = (bf16[192,256]{1,0:T(8,128)(2,1)S(1)}, bf16[192,256]{1,0:T(8,128)(2,1)S(1)}, f32[192,256]{1,0:T(8,128)}) fusion(pred[]{:T(512)S(6)} %lt.31, s32[256]{0:T(256)S(1)} %and_select_fusion, s32[192]{0:T(256)S(1)} %get-tuple-element.30, f32[192,256]{1,0:T(8,128)S(1)} %convolution_add_fusion.1, f32[256]{0:T(256)S(1)} %copy-done.12, ...), kind=kOutput, calls=%fused_computation.40 | convolution fusion | flops 403832832 | bytes 4262657 | tf_op jit(solution)/shard_map/dot_general | solution.py:28
  82.1 2.7 %convolution_convert_fusion = bf16[384,4096]{1,0:T(8,128)(2,1)} fusion(bf16[256,4096]{1,0:T(8,128)(2,1)S(1)} %copy-done.1, bf16[192,256]{1,0:T(8,128)(2,1)S(1)} %get-tuple-element.29, bf16[192,256]{1,0:T(8,128)(2,1)S(1)} %get-tuple-element.28), kind=kOutput, calls=%fused_computation | convolution fusion | flops 807272448 | bytes 5439488 | tf_op jit(solution)/shard_map/dot_general | solution.py:28
  84.8 6.8 %all-to-all-start.2 = ((bf16[16,24,4096]{2,1,0:T(8,128)(2,1)}), bf16[16,24,4096]{2,1,0:T(8,128)(2,1)}, u32[]{:S(2)}, u32[]{:S(2)}) async-start(bf16[16,24,4096]{2,1,0:T(8,128)(2,1)} %bitcast.25), calls=%async_computation.2 | async-start | bytes 6291456 | tf_op jit(solution)/shard_map/all_to_all | solution.py:214
  92.0 0.9 collective-permute-done.2
  93.2 12.5 %collective-permute-done.3 = f32[8,128]{1,0:T(8,128)S(1)} collective-permute-done((f32[8,128]{1,0:T(8,128)S(1)}, f32[8,128]{1,0:T(8,128)S(1)}, u32[]{:S(2)}, u32[]{:S(2)}) %collective-permute-start.3) | collective-permute-done | bytes 4128 | tf_op jit(solution)/shard_map/ppermute | solution.py:219
  106.1 38.6 %collective-permute-done.4 = f32[8,128]{1,0:T(8,128)S(1)} collective-permute-done((f32[8,128]{1,0:T(8,128)S(1)}, f32[8,128]{1,0:T(8,128)S(1)}, u32[]{:S(2)}, u32[]{:S(2)}) %collective-permute-start.4) | collective-permute-done | bytes 4128 | tf_op jit(solution)/shard_map/ppermute | solution.py:219
  145.0 14.5 %collective-permute-done.5 = f32[8,128]{1,0:T(8,128)S(1)} collective-permute-done((f32[8,128]{1,0:T(8,128)S(1)}, f32[8,128]{1,0:T(8,128)S(1)}, u32[]{:S(2)}, u32[]{:S(2)}) %collective-permute-start.5) | collective-permute-done | bytes 4128 | tf_op jit(solution)/shard_map/ppermute | solution.py:219
  159.5 2.2 all-to-all-done.2
  161.7 4.7 %rebuild.1 = (bf16[128,4096]{1,0:T(8,128)(2,1)}, bf16[384,4096]{1,0:T(8,128)(2,1)S(1)}) custom-call(bf16[384,128]{1,0:T(8,128)(2,1)S(1)} %convert_element_type.27.select_ref, bf16[128,384]{1,0:T(8,128)(2,1)S(1)} %convert_element_type.28.select_t_ref, bf16[384,4096]{1,0:T(8,128)(2,1)} %bitcast.6.returned_ref, bf16[128,4096]{1,0:T(8,128)(2,1)S(1)} %copy-done.3, ...), custom_call_target="tpu_custom_call" | custom-call | flops 805306368 | bytes 8388608 | tf_op jit(solution)/shard_map/rebuild/pallas_call | solution.py:75
  166.4 1.7 copy-done.4
  168.1 6.1 %all-to-all-start.3 = ((bf16[16,24,4096]{2,1,0:T(8,128)(2,1)}), bf16[16,24,4096]{2,1,0:T(8,128)(2,1)}, u32[]{:S(2)}, u32[]{:S(2)}) async-start(bf16[16,24,4096]{2,1,0:T(8,128)(2,1)} %bitcast.23), calls=%async_computation.3 | async-start | bytes 6291456 | tf_op jit(solution)/shard_map/all_to_all | solution.py:214
  174.7 69.5 %all-to-all-done.3 = bf16[16,24,4096]{2,1,0:T(8,128)(2,1)} async-done(((bf16[16,24,4096]{2,1,0:T(8,128)(2,1)}), bf16[16,24,4096]{2,1,0:T(8,128)(2,1)}, u32[]{:S(2)}, u32[]{:S(2)}) %all-to-all-start.3) | async-done | bytes 3145760 | tf_op jit(solution)/shard_map/all_to_all | solution.py:214
  244.2 1.6 copy-done.2
  245.8 9.6 %gradients.1 = (bf16[256,4096]{1,0:T(8,128)(2,1)}, bf16[4096,256]{1,0:T(8,128)(2,1)}, f32[1,256]{1,0:T(1,128)}) custom-call(s32[1]{0:T(128)} %bitcast.8.refs_0_, f32[8,128]{1,0:T(8,128)S(1)} %add.96.refs_1_, bf16[256,384]{1,0:T(8,128)(2,1)S(1)} %copy.29.refs_2_, f32[384,256]{1,0:T(8,128)S(1)} %pad_maximum_fusion.refs_3_, bf16[384,4096]{1,0:T(8,128)(2,1)} %bitcast.11.refs_4_, ...), custom_call_target="tpu_custom_call" | custom-call | flops 2415919104 | bytes 12582912 | tf_op jit(solution)/shard_map/gradients/pallas_call | solution.py:164
  (53 shorter events, 3.4 us)
Async XLA Ops:
  0.6 60.5 %copy-start = (bf16[4096,256]{1,0:T(8,128)(2,1)S(1)}, bf16[4096,256]{1,0:T(8,128)(2,1)}, u32[]{:S(2)}) copy-start(bf16[4096,256]{1,0:T(8,128)(2,1)} %param.8) | copy-start | bytes 6291460
  2.8 12.7 %collective-permute-start.1 = (s32[2,128]{1,0:T(2,128)S(1)}, s32[2,128]{1,0:T(2,128)S(1)}, u32[]{:S(2)}, u32[]{:S(2)}) collective-permute-start(s32[2,128]{1,0:T(2,128)S(1)} %bitcast.28), channel_id=1, source_target_pairs={{0,8},{1,9},{2,10},{3,11},{4,12},{5,13},{6,14},{7,15},{8,0},{9,1},... | collective-permute-start | bytes 3080 | tf_op jit(solution)/shard_map/ppermute | solution.py:219
  5.1 45.7 %collective-permute-start = (bf16[128,4096]{1,0:T(8,128)(2,1)}, bf16[128,4096]{1,0:T(8,128)(2,1)S(1)}, u32[]{:S(2)}, u32[]{:S(2)}) collective-permute-start(bf16[128,4096]{1,0:T(8,128)(2,1)} %act_ref.1), channel_id=1, source_target_pairs={{0,8},{1,9},{2,10},{3,11},{4,12},{5,13},{6,14},{7,15},{8,0},{9,1},... | collective-permute-start | bytes 3145736 | tf_op jit(solution)/shard_map/ppermute | solution.py:219
  8.3 42.6 %all-to-all-start = ((bf16[8,24,4096]{2,1,0:T(8,128)(2,1)}), bf16[8,24,4096]{2,1,0:T(8,128)(2,1)}, u32[]{:S(2)}, u32[]{:S(2)}) async-start(bf16[8,24,4096]{2,1,0:T(8,128)(2,1)} %bitcast.26), calls=%async_computation | async-start | bytes 3145728 | tf_op jit(solution)/shard_map/all_to_all | solution.py:214
  52.6 8.5 %copy-start.12 = (f32[256]{0:T(256)S(1)}, f32[256]{0:T(256)}, u32[]{:S(2)}) copy-start(f32[256]{0:T(256)} %param.9) | copy-start | bytes 3076
  52.6 26.7 %all-to-all-start.1 = ((bf16[8,24,4096]{2,1,0:T(8,128)(2,1)}), bf16[8,24,4096]{2,1,0:T(8,128)(2,1)}, u32[]{:S(2)}, u32[]{:S(2)}) async-start(bf16[8,24,4096]{2,1,0:T(8,128)(2,1)} %bitcast.27), calls=%async_computation.1 | async-start | bytes 3145728 | tf_op jit(solution)/shard_map/all_to_all | solution.py:214
  63.1 19.0 %copy-start.8 = (f32[192,256]{1,0:T(8,128)}, f32[192,256]{1,0:T(8,128)S(1)}, u32[]{:S(2)}) copy-start(f32[192,256]{1,0:T(8,128)S(1)} %convolution_add_fusion.1) | copy-start | bytes 589828
  79.3 2.8 %copy-start.1 = (bf16[256,4096]{1,0:T(8,128)(2,1)S(1)}, bf16[256,4096]{1,0:T(8,128)(2,1)}, u32[]{:S(2)}) copy-start(bf16[256,4096]{1,0:T(8,128)(2,1)} %refs_5_.1) | copy-start | bytes 6291460
  82.1 2.7 %copy-start.6 = (bf16[192,256]{1,0:T(8,128)(2,1)}, bf16[192,256]{1,0:T(8,128)(2,1)S(1)}, u32[]{:S(2)}) copy-start(bf16[192,256]{1,0:T(8,128)(2,1)S(1)} %get-tuple-element.29) | copy-start | bytes 294916
  84.8 6.8 %copy-start.11 = (f32[8,128]{1,0:T(8,128)S(1)}, f32[8,128]{1,0:T(8,128)}, u32[]{:S(2)}) copy-start(f32[8,128]{1,0:T(8,128)} %squares.1) | copy-start | bytes 12292
  84.8 76.9 %copy-start.3 = (bf16[128,4096]{1,0:T(8,128)(2,1)S(1)}, bf16[128,4096]{1,0:T(8,128)(2,1)}, u32[]{:S(2)}) copy-start(bf16[128,4096]{1,0:T(8,128)(2,1)} %act_ref.1) | copy-start | bytes 3145732
  84.8 76.9 %copy-start.5 = (f32[4096]{0:T(1024)S(1)}, f32[4096]{0:T(1024)}, u32[]{:S(2)}) copy-start(f32[4096]{0:T(1024)} %param.11) | copy-start | bytes 49156
  84.8 76.9 %all-to-all-start.2 = ((bf16[16,24,4096]{2,1,0:T(8,128)(2,1)}), bf16[16,24,4096]{2,1,0:T(8,128)(2,1)}, u32[]{:S(2)}, u32[]{:S(2)}) async-start(bf16[16,24,4096]{2,1,0:T(8,128)(2,1)} %bitcast.25), calls=%async_computation.2 | async-start | bytes 6291456 | tf_op jit(solution)/shard_map/all_to_all | solution.py:214
  91.6 1.3 collective-permute-start.2
  92.9 12.8 %collective-permute-start.3 = (f32[8,128]{1,0:T(8,128)S(1)}, f32[8,128]{1,0:T(8,128)S(1)}, u32[]{:S(2)}, u32[]{:S(2)}) collective-permute-start(f32[8,128]{1,0:T(8,128)S(1)} %add.93), channel_id=1, source_target_pairs={{0,2},{1,3},{2,0},{3,1},{4,6},{5,7},{6,4},{7,5},{8,10},{9,11},{10,... | collective-permute-start | bytes 12296 | tf_op jit(solution)/shard_map/ppermute | solution.py:219
  105.7 39.0 %collective-permute-start.4 = (f32[8,128]{1,0:T(8,128)S(1)}, f32[8,128]{1,0:T(8,128)S(1)}, u32[]{:S(2)}, u32[]{:S(2)}) collective-permute-start(f32[8,128]{1,0:T(8,128)S(1)} %add.94), channel_id=1, source_target_pairs={{0,4},{1,5},{2,6},{3,7},{4,0},{5,1},{6,2},{7,3},{8,12},{9,13},{10,... | collective-permute-start | bytes 12296 | tf_op jit(solution)/shard_map/ppermute | solution.py:219
  144.7 14.7 %collective-permute-start.5 = (f32[8,128]{1,0:T(8,128)S(1)}, f32[8,128]{1,0:T(8,128)S(1)}, u32[]{:S(2)}, u32[]{:S(2)}) collective-permute-start(f32[8,128]{1,0:T(8,128)S(1)} %add.95), channel_id=1, source_target_pairs={{0,8},{1,9},{2,10},{3,11},{4,12},{5,13},{6,14},{7,15},{8,0},{9,1},... | collective-permute-start | bytes 12296 | tf_op jit(solution)/shard_map/ppermute | solution.py:219
  166.4 1.7 copy-start.4
  168.1 6.1 %copy-start.7 = (bf16[192,256]{1,0:T(8,128)(2,1)S(1)}, bf16[192,256]{1,0:T(8,128)(2,1)}, u32[]{:S(2)}) copy-start(bf16[192,256]{1,0:T(8,128)(2,1)} %copy-done.6) | copy-start | bytes 294916
  168.1 6.3 %copy-start.9 = (f32[192,256]{1,0:T(8,128)S(1)}, f32[192,256]{1,0:T(8,128)}, u32[]{:S(2)}) copy-start(f32[192,256]{1,0:T(8,128)} %copy-done.8) | copy-start | bytes 589828
  168.1 6.3 %copy-start.10 = (f32[192,256]{1,0:T(8,128)S(1)}, f32[192,256]{1,0:T(8,128)}, u32[]{:S(2)}) copy-start(f32[192,256]{1,0:T(8,128)} %get-tuple-element.32) | copy-start | bytes 589828
  168.1 76.1 %all-to-all-start.3 = ((bf16[16,24,4096]{2,1,0:T(8,128)(2,1)}), bf16[16,24,4096]{2,1,0:T(8,128)(2,1)}, u32[]{:S(2)}, u32[]{:S(2)}) async-start(bf16[16,24,4096]{2,1,0:T(8,128)(2,1)} %bitcast.23), calls=%async_computation.3 | async-start | bytes 6291456 | tf_op jit(solution)/shard_map/all_to_all | solution.py:214
  244.2 1.6 copy-start.2

commit v4 on v2

--- a/solution.py
+++ b/solution.py
@@ -7,6 +7,9 @@
 
 BLOCK = 64
 LOSS_SCALE = 0.5
+PIECES = 2
+COPIES = 4
+VMEM_LIMIT = 32 * 1024 * 1024
 F32 = jnp.float32
 BF16 = jnp.bfloat16
 
@@ -50,6 +53,147 @@
         ),
         name="squares",
     )(rows)
+
+
+def pass_kernel(value_ref, same_ref):
+    same_ref[...] = value_ref[...]
+
+
+def beside(value):
+    return pl.pallas_call(
+        pass_kernel,
+        out_shape=jax.ShapeDtypeStruct(value.shape, value.dtype),
+        in_specs=[pl.BlockSpec(memory_space=pltpu.VMEM)],
+        out_specs=pl.BlockSpec(memory_space=pltpu.VMEM),
+        cost_estimate=pl.CostEstimate(flops=50_000_000_000, bytes_accessed=8192, transcendentals=0),
+        name="beside",
+    )(value)
+
+
+def home_kernel(select_t_ref, returned_ref, far_ref, act_ref, bias_ref, full_ref, errors_ref):
+    full = bias_ref[...] + dot(select_t_ref[...], returned_ref[...], 1, 0)
+    full = full + far_ref[...].astype(F32)
+    full_ref[...] = full.astype(BF16)
+    errors = (full - act_ref[...].astype(F32)).astype(BF16)
+    errors_ref[...] = errors
+
+
+def rebuild(select_t, returned, far, activations, dec_bias):
+    tokens, slots = select_t.shape
+    features = activations.shape[1]
+    width = features // PIECES
+
+    def columns(rows):
+        return pl.BlockSpec((rows, width), lambda i: (0, i))
+
+    def whole(rows, cols):
+        return pl.BlockSpec((rows, cols), lambda i: (0, 0))
+
+    return pl.pallas_call(
+        home_kernel,
+        grid=(PIECES,),
+        out_shape=[
+            jax.ShapeDtypeStruct((tokens, features), BF16),
+            jax.ShapeDtypeStruct((tokens, features), BF16),
+        ],
+        in_specs=[
+            whole(tokens, slots),
+            columns(slots),
+            columns(tokens),
+            columns(tokens),
+            columns(1),
+        ],
+        out_specs=[columns(tokens), columns(tokens)],
+        cost_estimate=pl.CostEstimate(
+            flops=2 * slots * tokens * features,
+            bytes_accessed=2 * (slots + 4 * tokens) * features,
+            transcendentals=0,
+        ),
+        compiler_params=pltpu.CompilerParams(vmem_limit_bytes=VMEM_LIMIT),
+        name="rebuild",
+    )(select_t, returned, far, activations, dec_bias)
+
+
+def grads_kernel(
+    count,
+    squares_ref,
+    code_own_ref,
+    code_held_ref,
+    slope_own_ref,
+    slope_held_ref,
+    dec_ref,
+    own_ref,
+    held_ref,
+    got_own_ref,
+    got_held_ref,
+    dec_grad_ref,
+    enc_grad_ref,
+    bias_grad_ref,
+    dec_out_ref,
+    enc_out_ref,
+    sems,
+):
+    scale = LOSS_SCALE / (squares_ref[0:1, 0:1] / count + 1e-06)
+    width = dec_ref.shape[1] // COPIES
+    copies = []
+    grad_own = grad_held = None
+    for i in range(COPIES):
+        piece = slice(i * width, (i + 1) * width)
+        got_own, got_held, dec = got_own_ref[:, piece], got_held_ref[:, piece], dec_ref[:, piece]
+        dec_grad = dot(code_own_ref[...], got_own, 1, 0) + dot(code_held_ref[...], got_held, 1, 0)
+        dec_out_ref[i] = (dec_grad * scale).astype(BF16)
+        copies.append(
+            pltpu.make_async_copy(dec_out_ref.at[i], dec_grad_ref.at[:, piece], sems.at[i])
+        )
+        copies[-1].start()
+        part_own, part_held = dot(got_own, dec, 1, 1), dot(got_held, dec, 1, 1)
+        grad_own = part_own if i == 0 else grad_own + part_own
+        grad_held = part_held if i == 0 else grad_held + part_held
+    grad_own = grad_own * (slope_own_ref[...] * scale)
+    grad_held = grad_held * (slope_held_ref[...] * scale)
+    bias_grad_ref[...] = jnp.sum(grad_own, axis=0, keepdims=True) + jnp.sum(
+        grad_held, axis=0, keepdims=True
+    )
+    grad_own, grad_held = grad_own.astype(BF16), grad_held.astype(BF16)
+    for i in range(COPIES):
+        piece = slice(i * width, (i + 1) * width)
+        enc_grad = dot(own_ref[:, piece], grad_own, 0, 0) + dot(held_ref[:, piece], grad_held, 0, 0)
+        enc_out_ref[i] = enc_grad.astype(BF16)
+        copies.append(
+            pltpu.make_async_copy(enc_out_ref.at[i], enc_grad_ref.at[piece], sems.at[COPIES + i])
+        )
+        copies[-1].start()
+    for copy in copies:
+        copy.wait()
+
+
+def gradients(count, squares, codes, slopes, dec_weight, rows, got):
+    latents, features = dec_weight.shape
+    slots = got[0].shape[0]
+    width = features // COPIES
+    vmem = pl.BlockSpec(memory_space=pltpu.VMEM)
+    return pl.pallas_call(
+        lambda *refs: grads_kernel(count, *refs),
+        out_shape=[
+            jax.ShapeDtypeStruct((latents, features), BF16),
+            jax.ShapeDtypeStruct((features, latents), BF16),
+            jax.ShapeDtypeStruct((1, latents), F32),
+        ],
+        in_specs=[vmem] * 10,
+        out_specs=[pl.BlockSpec(memory_space=pl.ANY)] * 2 + [vmem],
+        scratch_shapes=[
+            pltpu.VMEM((COPIES, latents, width), BF16),
+            pltpu.VMEM((COPIES, width, latents), BF16),
+            pltpu.SemaphoreType.DMA((2 * COPIES,)),
+        ],
+        cost_estimate=pl.CostEstimate(
+            flops=12 * slots * latents * features,
+            bytes_accessed=2 * features * (4 * slots + 3 * latents),
+            transcendentals=0,
+        ),
+        compiler_params=pltpu.CompilerParams(vmem_limit_bytes=VMEM_LIMIT),
+        name="gradients",
+    )(squares, codes[0].T, codes[1].T, *slopes, dec_weight, *rows, *got)
 
 
 def per_device(activations, block_ids, enc_weight, enc_bias, dec_weight, dec_bias):
@@ -65,16 +209,30 @@
     half_slots = half * dev_slots
     halves = [list(range(half)), list(range(half, devices))]
 
-    def exchange(rows, groups=None):
-        return lax.all_to_all(
-            rows, "lat", split_axis=0, concat_axis=0, axis_index_groups=groups, tiled=True
-        )
-
     def swap(rows, step=half):
         return lax.ppermute(rows, "lat", [(i, i ^ step) for i in range(devices)])
 
     def pick(select, rows):
         return dot(select, rows, 1, 0).astype(BF16)
+
+    def exchange(rows):
+        return lax.all_to_all(
+            rows, "lat", split_axis=0, concat_axis=0, axis_index_groups=halves, tiled=True
+        )
+
+    by_swaps = half <= 8
+
+    def exchange_held(left, right):
+        if not by_swaps:
+            return exchange(pick(left, right))
+        parts = [left[k * dev_slots : (k + 1) * dev_slots] for k in range(half)]
+        parts = [pick(part, right) for part in parts]
+        return jnp.concatenate(parts[:1] + [swap(parts[k], k) for k in range(1, half)], axis=0)
+
+    steps = [1 << i for i in range((devices - 1).bit_length())]
+
+    def more(squares):
+        return squares + swap(squares, steps.pop(0)) if steps else squares
 
     held = swap(activations)
     squares = sum_of_squares(activations)
@@ -86,56 +244,62 @@
     slot_of = flat_ids * capacity + jnp.sum(same.astype(jnp.int32), axis=1)
     slot_of = slot_of.reshape(tok_rows, active_count).T
     slot_held = swap(slot_of)
-    lower = lax.axis_index("lat") < half
-    slots = jnp.arange(2 * half_slots, dtype=jnp.int32)
+    me = lax.axis_index("lat")
+    slots = jnp.arange(half_slots, dtype=jnp.int32)
+    names = slots + (me // half) * half_slots
+    names_held = names
+    if by_swaps:
+        names_held = ((slots // dev_slots) ^ me) * dev_slots + slots % dev_slots
 
     def selection(slot, names):
         return jnp.any(names[:, None, None] == slot[None, :, :], axis=1).astype(BF16)
 
-    select = selection(slot_of, slots)
-    names = slots[:half_slots] + jnp.where(lower, 0, half_slots)
-
-    got_own = exchange(pick(selection(slot_of, names), activations), halves)
+    def selection_t(slot, names):
+        return jnp.any(names[None, None, :] == slot.T[:, :, None], axis=1).astype(BF16)
+
+    select = selection(slot_of, names)
+    got_own = exchange(pick(select, activations))
     held, slot_held, got_own, squares = together(held, slot_held, got_own, squares)
-    got_held = exchange(pick(selection(slot_held, names), held), halves)
-
-    row_block = (slots[:half_slots] % dev_slots) // capacity
+    select_held = selection(slot_held, names_held)
+    got_held = exchange_held(select_held, held)
+    got_held, squares = together(got_held, more(squares))
+
+    row_block = (slots % dev_slots) // capacity
     own = row_block[:, None] == (jnp.arange(local_latents, dtype=jnp.int32) // BLOCK)[None, :]
 
     def encode(rows):
         output, slopes = activate(dot(rows, enc_weight, 1, 0) + enc_bias[None, :])
         return jnp.where(own, output, 0.0).astype(BF16), jnp.where(own, slopes, 0.0)
 
-    def ordered(own_part, held_part):
-        first = jnp.where(lower, own_part, held_part)
-        second = jnp.where(lower, held_part, own_part)
-        return jnp.concatenate([first, second], axis=0)
-
     code_own, slope_own = encode(got_own)
     code_held, slope_held = encode(got_held)
-    code_rows, slopes = ordered(code_own, code_held), ordered(slope_own, slope_held)
-
-    returned = exchange(dot(code_rows, dec_weight, 1, 0).astype(BF16))
-    step = 1
-    while step < devices:
-        squares = squares + swap(squares, step)
-        step *= 2
-    returned, squares = together(returned, squares)
-    full = dec_bias[None, :] + dot(select, returned, 0, 0)
-    errors = (full - activations.astype(F32)).astype(BF16)
-    got_errors = exchange(pick(select, errors))
-
-    mean_square = squares[0, 0] / (tok_rows * devices * feature_dim) + 1e-06
-    scale = LOSS_SCALE / mean_square
-    code_grad = dot(got_errors, dec_weight, 1, 1) * (slopes * scale)
-    bias_grad = jnp.sum(code_grad, axis=0)
-    code_grad = code_grad.astype(BF16)
-    lower_grad, upper_grad = code_grad[:half_slots], code_grad[half_slots:]
-    grad_own = jnp.where(lower, lower_grad, upper_grad)
-    grad_held = jnp.where(lower, upper_grad, lower_grad)
-    enc_grad = (dot(got_own, grad_own, 0, 0) + dot(got_held, grad_held, 0, 0)).astype(BF16)
-    dec_grad = (dot(code_rows, got_errors, 0, 0) * scale).astype(BF16)
-    return (full.astype(BF16), enc_grad, dec_grad, bias_grad)
+
+    back_held = exchange_held(code_held, dec_weight)
+    back_held, code_own, squares, dec_bias = together(
+        back_held, code_own, more(squares), dec_bias[None, :]
+    )
+    far = swap(pick(selection_t(slot_held, names_held), back_held))
+    back_own = exchange(pick(code_own, dec_weight))
+    far, back_own, squares, dec_bias = together(far, back_own, more(squares), beside(dec_bias))
+    while steps:
+        squares = more(squares)
+    full, errors = rebuild(selection_t(slot_of, names), back_own, far, activations, dec_bias)
+
+    errors, slope_own = together(errors, slope_own)
+    far = swap(errors)
+    err_own = exchange(pick(select, errors))
+    far, err_own, slope_own = together(far, err_own, beside(slope_own))
+    err_held = exchange_held(select_held, far)
+    dec_grad, enc_grad, bias_grad = gradients(
+        tok_rows * devices * feature_dim,
+        squares,
+        (code_own, code_held),
+        (slope_own, slope_held),
+        dec_weight,
+        (got_own, got_held),
+        (err_own, err_held),
+    )
+    return (full, enc_grad, dec_grad, bias_grad.reshape(local_latents))
 
 
 def solution(mesh):

time: 258 us -> 268 us (1.039); the launches traced: 258 us -> 264 us
  waiting for transfers between devices: 188 us -> 143 us
  starting transfers between devices: 29.9 us -> 58 us
  Pallas kernels: 2.14 us -> 15.5 us
  local copies, waits for them, and re-layouts: 1.82 us -> 10.7 us
    all_to_all x4 -> x3, waiting for transfers between devices: 86.3 us -> 11.6 us  [exchange(): lax.all_to_all(rows, 'lat', split_axis=0, concat_axis=0, axis_index_group...]
    ppermute x6 -> x29, starting transfers between devices: 3.52 us -> 37.8 us  [swap(): return lax.ppermute(rows, 'lat', [(i, i ^ step) for i in range(devices)])]
    ppermute x6 -> x29, waiting for transfers between devices: 102 us -> 131 us  [swap(): return lax.ppermute(rows, 'lat', [(i, i ^ step) for i in range(devices)])]
    pallas_call x0 -> x4, Pallas kernels: none -> 13.4 us  [the longest x1 7.3 us: gradients(): pl.pallas_call(lambda *refs: grads_kernel(count, *refs), out_shape=[jax.S...]
    unnamed x11 -> x49, local copies, waits for them, and re-layouts: 0.96 us -> 7.54 us
    all_to_all x4 -> x3, starting transfers between devices: 26.4 us -> 20.1 us  [exchange(): lax.all_to_all(rows, 'lat', split_axis=0, concat_axis=0, axis_index_group...]
    dot_general x11 -> x30, matrix products: 32.8 us -> 34 us  [dot(): return lax.dot_general(left, right, dims, preferred_element_type=F32)]
  transfers between devices with their start and end apart: 10 -> 32, of which waited for: 8 -> 18; matrix products, arithmetic and copies ran while one was open for 3% -> 8% of each run, Pallas kernels for 1% -> 2%
where the time goes in v4:
time: 268 us; the launch traced here: 264 us
  waiting for transfers between devices  143 us (53%)
  starting transfers between devices  58 us (22%)
  matrix products  34 us (13%)
  Pallas kernels  15.5 us (6%)
  local copies, waits for them, and re-layouts  10.7 us (4%)
    ppermute x29, waiting for transfers between devices, swap(): return lax.ppermute(rows, 'lat', [(i, i ^ step) for i in range(devices)])  131 us
    ppermute x29, starting transfers between devices, swap(): return lax.ppermute(rows, 'lat', [(i, i ^ step) for i in range(devices)])  37.8 us
    dot_general x30, matrix products, dot(): return lax.dot_general(left, right, dims, preferred_element_type=F32)  34 us
    all_to_all x3, starting transfers between devices, exchange(): lax.all_to_all(rows, 'lat', split_axis=0, concat_axis=0, axis_index_group...  20.1 us
    all_to_all x3, waiting for transfers between devices, exchange(): lax.all_to_all(rows, 'lat', split_axis=0, concat_axis=0, axis_index_group...  11.6 us
    unnamed x49, local copies, waits for them, and re-layouts  7.54 us
    pallas_call x1, Pallas kernels, gradients(): pl.pallas_call(lambda *refs: grads_kernel(count, *refs), out_shape=[jax.S...  7.3 us
  transfers between devices with their start and end apart: 32, of which 18 were waited for; matrix products, arithmetic and copies ran while one was open for 8% of the time, Pallas kernels for 2%

profile of v4, /device:TPU:13, one launch (start us, length us, event | category | flops | bytes accessed | tf_op | source)
XLA Modules:
  0.0 263.9 jit_solution(14712773366453208075)
XLA Ops:
  5.3 2.9 %convolution_convert_fusion.2 = bf16[192,4096]{1,0:T(8,128)(2,1)} fusion(pred[192,128]{1,0:T(8,128)(4,1)S(1)} %compare_reduce_fusion.2, bf16[128,4096]{1,0:T(8,128)(2,1)} %act_ref.1), kind=kOutput, calls=%fused_computation.2 | convolution fusion | flops 202113024 | bytes 2646016 | tf_op jit(solution)/shard_map/dot_general | solution.py:29
  8.2 5.2 %all-to-all-start = ((bf16[8,24,4096]{2,1,0:T(8,128)(2,1)}), bf16[8,24,4096]{2,1,0:T(8,128)(2,1)}, u32[]{:S(2)}, u32[]{:S(2)}) async-start(bf16[8,24,4096]{2,1,0:T(8,128)(2,1)} %bitcast.52), calls=%async_computation | async-start | bytes 3145728 | tf_op jit(solution)/shard_map/all_to_all | solution.py:219
  15.8 35.0 %collective-permute-done = bf16[128,4096]{1,0:T(8,128)(2,1)S(1)} collective-permute-done((bf16[128,4096]{1,0:T(8,128)(2,1)}, bf16[128,4096]{1,0:T(8,128)(2,1)S(1)}, u32[]{:S(2)}, u32[]{:S(2)}) %collective-permute-start) | collective-permute-done | bytes 1048608 | tf_op jit(solution)/shard_map/ppermute | solution.py:213
  61.3 4.3 %collective-permute-start.8 = (bf16[24,4096]{1,0:T(8,128)(2,1)S(1)}, bf16[24,4096]{1,0:T(8,128)(2,1)S(1)}, u32[]{:S(2)}, u32[]{:S(2)}) collective-permute-start(bf16[24,4096]{1,0:T(8,128)(2,1)S(1)} %convolution_convert_fusion.20), channel_id=1, source_target_pairs={{0,7},{1,6},{2,5},{3,4},{4,3},{5,2},{6,1},{7,0},{8,15},{9,14},{10,... | collective-permute-start | bytes 589832 | tf_op jit(solution)/shard_map/ppermute | solution.py:213
  66.5 2.6 collective-permute-done.6
  69.2 4.3 %collective-permute-done.7 = bf16[24,4096]{1,0:T(8,128)(2,1)S(1)} collective-permute-done((bf16[24,4096]{1,0:T(8,128)(2,1)S(1)}, bf16[24,4096]{1,0:T(8,128)(2,1)S(1)}, u32[]{:S(2)}, u32[]{:S(2)}) %collective-permute-start.7) | collective-permute-done | bytes 196640 | tf_op jit(solution)/shard_map/ppermute | solution.py:213
  73.5 4.2 %collective-permute-done.8 = bf16[24,4096]{1,0:T(8,128)(2,1)S(1)} collective-permute-done((bf16[24,4096]{1,0:T(8,128)(2,1)S(1)}, bf16[24,4096]{1,0:T(8,128)(2,1)S(1)}, u32[]{:S(2)}, u32[]{:S(2)}) %collective-permute-start.8) | collective-permute-done | bytes 196640 | tf_op jit(solution)/shard_map/ppermute | solution.py:213
  79.0 3.1 %compare_select_fusion = (f32[192,256]{1,0:T(8,128)}, bf16[192,256]{1,0:T(8,128)(2,1)S(1)}, bf16[192,256]{1,0:T(8,128)(2,1)S(1)}, f32[192,256]{1,0:T(8,128)}) fusion(f32[192,256]{1,0:T(8,128)S(1)} %get-tuple-element.59, s32[256]{0:T(256)} %copy-done.14, s32[192]{0:T(256)S(1)} %and_select_fusion.1, f32[256]{0:T(256)S(1)} %copy-done.13, ...), kind=kOutput, calls=%fused_computation.33 | convolution fusion | flops 404815872 | bytes 4459264 | tf_op jit(solution)/shard_map/dot_general | solution.py:29
  104.0 2.6 collective-permute-done.15
  107.3 3.9 %collective-permute-done.16 = bf16[24,4096]{1,0:T(8,128)(2,1)S(1)} collective-permute-done((bf16[24,4096]{1,0:T(8,128)(2,1)S(1)}, bf16[24,4096]{1,0:T(8,128)(2,1)S(1)}, u32[]{:S(2)}, u32[]{:S(2)}) %collective-permute-start.16) | collective-permute-done | bytes 196640 | tf_op jit(solution)/shard_map/ppermute | solution.py:213
  113.0 2.9 %convolution_convert_fusion.3 = bf16[128,4096]{1,0:T(8,128)(2,1)} fusion(pred[128,192]{0,1:T(8,128)(4,1)S(1)} %compare_reduce_fusion.1, bf16[192,4096]{1,0:T(8,128)(2,1)} %constant_dynamic-update-slice_fusion.7), kind=kOutput, calls=%fused_computation.3 | convolution fusion | flops 201850880 | bytes 2646016 | tf_op jit(solution)/shard_map/dot_general | solution.py:29
  115.9 2.4 collective-permute-start.18
  120.0 7.2 %all-to-all-start.1 = ((bf16[8,24,4096]{2,1,0:T(8,128)(2,1)}), bf16[8,24,4096]{2,1,0:T(8,128)(2,1)}, u32[]{:S(2)}, u32[]{:S(2)}) async-start(bf16[8,24,4096]{2,1,0:T(8,128)(2,1)} %bitcast.54), calls=%async_computation.1 | async-start | bytes 3145728 | tf_op jit(solution)/shard_map/all_to_all | solution.py:219
  129.7 33.6 %collective-permute-done.18.far_ref = bf16[128,4096]{1,0:T(8,128)(2,1)} collective-permute-done((bf16[128,4096]{1,0:T(8,128)(2,1)}, bf16[128,4096]{1,0:T(8,128)(2,1)}, u32[]{:S(2)}, u32[]{:S(2)}) %collective-permute-start.18) | collective-permute-done | bytes 1048608 | tf_op jit(solution)/shard_map/ppermute | solution.py:213
  163.3 3.6 %all-to-all-done.1 = bf16[8,24,4096]{2,1,0:T(8,128)(2,1)} async-done(((bf16[8,24,4096]{2,1,0:T(8,128)(2,1)}), bf16[8,24,4096]{2,1,0:T(8,128)(2,1)}, u32[]{:S(2)}, u32[]{:S(2)}) %all-to-all-start.1) | async-done | bytes 1572896 | tf_op jit(solution)/shard_map/all_to_all | solution.py:219
  167.6 3.0 %rebuild.1 = (bf16[128,4096]{1,0:T(8,128)(2,1)}, bf16[128,4096]{1,0:T(8,128)(2,1)}) custom-call(bf16[128,192]{1,0:T(8,128)(2,1)S(1)} %copy.33.select_t_ref, bf16[192,4096]{1,0:T(8,128)(2,1)} %bitcast.6.returned_ref, bf16[128,4096]{1,0:T(8,128)(2,1)} %collective-permute-done.18.far_ref, bf16[128,4096]{1,0:T(8,128)(2,1)S(1)} %copy-done.4, f32[1,4096]{1,0:T(1,128)S(1)} %copy-done.9), custom_call_target="tpu_custom_call" | custom-call | flops 201326592 | bytes 5767168 | tf_op jit(solution)/shard_map/rebuild/pallas_call | solution.py:92
  170.6 3.0 %convolution_convert_fusion = bf16[192,4096]{1,0:T(8,128)(2,1)} fusion(pred[192,128]{1,0:T(8,128)(4,1)S(1)} %compare_reduce_fusion.2, bf16[128,4096]{1,0:T(8,128)(2,1)} %get-tuple-element.44), kind=kOutput, calls=%fused_computation | convolution fusion | flops 202113024 | bytes 2646016 | tf_op jit(solution)/shard_map/dot_general | solution.py:29
  175.9 7.8 %all-to-all-start.2 = ((bf16[8,24,4096]{2,1,0:T(8,128)(2,1)}), bf16[8,24,4096]{2,1,0:T(8,128)(2,1)}, u32[]{:S(2)}, u32[]{:S(2)}) async-start(bf16[8,24,4096]{2,1,0:T(8,128)(2,1)} %bitcast.53), calls=%async_computation.2 | async-start | bytes 3145728 | tf_op jit(solution)/shard_map/all_to_all | solution.py:219
  185.3 30.0 %collective-permute-done.20 = f32[8,128]{1,0:T(8,128)S(1)} collective-permute-done((f32[8,128]{1,0:T(8,128)S(1)}, f32[8,128]{1,0:T(8,128)S(1)}, u32[]{:S(2)}, u32[]{:S(2)}) %collective-permute-start.20) | collective-permute-done | bytes 4128 | tf_op jit(solution)/shard_map/ppermute | solution.py:213
  215.3 8.0 %all-to-all-done.2 = bf16[8,24,4096]{2,1,0:T(8,128)(2,1)} async-done(((bf16[8,24,4096]{2,1,0:T(8,128)(2,1)}), bf16[8,24,4096]{2,1,0:T(8,128)(2,1)}, u32[]{:S(2)}, u32[]{:S(2)}) %all-to-all-start.2) | async-done | bytes 1572896 | tf_op jit(solution)/shard_map/all_to_all | solution.py:219
  245.9 2.7 %collective-permute-done.26 = bf16[24,4096]{1,0:T(8,128)(2,1)S(1)} collective-permute-done((bf16[24,4096]{1,0:T(8,128)(2,1)S(1)}, bf16[24,4096]{1,0:T(8,128)(2,1)S(1)}, u32[]{:S(2)}, u32[]{:S(2)}) %collective-permute-start.26) | collective-permute-done | bytes 196640 | tf_op jit(solution)/shard_map/ppermute | solution.py:213
  248.6 3.5 %collective-permute-done.27 = bf16[24,4096]{1,0:T(8,128)(2,1)S(1)} collective-permute-done((bf16[24,4096]{1,0:T(8,128)(2,1)S(1)}, bf16[24,4096]{1,0:T(8,128)(2,1)S(1)}, u32[]{:S(2)}, u32[]{:S(2)}) %collective-permute-start.27) | collective-permute-done | bytes 196640 | tf_op jit(solution)/shard_map/ppermute | solution.py:213
  252.1 4.2 %collective-permute-done.28 = bf16[24,4096]{1,0:T(8,128)(2,1)S(1)} collective-permute-done((bf16[24,4096]{1,0:T(8,128)(2,1)S(1)}, bf16[24,4096]{1,0:T(8,128)(2,1)S(1)}, u32[]{:S(2)}, u32[]{:S(2)}) %collective-permute-start.28) | collective-permute-done | bytes 196640 | tf_op jit(solution)/shard_map/ppermute | solution.py:213
  256.4 7.3 %gradients.1 = (bf16[256,4096]{1,0:T(8,128)(2,1)}, bf16[4096,256]{1,0:T(8,128)(2,1)}, f32[1,256]{1,0:T(1,128)}) custom-call(f32[8,128]{1,0:T(8,128)S(1)} %add.158.refs_0_, bf16[256,192]{1,0:T(8,128)(2,1)S(1)} %copy.34.refs_1_, bf16[256,192]{1,0:T(8,128)(2,1)S(1)} %copy.35.refs_2_, f32[192,256]{1,0:T(8,128)S(1)} %copy-done.8, f32[192,256]{1,0:T(8,128)S(1)} %copy-done.7, ...), custom_call_target="tpu_custom_call" | custom-call | flops 2415919104 | bytes 12582912 | tf_op jit(solution)/shard_map/gradients/pallas_call | solution.py:175
  (148 shorter events, 75.4 us)
Async XLA Ops:
  2.8 13.0 %collective-permute-start.1 = (s32[2,128]{1,0:T(2,128)S(1)}, s32[2,128]{1,0:T(2,128)S(1)}, u32[]{:S(2)}, u32[]{:S(2)}) collective-permute-start(s32[2,128]{1,0:T(2,128)S(1)} %bitcast.56), channel_id=1, source_target_pairs={{0,8},{1,9},{2,10},{3,11},{4,12},{5,13},{6,14},{7,15},{8,0},{9,1},... | collective-permute-start | bytes 3080 | tf_op jit(solution)/shard_map/ppermute | solution.py:213
  5.1 45.7 %collective-permute-start = (bf16[128,4096]{1,0:T(8,128)(2,1)}, bf16[128,4096]{1,0:T(8,128)(2,1)S(1)}, u32[]{:S(2)}, u32[]{:S(2)}) collective-permute-start(bf16[128,4096]{1,0:T(8,128)(2,1)} %act_ref.1), channel_id=1, source_target_pairs={{0,8},{1,9},{2,10},{3,11},{4,12},{5,13},{6,14},{7,15},{8,0},{9,1},... | collective-permute-start | bytes 3145736 | tf_op jit(solution)/shard_map/ppermute | solution.py:213
  8.2 42.6 %all-to-all-start = ((bf16[8,24,4096]{2,1,0:T(8,128)(2,1)}), bf16[8,24,4096]{2,1,0:T(8,128)(2,1)}, u32[]{:S(2)}, u32[]{:S(2)}) async-start(bf16[8,24,4096]{2,1,0:T(8,128)(2,1)} %bitcast.52), calls=%async_computation | async-start | bytes 3145728 | tf_op jit(solution)/shard_map/all_to_all | solution.py:219
  55.6 10.9 %collective-permute-start.4 = (bf16[24,4096]{1,0:T(8,128)(2,1)S(1)}, bf16[24,4096]{1,0:T(8,128)(2,1)S(1)}, u32[]{:S(2)}, u32[]{:S(2)}) collective-permute-start(bf16[24,4096]{1,0:T(8,128)(2,1)S(1)} %convolution_convert_fusion.24), channel_id=1, source_target_pairs={{0,3},{1,2},{2,1},{3,0},{4,7},{5,6},{6,5},{7,4},{8,11},{9,10},{10,... | collective-permute-start | bytes 589832 | tf_op jit(solution)/shard_map/ppermute | solution.py:213
  57.5 9.0 %collective-permute-start.5 = (bf16[24,4096]{1,0:T(8,128)(2,1)S(1)}, bf16[24,4096]{1,0:T(8,128)(2,1)S(1)}, u32[]{:S(2)}, u32[]{:S(2)}) collective-permute-start(bf16[24,4096]{1,0:T(8,128)(2,1)S(1)} %convolution_convert_fusion.23), channel_id=1, source_target_pairs={{0,4},{1,5},{2,6},{3,7},{4,0},{5,1},{6,2},{7,3},{8,12},{9,13},{10,... | collective-permute-start | bytes 589832 | tf_op jit(solution)/shard_map/ppermute | solution.py:213
  59.6 9.5 %collective-permute-start.6 = (bf16[24,4096]{1,0:T(8,128)(2,1)S(1)}, bf16[24,4096]{1,0:T(8,128)(2,1)S(1)}, u32[]{:S(2)}, u32[]{:S(2)}) collective-permute-start(bf16[24,4096]{1,0:T(8,128)(2,1)S(1)} %convolution_convert_fusion.22), channel_id=1, source_target_pairs={{0,5},{1,4},{2,7},{3,6},{4,1},{5,0},{6,3},{7,2},{8,13},{9,12},{10,... | collective-permute-start | bytes 589832 | tf_op jit(solution)/shard_map/ppermute | solution.py:213
  59.7 13.8 %collective-permute-start.7 = (bf16[24,4096]{1,0:T(8,128)(2,1)S(1)}, bf16[24,4096]{1,0:T(8,128)(2,1)S(1)}, u32[]{:S(2)}, u32[]{:S(2)}) collective-permute-start(bf16[24,4096]{1,0:T(8,128)(2,1)S(1)} %convolution_convert_fusion.21), channel_id=1, source_target_pairs={{0,6},{1,7},{2,4},{3,5},{4,2},{5,3},{6,0},{7,1},{8,14},{9,15},{10,... | collective-permute-start | bytes 589832 | tf_op jit(solution)/shard_map/ppermute | solution.py:213
  61.3 16.4 %collective-permute-start.8 = (bf16[24,4096]{1,0:T(8,128)(2,1)S(1)}, bf16[24,4096]{1,0:T(8,128)(2,1)S(1)}, u32[]{:S(2)}, u32[]{:S(2)}) collective-permute-start(bf16[24,4096]{1,0:T(8,128)(2,1)S(1)} %convolution_convert_fusion.20), channel_id=1, source_target_pairs={{0,7},{1,6},{2,5},{3,4},{4,3},{5,2},{6,1},{7,0},{8,15},{9,14},{10,... | collective-permute-start | bytes 589832 | tf_op jit(solution)/shard_map/ppermute | solution.py:213
  90.5 11.0 %collective-permute-start.12 = (bf16[24,4096]{1,0:T(8,128)(2,1)S(1)}, bf16[24,4096]{1,0:T(8,128)(2,1)S(1)}, u32[]{:S(2)}, u32[]{:S(2)}) collective-permute-start(bf16[24,4096]{1,0:T(8,128)(2,1)S(1)} %convolution_convert_fusion.16), channel_id=1, source_target_pairs={{0,3},{1,2},{2,1},{3,0},{4,7},{5,6},{6,5},{7,4},{8,11},{9,10},{10,... | collective-permute-start | bytes 589832 | tf_op jit(solution)/shard_map/ppermute | solution.py:213
  91.8 10.4 %collective-permute-start.13 = (bf16[24,4096]{1,0:T(8,128)(2,1)S(1)}, bf16[24,4096]{1,0:T(8,128)(2,1)S(1)}, u32[]{:S(2)}, u32[]{:S(2)}) collective-permute-start(bf16[24,4096]{1,0:T(8,128)(2,1)S(1)} %convolution_convert_fusion.15), channel_id=1, source_target_pairs={{0,4},{1,5},{2,6},{3,7},{4,0},{5,1},{6,2},{7,3},{8,12},{9,13},{10,... | collective-permute-start | bytes 589832 | tf_op jit(solution)/shard_map/ppermute | solution.py:213
  93.8 9.5 %collective-permute-start.14 = (bf16[24,4096]{1,0:T(8,128)(2,1)S(1)}, bf16[24,4096]{1,0:T(8,128)(2,1)S(1)}, u32[]{:S(2)}, u32[]{:S(2)}) collective-permute-start(bf16[24,4096]{1,0:T(8,128)(2,1)S(1)} %convolution_convert_fusion.14), channel_id=1, source_target_pairs={{0,5},{1,4},{2,7},{3,6},{4,1},{5,0},{6,3},{7,2},{8,13},{9,12},{10,... | collective-permute-start | bytes 589832 | tf_op jit(solution)/shard_map/ppermute | solution.py:213
  95.0 11.6 %collective-permute-start.15 = (bf16[24,4096]{1,0:T(8,128)(2,1)S(1)}, bf16[24,4096]{1,0:T(8,128)(2,1)S(1)}, u32[]{:S(2)}, u32[]{:S(2)}) collective-permute-start(bf16[24,4096]{1,0:T(8,128)(2,1)S(1)} %convolution_convert_fusion.13), channel_id=1, source_target_pairs={{0,6},{1,7},{2,4},{3,5},{4,2},{5,3},{6,0},{7,1},{8,14},{9,15},{10,... | collective-permute-start | bytes 589832 | tf_op jit(solution)/shard_map/ppermute | solution.py:213
  97.8 13.3 %collective-permute-start.16 = (bf16[24,4096]{1,0:T(8,128)(2,1)S(1)}, bf16[24,4096]{1,0:T(8,128)(2,1)S(1)}, u32[]{:S(2)}, u32[]{:S(2)}) collective-permute-start(bf16[24,4096]{1,0:T(8,128)(2,1)S(1)} %convolution_convert_fusion.12), channel_id=1, source_target_pairs={{0,7},{1,6},{2,5},{3,4},{4,3},{5,2},{6,1},{7,0},{8,15},{9,14},{10,... | collective-permute-start | bytes 589832 | tf_op jit(solution)/shard_map/ppermute | solution.py:213
  111.8 17.8 %collective-permute-start.19 = (f32[8,128]{1,0:T(8,128)S(1)}, f32[8,128]{1,0:T(8,128)S(1)}, u32[]{:S(2)}, u32[]{:S(2)}) collective-permute-start(f32[8,128]{1,0:T(8,128)S(1)} %add.156), channel_id=1, source_target_pairs={{0,4},{1,5},{2,6},{3,7},{4,0},{5,1},{6,2},{7,3},{8,12},{9,13},{10,... | collective-permute-start | bytes 12296 | tf_op jit(solution)/shard_map/ppermute | solution.py:213
  115.9 47.4 %collective-permute-start.18 = (bf16[128,4096]{1,0:T(8,128)(2,1)}, bf16[128,4096]{1,0:T(8,128)(2,1)}, u32[]{:S(2)}, u32[]{:S(2)}) collective-permute-start(bf16[128,4096]{1,0:T(8,128)(2,1)} %convolution_convert_fusion.3), channel_id=1, source_target_pairs={{0,8},{1,9},{2,10},{3,11},{4,12},{5,13},{6,14},{7,15},{8,0},{9,1},... | collective-permute-start | bytes 3145736 | tf_op jit(solution)/shard_map/ppermute | solution.py:213
  120.0 46.8 %all-to-all-start.1 = ((bf16[8,24,4096]{2,1,0:T(8,128)(2,1)}), bf16[8,24,4096]{2,1,0:T(8,128)(2,1)}, u32[]{:S(2)}, u32[]{:S(2)}) async-start(bf16[8,24,4096]{2,1,0:T(8,128)(2,1)} %bitcast.54), calls=%async_computation.1 | async-start | bytes 3145728 | tf_op jit(solution)/shard_map/all_to_all | solution.py:219
  170.6 44.7 %collective-permute-start.21 = (bf16[128,4096]{1,0:T(8,128)(2,1)}, bf16[128,4096]{1,0:T(8,128)(2,1)}, u32[]{:S(2)}, u32[]{:S(2)}) collective-permute-start(bf16[128,4096]{1,0:T(8,128)(2,1)} %get-tuple-element.44), channel_id=1, source_target_pairs={{0,8},{1,9},{2,10},{3,11},{4,12},{5,13},{6,14},{7,15},{8,0},{9,1},... | collective-permute-start | bytes 3145736 | tf_op jit(solution)/shard_map/ppermute | solution.py:213
  173.6 41.7 %collective-permute-start.20 = (f32[8,128]{1,0:T(8,128)S(1)}, f32[8,128]{1,0:T(8,128)S(1)}, u32[]{:S(2)}, u32[]{:S(2)}) collective-permute-start(f32[8,128]{1,0:T(8,128)S(1)} %add.157), channel_id=1, source_target_pairs={{0,8},{1,9},{2,10},{3,11},{4,12},{5,13},{6,14},{7,15},{8,0},{9,1},... | collective-permute-start | bytes 12296 | tf_op jit(solution)/shard_map/ppermute | solution.py:213
  175.9 47.4 %all-to-all-start.2 = ((bf16[8,24,4096]{2,1,0:T(8,128)(2,1)}), bf16[8,24,4096]{2,1,0:T(8,128)(2,1)}, u32[]{:S(2)}, u32[]{:S(2)}) async-start(bf16[8,24,4096]{2,1,0:T(8,128)(2,1)} %bitcast.53), calls=%async_computation.2 | async-start | bytes 3145728 | tf_op jit(solution)/shard_map/all_to_all | solution.py:219
  235.0 10.9 %collective-permute-start.24 = (bf16[24,4096]{1,0:T(8,128)(2,1)S(1)}, bf16[24,4096]{1,0:T(8,128)(2,1)S(1)}, u32[]{:S(2)}, u32[]{:S(2)}) collective-permute-start(bf16[24,4096]{1,0:T(8,128)(2,1)S(1)} %convolution_convert_fusion.8), channel_id=1, source_target_pairs={{0,3},{1,2},{2,1},{3,0},{4,7},{5,6},{6,5},{7,4},{8,11},{9,10},{10,... | collective-permute-start | bytes 589832 | tf_op jit(solution)/shard_map/ppermute | solution.py:213
  236.4 9.5 %collective-permute-start.25 = (bf16[24,4096]{1,0:T(8,128)(2,1)S(1)}, bf16[24,4096]{1,0:T(8,128)(2,1)S(1)}, u32[]{:S(2)}, u32[]{:S(2)}) collective-permute-start(bf16[24,4096]{1,0:T(8,128)(2,1)S(1)} %convolution_convert_fusion.7), channel_id=1, source_target_pairs={{0,4},{1,5},{2,6},{3,7},{4,0},{5,1},{6,2},{7,3},{8,12},{9,13},{10,... | collective-permute-start | bytes 589832 | tf_op jit(solution)/shard_map/ppermute | solution.py:213
  238.6 10.0 %collective-permute-start.26 = (bf16[24,4096]{1,0:T(8,128)(2,1)S(1)}, bf16[24,4096]{1,0:T(8,128)(2,1)S(1)}, u32[]{:S(2)}, u32[]{:S(2)}) collective-permute-start(bf16[24,4096]{1,0:T(8,128)(2,1)S(1)} %convolution_convert_fusion.6), channel_id=1, source_target_pairs={{0,5},{1,4},{2,7},{3,6},{4,1},{5,0},{6,3},{7,2},{8,13},{9,12},{10,... | collective-permute-start | bytes 589832 | tf_op jit(solution)/shard_map/ppermute | solution.py:213
  240.3 11.8 %collective-permute-start.27 = (bf16[24,4096]{1,0:T(8,128)(2,1)S(1)}, bf16[24,4096]{1,0:T(8,128)(2,1)S(1)}, u32[]{:S(2)}, u32[]{:S(2)}) collective-permute-start(bf16[24,4096]{1,0:T(8,128)(2,1)S(1)} %convolution_convert_fusion.5), channel_id=1, source_target_pairs={{0,6},{1,7},{2,4},{3,5},{4,2},{5,3},{6,0},{7,1},{8,14},{9,15},{10,... | collective-permute-start | bytes 589832 | tf_op jit(solution)/shard_map/ppermute | solution.py:213
  242.1 14.3 %collective-permute-start.28 = (bf16[24,4096]{1,0:T(8,128)(2,1)S(1)}, bf16[24,4096]{1,0:T(8,128)(2,1)S(1)}, u32[]{:S(2)}, u32[]{:S(2)}) collective-permute-start(bf16[24,4096]{1,0:T(8,128)(2,1)S(1)} %convolution_convert_fusion.4), channel_id=1, source_target_pairs={{0,7},{1,6},{2,5},{3,4},{4,3},{5,2},{6,1},{7,0},{8,15},{9,14},{10,... | collective-permute-start | bytes 589832 | tf_op jit(solution)/shard_map/ppermute | solution.py:213
  (23 other events, 385.1 us)

commit v5 on v2

--- a/solution.py
+++ b/solution.py
@@ -7,6 +7,8 @@
 
 BLOCK = 64
 LOSS_SCALE = 0.5
+PIECES = 4
+VMEM_LIMIT = 28 * 1024 * 1024
 F32 = jnp.float32
 BF16 = jnp.bfloat16
 
@@ -50,6 +52,217 @@
         ),
         name="squares",
     )(rows)
+
+
+VMEM_SPEC = pl.BlockSpec(memory_space=pltpu.VMEM)
+HBM_SPEC = pl.BlockSpec(memory_space=pltpu.HBM)
+
+
+def columns(ref, i):
+    width = ref.shape[1] // PIECES
+    return ref.at[:, i * width : (i + 1) * width]
+
+
+def fetch(source_ref, here_ref, sems):
+    copies = [
+        pltpu.make_async_copy(columns(source_ref, i), columns(here_ref, i), sems.at[i])
+        for i in range(PIECES)
+    ]
+    for copy in copies:
+        copy.start()
+    return copies
+
+
+def store(copies, here_ref, target_ref, sem):
+    copies.append(pltpu.make_async_copy(here_ref, target_ref, sem))
+    copies[-1].start()
+
+
+def encode_kernel(
+    slot_ref,
+    rows_ref,
+    enc_ref,
+    bias_ref,
+    own_ref,
+    dec_ref,
+    _,
+    code_ref,
+    slopes_ref,
+    partial_ref,
+    here_ref,
+    out_ref,
+    sems,
+):
+    copies = fetch(rows_ref, here_ref, sems.at[0])
+    slots = rows_ref.shape[0]
+    width = rows_ref.shape[1] // PIECES
+    preact = bias_ref[...]
+    for i, copy in enumerate(copies):
+        copy.wait()
+        preact = preact + dot(
+            columns(here_ref, i)[...], enc_ref[i * width : (i + 1) * width, :], 1, 0
+        )
+    output, slopes = activate(preact)
+    own = own_ref[...] > 0
+    code = jnp.where(own, output, 0.0).astype(BF16)
+    code_ref[...] = code
+    slopes_ref[...] = jnp.where(own, slopes, 0.0)
+    start = pl.multiple_of(slot_ref[0] * slots, slots)
+    target_ref = partial_ref.at[pl.ds(start, slots), :]
+    copies = []
+    for i in range(PIECES):
+        columns(out_ref, i)[...] = dot(code, columns(dec_ref, i)[...], 1, 0).astype(BF16)
+        store(copies, columns(out_ref, i), columns(target_ref, i), sems.at[1, i])
+    for copy in copies:
+        copy.wait()
+
+
+def encode(place, rows, enc_weight, enc_bias, own, dec_weight, partial_value):
+    slots, features = rows.shape
+    latents = enc_weight.shape[1]
+    return pl.pallas_call(
+        encode_kernel,
+        out_shape=[
+            jax.ShapeDtypeStruct((slots, latents), BF16),
+            jax.ShapeDtypeStruct((slots, latents), F32),
+            jax.ShapeDtypeStruct((2 * slots, features), BF16),
+        ],
+        in_specs=[pl.BlockSpec(memory_space=pltpu.SMEM), HBM_SPEC] + [VMEM_SPEC] * 4 + [HBM_SPEC],
+        out_specs=[VMEM_SPEC, VMEM_SPEC, HBM_SPEC],
+        input_output_aliases={6: 2},
+        scratch_shapes=[
+            pltpu.VMEM((slots, features), BF16),
+            pltpu.VMEM((slots, features), BF16),
+            pltpu.SemaphoreType.DMA((2, PIECES)),
+        ],
+        cost_estimate=pl.CostEstimate(
+            flops=4 * slots * latents * features,
+            bytes_accessed=4 * features * (slots + latents),
+            transcendentals=slots * latents,
+        ),
+        compiler_params=pltpu.CompilerParams(vmem_limit_bytes=VMEM_LIMIT),
+        name="encode",
+    )(place, rows, enc_weight, enc_bias, own, dec_weight, partial_value)
+
+
+def home_kernel(
+    select_ref,
+    select_t_ref,
+    act_ref,
+    bias_ref,
+    returned_ref,
+    full_ref,
+    send_ref,
+    here_ref,
+    full_out_ref,
+    send_out_ref,
+    sems,
+):
+    stores = []
+    for i, copy in enumerate(fetch(returned_ref, here_ref, sems.at[0])):
+        copy.wait()
+        full = dot(select_t_ref[...], columns(here_ref, i)[...], 1, 0) + columns(bias_ref, i)[...]
+        errors = (full - columns(act_ref, i)[...].astype(F32)).astype(BF16)
+        columns(send_out_ref, i)[...] = dot(select_ref[...], errors, 1, 0).astype(BF16)
+        store(stores, columns(send_out_ref, i), columns(send_ref, i), sems.at[1, i])
+        columns(full_out_ref, i)[...] = full.astype(BF16)
+        store(stores, columns(full_out_ref, i), columns(full_ref, i), sems.at[2, i])
+    for copy in stores:
+        copy.wait()
+
+
+def rebuild(select, select_t, returned, activations, dec_bias):
+    slots, tokens = select.shape
+    features = activations.shape[1]
+    return pl.pallas_call(
+        home_kernel,
+        out_shape=[
+            pltpu.HBM((tokens, features), BF16),
+            pltpu.HBM((slots, features), BF16),
+        ],
+        in_specs=[VMEM_SPEC] * 4 + [HBM_SPEC],
+        out_specs=[HBM_SPEC, HBM_SPEC],
+        scratch_shapes=[
+            pltpu.VMEM((slots, features), BF16),
+            pltpu.VMEM((tokens, features), BF16),
+            pltpu.VMEM((slots, features), BF16),
+            pltpu.SemaphoreType.DMA((3, PIECES)),
+        ],
+        cost_estimate=pl.CostEstimate(
+            flops=4 * slots * tokens * features,
+            bytes_accessed=4 * (slots + tokens) * features,
+            transcendentals=0,
+        ),
+        compiler_params=pltpu.CompilerParams(vmem_limit_bytes=VMEM_LIMIT),
+        name="rebuild",
+    )(select, select_t, activations, dec_bias, returned)
+
+
+def grads_kernel(
+    count,
+    squares_ref,
+    code_t_ref,
+    slopes_ref,
+    dec_t_ref,
+    rows_t_ref,
+    got_ref,
+    dec_grad_ref,
+    enc_grad_ref,
+    bias_grad_ref,
+    here_ref,
+    dec_out_ref,
+    enc_out_ref,
+    sems,
+):
+    copies = fetch(got_ref, here_ref, sems.at[0])
+    scale = LOSS_SCALE / (squares_ref[0:1, 0:1] / count + 1e-06)
+    width = got_ref.shape[1] // PIECES
+    stores = []
+    code_grad = None
+    for i, copy in enumerate(copies):
+        copy.wait()
+        got = columns(here_ref, i)[...]
+        columns(dec_out_ref, i)[...] = (dot(code_t_ref[...], got, 1, 0) * scale).astype(BF16)
+        store(stores, columns(dec_out_ref, i), columns(dec_grad_ref, i), sems.at[1, i])
+        part = dot(got, dec_t_ref[i * width : (i + 1) * width, :], 1, 0)
+        code_grad = part if i == 0 else code_grad + part
+    code_grad = code_grad * (slopes_ref[...] * scale)
+    bias_grad_ref[...] = jnp.sum(code_grad, axis=0, keepdims=True)
+    code_grad = code_grad.astype(BF16)
+    for i in range(PIECES):
+        piece = slice(i * width, (i + 1) * width)
+        enc_out_ref[piece, :] = dot(rows_t_ref[piece, :], code_grad, 1, 0).astype(BF16)
+        store(stores, enc_out_ref.at[piece], enc_grad_ref.at[piece], sems.at[2, i])
+    for copy in stores:
+        copy.wait()
+
+
+def gradients(count, squares, code_t, slopes, dec_t, rows_t, got_errors):
+    latents, slots = code_t.shape
+    features = dec_t.shape[0]
+    return pl.pallas_call(
+        lambda *refs: grads_kernel(count, *refs),
+        out_shape=[
+            jax.ShapeDtypeStruct((latents, features), BF16),
+            jax.ShapeDtypeStruct((features, latents), BF16),
+            jax.ShapeDtypeStruct((1, latents), F32),
+        ],
+        in_specs=[VMEM_SPEC] * 5 + [HBM_SPEC],
+        out_specs=[HBM_SPEC, HBM_SPEC, VMEM_SPEC],
+        scratch_shapes=[
+            pltpu.VMEM((slots, features), BF16),
+            pltpu.VMEM((latents, features), BF16),
+            pltpu.VMEM((features, latents), BF16),
+            pltpu.SemaphoreType.DMA((3, PIECES)),
+        ],
+        cost_estimate=pl.CostEstimate(
+            flops=6 * slots * latents * features,
+            bytes_accessed=2 * features * (2 * slots + 3 * latents),
+            transcendentals=0,
+        ),
+        compiler_params=pltpu.CompilerParams(vmem_limit_bytes=VMEM_LIMIT),
+        name="gradients",
+    )(squares, code_t, slopes, dec_t, rows_t, got_errors)
 
 
 def per_device(activations, block_ids, enc_weight, enc_bias, dec_weight, dec_bias):
@@ -93,6 +306,7 @@
         return jnp.any(names[:, None, None] == slot[None, :, :], axis=1).astype(BF16)
 
     select = selection(slot_of, slots)
+    select_t = jnp.any(slots[None, :, None] == slot_of.T[:, None, :], axis=2).astype(BF16)
     names = slots[:half_slots] + jnp.where(lower, 0, half_slots)
 
     got_own = exchange(pick(selection(slot_of, names), activations), halves)
@@ -102,40 +316,38 @@
     row_block = (slots[:half_slots] % dev_slots) // capacity
     own = row_block[:, None] == (jnp.arange(local_latents, dtype=jnp.int32) // BLOCK)[None, :]
 
-    def encode(rows):
-        output, slopes = activate(dot(rows, enc_weight, 1, 0) + enc_bias[None, :])
-        return jnp.where(own, output, 0.0).astype(BF16), jnp.where(own, slopes, 0.0)
+    own = own.astype(F32)
+    place = jnp.where(lower, 0, 1).astype(jnp.int32).reshape(1)
+    bias_row = enc_bias[None, :]
+    partial_value = jnp.zeros((2 * half_slots, feature_dim), BF16)
+    code_own, slope_own, partial_value = encode(
+        place, got_own, enc_weight, bias_row, own, dec_weight, partial_value
+    )
+    code_held, slope_held, partial_value = encode(
+        1 - place, got_held, enc_weight, bias_row, own, dec_weight, partial_value
+    )
+    returned = exchange(partial_value)
 
     def ordered(own_part, held_part):
         first = jnp.where(lower, own_part, held_part)
         second = jnp.where(lower, held_part, own_part)
         return jnp.concatenate([first, second], axis=0)
 
-    code_own, slope_own = encode(got_own)
-    code_held, slope_held = encode(got_held)
-    code_rows, slopes = ordered(code_own, code_held), ordered(slope_own, slope_held)
-
-    returned = exchange(dot(code_rows, dec_weight, 1, 0).astype(BF16))
+    code_t = ordered(code_own, code_held).T
+    slopes = ordered(slope_own, slope_held)
+    rows_t = ordered(got_own, got_held).T
+
     step = 1
     while step < devices:
         squares = squares + swap(squares, step)
         step *= 2
     returned, squares = together(returned, squares)
-    full = dec_bias[None, :] + dot(select, returned, 0, 0)
-    errors = (full - activations.astype(F32)).astype(BF16)
-    got_errors = exchange(pick(select, errors))
-
-    mean_square = squares[0, 0] / (tok_rows * devices * feature_dim) + 1e-06
-    scale = LOSS_SCALE / mean_square
-    code_grad = dot(got_errors, dec_weight, 1, 1) * (slopes * scale)
-    bias_grad = jnp.sum(code_grad, axis=0)
-    code_grad = code_grad.astype(BF16)
-    lower_grad, upper_grad = code_grad[:half_slots], code_grad[half_slots:]
-    grad_own = jnp.where(lower, lower_grad, upper_grad)
-    grad_held = jnp.where(lower, upper_grad, lower_grad)
-    enc_grad = (dot(got_own, grad_own, 0, 0) + dot(got_held, grad_held, 0, 0)).astype(BF16)
-    dec_grad = (dot(code_rows, got_errors, 0, 0) * scale).astype(BF16)
-    return (full.astype(BF16), enc_grad, dec_grad, bias_grad)
+    full, send_errors = rebuild(select, select_t, returned, activations, dec_bias[None, :])
+    got_errors = exchange(send_errors)
+    dec_grad, enc_grad, bias_grad = gradients(
+        tok_rows * devices * feature_dim, squares, code_t, slopes, dec_weight.T, rows_t, got_errors
+    )
+    return (full, enc_grad, dec_grad, bias_grad.reshape(local_latents))
 
 
 def solution(mesh):

time: 258 us -> 254 us (0.984)
  matrix products: 32.8 us -> 4.64 us
  local copies, waits for them, and re-layouts: 1.82 us -> 22.6 us
  Pallas kernels: 2.14 us -> 20.8 us
  waiting for transfers between devices: 188 us -> 170 us
  other arithmetic: 1.43 us -> 5.12 us
    dot_general x11 -> x2, matrix products: 32.8 us -> 4.64 us  [dot(): return lax.dot_general(left, right, dims, preferred_element_type=F32)]
    pallas_call x0 -> x4, Pallas kernels: none -> 18.7 us  [the longest x1 7.15 us: gradients(): pl.pallas_call(lambda *refs: grads_kernel(count, *refs), out_shape=[jax.S...]
    all_to_all x4, waiting for transfers between devices: 86.3 us -> 70.6 us  [exchange(): lax.all_to_all(rows, 'lat', split_axis=0, concat_axis=0, axis_index_group...]
    unnamed x11 -> x38, local copies, waits for them, and re-layouts: 0.96 us -> 12.4 us
    all_to_all x0 -> x1, local copies, waits for them, and re-layouts: none -> 3.89 us  [exchange(): lax.all_to_all(rows, 'lat', split_axis=0, concat_axis=0, axis_index_group...]
    optimization_barrier x0 -> x1, local copies, waits for them, and re-layouts: none -> 3.15 us  [together(): return lax.optimization_barrier(values)]
  transfers between devices with their start and end apart: 10 -> 10, of which waited for: 8 -> 9; matrix products, arithmetic and copies ran while one was open for 3% -> 8% of each run, Pallas kernels for 1% -> 2%
where the time goes in v5:
time: 254 us; the launch traced here: 253 us
  waiting for transfers between devices  170 us (67%)
  starting transfers between devices  28.8 us (11%)
  local copies, waits for them, and re-layouts  22.6 us (9%)
  Pallas kernels  20.8 us (8%)
  other arithmetic  5.12 us (2%)
  matrix products  4.64 us (2%)
    ppermute x6, waiting for transfers between devices, swap(): return lax.ppermute(rows, 'lat', [(i, i ^ step) for i in range(devices)])  99.8 us
    all_to_all x4, waiting for transfers between devices, exchange(): lax.all_to_all(rows, 'lat', split_axis=0, concat_axis=0, axis_index_group...  70.6 us
    all_to_all x4, starting transfers between devices, exchange(): lax.all_to_all(rows, 'lat', split_axis=0, concat_axis=0, axis_index_group...  25.2 us
    unnamed x38, local copies, waits for them, and re-layouts  12.4 us
    pallas_call x1, Pallas kernels, gradients(): pl.pallas_call(lambda *refs: grads_kernel(count, *refs), out_shape=[jax.S...  7.15 us
    pallas_call x2, Pallas kernels, encode(): pl.pallas_call(encode_kernel, out_shape=[jax.ShapeDtypeStruct((slots, lat...  6.97 us
  transfers between devices with their start and end apart: 10, of which 9 were waited for; matrix products, arithmetic and copies ran while one was open for 8% of the time, Pallas kernels for 2%

profile of v5, /device:TPU:13, one launch (start us, length us, event | category | flops | bytes accessed | tf_op | source)
XLA Modules:
  0.0 253.3 jit_solution(13089537354443311824)
XLA Ops:
  0.6 2.4 collective-permute-start
  5.2 2.9 %convolution_convert_fusion.1 = bf16[192,4096]{1,0:T(8,128)(2,1)} fusion(pred[192,128]{1,0:T(8,128)(4,1)S(1)} %compare_reduce_fusion.1, bf16[128,4096]{1,0:T(8,128)(2,1)} %act_ref.1), kind=kOutput, calls=%fused_computation.1 | convolution fusion | flops 202113024 | bytes 2646016 | tf_op jit(solution)/shard_map/dot_general | solution.py:28
  8.1 5.1 %all-to-all-start = ((bf16[8,24,4096]{2,1,0:T(8,128)(2,1)}), bf16[8,24,4096]{2,1,0:T(8,128)(2,1)S(1)}, u32[]{:S(2)}, u32[]{:S(2)}) async-start(bf16[8,24,4096]{2,1,0:T(8,128)(2,1)} %bitcast.3), calls=%async_computation | async-start | bytes 3145728 | tf_op jit(solution)/shard_map/all_to_all | solution.py:282
  13.2 2.1 squares.1
  15.4 33.3 %collective-permute-done.1 = s32[2,128]{1,0:T(2,128)S(1)} collective-permute-done((s32[2,128]{1,0:T(2,128)S(1)}, s32[2,128]{1,0:T(2,128)S(1)}, u32[]{:S(2)}, u32[]{:S(2)}) %collective-permute-start.1) | collective-permute-done | bytes 1056 | tf_op jit(solution)/shard_map/ppermute | solution.py:287
  48.6 3.2 %all-to-all-done = bf16[8,24,4096]{2,1,0:T(8,128)(2,1)S(1)} async-done(((bf16[8,24,4096]{2,1,0:T(8,128)(2,1)}), bf16[8,24,4096]{2,1,0:T(8,128)(2,1)S(1)}, u32[]{:S(2)}, u32[]{:S(2)}) %all-to-all-start) | async-done | bytes 1572896 | tf_op jit(solution)/shard_map/all_to_all | solution.py:282
  51.9 1.7 convolution_convert_fusion
  53.6 7.0 %all-to-all-start.1 = ((bf16[8,24,4096]{2,1,0:T(8,128)(2,1)}), bf16[8,24,4096]{2,1,0:T(8,128)(2,1)}, u32[]{:S(2)}, u32[]{:S(2)}) async-start(bf16[8,24,4096]{2,1,0:T(8,128)(2,1)} %bitcast.5), calls=%async_computation.1 | async-start | bytes 3145728 | tf_op jit(solution)/shard_map/all_to_all | solution.py:282
  60.8 2.0 broadcast_in_dim.8._
  65.8 3.1 %encode.2 = (bf16[192,256]{1,0:T(8,128)(2,1)S(1)}, f32[192,256]{1,0:T(8,128)S(1)}, bf16[384,4096]{1,0:T(8,128)(2,1)}) custom-call(s32[1]{0:T(128)} %bitcast.2.slot_ref, bf16[192,4096]{1,0:T(8,128)(2,1)S(1)} %bitcast.23, bf16[4096,256]{1,0:T(8,128)(2,1)S(1)} %copy-done.3, f32[1,256]{1,0:T(1,128)S(1)} %bitcast.26, ...), custom_call_target="tpu_custom_call", output_to_operand_aliasing={{2}: (6, {})} | custom-call | flops 805306368 | bytes 7340032 | tf_op jit(solution)/shard_map/encode/pallas_call | solution.py:123
  69.5 9.3 %all-to-all-done.1 = bf16[8,24,4096]{2,1,0:T(8,128)(2,1)} async-done(((bf16[8,24,4096]{2,1,0:T(8,128)(2,1)}), bf16[8,24,4096]{2,1,0:T(8,128)(2,1)}, u32[]{:S(2)}, u32[]{:S(2)}) %all-to-all-start.1) | async-done | bytes 1572896 | tf_op jit(solution)/shard_map/all_to_all | solution.py:282
  80.4 3.9 %encode.3 = (bf16[192,256]{1,0:T(8,128)(2,1)S(1)}, f32[192,256]{1,0:T(8,128)S(1)}, bf16[384,4096]{1,0:T(8,128)(2,1)}) custom-call(s32[1]{0:T(128)S(6)} %sub.19.slot_ref, bf16[192,4096]{1,0:T(8,128)(2,1)} %bitcast.6.rows_ref, bf16[4096,256]{1,0:T(8,128)(2,1)S(1)} %copy-done.4, f32[1,256]{1,0:T(1,128)S(1)} %bitcast.27, ...), custom_call_target="tpu_custom_call", output_to_operand_aliasing={{2}: (6, {})} | custom-call | flops 805306368 | bytes 7340032 | tf_op jit(solution)/shard_map/encode/pallas_call | solution.py:123
  85.7 6.5 %all-to-all-start.2 = ((bf16[16,24,4096]{2,1,0:T(8,128)(2,1)}), bf16[16,24,4096]{2,1,0:T(8,128)(2,1)}, u32[]{:S(2)}, u32[]{:S(2)}) async-start(bf16[16,24,4096]{2,1,0:T(8,128)(2,1)} %bitcast.8), calls=%async_computation.2 | async-start | bytes 6291456 | tf_op jit(solution)/shard_map/all_to_all | solution.py:282
  93.8 12.5 %collective-permute-done.3 = f32[8,128]{1,0:T(8,128)S(1)} collective-permute-done((f32[8,128]{1,0:T(8,128)S(1)}, f32[8,128]{1,0:T(8,128)S(1)}, u32[]{:S(2)}, u32[]{:S(2)}) %collective-permute-start.3) | collective-permute-done | bytes 4128 | tf_op jit(solution)/shard_map/ppermute | solution.py:287
  106.7 38.6 %collective-permute-done.4 = f32[8,128]{1,0:T(8,128)S(1)} collective-permute-done((f32[8,128]{1,0:T(8,128)S(1)}, f32[8,128]{1,0:T(8,128)S(1)}, u32[]{:S(2)}, u32[]{:S(2)}) %collective-permute-start.4) | collective-permute-done | bytes 4128 | tf_op jit(solution)/shard_map/ppermute | solution.py:287
  145.6 14.5 %collective-permute-done.5 = f32[8,128]{1,0:T(8,128)S(1)} collective-permute-done((f32[8,128]{1,0:T(8,128)S(1)}, f32[8,128]{1,0:T(8,128)S(1)}, u32[]{:S(2)}, u32[]{:S(2)}) %collective-permute-start.5) | collective-permute-done | bytes 4128 | tf_op jit(solution)/shard_map/ppermute | solution.py:287
  162.3 4.5 %rebuild.1 = (bf16[128,4096]{1,0:T(8,128)(2,1)}, bf16[384,4096]{1,0:T(8,128)(2,1)}) custom-call(bf16[384,128]{1,0:T(8,128)(2,1)S(1)} %convert_element_type.23.select_ref, bf16[128,384]{1,0:T(8,128)(2,1)S(1)} %convert_element_type.24.select_t_ref, bf16[128,4096]{1,0:T(8,128)(2,1)S(1)} %copy-done.6, f32[1,4096]{1,0:T(1,128)S(1)} %bitcast.25, ...), custom_call_target="tpu_custom_call" | custom-call | flops 805306368 | bytes 8388608 | tf_op jit(solution)/shard_map/rebuild/pallas_call | solution.py:177
  166.9 6.6 %all-to-all-start.3 = ((bf16[16,24,4096]{2,1,0:T(8,128)(2,1)}), bf16[16,24,4096]{2,1,0:T(8,128)(2,1)}, u32[]{:S(2)}, u32[]{:S(2)}) async-start(bf16[16,24,4096]{2,1,0:T(8,128)(2,1)} %bitcast.28), calls=%async_computation.3 | async-start | bytes 6291456 | tf_op jit(solution)/shard_map/all_to_all | solution.py:282
  173.5 2.5 copy.46
  175.9 3.1 %copy.47 = bf16[192,4096]{0,1:T(8,128)(2,1)S(1)} copy(bf16[192,4096]{1,0:T(8,128)(2,1)} %bitcast.22) | data formatting | bytes 3145728 | tf_op jit(solution)/shard_map/optimization_barrier | solution.py:32
  179.1 3.9 %copy.48 = bf16[192,4096]{0,1:T(8,128)(2,1)} copy(bf16[192,4096]{1,0:T(8,128)(2,1)} %bitcast.6.rows_ref) | data formatting | bytes 3145728 | tf_op jit(solution)/shard_map/all_to_all | solution.py:282
  184.0 1.9 broadcast_select_fusion.1
  187.0 56.5 %all-to-all-done.3 = bf16[16,24,4096]{2,1,0:T(8,128)(2,1)} async-done(((bf16[16,24,4096]{2,1,0:T(8,128)(2,1)}), bf16[16,24,4096]{2,1,0:T(8,128)(2,1)}, u32[]{:S(2)}, u32[]{:S(2)}) %all-to-all-start.3) | async-done | bytes 3145760 | tf_op jit(solution)/shard_map/all_to_all | solution.py:282
  246.0 7.2 %gradients.1 = (bf16[256,4096]{1,0:T(8,128)(2,1)}, bf16[4096,256]{1,0:T(8,128)(2,1)}, f32[1,256]{1,0:T(1,128)}) custom-call(f32[8,128]{1,0:T(8,128)S(1)} %copy-done.15, bf16[256,384]{1,0:T(8,128)(2,1)S(1)} %copy-done.7, f32[384,256]{1,0:T(8,128)S(1)} %pad_maximum_fusion.refs_2_, bf16[4096,256]{1,0:T(8,128)(2,1)S(1)} %bitcast.24, ...), custom_call_target="tpu_custom_call" | custom-call | flops 2415919104 | bytes 12582912 | tf_op jit(solution)/shard_map/gradients/pallas_call | solution.py:243
  (70 shorter events, 18.0 us)
Async XLA Ops:
  0.6 48.0 %collective-permute-start = (bf16[128,4096]{1,0:T(8,128)(2,1)}, bf16[128,4096]{1,0:T(8,128)(2,1)S(1)}, u32[]{:S(2)}, u32[]{:S(2)}) collective-permute-start(bf16[128,4096]{1,0:T(8,128)(2,1)} %act_ref.1), channel_id=1, source_target_pairs={{0,8},{1,9},{2,10},{3,11},{4,12},{5,13},{6,14},{7,15},{8,0},{9,1},... | collective-permute-start | bytes 3145736 | tf_op jit(solution)/shard_map/ppermute | solution.py:287
  5.0 43.6 %collective-permute-start.1 = (s32[2,128]{1,0:T(2,128)S(1)}, s32[2,128]{1,0:T(2,128)S(1)}, u32[]{:S(2)}, u32[]{:S(2)}) collective-permute-start(s32[2,128]{1,0:T(2,128)S(1)} %bitcast.29), channel_id=1, source_target_pairs={{0,8},{1,9},{2,10},{3,11},{4,12},{5,13},{6,14},{7,15},{8,0},{9,1},... | collective-permute-start | bytes 3080 | tf_op jit(solution)/shard_map/ppermute | solution.py:287
  8.1 43.6 %all-to-all-start = ((bf16[8,24,4096]{2,1,0:T(8,128)(2,1)}), bf16[8,24,4096]{2,1,0:T(8,128)(2,1)S(1)}, u32[]{:S(2)}, u32[]{:S(2)}) async-start(bf16[8,24,4096]{2,1,0:T(8,128)(2,1)} %bitcast.3), calls=%async_computation | async-start | bytes 3145728 | tf_op jit(solution)/shard_map/all_to_all | solution.py:282
  51.8 1.8 copy-start.1
  53.6 25.2 %all-to-all-start.1 = ((bf16[8,24,4096]{2,1,0:T(8,128)(2,1)}), bf16[8,24,4096]{2,1,0:T(8,128)(2,1)}, u32[]{:S(2)}, u32[]{:S(2)}) async-start(bf16[8,24,4096]{2,1,0:T(8,128)(2,1)} %bitcast.5), calls=%async_computation.1 | async-start | bytes 3145728 | tf_op jit(solution)/shard_map/all_to_all | solution.py:282
  60.7 2.2 copy-start
  60.7 2.2 copy-start.16
  62.8 1.4 copy-start.2
  64.2 1.6 copy-start.3
  78.8 1.6 copy-start.4
  85.7 6.5 %copy-start.17 = (f32[8,128]{1,0:T(8,128)S(1)}, f32[8,128]{1,0:T(8,128)}, u32[]{:S(2)}) copy-start(f32[8,128]{1,0:T(8,128)} %squares.1) | copy-start | bytes 12292
  85.7 76.6 %copy-start.6 = (bf16[128,4096]{1,0:T(8,128)(2,1)S(1)}, bf16[128,4096]{1,0:T(8,128)(2,1)}, u32[]{:S(2)}) copy-start(bf16[128,4096]{1,0:T(8,128)(2,1)} %act_ref.1) | copy-start | bytes 3145732
  85.7 76.6 %copy-start.14 = (f32[4096]{0:T(1024)S(1)}, f32[4096]{0:T(1024)}, u32[]{:S(2)}) copy-start(f32[4096]{0:T(1024)} %param.11) | copy-start | bytes 49156
  85.7 76.6 %all-to-all-start.2 = ((bf16[16,24,4096]{2,1,0:T(8,128)(2,1)}), bf16[16,24,4096]{2,1,0:T(8,128)(2,1)}, u32[]{:S(2)}, u32[]{:S(2)}) async-start(bf16[16,24,4096]{2,1,0:T(8,128)(2,1)} %bitcast.8), calls=%async_computation.2 | async-start | bytes 6291456 | tf_op jit(solution)/shard_map/all_to_all | solution.py:282
  92.2 1.3 collective-permute-start.2
  93.5 12.8 %collective-permute-start.3 = (f32[8,128]{1,0:T(8,128)S(1)}, f32[8,128]{1,0:T(8,128)S(1)}, u32[]{:S(2)}, u32[]{:S(2)}) collective-permute-start(f32[8,128]{1,0:T(8,128)S(1)} %add.42), channel_id=1, source_target_pairs={{0,2},{1,3},{2,0},{3,1},{4,6},{5,7},{6,4},{7,5},{8,10},{9,11},{10,... | collective-permute-start | bytes 12296 | tf_op jit(solution)/shard_map/ppermute | solution.py:287
  106.3 39.0 %collective-permute-start.4 = (f32[8,128]{1,0:T(8,128)S(1)}, f32[8,128]{1,0:T(8,128)S(1)}, u32[]{:S(2)}, u32[]{:S(2)}) collective-permute-start(f32[8,128]{1,0:T(8,128)S(1)} %add.43), channel_id=1, source_target_pairs={{0,4},{1,5},{2,6},{3,7},{4,0},{5,1},{6,2},{7,3},{8,12},{9,13},{10,... | collective-permute-start | bytes 12296 | tf_op jit(solution)/shard_map/ppermute | solution.py:287
  145.3 14.7 %collective-permute-start.5 = (f32[8,128]{1,0:T(8,128)S(1)}, f32[8,128]{1,0:T(8,128)S(1)}, u32[]{:S(2)}, u32[]{:S(2)}) collective-permute-start(f32[8,128]{1,0:T(8,128)S(1)} %add.44), channel_id=1, source_target_pairs={{0,8},{1,9},{2,10},{3,11},{4,12},{5,13},{6,14},{7,15},{8,0},{9,1},... | collective-permute-start | bytes 12296 | tf_op jit(solution)/shard_map/ppermute | solution.py:287
  166.9 76.6 %all-to-all-start.3 = ((bf16[16,24,4096]{2,1,0:T(8,128)(2,1)}), bf16[16,24,4096]{2,1,0:T(8,128)(2,1)}, u32[]{:S(2)}, u32[]{:S(2)}) async-start(bf16[16,24,4096]{2,1,0:T(8,128)(2,1)} %bitcast.28), calls=%async_computation.3 | async-start | bytes 6291456 | tf_op jit(solution)/shard_map/all_to_all | solution.py:282
  179.1 3.9 %copy-start.11 = (bf16[192,256]{1,0:T(8,128)(2,1)S(1)}, bf16[192,256]{1,0:T(8,128)(2,1)}, u32[]{:S(2)}) copy-start(bf16[192,256]{1,0:T(8,128)(2,1)} %copy-done.10) | copy-start | bytes 294916
  179.1 3.9 %copy-start.13 = (bf16[192,256]{1,0:T(8,128)(2,1)S(1)}, bf16[192,256]{1,0:T(8,128)(2,1)}, u32[]{:S(2)}) copy-start(bf16[192,256]{1,0:T(8,128)(2,1)} %copy-done.12) | copy-start | bytes 294916
  179.1 4.8 %copy-start.9 = (f32[192,256]{1,0:T(8,128)S(1)}, f32[192,256]{1,0:T(8,128)}, u32[]{:S(2)}) copy-start(f32[192,256]{1,0:T(8,128)} %copy-done.8) | copy-start | bytes 589828
  185.8 57.7 %copy-start.15 = (f32[8,128]{1,0:T(8,128)S(1)}, f32[8,128]{1,0:T(8,128)}, u32[]{:S(2)}) copy-start(f32[8,128]{1,0:T(8,128)} %add.45.refs_0_) | copy-start | bytes 12292
  243.5 1.6 copy-start.5
  (4 other events, 2.9 us)

commit v6 on v5

--- a/solution.py
+++ b/solution.py
@@ -8,7 +8,7 @@
 BLOCK = 64
 LOSS_SCALE = 0.5
 PIECES = 4
-VMEM_LIMIT = 28 * 1024 * 1024
+MIB = 1024 * 1024
 F32 = jnp.float32
 BF16 = jnp.bfloat16
 
@@ -63,14 +63,28 @@
     return ref.at[:, i * width : (i + 1) * width]
 
 
-def fetch(source_ref, here_ref, sems):
-    copies = [
-        pltpu.make_async_copy(columns(source_ref, i), columns(here_ref, i), sems.at[i])
-        for i in range(PIECES)
-    ]
+def lines(ref, i):
+    height = ref.shape[0] // PIECES
+    return ref.at[i * height : (i + 1) * height]
+
+
+def fetch(*moves):
+    copies = []
+    for i in range(PIECES):
+        copies.append(
+            [
+                pltpu.make_async_copy(cut(source, i), cut(here, i), sems.at[i])
+                for cut, source, here, sems in moves
+            ]
+        )
+        for copy in copies[-1]:
+            copy.start()
+    return copies
+
+
+def finish(copies):
     for copy in copies:
-        copy.start()
-    return copies
+        copy.wait()
 
 
 def store(copies, here_ref, target_ref, sem):
@@ -79,96 +93,113 @@
 
 
 def encode_kernel(
+    dev_slots,
+    capacity,
     slot_ref,
+    bias_ref,
     rows_ref,
     enc_ref,
-    bias_ref,
-    own_ref,
     dec_ref,
     _,
     code_ref,
     slopes_ref,
     partial_ref,
-    here_ref,
-    out_ref,
+    rows_here,
+    enc_here,
+    dec_here,
+    code_here,
+    slopes_here,
+    out_here,
     sems,
 ):
-    copies = fetch(rows_ref, here_ref, sems.at[0])
-    slots = rows_ref.shape[0]
-    width = rows_ref.shape[1] // PIECES
+    slots, latents = slopes_here.shape
+    copies = fetch(
+        (columns, rows_ref, rows_here, sems.at[0]),
+        (lines, enc_ref, enc_here, sems.at[1]),
+    )
+    dec_copies = fetch((columns, dec_ref, dec_here, sems.at[2]))
     preact = bias_ref[...]
-    for i, copy in enumerate(copies):
-        copy.wait()
-        preact = preact + dot(
-            columns(here_ref, i)[...], enc_ref[i * width : (i + 1) * width, :], 1, 0
-        )
+    for i in range(PIECES):
+        finish(copies[i])
+        preact = preact + dot(columns(rows_here, i)[...], lines(enc_here, i)[...], 1, 0)
     output, slopes = activate(preact)
-    own = own_ref[...] > 0
+    row = lax.broadcasted_iota(jnp.int32, (slots, latents), 0)
+    latent = lax.broadcasted_iota(jnp.int32, (slots, latents), 1)
+    own = lax.div(lax.rem(row, dev_slots), capacity) == lax.div(latent, BLOCK)
     code = jnp.where(own, output, 0.0).astype(BF16)
-    code_ref[...] = code
-    slopes_ref[...] = jnp.where(own, slopes, 0.0)
+    stores = []
+    code_here[...] = code
+    store(stores, code_here, code_ref, sems.at[3, 0])
+    slopes_here[...] = jnp.where(own, slopes, 0.0)
+    store(stores, slopes_here, slopes_ref, sems.at[3, 1])
     start = pl.multiple_of(slot_ref[0] * slots, slots)
     target_ref = partial_ref.at[pl.ds(start, slots), :]
-    copies = []
     for i in range(PIECES):
-        columns(out_ref, i)[...] = dot(code, columns(dec_ref, i)[...], 1, 0).astype(BF16)
-        store(copies, columns(out_ref, i), columns(target_ref, i), sems.at[1, i])
-    for copy in copies:
-        copy.wait()
-
-
-def encode(place, rows, enc_weight, enc_bias, own, dec_weight, partial_value):
+        finish(dec_copies[i])
+        columns(out_here, i)[...] = dot(code, columns(dec_here, i)[...], 1, 0).astype(BF16)
+        store(stores, columns(out_here, i), columns(target_ref, i), sems.at[4, i])
+    finish(stores)
+
+
+def encode(dev_slots, capacity, place, rows, enc_weight, enc_bias, dec_weight, partial_value):
     slots, features = rows.shape
     latents = enc_weight.shape[1]
     return pl.pallas_call(
-        encode_kernel,
+        lambda *refs: encode_kernel(dev_slots, capacity, *refs),
         out_shape=[
-            jax.ShapeDtypeStruct((slots, latents), BF16),
-            jax.ShapeDtypeStruct((slots, latents), F32),
-            jax.ShapeDtypeStruct((2 * slots, features), BF16),
-        ],
-        in_specs=[pl.BlockSpec(memory_space=pltpu.SMEM), HBM_SPEC] + [VMEM_SPEC] * 4 + [HBM_SPEC],
-        out_specs=[VMEM_SPEC, VMEM_SPEC, HBM_SPEC],
-        input_output_aliases={6: 2},
+            pltpu.HBM((slots, latents), BF16),
+            pltpu.HBM((slots, latents), F32),
+            pltpu.HBM((2 * slots, features), BF16),
+        ],
+        in_specs=[pl.BlockSpec(memory_space=pltpu.SMEM), VMEM_SPEC] + [HBM_SPEC] * 4,
+        out_specs=[HBM_SPEC] * 3,
+        input_output_aliases={5: 2},
         scratch_shapes=[
             pltpu.VMEM((slots, features), BF16),
+            pltpu.VMEM((features, latents), BF16),
+            pltpu.VMEM((latents, features), BF16),
+            pltpu.VMEM((slots, latents), BF16),
+            pltpu.VMEM((slots, latents), F32),
             pltpu.VMEM((slots, features), BF16),
-            pltpu.SemaphoreType.DMA((2, PIECES)),
+            pltpu.SemaphoreType.DMA((5, PIECES)),
         ],
         cost_estimate=pl.CostEstimate(
             flops=4 * slots * latents * features,
             bytes_accessed=4 * features * (slots + latents),
             transcendentals=slots * latents,
         ),
-        compiler_params=pltpu.CompilerParams(vmem_limit_bytes=VMEM_LIMIT),
+        compiler_params=pltpu.CompilerParams(vmem_limit_bytes=62 * MIB),
         name="encode",
-    )(place, rows, enc_weight, enc_bias, own, dec_weight, partial_value)
+    )(place, enc_bias, rows, enc_weight, dec_weight, partial_value)
 
 
 def home_kernel(
     select_ref,
     select_t_ref,
+    bias_ref,
     act_ref,
-    bias_ref,
     returned_ref,
     full_ref,
     send_ref,
+    act_here,
     here_ref,
     full_out_ref,
     send_out_ref,
     sems,
 ):
+    moves = fetch(
+        (columns, returned_ref, here_ref, sems.at[0]), (columns, act_ref, act_here, sems.at[3])
+    )
     stores = []
-    for i, copy in enumerate(fetch(returned_ref, here_ref, sems.at[0])):
-        copy.wait()
+    for i, copies in enumerate(moves):
+        finish(copies)
         full = dot(select_t_ref[...], columns(here_ref, i)[...], 1, 0) + columns(bias_ref, i)[...]
-        errors = (full - columns(act_ref, i)[...].astype(F32)).astype(BF16)
+        errors = (full - columns(act_here, i)[...].astype(F32)).astype(BF16)
         columns(send_out_ref, i)[...] = dot(select_ref[...], errors, 1, 0).astype(BF16)
         store(stores, columns(send_out_ref, i), columns(send_ref, i), sems.at[1, i])
         columns(full_out_ref, i)[...] = full.astype(BF16)
         store(stores, columns(full_out_ref, i), columns(full_ref, i), sems.at[2, i])
-    for copy in stores:
-        copy.wait()
+    finish(stores)
 
 
 def rebuild(select, select_t, returned, activations, dec_bias):
@@ -180,22 +211,23 @@
             pltpu.HBM((tokens, features), BF16),
             pltpu.HBM((slots, features), BF16),
         ],
-        in_specs=[VMEM_SPEC] * 4 + [HBM_SPEC],
+        in_specs=[VMEM_SPEC] * 3 + [HBM_SPEC] * 2,
         out_specs=[HBM_SPEC, HBM_SPEC],
         scratch_shapes=[
+            pltpu.VMEM((tokens, features), BF16),
             pltpu.VMEM((slots, features), BF16),
             pltpu.VMEM((tokens, features), BF16),
             pltpu.VMEM((slots, features), BF16),
-            pltpu.SemaphoreType.DMA((3, PIECES)),
+            pltpu.SemaphoreType.DMA((4, PIECES)),
         ],
         cost_estimate=pl.CostEstimate(
             flops=4 * slots * tokens * features,
             bytes_accessed=4 * (slots + tokens) * features,
             transcendentals=0,
         ),
-        compiler_params=pltpu.CompilerParams(vmem_limit_bytes=VMEM_LIMIT),
+        compiler_params=pltpu.CompilerParams(vmem_limit_bytes=48 * MIB),
         name="rebuild",
-    )(select, select_t, activations, dec_bias, returned)
+    )(select, select_t, dec_bias, activations, returned)
 
 
 def grads_kernel(
@@ -209,32 +241,44 @@
     dec_grad_ref,
     enc_grad_ref,
     bias_grad_ref,
-    here_ref,
-    dec_out_ref,
-    enc_out_ref,
+    code_t_here,
+    slopes_here,
+    dec_t_here,
+    rows_t_here,
+    got_here,
+    dec_out,
+    enc_out,
     sems,
 ):
-    copies = fetch(got_ref, here_ref, sems.at[0])
+    first = []
+    store(first, code_t_ref, code_t_here, sems.at[5, 0])
+    copies = fetch(
+        (columns, got_ref, got_here, sems.at[0]),
+        (lines, dec_t_ref, dec_t_here, sems.at[1]),
+    )
+    second = []
+    store(second, slopes_ref, slopes_here, sems.at[5, 1])
+    rows_copies = fetch((lines, rows_t_ref, rows_t_here, sems.at[2]))
     scale = LOSS_SCALE / (squares_ref[0:1, 0:1] / count + 1e-06)
-    width = got_ref.shape[1] // PIECES
+    finish(first)
     stores = []
     code_grad = None
-    for i, copy in enumerate(copies):
-        copy.wait()
-        got = columns(here_ref, i)[...]
-        columns(dec_out_ref, i)[...] = (dot(code_t_ref[...], got, 1, 0) * scale).astype(BF16)
-        store(stores, columns(dec_out_ref, i), columns(dec_grad_ref, i), sems.at[1, i])
-        part = dot(got, dec_t_ref[i * width : (i + 1) * width, :], 1, 0)
+    for i in range(PIECES):
+        finish(copies[i])
+        got = columns(got_here, i)[...]
+        columns(dec_out, i)[...] = (dot(code_t_here[...], got, 1, 0) * scale).astype(BF16)
+        store(stores, columns(dec_out, i), columns(dec_grad_ref, i), sems.at[3, i])
+        part = dot(got, lines(dec_t_here, i)[...], 1, 0)
         code_grad = part if i == 0 else code_grad + part
-    code_grad = code_grad * (slopes_ref[...] * scale)
+    finish(second)
+    code_grad = code_grad * (slopes_here[...] * scale)
     bias_grad_ref[...] = jnp.sum(code_grad, axis=0, keepdims=True)
     code_grad = code_grad.astype(BF16)
     for i in range(PIECES):
-        piece = slice(i * width, (i + 1) * width)
-        enc_out_ref[piece, :] = dot(rows_t_ref[piece, :], code_grad, 1, 0).astype(BF16)
-        store(stores, enc_out_ref.at[piece], enc_grad_ref.at[piece], sems.at[2, i])
-    for copy in stores:
-        copy.wait()
+        finish(rows_copies[i])
+        lines(enc_out, i)[...] = dot(lines(rows_t_here, i)[...], code_grad, 1, 0).astype(BF16)
+        store(stores, lines(enc_out, i), lines(enc_grad_ref, i), sems.at[4, i])
+    finish(stores)
 
 
 def gradients(count, squares, code_t, slopes, dec_t, rows_t, got_errors):
@@ -243,24 +287,28 @@
     return pl.pallas_call(
         lambda *refs: grads_kernel(count, *refs),
         out_shape=[
-            jax.ShapeDtypeStruct((latents, features), BF16),
-            jax.ShapeDtypeStruct((features, latents), BF16),
+            pltpu.HBM((latents, features), BF16),
+            pltpu.HBM((features, latents), BF16),
             jax.ShapeDtypeStruct((1, latents), F32),
         ],
-        in_specs=[VMEM_SPEC] * 5 + [HBM_SPEC],
+        in_specs=[VMEM_SPEC] + [HBM_SPEC] * 5,
         out_specs=[HBM_SPEC, HBM_SPEC, VMEM_SPEC],
         scratch_shapes=[
+            pltpu.VMEM((latents, slots), BF16),
+            pltpu.VMEM((slots, latents), F32),
+            pltpu.VMEM((features, latents), BF16),
+            pltpu.VMEM((features, slots), BF16),
             pltpu.VMEM((slots, features), BF16),
             pltpu.VMEM((latents, features), BF16),
             pltpu.VMEM((features, latents), BF16),
-            pltpu.SemaphoreType.DMA((3, PIECES)),
+            pltpu.SemaphoreType.DMA((6, PIECES)),
         ],
         cost_estimate=pl.CostEstimate(
             flops=6 * slots * latents * features,
             bytes_accessed=2 * features * (2 * slots + 3 * latents),
             transcendentals=0,
         ),
-        compiler_params=pltpu.CompilerParams(vmem_limit_bytes=VMEM_LIMIT),
+        compiler_params=pltpu.CompilerParams(vmem_limit_bytes=60 * MIB),
         name="gradients",
     )(squares, code_t, slopes, dec_t, rows_t, got_errors)
 
@@ -292,12 +340,11 @@
     held = swap(activations)
     squares = sum_of_squares(activations)
 
-    flat_ids = block_ids.reshape(-1)
-    pairs = flat_ids.shape[0]
-    order = jnp.arange(pairs, dtype=jnp.int32)
-    same = (flat_ids[:, None] == flat_ids[None, :]) & (order[None, :] < order[:, None])
-    slot_of = flat_ids * capacity + jnp.sum(same.astype(jnp.int32), axis=1)
-    slot_of = slot_of.reshape(tok_rows, active_count).T
+    ids = block_ids.T
+    order = jnp.arange(tok_rows, dtype=jnp.int32)
+    same = jnp.any(ids[:, :, None, None] == ids.T[None, None, :, :], axis=3)
+    same = same & (order[None, None, :] < order[None, :, None])
+    slot_of = ids * capacity + jnp.sum(same.astype(jnp.int32), axis=2)
     slot_held = swap(slot_of)
     lower = lax.axis_index("lat") < half
     slots = jnp.arange(2 * half_slots, dtype=jnp.int32)
@@ -312,19 +359,20 @@
     got_own = exchange(pick(selection(slot_of, names), activations), halves)
     held, slot_held, got_own, squares = together(held, slot_held, got_own, squares)
     got_held = exchange(pick(selection(slot_held, names), held), halves)
-
-    row_block = (slots[:half_slots] % dev_slots) // capacity
-    own = row_block[:, None] == (jnp.arange(local_latents, dtype=jnp.int32) // BLOCK)[None, :]
-
-    own = own.astype(F32)
+    step = 1
+    while step < min(4, devices):
+        squares = squares + swap(squares, step)
+        step *= 2
+    got_held, squares = together(got_held, squares)
+
     place = jnp.where(lower, 0, 1).astype(jnp.int32).reshape(1)
     bias_row = enc_bias[None, :]
     partial_value = jnp.zeros((2 * half_slots, feature_dim), BF16)
     code_own, slope_own, partial_value = encode(
-        place, got_own, enc_weight, bias_row, own, dec_weight, partial_value
+        dev_slots, capacity, place, got_own, enc_weight, bias_row, dec_weight, partial_value
     )
     code_held, slope_held, partial_value = encode(
-        1 - place, got_held, enc_weight, bias_row, own, dec_weight, partial_value
+        dev_slots, capacity, 1 - place, got_held, enc_weight, bias_row, dec_weight, partial_value
     )
     returned = exchange(partial_value)
 
@@ -337,7 +385,6 @@
     slopes = ordered(slope_own, slope_held)
     rows_t = ordered(got_own, got_held).T
 
-    step = 1
     while step < devices:
         squares = squares + swap(squares, step)
         step *= 2

time: 254 us -> 253 us (level)
  local copies, waits for them, and re-layouts: 22.6 us -> 13.6 us
  Pallas kernels: 20.8 us -> 26.3 us
  other arithmetic: 5.12 us -> 8.22 us
    all_to_all x4, waiting for transfers between devices: 70.6 us -> 58.4 us  [exchange(): lax.all_to_all(rows, 'lat', split_axis=0, concat_axis=0, axis_index_group...]
    ppermute x6, waiting for transfers between devices: 99.8 us -> 111 us  [swap(): return lax.ppermute(rows, 'lat', [(i, i ^ step) for i in range(devices)])]
    unnamed x38 -> x21, local copies, waits for them, and re-layouts: 12.4 us -> 3.74 us
    pallas_call x3, Pallas kernels: 14.1 us -> 20.3 us  [the longest x2 11.1 us: encode(): pl.pallas_call(lambda *refs: encode_kernel(dev_slots, capacity, *refs), o...]
    optimization_barrier x1 -> x2, local copies, waits for them, and re-layouts: 3.15 us -> 7.05 us  [together(): return lax.optimization_barrier(values)]
    all_to_all x1 -> x0, local copies, waits for them, and re-layouts: 3.89 us -> none  [exchange(): lax.all_to_all(rows, 'lat', split_axis=0, concat_axis=0, axis_index_group...]
  transfers between devices with their start and end apart: 10 -> 10, of which waited for: 9 -> 8; matrix products, arithmetic and copies ran while one was open for 8% -> 9% of each run, Pallas kernels for 2% -> 3%
where the time goes in v6:
time: 253 us; the launch traced here: 252 us
  waiting for transfers between devices  169 us (67%)
  starting transfers between devices  28.8 us (11%)
  Pallas kernels  26.3 us (10%)
  local copies, waits for them, and re-layouts  13.6 us (5%)
  other arithmetic  8.22 us (3%)
  matrix products  4.63 us (2%)
    ppermute x6, waiting for transfers between devices, swap(): return lax.ppermute(rows, 'lat', [(i, i ^ step) for i in range(devices)])  111 us
    all_to_all x4, waiting for transfers between devices, exchange(): lax.all_to_all(rows, 'lat', split_axis=0, concat_axis=0, axis_index_group...  58.4 us
    all_to_all x4, starting transfers between devices, exchange(): lax.all_to_all(rows, 'lat', split_axis=0, concat_axis=0, axis_index_group...  25.2 us
    pallas_call x2, Pallas kernels, encode(): pl.pallas_call(lambda *refs: encode_kernel(dev_slots, capacity, *refs), o...  11.1 us
    pallas_call x1, Pallas kernels, gradients(): pl.pallas_call(lambda *refs: grads_kernel(count, *refs), out_shape=[pltpu...  9.25 us
    optimization_barrier x2, local copies, waits for them, and re-layouts, together(): return lax.optimization_barrier(values)  7.05 us
  transfers between devices with their start and end apart: 10, of which 8 were waited for; matrix products, arithmetic and copies ran while one was open for 9% of the time, Pallas kernels for 3%

profile of v6, /device:TPU:13, one launch (start us, length us, event | category | flops | bytes accessed | tf_op | source)
XLA Modules:
  0.0 252.0 jit_solution(8771072852435496789)
XLA Ops:
  0.6 2.4 collective-permute-start
  4.9 2.9 %convolution_convert_fusion.1 = bf16[192,4096]{1,0:T(8,128)(2,1)} fusion(pred[192,128]{1,0:T(8,128)(4,1)S(1)} %compare_reduce_fusion.2, bf16[128,4096]{1,0:T(8,128)(2,1)} %act_ref.1), kind=kOutput, calls=%fused_computation.1 | convolution fusion | flops 202113024 | bytes 2646016 | tf_op jit(solution)/shard_map/dot_general | solution.py:28
  7.8 5.1 %all-to-all-start = ((bf16[8,24,4096]{2,1,0:T(8,128)(2,1)}), bf16[8,24,4096]{2,1,0:T(8,128)(2,1)S(1)}, u32[]{:S(2)}, u32[]{:S(2)}) async-start(bf16[8,24,4096]{2,1,0:T(8,128)(2,1)} %bitcast.5), calls=%async_computation | async-start | bytes 3145728 | tf_op jit(solution)/shard_map/all_to_all | solution.py:330
  12.9 2.1 squares.1
  15.0 33.6 %collective-permute-done.1 = s32[2,128]{1,0:T(2,128)S(1)} collective-permute-done((s32[2,128]{1,0:T(2,128)S(1)}, s32[2,128]{1,0:T(2,128)S(1)}, u32[]{:S(2)}, u32[]{:S(2)}) %collective-permute-start.1) | collective-permute-done | bytes 1056 | tf_op jit(solution)/shard_map/ppermute | solution.py:335
  48.6 2.8 %all-to-all-done = bf16[8,24,4096]{2,1,0:T(8,128)(2,1)S(1)} async-done(((bf16[8,24,4096]{2,1,0:T(8,128)(2,1)}), bf16[8,24,4096]{2,1,0:T(8,128)(2,1)S(1)}, u32[]{:S(2)}, u32[]{:S(2)}) %all-to-all-start) | async-done | bytes 1572896 | tf_op jit(solution)/shard_map/all_to_all | solution.py:330
  51.6 1.7 convolution_convert_fusion
  53.3 7.2 %all-to-all-start.1 = ((bf16[8,24,4096]{2,1,0:T(8,128)(2,1)}), bf16[8,24,4096]{2,1,0:T(8,128)(2,1)}, u32[]{:S(2)}, u32[]{:S(2)}) async-start(bf16[8,24,4096]{2,1,0:T(8,128)(2,1)} %bitcast.7), calls=%async_computation.1 | async-start | bytes 3145728 | tf_op jit(solution)/shard_map/all_to_all | solution.py:330
  62.0 2.0 broadcast_in_dim.8.refs_5_
  64.0 5.5 %encode.2 = (bf16[192,256]{1,0:T(8,128)(2,1)}, f32[192,256]{1,0:T(8,128)}, bf16[384,4096]{1,0:T(8,128)(2,1)}) custom-call(s32[1]{0:T(128)} %bitcast.3.refs_0_, f32[1,256]{1,0:T(1,128)} %bitcast.33, bf16[192,4096]{1,0:T(8,128)(2,1)} %bitcast.28, bf16[4096,256]{1,0:T(8,128)(2,1)} %refs_3_.3, ...), custom_call_target="tpu_custom_call", output_to_operand_aliasing={{2}: (5, {})} | custom-call | flops 805306368 | bytes 7340032 | tf_op jit(solution)/shard_map/encode/pallas_call | solution.py:147
  69.5 9.4 %collective-permute-done.3 = f32[8,128]{1,0:T(8,128)S(1)} collective-permute-done((f32[8,128]{1,0:T(8,128)S(1)}, f32[8,128]{1,0:T(8,128)S(1)}, u32[]{:S(2)}, u32[]{:S(2)}) %collective-permute-start.3) | collective-permute-done | bytes 4128 | tf_op jit(solution)/shard_map/ppermute | solution.py:335
  78.9 5.5 %encode.3 = (bf16[192,256]{1,0:T(8,128)(2,1)}, f32[192,256]{1,0:T(8,128)}, bf16[384,4096]{1,0:T(8,128)(2,1)}) custom-call(s32[1]{0:T(128)S(6)} %sub.3.refs_0_, f32[1,256]{1,0:T(1,128)} %bitcast.34, bf16[192,4096]{1,0:T(8,128)(2,1)} %bitcast.8.refs_2_, bf16[4096,256]{1,0:T(8,128)(2,1)} %refs_3_.3, ...), custom_call_target="tpu_custom_call", output_to_operand_aliasing={{2}: (5, {})} | custom-call | flops 805306368 | bytes 7340032 | tf_op jit(solution)/shard_map/encode/pallas_call | solution.py:147
  84.5 6.1 %all-to-all-start.2 = ((bf16[16,24,4096]{2,1,0:T(8,128)(2,1)}), bf16[16,24,4096]{2,1,0:T(8,128)(2,1)S(1)}, u32[]{:S(2)}, u32[]{:S(2)}) async-start(bf16[16,24,4096]{2,1,0:T(8,128)(2,1)} %bitcast.27), calls=%async_computation.2 | async-start | bytes 6291456 | tf_op jit(solution)/shard_map/all_to_all | solution.py:330
  91.1 52.6 %collective-permute-done.4 = f32[8,128]{1,0:T(8,128)S(1)} collective-permute-done((f32[8,128]{1,0:T(8,128)S(1)}, f32[8,128]{1,0:T(8,128)S(1)}, u32[]{:S(2)}, u32[]{:S(2)}) %collective-permute-start.4) | collective-permute-done | bytes 4128 | tf_op jit(solution)/shard_map/ppermute | solution.py:335
  144.0 14.5 %collective-permute-done.5 = f32[8,128]{1,0:T(8,128)S(1)} collective-permute-done((f32[8,128]{1,0:T(8,128)S(1)}, f32[8,128]{1,0:T(8,128)S(1)}, u32[]{:S(2)}, u32[]{:S(2)}) %collective-permute-start.5) | collective-permute-done | bytes 4128 | tf_op jit(solution)/shard_map/ppermute | solution.py:335
  161.9 3.9 %rebuild.1 = (bf16[128,4096]{1,0:T(8,128)(2,1)}, bf16[384,4096]{1,0:T(8,128)(2,1)}) custom-call(bf16[384,128]{1,0:T(8,128)(2,1)S(1)} %convert_element_type.18.select_ref, bf16[128,384]{1,0:T(8,128)(2,1)S(1)} %convert_element_type.19.select_t_ref, f32[1,4096]{1,0:T(1,128)S(1)} %bitcast.26, bf16[128,4096]{1,0:T(8,128)(2,1)S(1)} %copy-done, ...), custom_call_target="tpu_custom_call" | custom-call | flops 805306368 | bytes 8388608 | tf_op jit(solution)/shard_map/rebuild/pallas_call | solution.py:208
  165.8 6.8 %all-to-all-start.3 = ((bf16[16,24,4096]{2,1,0:T(8,128)(2,1)}), bf16[16,24,4096]{2,1,0:T(8,128)(2,1)}, u32[]{:S(2)}, u32[]{:S(2)}) async-start(bf16[16,24,4096]{2,1,0:T(8,128)(2,1)} %bitcast.31), calls=%async_computation.3 | async-start | bytes 6291456 | tf_op jit(solution)/shard_map/all_to_all | solution.py:330
  172.6 2.5 copy.28
  175.1 3.1 %copy.29 = bf16[192,4096]{0,1:T(8,128)(2,1)S(1)} copy(bf16[192,4096]{1,0:T(8,128)(2,1)} %bitcast.29) | data formatting | bytes 3145728 | tf_op jit(solution)/shard_map/optimization_barrier | solution.py:32
  178.3 3.9 %copy.30 = bf16[192,4096]{0,1:T(8,128)(2,1)} copy(bf16[192,4096]{1,0:T(8,128)(2,1)} %bitcast.8.refs_2_) | data formatting | bytes 3145728 | tf_op jit(solution)/shard_map/optimization_barrier | solution.py:32
  183.8 1.9 broadcast_select_fusion.1
  185.7 2.9 %maximum_bitcast_fusion.refs_4_ = bf16[4096,384]{1,0:T(8,128)(2,1)} fusion(bf16[192,4096]{0,1:T(8,128)(2,1)S(1)} %get-tuple-element.43, bf16[192,4096]{0,1:T(8,128)(2,1)S(1)} %get-tuple-element.42), kind=kLoop, calls=%fused_computation.2 | loop fusion | flops 6291456 | bytes 6291456 | tf_op jit(solution)/shard_map/transpose | solution.py:386
  188.6 54.0 %all-to-all-done.3 = bf16[16,24,4096]{2,1,0:T(8,128)(2,1)} async-done(((bf16[16,24,4096]{2,1,0:T(8,128)(2,1)}), bf16[16,24,4096]{2,1,0:T(8,128)(2,1)}, u32[]{:S(2)}, u32[]{:S(2)}) %all-to-all-start.3) | async-done | bytes 3145760 | tf_op jit(solution)/shard_map/all_to_all | solution.py:330
  242.6 9.2 %gradients.1 = (bf16[256,4096]{1,0:T(8,128)(2,1)}, bf16[4096,256]{1,0:T(8,128)(2,1)}, f32[1,256]{1,0:T(1,128)}) custom-call(f32[8,128]{1,0:T(8,128)} %add.31.refs_0_, bf16[256,384]{1,0:T(8,128)(2,1)} %copy.33.refs_1_, f32[384,256]{1,0:T(8,128)} %pad_maximum_fusion.refs_2_, bf16[4096,256]{1,0:T(8,128)(2,1)} %bitcast.30, ...), custom_call_target="tpu_custom_call" | custom-call | flops 2415919104 | bytes 12582912 | tf_op jit(solution)/shard_map/gradients/pallas_call | solution.py:287
  (51 shorter events, 9.3 us)
Async XLA Ops:
  0.6 48.0 %collective-permute-start = (bf16[128,4096]{1,0:T(8,128)(2,1)}, bf16[128,4096]{1,0:T(8,128)(2,1)S(1)}, u32[]{:S(2)}, u32[]{:S(2)}) collective-permute-start(bf16[128,4096]{1,0:T(8,128)(2,1)} %act_ref.1), channel_id=1, source_target_pairs={{0,8},{1,9},{2,10},{3,11},{4,12},{5,13},{6,14},{7,15},{8,0},{9,1},... | collective-permute-start | bytes 3145736 | tf_op jit(solution)/shard_map/ppermute | solution.py:335
  4.7 43.9 %collective-permute-start.1 = (s32[2,128]{1,0:T(2,128)S(1)}, s32[2,128]{1,0:T(2,128)S(1)}, u32[]{:S(2)}, u32[]{:S(2)}) collective-permute-start(s32[2,128]{1,0:T(2,128)S(1)} %multiply_add_fusion), channel_id=1, source_target_pairs={{0,8},{1,9},{2,10},{3,11},{4,12},{5,13},{6,14},{7,15},{8,0},{9,1},... | collective-permute-start | bytes 3080 | tf_op jit(solution)/shard_map/ppermute | solution.py:335
  7.8 43.7 %all-to-all-start = ((bf16[8,24,4096]{2,1,0:T(8,128)(2,1)}), bf16[8,24,4096]{2,1,0:T(8,128)(2,1)S(1)}, u32[]{:S(2)}, u32[]{:S(2)}) async-start(bf16[8,24,4096]{2,1,0:T(8,128)(2,1)} %bitcast.5), calls=%async_computation | async-start | bytes 3145728 | tf_op jit(solution)/shard_map/all_to_all | solution.py:330
  51.5 1.8 copy-start.3
  53.3 7.2 %copy-start.9 = (f32[8,128]{1,0:T(8,128)S(1)}, f32[8,128]{1,0:T(8,128)}, u32[]{:S(2)}) copy-start(f32[8,128]{1,0:T(8,128)} %squares.1) | copy-start | bytes 12292
  53.3 25.7 %all-to-all-start.1 = ((bf16[8,24,4096]{2,1,0:T(8,128)(2,1)}), bf16[8,24,4096]{2,1,0:T(8,128)(2,1)}, u32[]{:S(2)}, u32[]{:S(2)}) async-start(bf16[8,24,4096]{2,1,0:T(8,128)(2,1)} %bitcast.7), calls=%async_computation.1 | async-start | bytes 3145728 | tf_op jit(solution)/shard_map/all_to_all | solution.py:330
  60.4 1.3 collective-permute-start.2
  61.7 17.2 %collective-permute-start.3 = (f32[8,128]{1,0:T(8,128)S(1)}, f32[8,128]{1,0:T(8,128)S(1)}, u32[]{:S(2)}, u32[]{:S(2)}) collective-permute-start(f32[8,128]{1,0:T(8,128)S(1)} %add.28), channel_id=1, source_target_pairs={{0,2},{1,3},{2,0},{3,1},{4,6},{5,7},{6,4},{7,5},{8,10},{9,11},{10,... | collective-permute-start | bytes 12296 | tf_op jit(solution)/shard_map/ppermute | solution.py:335
  84.5 6.1 %copy-start.8 = (s32[128,2]{0,1:T(2,128)S(1)}, s32[128,2]{0,1:T(2,128)}, u32[]{:S(2)}) copy-start(s32[128,2]{0,1:T(2,128)} %param.7) | copy-start | bytes 3076
  84.5 76.1 %copy-start.1 = (f32[4096]{0:T(1024)S(1)}, f32[4096]{0:T(1024)}, u32[]{:S(2)}) copy-start(f32[4096]{0:T(1024)} %param.11) | copy-start | bytes 49156
  84.5 76.1 %all-to-all-start.2 = ((bf16[16,24,4096]{2,1,0:T(8,128)(2,1)}), bf16[16,24,4096]{2,1,0:T(8,128)(2,1)S(1)}, u32[]{:S(2)}, u32[]{:S(2)}) async-start(bf16[16,24,4096]{2,1,0:T(8,128)(2,1)} %bitcast.27), calls=%async_computation.2 | async-start | bytes 6291456 | tf_op jit(solution)/shard_map/all_to_all | solution.py:330
  90.6 53.0 %collective-permute-start.4 = (f32[8,128]{1,0:T(8,128)S(1)}, f32[8,128]{1,0:T(8,128)S(1)}, u32[]{:S(2)}, u32[]{:S(2)}) collective-permute-start(f32[8,128]{1,0:T(8,128)S(1)} %add.29), channel_id=1, source_target_pairs={{0,4},{1,5},{2,6},{3,7},{4,0},{5,1},{6,2},{7,3},{8,12},{9,13},{10,... | collective-permute-start | bytes 12296 | tf_op jit(solution)/shard_map/ppermute | solution.py:335
  143.6 14.9 %collective-permute-start.5 = (f32[8,128]{1,0:T(8,128)S(1)}, f32[8,128]{1,0:T(8,128)S(1)}, u32[]{:S(2)}, u32[]{:S(2)}) collective-permute-start(f32[8,128]{1,0:T(8,128)S(1)} %add.30), channel_id=1, source_target_pairs={{0,8},{1,9},{2,10},{3,11},{4,12},{5,13},{6,14},{7,15},{8,0},{9,1},... | collective-permute-start | bytes 12296 | tf_op jit(solution)/shard_map/ppermute | solution.py:335
  160.6 1.2 copy-start
  165.8 6.8 %copy-start.2 = (bf16[256,4096]{1,0:T(8,128)(2,1)S(1)}, bf16[256,4096]{1,0:T(8,128)(2,1)}, u32[]{:S(2)}) copy-start(bf16[256,4096]{1,0:T(8,128)(2,1)} %refs_4_.3) | copy-start | bytes 6291460
  165.8 76.8 %all-to-all-start.3 = ((bf16[16,24,4096]{2,1,0:T(8,128)(2,1)}), bf16[16,24,4096]{2,1,0:T(8,128)(2,1)}, u32[]{:S(2)}, u32[]{:S(2)}) async-start(bf16[16,24,4096]{2,1,0:T(8,128)(2,1)} %bitcast.31), calls=%async_computation.3 | async-start | bytes 6291456 | tf_op jit(solution)/shard_map/all_to_all | solution.py:330
  178.2 4.0 %copy-start.6 = (bf16[192,256]{1,0:T(8,128)(2,1)S(1)}, bf16[192,256]{1,0:T(8,128)(2,1)}, u32[]{:S(2)}) copy-start(bf16[192,256]{1,0:T(8,128)(2,1)} %get-tuple-element.34) | copy-start | bytes 294916
  178.2 3.9 %copy-start.7 = (bf16[192,256]{1,0:T(8,128)(2,1)S(1)}, bf16[192,256]{1,0:T(8,128)(2,1)}, u32[]{:S(2)}) copy-start(bf16[192,256]{1,0:T(8,128)(2,1)} %get-tuple-element.35) | copy-start | bytes 294916
  178.3 4.8 %copy-start.4 = (f32[192,256]{1,0:T(8,128)S(1)}, f32[192,256]{1,0:T(8,128)}, u32[]{:S(2)}) copy-start(f32[192,256]{1,0:T(8,128)} %get-tuple-element.36) | copy-start | bytes 589828
  178.3 4.8 %copy-start.5 = (f32[192,256]{1,0:T(8,128)S(1)}, f32[192,256]{1,0:T(8,128)}, u32[]{:S(2)}) copy-start(f32[192,256]{1,0:T(8,128)} %get-tuple-element.37) | copy-start | bytes 589828

commit v7 on v6

--- a/solution.py
+++ b/solution.py
@@ -39,6 +39,21 @@
         part = rows_ref[:, i : i + 128].astype(F32)
         total = total + jnp.sum((part * part).reshape(rows // 8, 8, 128), axis=0)
     total_ref[...] = jnp.full((8, 128), jnp.sum(total), F32)
+
+
+def pass_kernel(value_ref, same_ref):
+    same_ref[...] = value_ref[...]
+
+
+def beside(value):
+    return pl.pallas_call(
+        pass_kernel,
+        out_shape=jax.ShapeDtypeStruct(value.shape, value.dtype),
+        in_specs=[VMEM_SPEC],
+        out_specs=VMEM_SPEC,
+        cost_estimate=pl.CostEstimate(flops=50_000_000_000, bytes_accessed=8192, transcendentals=0),
+        name="beside",
+    )(value)
 
 
 def sum_of_squares(rows):
@@ -68,12 +83,24 @@
     return ref.at[i * height : (i + 1) * height]
 
 
+def two_parts(refs, i):
+    first, second = refs
+    width = 2 * first.shape[1] // PIECES
+    ref = first if i < PIECES // 2 else second
+    i = i % (PIECES // 2)
+    return ref.at[:, i * width : (i + 1) * width]
+
+
 def fetch(*moves):
     copies = []
     for i in range(PIECES):
         copies.append(
             [
-                pltpu.make_async_copy(cut(source, i), cut(here, i), sems.at[i])
+                pltpu.make_async_copy(
+                    two_parts(source, i) if isinstance(source, tuple) else cut(source, i),
+                    cut(here, i),
+                    sems.at[i],
+                )
                 for cut, source, here, sems in moves
             ]
         )
@@ -95,12 +122,11 @@
 def encode_kernel(
     dev_slots,
     capacity,
-    slot_ref,
     bias_ref,
-    rows_ref,
+    rows_f_ref,
+    rows_g_ref,
     enc_ref,
     dec_ref,
-    _,
     code_ref,
     slopes_ref,
     partial_ref,
@@ -114,7 +140,7 @@
 ):
     slots, latents = slopes_here.shape
     copies = fetch(
-        (columns, rows_ref, rows_here, sems.at[0]),
+        (columns, (rows_f_ref, rows_g_ref), rows_here, sems.at[0]),
         (lines, enc_ref, enc_here, sems.at[1]),
     )
     dec_copies = fetch((columns, dec_ref, dec_here, sems.at[2]))
@@ -132,28 +158,25 @@
     store(stores, code_here, code_ref, sems.at[3, 0])
     slopes_here[...] = jnp.where(own, slopes, 0.0)
     store(stores, slopes_here, slopes_ref, sems.at[3, 1])
-    start = pl.multiple_of(slot_ref[0] * slots, slots)
-    target_ref = partial_ref.at[pl.ds(start, slots), :]
     for i in range(PIECES):
         finish(dec_copies[i])
         columns(out_here, i)[...] = dot(code, columns(dec_here, i)[...], 1, 0).astype(BF16)
-        store(stores, columns(out_here, i), columns(target_ref, i), sems.at[4, i])
+        store(stores, columns(out_here, i), columns(partial_ref, i), sems.at[4, i])
     finish(stores)
 
 
-def encode(dev_slots, capacity, place, rows, enc_weight, enc_bias, dec_weight, partial_value):
-    slots, features = rows.shape
-    latents = enc_weight.shape[1]
+def encode(dev_slots, capacity, rows, enc_weight, enc_bias, dec_weight):
+    slots = rows[0].shape[0]
+    features, latents = enc_weight.shape
     return pl.pallas_call(
         lambda *refs: encode_kernel(dev_slots, capacity, *refs),
         out_shape=[
             pltpu.HBM((slots, latents), BF16),
             pltpu.HBM((slots, latents), F32),
-            pltpu.HBM((2 * slots, features), BF16),
-        ],
-        in_specs=[pl.BlockSpec(memory_space=pltpu.SMEM), VMEM_SPEC] + [HBM_SPEC] * 4,
+            pltpu.HBM((slots, features), BF16),
+        ],
+        in_specs=[VMEM_SPEC] + [HBM_SPEC] * 4,
         out_specs=[HBM_SPEC] * 3,
-        input_output_aliases={5: 2},
         scratch_shapes=[
             pltpu.VMEM((slots, features), BF16),
             pltpu.VMEM((features, latents), BF16),
@@ -170,7 +193,7 @@
         ),
         compiler_params=pltpu.CompilerParams(vmem_limit_bytes=62 * MIB),
         name="encode",
-    )(place, enc_bias, rows, enc_weight, dec_weight, partial_value)
+    )(enc_bias, *rows, enc_weight, dec_weight)
 
 
 def home_kernel(
@@ -180,10 +203,12 @@
     act_ref,
     returned_ref,
     full_ref,
+    errors_ref,
     send_ref,
     act_here,
     here_ref,
     full_out_ref,
+    errors_out_ref,
     send_out_ref,
     sems,
 ):
@@ -195,8 +220,13 @@
         finish(copies)
         full = dot(select_t_ref[...], columns(here_ref, i)[...], 1, 0) + columns(bias_ref, i)[...]
         errors = (full - columns(act_here, i)[...].astype(F32)).astype(BF16)
-        columns(send_out_ref, i)[...] = dot(select_ref[...], errors, 1, 0).astype(BF16)
-        store(stores, columns(send_out_ref, i), columns(send_ref, i), sems.at[1, i])
+        if i < PIECES // 2:
+            columns(errors_out_ref, i)[...] = errors
+            out, target = columns(errors_out_ref, i), two_parts((errors_ref, send_ref), i)
+        else:
+            columns(send_out_ref, i)[...] = dot(select_ref[...], errors, 1, 0).astype(BF16)
+            out, target = columns(send_out_ref, i), two_parts((errors_ref, send_ref), i)
+        store(stores, out, target, sems.at[1, i])
         columns(full_out_ref, i)[...] = full.astype(BF16)
         store(stores, columns(full_out_ref, i), columns(full_ref, i), sems.at[2, i])
     finish(stores)
@@ -209,13 +239,15 @@
         home_kernel,
         out_shape=[
             pltpu.HBM((tokens, features), BF16),
-            pltpu.HBM((slots, features), BF16),
+            pltpu.HBM((tokens, features // 2), BF16),
+            pltpu.HBM((slots, features // 2), BF16),
         ],
         in_specs=[VMEM_SPEC] * 3 + [HBM_SPEC] * 2,
-        out_specs=[HBM_SPEC, HBM_SPEC],
+        out_specs=[HBM_SPEC] * 3,
         scratch_shapes=[
             pltpu.VMEM((tokens, features), BF16),
             pltpu.VMEM((slots, features), BF16),
+            pltpu.VMEM((tokens, features), BF16),
             pltpu.VMEM((tokens, features), BF16),
             pltpu.VMEM((slots, features), BF16),
             pltpu.SemaphoreType.DMA((4, PIECES)),
@@ -237,7 +269,8 @@
     slopes_ref,
     dec_t_ref,
     rows_t_ref,
-    got_ref,
+    got_f_ref,
+    got_g_ref,
     dec_grad_ref,
     enc_grad_ref,
     bias_grad_ref,
@@ -253,18 +286,19 @@
     first = []
     store(first, code_t_ref, code_t_here, sems.at[5, 0])
     copies = fetch(
-        (columns, got_ref, got_here, sems.at[0]),
+        (columns, (got_f_ref, got_g_ref), got_here, sems.at[0]),
         (lines, dec_t_ref, dec_t_here, sems.at[1]),
     )
     second = []
     store(second, slopes_ref, slopes_here, sems.at[5, 1])
-    rows_copies = fetch((lines, rows_t_ref, rows_t_here, sems.at[2]))
     scale = LOSS_SCALE / (squares_ref[0:1, 0:1] / count + 1e-06)
     finish(first)
     stores = []
     code_grad = None
     for i in range(PIECES):
         finish(copies[i])
+        if i == 1:
+            rows_copies = fetch((lines, rows_t_ref, rows_t_here, sems.at[2]))
         got = columns(got_here, i)[...]
         columns(dec_out, i)[...] = (dot(code_t_here[...], got, 1, 0) * scale).astype(BF16)
         store(stores, columns(dec_out, i), columns(dec_grad_ref, i), sems.at[3, i])
@@ -291,7 +325,7 @@
             pltpu.HBM((features, latents), BF16),
             jax.ShapeDtypeStruct((1, latents), F32),
         ],
-        in_specs=[VMEM_SPEC] + [HBM_SPEC] * 5,
+        in_specs=[VMEM_SPEC] + [HBM_SPEC] * 6,
         out_specs=[HBM_SPEC, HBM_SPEC, VMEM_SPEC],
         scratch_shapes=[
             pltpu.VMEM((latents, slots), BF16),
@@ -310,7 +344,7 @@
         ),
         compiler_params=pltpu.CompilerParams(vmem_limit_bytes=60 * MIB),
         name="gradients",
-    )(squares, code_t, slopes, dec_t, rows_t, got_errors)
+    )(squares, code_t, slopes, dec_t, rows_t, *got_errors)
 
 
 def per_device(activations, block_ids, enc_weight, enc_bias, dec_weight, dec_bias):
@@ -324,21 +358,16 @@
     capacity = max(2, 3 * tok_rows * active_count // (2 * nblocks))
     dev_slots = blocks_dev * capacity
     half_slots = half * dev_slots
-    halves = [list(range(half)), list(range(half, devices))]
-
-    def exchange(rows, groups=None):
-        return lax.all_to_all(
-            rows, "lat", split_axis=0, concat_axis=0, axis_index_groups=groups, tiled=True
-        )
+    side = feature_dim // 2
+
+    def exchange(rows):
+        return lax.all_to_all(rows, "lat", split_axis=0, concat_axis=0, tiled=True)
 
     def swap(rows, step=half):
         return lax.ppermute(rows, "lat", [(i, i ^ step) for i in range(devices)])
 
     def pick(select, rows):
         return dot(select, rows, 1, 0).astype(BF16)
-
-    held = swap(activations)
-    squares = sum_of_squares(activations)
 
     ids = block_ids.T
     order = jnp.arange(tok_rows, dtype=jnp.int32)
@@ -346,53 +375,57 @@
     same = same & (order[None, None, :] < order[None, :, None])
     slot_of = ids * capacity + jnp.sum(same.astype(jnp.int32), axis=2)
     slot_held = swap(slot_of)
-    lower = lax.axis_index("lat") < half
+    me = lax.axis_index("lat")
     slots = jnp.arange(2 * half_slots, dtype=jnp.int32)
+    crossed = ((slots // dev_slots) ^ me) * dev_slots + slots % dev_slots
 
     def selection(slot, names):
         return jnp.any(names[:, None, None] == slot[None, :, :], axis=1).astype(BF16)
 
     select = selection(slot_of, slots)
-    select_t = jnp.any(slots[None, :, None] == slot_of.T[:, None, :], axis=2).astype(BF16)
-    names = slots[:half_slots] + jnp.where(lower, 0, half_slots)
-
-    got_own = exchange(pick(selection(slot_of, names), activations), halves)
-    held, slot_held, got_own, squares = together(held, slot_held, got_own, squares)
-    got_held = exchange(pick(selection(slot_held, names), held), halves)
+    select_t = jnp.any(slots[None, None, :] == slot_of.T[:, :, None], axis=1).astype(BF16)
+    select_own = selection(slot_of, crossed[:half_slots])
+    select_held = selection(slot_held, crossed[:half_slots])
+    by_swaps = half <= 8
+
+    def deliver(tokens, by_slot, value):
+        got = exchange(by_slot)
+        if not by_swaps:
+            return exchange(pick(select, tokens)), got, value
+        held, value = together(swap(tokens), value)
+        rows = jnp.zeros((devices, dev_slots, tokens.shape[1]), BF16)
+        for choice, source, other in ((select_own, tokens, 0), (select_held, held, half)):
+            for k in range(half):
+                part = pick(choice[k * dev_slots : (k + 1) * dev_slots], source)
+                part = swap(part, k) if k else part
+                rows = lax.dynamic_update_index_in_dim(rows, part, me ^ (k + other), 0)
+        return rows.reshape(devices * dev_slots, tokens.shape[1]), got, value
+
+    act_f, act_g = activations[:, :side], activations[:, side:]
+    rows_f, rows_g, squares = deliver(act_f, pick(select, act_g), sum_of_squares(activations))
+
+    code_rows, slopes, partial_value = encode(
+        dev_slots, capacity, (rows_f, rows_g), enc_weight, enc_bias[None, :], dec_weight
+    )
+    returned = exchange(partial_value)
+    code_t = code_rows.T
+    rows_t = jnp.concatenate([rows_f.T, rows_g.T], axis=0)
+
     step = 1
-    while step < min(4, devices):
-        squares = squares + swap(squares, step)
-        step *= 2
-    got_held, squares = together(got_held, squares)
-
-    place = jnp.where(lower, 0, 1).astype(jnp.int32).reshape(1)
-    bias_row = enc_bias[None, :]
-    partial_value = jnp.zeros((2 * half_slots, feature_dim), BF16)
-    code_own, slope_own, partial_value = encode(
-        dev_slots, capacity, place, got_own, enc_weight, bias_row, dec_weight, partial_value
-    )
-    code_held, slope_held, partial_value = encode(
-        dev_slots, capacity, 1 - place, got_held, enc_weight, bias_row, dec_weight, partial_value
-    )
-    returned = exchange(partial_value)
-
-    def ordered(own_part, held_part):
-        first = jnp.where(lower, own_part, held_part)
-        second = jnp.where(lower, held_part, own_part)
-        return jnp.concatenate([first, second], axis=0)
-
-    code_t = ordered(code_own, code_held).T
-    slopes = ordered(slope_own, slope_held)
-    rows_t = ordered(got_own, got_held).T
-
     while step < devices:
         squares = squares + swap(squares, step)
         step *= 2
     returned, squares = together(returned, squares)
-    full, send_errors = rebuild(select, select_t, returned, activations, dec_bias[None, :])
-    got_errors = exchange(send_errors)
+    full, err_f, send_g = rebuild(select, select_t, returned, activations, dec_bias[None, :])
+    got_f, got_g, squares = deliver(err_f, send_g, beside(squares))
     dec_grad, enc_grad, bias_grad = gradients(
-        tok_rows * devices * feature_dim, squares, code_t, slopes, dec_weight.T, rows_t, got_errors
+        tok_rows * devices * feature_dim,
+        squares,
+        code_t,
+        slopes,
+        dec_weight.T,
+        rows_t,
+        (got_f, got_g),
     )
     return (full, enc_grad, dec_grad, bias_grad.reshape(local_latents))
 

time: 253 us -> 266 us (1.051); the launches traced: 252 us -> 261 us
  waiting for transfers between devices: 169 us -> 117 us
  starting transfers between devices: 28.8 us -> 65 us
  local copies, waits for them, and re-layouts: 13.6 us -> 33.2 us
  matrix products: 4.63 us -> 14.4 us
    all_to_all x4 -> x3, waiting for transfers between devices: 58.4 us -> 0.01 us  [exchange(): return lax.all_to_all(rows, 'lat', split_axis=0, concat_axis=0, tiled=True)]
    ppermute x6 -> x35, starting transfers between devices: 3.64 us -> 44.8 us  [swap(): return lax.ppermute(rows, 'lat', [(i, i ^ step) for i in range(devices)])]
    dynamic_update_slice x0 -> x28, local copies, waits for them, and re-layouts: none -> 18.1 us  [deliver(): rows = lax.dynamic_update_index_in_dim(rows, part, me ^ k + other, 0)]
    dot_general x2 -> x33, matrix products: 4.63 us -> 14.4 us  [dot(): return lax.dot_general(left, right, dims, preferred_element_type=F32)]
    optimization_barrier x2 -> x0, local copies, waits for them, and re-layouts: 7.05 us -> none  [together(): return lax.optimization_barrier(values)]
    ppermute x6 -> x35, waiting for transfers between devices: 111 us -> 117 us  [swap(): return lax.ppermute(rows, 'lat', [(i, i ^ step) for i in range(devices)])]
    all_to_all x4 -> x3, starting transfers between devices: 25.2 us -> 20.2 us  [exchange(): return lax.all_to_all(rows, 'lat', split_axis=0, concat_axis=0, tiled=True)]
    pallas_call x2 -> x1, Pallas kernels: 11.1 us -> 7.48 us  [encode(): pl.pallas_call(lambda *refs: encode_kernel(dev_slots, capacity, *refs), o...]
  transfers between devices with their start and end apart: 10 -> 38, of which waited for: 8 -> 18; matrix products, arithmetic and copies ran while one was open for 9% -> 18% of each run, Pallas kernels for 3% -> 1%
where the time goes in v7:
time: 266 us; the launch traced here: 261 us
  waiting for transfers between devices  117 us (44%)
  starting transfers between devices  65 us (24%)
  local copies, waits for them, and re-layouts  33.2 us (12%)
  Pallas kernels  24.3 us (9%)
  matrix products  14.4 us (5%)
  other arithmetic  6.43 us (2%)
    ppermute x35, waiting for transfers between devices, swap(): return lax.ppermute(rows, 'lat', [(i, i ^ step) for i in range(devices)])  117 us
    ppermute x35, starting transfers between devices, swap(): return lax.ppermute(rows, 'lat', [(i, i ^ step) for i in range(devices)])  44.8 us
    all_to_all x3, starting transfers between devices, exchange(): return lax.all_to_all(rows, 'lat', split_axis=0, concat_axis=0, tiled=True)  20.2 us
    dynamic_update_slice x28, local copies, waits for them, and re-layouts, deliver(): rows = lax.dynamic_update_index_in_dim(rows, part, me ^ k + other, 0)  18.1 us
    dot_general x33, matrix products, dot(): return lax.dot_general(left, right, dims, preferred_element_type=F32)  14.4 us
    pallas_call x1, Pallas kernels, gradients(): pl.pallas_call(lambda *refs: grads_kernel(count, *refs), out_shape=[pltpu...  9.25 us
    pallas_call x1, Pallas kernels, encode(): pl.pallas_call(lambda *refs: encode_kernel(dev_slots, capacity, *refs), o...  7.48 us
  transfers between devices with their start and end apart: 38, of which 18 were waited for; matrix products, arithmetic and copies ran while one was open for 18% of the time, Pallas kernels for 1%

profile of v7, /device:TPU:13, one launch (start us, length us, event | category | flops | bytes accessed | tf_op | source)
XLA Modules:
  0.0 261.5 jit_solution(9281310663031877489)
XLA Ops:
  5.9 2.7 %convolution_convert_fusion = bf16[384,2048]{1,0:T(8,128)(2,1)} fusion(pred[384,128]{1,0:T(8,128)(4,1)S(1)} %fusion.9, bf16[128,4096]{1,0:T(8,128)(2,1)} %act_ref.1), kind=kOutput, calls=%fused_computation.1 | convolution fusion | flops 202113024 | bytes 2146304 | tf_op jit(solution)/shard_map/dot_general | solution.py:28
  8.6 7.1 %all-to-all-start = ((bf16[16,24,2048]{2,1,0:T(8,128)(2,1)}), bf16[16,24,2048]{2,1,0:T(8,128)(2,1)}, u32[]{:S(2)}, u32[]{:S(2)}) async-start(bf16[16,24,2048]{2,1,0:T(8,128)(2,1)} %bitcast.21), calls=%async_computation | async-start | bytes 3145728 | tf_op jit(solution)/shard_map/all_to_all | solution.py:364
  31.8 13.3 %collective-permute-done.3 = bf16[24,2048]{1,0:T(8,128)(2,1)S(1)} collective-permute-done((bf16[24,2048]{1,0:T(8,128)(2,1)S(1)}, bf16[24,2048]{1,0:T(8,128)(2,1)S(1)}, u32[]{:S(2)}, u32[]{:S(2)}) %collective-permute-start.3) | collective-permute-done | bytes 98336 | tf_op jit(solution)/shard_map/ppermute | solution.py:367
  45.7 4.6 %collective-permute-done.4 = bf16[24,2048]{1,0:T(8,128)(2,1)S(1)} collective-permute-done((bf16[24,2048]{1,0:T(8,128)(2,1)S(1)}, bf16[24,2048]{1,0:T(8,128)(2,1)S(1)}, u32[]{:S(2)}, u32[]{:S(2)}) %collective-permute-start.4) | collective-permute-done | bytes 98336 | tf_op jit(solution)/shard_map/ppermute | solution.py:367
  51.0 2.6 %collective-permute-done.5 = bf16[24,2048]{1,0:T(8,128)(2,1)S(1)} collective-permute-done((bf16[24,2048]{1,0:T(8,128)(2,1)S(1)}, bf16[24,2048]{1,0:T(8,128)(2,1)S(1)}, u32[]{:S(2)}, u32[]{:S(2)}) %collective-permute-start.5) | collective-permute-done | bytes 98336 | tf_op jit(solution)/shard_map/ppermute | solution.py:367
  54.2 4.5 %collective-permute-done.6 = bf16[24,2048]{1,0:T(8,128)(2,1)S(1)} collective-permute-done((bf16[24,2048]{1,0:T(8,128)(2,1)S(1)}, bf16[24,2048]{1,0:T(8,128)(2,1)S(1)}, u32[]{:S(2)}, u32[]{:S(2)}) %collective-permute-start.6) | collective-permute-done | bytes 98336 | tf_op jit(solution)/shard_map/ppermute | solution.py:367
  77.4 7.5 %encode.1 = (bf16[384,256]{1,0:T(8,128)(2,1)}, f32[384,256]{1,0:T(8,128)}, bf16[384,4096]{1,0:T(8,128)(2,1)}) custom-call(f32[1,256]{1,0:T(1,128)} %bitcast.125, bf16[384,2048]{1,0:T(8,128)(2,1)} %bitcast.20.refs_1_, bf16[384,2048]{1,0:T(8,128)(2,1)} %bitcast.22.refs_2_, bf16[4096,256]{1,0:T(8,128)(2,1)} %refs_3_.1, bf16[256,4096]{1,0:T(8,128)(2,1)} %refs_4_.1), custom_call_target="tpu_custom_call" | custom-call | flops 1610612736 | bytes 10485760 | tf_op jit(solution)/shard_map/encode/pallas_call | solution.py:171
  84.9 7.2 %all-to-all-start.1 = ((bf16[16,24,4096]{2,1,0:T(8,128)(2,1)}), bf16[16,24,4096]{2,1,0:T(8,128)(2,1)}, u32[]{:S(2)}, u32[]{:S(2)}) async-start(bf16[16,24,4096]{2,1,0:T(8,128)(2,1)} %bitcast.121), calls=%async_computation.1 | async-start | bytes 6291456 | tf_op jit(solution)/shard_map/all_to_all | solution.py:364
  93.7 12.5 %collective-permute-done.17 = f32[8,128]{1,0:T(8,128)S(1)} collective-permute-done((f32[8,128]{1,0:T(8,128)S(1)}, f32[8,128]{1,0:T(8,128)S(1)}, u32[]{:S(2)}, u32[]{:S(2)}) %collective-permute-start.17) | collective-permute-done | bytes 4128 | tf_op jit(solution)/shard_map/ppermute | solution.py:367
  106.5 38.7 %collective-permute-done.18 = f32[8,128]{1,0:T(8,128)S(1)} collective-permute-done((f32[8,128]{1,0:T(8,128)S(1)}, f32[8,128]{1,0:T(8,128)S(1)}, u32[]{:S(2)}, u32[]{:S(2)}) %collective-permute-start.18) | collective-permute-done | bytes 4128 | tf_op jit(solution)/shard_map/ppermute | solution.py:367
  145.5 4.1 %copy.25 = bf16[256,4096]{0,1:T(8,128)(2,1)} copy(bf16[256,4096]{1,0:T(8,128)(2,1)} %refs_4_.1) | data formatting | bytes 4194304 | tf_op args[4]
  149.6 10.4 %collective-permute-done.19 = f32[8,128]{1,0:T(8,128)S(1)} collective-permute-done((f32[8,128]{1,0:T(8,128)S(1)}, f32[8,128]{1,0:T(8,128)S(1)}, u32[]{:S(2)}, u32[]{:S(2)}) %collective-permute-start.19) | collective-permute-done | bytes 4128 | tf_op jit(solution)/shard_map/ppermute | solution.py:367
  160.6 2.6 copy.26
  163.2 2.6 %copy.27 = bf16[384,2048]{0,1:T(8,128)(2,1)} copy(bf16[384,2048]{1,0:T(8,128)(2,1)} %bitcast.22.refs_2_) | data formatting | bytes 3145728 | tf_op jit(solution)/shard_map/all_to_all | solution.py:364
  166.6 3.8 %pad_maximum_fusion.refs_4_ = bf16[4096,384]{1,0:T(8,128)(2,1)} fusion(bf16[2048,384]{1,0:T(8,128)(2,1)} %bitcast.119, bf16[2048,384]{1,0:T(8,128)(2,1)} %bitcast.118), kind=kLoop, calls=%fused_computation | loop fusion | flops 6291456 | bytes 6291456 | tf_op jit(solution)/shard_map/concatenate | solution.py:412
  170.5 4.0 %rebuild.1 = (bf16[128,4096]{1,0:T(8,128)(2,1)}, bf16[128,2048]{1,0:T(8,128)(2,1)}, bf16[384,2048]{1,0:T(8,128)(2,1)}) custom-call(bf16[384,128]{1,0:T(8,128)(2,1)S(1)} %convert_element_type.111.select_ref, bf16[128,384]{1,0:T(8,128)(2,1)S(1)} %convert_element_type.112.select_t_ref, f32[1,4096]{1,0:T(1,128)S(1)} %bitcast.116, bf16[128,4096]{1,0:T(8,128)(2,1)S(1)} %copy-done, ...), custom_call_target="tpu_custom_call" | custom-call | flops 805306368 | bytes 8388608 | tf_op jit(solution)/shard_map/rebuild/pallas_call | solution.py:238
  179.1 3.2 %collective-permute-start.20 = (bf16[128,2048]{1,0:T(8,128)(2,1)S(1)}, bf16[128,2048]{1,0:T(8,128)(2,1)S(1)}, u32[]{:S(2)}, u32[]{:S(2)}) collective-permute-start(bf16[128,2048]{1,0:T(8,128)(2,1)S(1)} %copy-done.2), channel_id=1, source_target_pairs={{0,8},{1,9},{2,10},{3,11},{4,12},{5,13},{6,14},{7,15},{8,0},{9,1},... | collective-permute-start | bytes 1572872 | tf_op jit(solution)/shard_map/ppermute | solution.py:367
  183.5 5.9 %all-to-all-start.2 = ((bf16[16,24,2048]{2,1,0:T(8,128)(2,1)}), bf16[16,24,2048]{2,1,0:T(8,128)(2,1)S(1)}, u32[]{:S(2)}, u32[]{:S(2)}) async-start(bf16[16,24,2048]{2,1,0:T(8,128)(2,1)} %bitcast.122), calls=%async_computation.2 | async-start | bytes 3145728 | tf_op jit(solution)/shard_map/all_to_all | solution.py:364
  198.1 4.3 %collective-permute-start.26 = (bf16[24,2048]{1,0:T(8,128)(2,1)S(1)}, bf16[24,2048]{1,0:T(8,128)(2,1)S(1)}, u32[]{:S(2)}, u32[]{:S(2)}) collective-permute-start(bf16[24,2048]{1,0:T(8,128)(2,1)S(1)} %convolution_convert_fusion.10), channel_id=1, source_target_pairs={{0,6},{1,7},{2,4},{3,5},{4,2},{5,3},{6,0},{7,1},{8,14},{9,15},{10,... | collective-permute-start | bytes 294920 | tf_op jit(solution)/shard_map/ppermute | solution.py:367
  205.5 14.8 %collective-permute-done.24 = bf16[24,2048]{1,0:T(8,128)(2,1)S(1)} collective-permute-done((bf16[24,2048]{1,0:T(8,128)(2,1)S(1)}, bf16[24,2048]{1,0:T(8,128)(2,1)S(1)}, u32[]{:S(2)}, u32[]{:S(2)}) %collective-permute-start.24) | collective-permute-done | bytes 98336 | tf_op jit(solution)/shard_map/ppermute | solution.py:367
  220.9 4.5 %collective-permute-done.25 = bf16[24,2048]{1,0:T(8,128)(2,1)S(1)} collective-permute-done((bf16[24,2048]{1,0:T(8,128)(2,1)S(1)}, bf16[24,2048]{1,0:T(8,128)(2,1)S(1)}, u32[]{:S(2)}, u32[]{:S(2)}) %collective-permute-start.25) | collective-permute-done | bytes 98336 | tf_op jit(solution)/shard_map/ppermute | solution.py:367
  233.3 4.4 %collective-permute-start.29 = (bf16[24,2048]{1,0:T(8,128)(2,1)S(1)}, bf16[24,2048]{1,0:T(8,128)(2,1)S(1)}, u32[]{:S(2)}, u32[]{:S(2)}) collective-permute-start(bf16[24,2048]{1,0:T(8,128)(2,1)S(1)} %convolution_convert_fusion.6), channel_id=1, source_target_pairs={{0,2},{1,3},{2,0},{3,1},{4,6},{5,7},{6,4},{7,5},{8,10},{9,11},{10,... | collective-permute-start | bytes 294920 | tf_op jit(solution)/shard_map/ppermute | solution.py:367
  237.8 3.6 %collective-permute-start.31 = (bf16[24,2048]{1,0:T(8,128)(2,1)S(1)}, bf16[24,2048]{1,0:T(8,128)(2,1)S(1)}, u32[]{:S(2)}, u32[]{:S(2)}) collective-permute-start(bf16[24,2048]{1,0:T(8,128)(2,1)S(1)} %convolution_convert_fusion.4), channel_id=1, source_target_pairs={{0,4},{1,5},{2,6},{3,7},{4,0},{5,1},{6,2},{7,3},{8,12},{9,13},{10,... | collective-permute-start | bytes 294920 | tf_op jit(solution)/shard_map/ppermute | solution.py:367
  252.1 9.2 %gradients.1 = (bf16[256,4096]{1,0:T(8,128)(2,1)}, bf16[4096,256]{1,0:T(8,128)(2,1)}, f32[1,256]{1,0:T(1,128)}) custom-call(f32[8,128]{1,0:T(8,128)} %beside.1.refs_0_, bf16[256,384]{1,0:T(8,128)(2,1)} %bitcast.123, f32[384,256]{1,0:T(8,128)} %get-tuple-element.28.refs_2_, bf16[4096,256]{1,0:T(8,128)(2,1)} %bitcast.117, ...), custom_call_target="tpu_custom_call" | custom-call | flops 2415919104 | bytes 12582912 | tf_op jit(solution)/shard_map/gradients/pallas_call | solution.py:321
  (156 shorter events, 82.0 us)
Async XLA Ops:
  2.3 15.7 %collective-permute-start.7 = (s32[2,128]{1,0:T(2,128)S(1)}, s32[2,128]{1,0:T(2,128)S(1)}, u32[]{:S(2)}, u32[]{:S(2)}) collective-permute-start(s32[2,128]{1,0:T(2,128)S(1)} %multiply_add_fusion), channel_id=1, source_target_pairs={{0,8},{1,9},{2,10},{3,11},{4,12},{5,13},{6,14},{7,15},{8,0},{9,1},... | collective-permute-start | bytes 3080 | tf_op jit(solution)/shard_map/ppermute | solution.py:367
  5.7 53.6 %collective-permute-start.8 = (bf16[128,2048]{1,0:T(8,128)(2,1)S(1)}, bf16[128,2048]{1,0:T(8,128)(2,1)S(1)}, u32[]{:S(2)}, u32[]{:S(2)}) collective-permute-start(bf16[128,2048]{1,0:T(8,128)(2,1)S(1)} %slice.76), channel_id=1, source_target_pairs={{0,8},{1,9},{2,10},{3,11},{4,12},{5,13},{6,14},{7,15},{8,0},{9,1},... | collective-permute-start | bytes 1572872 | tf_op jit(solution)/shard_map/ppermute | solution.py:367
  8.6 68.8 %all-to-all-start = ((bf16[16,24,2048]{2,1,0:T(8,128)(2,1)}), bf16[16,24,2048]{2,1,0:T(8,128)(2,1)}, u32[]{:S(2)}, u32[]{:S(2)}) async-start(bf16[16,24,2048]{2,1,0:T(8,128)(2,1)} %bitcast.21), calls=%async_computation | async-start | bytes 3145728 | tf_op jit(solution)/shard_map/all_to_all | solution.py:364
  20.2 9.8 %collective-permute-start.2 = (bf16[24,2048]{1,0:T(8,128)(2,1)S(1)}, bf16[24,2048]{1,0:T(8,128)(2,1)S(1)}, u32[]{:S(2)}, u32[]{:S(2)}) collective-permute-start(bf16[24,2048]{1,0:T(8,128)(2,1)S(1)} %convolution_convert_fusion.29), channel_id=1, source_target_pairs={{0,3},{1,2},{2,1},{3,0},{4,7},{5,6},{6,5},{7,4},{8,11},{9,10},{10,... | collective-permute-start | bytes 294920 | tf_op jit(solution)/shard_map/ppermute | solution.py:367
  21.7 23.3 %collective-permute-start.3 = (bf16[24,2048]{1,0:T(8,128)(2,1)S(1)}, bf16[24,2048]{1,0:T(8,128)(2,1)S(1)}, u32[]{:S(2)}, u32[]{:S(2)}) collective-permute-start(bf16[24,2048]{1,0:T(8,128)(2,1)S(1)} %convolution_convert_fusion.28), channel_id=1, source_target_pairs={{0,4},{1,5},{2,6},{3,7},{4,0},{5,1},{6,2},{7,3},{8,12},{9,13},{10,... | collective-permute-start | bytes 294920 | tf_op jit(solution)/shard_map/ppermute | solution.py:367
  24.1 26.2 %collective-permute-start.4 = (bf16[24,2048]{1,0:T(8,128)(2,1)S(1)}, bf16[24,2048]{1,0:T(8,128)(2,1)S(1)}, u32[]{:S(2)}, u32[]{:S(2)}) collective-permute-start(bf16[24,2048]{1,0:T(8,128)(2,1)S(1)} %convolution_convert_fusion.27), channel_id=1, source_target_pairs={{0,5},{1,4},{2,7},{3,6},{4,1},{5,0},{6,3},{7,2},{8,13},{9,12},{10,... | collective-permute-start | bytes 294920 | tf_op jit(solution)/shard_map/ppermute | solution.py:367
  26.2 27.4 %collective-permute-start.5 = (bf16[24,2048]{1,0:T(8,128)(2,1)S(1)}, bf16[24,2048]{1,0:T(8,128)(2,1)S(1)}, u32[]{:S(2)}, u32[]{:S(2)}) collective-permute-start(bf16[24,2048]{1,0:T(8,128)(2,1)S(1)} %convolution_convert_fusion.26), channel_id=1, source_target_pairs={{0,6},{1,7},{2,4},{3,5},{4,2},{5,3},{6,0},{7,1},{8,14},{9,15},{10,... | collective-permute-start | bytes 294920 | tf_op jit(solution)/shard_map/ppermute | solution.py:367
  30.0 28.7 %collective-permute-start.6 = (bf16[24,2048]{1,0:T(8,128)(2,1)S(1)}, bf16[24,2048]{1,0:T(8,128)(2,1)S(1)}, u32[]{:S(2)}, u32[]{:S(2)}) collective-permute-start(bf16[24,2048]{1,0:T(8,128)(2,1)S(1)} %convolution_convert_fusion.25), channel_id=1, source_target_pairs={{0,7},{1,6},{2,5},{3,4},{4,3},{5,2},{6,1},{7,0},{8,15},{9,14},{10,... | collective-permute-start | bytes 294920 | tf_op jit(solution)/shard_map/ppermute | solution.py:367
  62.6 9.1 %collective-permute-start.11 = (bf16[24,2048]{1,0:T(8,128)(2,1)S(1)}, bf16[24,2048]{1,0:T(8,128)(2,1)S(1)}, u32[]{:S(2)}, u32[]{:S(2)}) collective-permute-start(bf16[24,2048]{1,0:T(8,128)(2,1)S(1)} %convolution_convert_fusion.21), channel_id=1, source_target_pairs={{0,3},{1,2},{2,1},{3,0},{4,7},{5,6},{6,5},{7,4},{8,11},{9,10},{10,... | collective-permute-start | bytes 294920 | tf_op jit(solution)/shard_map/ppermute | solution.py:367
  84.9 85.6 %all-to-all-start.1 = ((bf16[16,24,4096]{2,1,0:T(8,128)(2,1)}), bf16[16,24,4096]{2,1,0:T(8,128)(2,1)}, u32[]{:S(2)}, u32[]{:S(2)}) async-start(bf16[16,24,4096]{2,1,0:T(8,128)(2,1)} %bitcast.121), calls=%async_computation.1 | async-start | bytes 6291456 | tf_op jit(solution)/shard_map/all_to_all | solution.py:364
  93.4 12.8 %collective-permute-start.17 = (f32[8,128]{1,0:T(8,128)S(1)}, f32[8,128]{1,0:T(8,128)S(1)}, u32[]{:S(2)}, u32[]{:S(2)}) collective-permute-start(f32[8,128]{1,0:T(8,128)S(1)} %add.113), channel_id=1, source_target_pairs={{0,2},{1,3},{2,0},{3,1},{4,6},{5,7},{6,4},{7,5},{8,10},{9,11},{10,... | collective-permute-start | bytes 12296 | tf_op jit(solution)/shard_map/ppermute | solution.py:367
  106.2 39.0 %collective-permute-start.18 = (f32[8,128]{1,0:T(8,128)S(1)}, f32[8,128]{1,0:T(8,128)S(1)}, u32[]{:S(2)}, u32[]{:S(2)}) collective-permute-start(f32[8,128]{1,0:T(8,128)S(1)} %add.114), channel_id=1, source_target_pairs={{0,4},{1,5},{2,6},{3,7},{4,0},{5,1},{6,2},{7,3},{8,12},{9,13},{10,... | collective-permute-start | bytes 12296 | tf_op jit(solution)/shard_map/ppermute | solution.py:367
  145.3 14.7 %collective-permute-start.19 = (f32[8,128]{1,0:T(8,128)S(1)}, f32[8,128]{1,0:T(8,128)S(1)}, u32[]{:S(2)}, u32[]{:S(2)}) collective-permute-start(f32[8,128]{1,0:T(8,128)S(1)} %add.115), channel_id=1, source_target_pairs={{0,8},{1,9},{2,10},{3,11},{4,12},{5,13},{6,14},{7,15},{8,0},{9,1},... | collective-permute-start | bytes 12296 | tf_op jit(solution)/shard_map/ppermute | solution.py:367
  179.1 52.0 %collective-permute-start.20 = (bf16[128,2048]{1,0:T(8,128)(2,1)S(1)}, bf16[128,2048]{1,0:T(8,128)(2,1)S(1)}, u32[]{:S(2)}, u32[]{:S(2)}) collective-permute-start(bf16[128,2048]{1,0:T(8,128)(2,1)S(1)} %copy-done.2), channel_id=1, source_target_pairs={{0,8},{1,9},{2,10},{3,11},{4,12},{5,13},{6,14},{7,15},{8,0},{9,1},... | collective-permute-start | bytes 1572872 | tf_op jit(solution)/shard_map/ppermute | solution.py:367
  183.5 67.3 %all-to-all-start.2 = ((bf16[16,24,2048]{2,1,0:T(8,128)(2,1)}), bf16[16,24,2048]{2,1,0:T(8,128)(2,1)S(1)}, u32[]{:S(2)}, u32[]{:S(2)}) async-start(bf16[16,24,2048]{2,1,0:T(8,128)(2,1)} %bitcast.122), calls=%async_computation.2 | async-start | bytes 3145728 | tf_op jit(solution)/shard_map/all_to_all | solution.py:364
  190.1 13.2 %collective-permute-start.23 = (bf16[24,2048]{1,0:T(8,128)(2,1)S(1)}, bf16[24,2048]{1,0:T(8,128)(2,1)S(1)}, u32[]{:S(2)}, u32[]{:S(2)}) collective-permute-start(bf16[24,2048]{1,0:T(8,128)(2,1)S(1)} %convolution_convert_fusion.13), channel_id=1, source_target_pairs={{0,3},{1,2},{2,1},{3,0},{4,7},{5,6},{6,5},{7,4},{8,11},{9,10},{10,... | collective-permute-start | bytes 294920 | tf_op jit(solution)/shard_map/ppermute | solution.py:367
  191.6 28.7 %collective-permute-start.24 = (bf16[24,2048]{1,0:T(8,128)(2,1)S(1)}, bf16[24,2048]{1,0:T(8,128)(2,1)S(1)}, u32[]{:S(2)}, u32[]{:S(2)}) collective-permute-start(bf16[24,2048]{1,0:T(8,128)(2,1)S(1)} %convolution_convert_fusion.12), channel_id=1, source_target_pairs={{0,4},{1,5},{2,6},{3,7},{4,0},{5,1},{6,2},{7,3},{8,12},{9,13},{10,... | collective-permute-start | bytes 294920 | tf_op jit(solution)/shard_map/ppermute | solution.py:367
  194.1 31.3 %collective-permute-start.25 = (bf16[24,2048]{1,0:T(8,128)(2,1)S(1)}, bf16[24,2048]{1,0:T(8,128)(2,1)S(1)}, u32[]{:S(2)}, u32[]{:S(2)}) collective-permute-start(bf16[24,2048]{1,0:T(8,128)(2,1)S(1)} %convolution_convert_fusion.11), channel_id=1, source_target_pairs={{0,5},{1,4},{2,7},{3,6},{4,1},{5,0},{6,3},{7,2},{8,13},{9,12},{10,... | collective-permute-start | bytes 294920 | tf_op jit(solution)/shard_map/ppermute | solution.py:367
  198.1 30.2 %collective-permute-start.26 = (bf16[24,2048]{1,0:T(8,128)(2,1)S(1)}, bf16[24,2048]{1,0:T(8,128)(2,1)S(1)}, u32[]{:S(2)}, u32[]{:S(2)}) collective-permute-start(bf16[24,2048]{1,0:T(8,128)(2,1)S(1)} %convolution_convert_fusion.10), channel_id=1, source_target_pairs={{0,6},{1,7},{2,4},{3,5},{4,2},{5,3},{6,0},{7,1},{8,14},{9,15},{10,... | collective-permute-start | bytes 294920 | tf_op jit(solution)/shard_map/ppermute | solution.py:367
  203.3 27.1 %collective-permute-start.27 = (bf16[24,2048]{1,0:T(8,128)(2,1)S(1)}, bf16[24,2048]{1,0:T(8,128)(2,1)S(1)}, u32[]{:S(2)}, u32[]{:S(2)}) collective-permute-start(bf16[24,2048]{1,0:T(8,128)(2,1)S(1)} %convolution_convert_fusion.9), channel_id=1, source_target_pairs={{0,7},{1,6},{2,5},{3,4},{4,3},{5,2},{6,1},{7,0},{8,15},{9,14},{10,... | collective-permute-start | bytes 294920 | tf_op jit(solution)/shard_map/ppermute | solution.py:367
  232.4 9.8 %collective-permute-start.28 = (bf16[24,2048]{1,0:T(8,128)(2,1)S(1)}, bf16[24,2048]{1,0:T(8,128)(2,1)S(1)}, u32[]{:S(2)}, u32[]{:S(2)}) collective-permute-start(bf16[24,2048]{1,0:T(8,128)(2,1)S(1)} %convolution_convert_fusion.7), channel_id=1, source_target_pairs={{0,1},{1,0},{2,3},{3,2},{4,5},{5,4},{6,7},{7,6},{8,9},{9,8},{10,11... | collective-permute-start | bytes 294920 | tf_op jit(solution)/shard_map/ppermute | solution.py:367
  233.3 11.0 %collective-permute-start.29 = (bf16[24,2048]{1,0:T(8,128)(2,1)S(1)}, bf16[24,2048]{1,0:T(8,128)(2,1)S(1)}, u32[]{:S(2)}, u32[]{:S(2)}) collective-permute-start(bf16[24,2048]{1,0:T(8,128)(2,1)S(1)} %convolution_convert_fusion.6), channel_id=1, source_target_pairs={{0,2},{1,3},{2,0},{3,1},{4,6},{5,7},{6,4},{7,5},{8,10},{9,11},{10,... | collective-permute-start | bytes 294920 | tf_op jit(solution)/shard_map/ppermute | solution.py:367
  237.8 8.7 %collective-permute-start.30 = (bf16[24,2048]{1,0:T(8,128)(2,1)S(1)}, bf16[24,2048]{1,0:T(8,128)(2,1)S(1)}, u32[]{:S(2)}, u32[]{:S(2)}) collective-permute-start(bf16[24,2048]{1,0:T(8,128)(2,1)S(1)} %convolution_convert_fusion.5), channel_id=1, source_target_pairs={{0,3},{1,2},{2,1},{3,0},{4,7},{5,6},{6,5},{7,4},{8,11},{9,10},{10,... | collective-permute-start | bytes 294920 | tf_op jit(solution)/shard_map/ppermute | solution.py:367
  237.8 9.3 %collective-permute-start.31 = (bf16[24,2048]{1,0:T(8,128)(2,1)S(1)}, bf16[24,2048]{1,0:T(8,128)(2,1)S(1)}, u32[]{:S(2)}, u32[]{:S(2)}) collective-permute-start(bf16[24,2048]{1,0:T(8,128)(2,1)S(1)} %convolution_convert_fusion.4), channel_id=1, source_target_pairs={{0,4},{1,5},{2,6},{3,7},{4,0},{5,1},{6,2},{7,3},{8,12},{9,13},{10,... | collective-permute-start | bytes 294920 | tf_op jit(solution)/shard_map/ppermute | solution.py:367
  (21 other events, 129.8 us)

commit v8 on v7

--- a/solution.py
+++ b/solution.py
@@ -388,21 +388,31 @@
     select_held = selection(slot_held, crossed[:half_slots])
     by_swaps = half <= 8
 
-    def deliver(tokens, by_slot, value):
-        got = exchange(by_slot)
+    def deliver(tokens, by_slot_from, by_slot, value):
         if not by_swaps:
-            return exchange(pick(select, tokens)), got, value
-        held, value = together(swap(tokens), value)
+            return exchange(pick(select, tokens)), exchange(by_slot(by_slot_from)), value
+        cuts = [slice(k * dev_slots, (k + 1) * dev_slots) for k in range(half)]
+        own = [pick(select_own[cut], tokens) for cut in cuts]
+        own = [own[0]] + list(together(*own[1:], by_slot_from))
+        by_slot_from = own.pop()
+        held = swap(tokens)
+        got = exchange(by_slot(by_slot_from))
+        held, value = together(held, value)
         rows = jnp.zeros((devices, dev_slots, tokens.shape[1]), BF16)
-        for choice, source, other in ((select_own, tokens, 0), (select_held, held, half)):
-            for k in range(half):
-                part = pick(choice[k * dev_slots : (k + 1) * dev_slots], source)
-                part = swap(part, k) if k else part
-                rows = lax.dynamic_update_index_in_dim(rows, part, me ^ (k + other), 0)
+        far_first = list(range(half // 2, half)) + list(range(half // 2))
+        for k in far_first:
+            part = swap(own[k], k) if k else own[k]
+            rows = lax.dynamic_update_index_in_dim(rows, part, me ^ k, 0)
+        for k in far_first:
+            part = pick(select_held[cuts[k]], held)
+            part = swap(part, k) if k else part
+            rows = lax.dynamic_update_index_in_dim(rows, part, me ^ (k + half), 0)
         return rows.reshape(devices * dev_slots, tokens.shape[1]), got, value
 
     act_f, act_g = activations[:, :side], activations[:, side:]
-    rows_f, rows_g, squares = deliver(act_f, pick(select, act_g), sum_of_squares(activations))
+    rows_f, rows_g, squares = deliver(
+        act_f, act_g, lambda rows: pick(select, rows), sum_of_squares(activations)
+    )
 
     code_rows, slopes, partial_value = encode(
         dev_slots, capacity, (rows_f, rows_g), enc_weight, enc_bias[None, :], dec_weight
@@ -411,19 +421,21 @@
     code_t = code_rows.T
     rows_t = jnp.concatenate([rows_f.T, rows_g.T], axis=0)
 
-    step = 1
-    while step < devices:
+    dec_t = dec_weight.T
+    steps = [1 << i for i in range((devices - 1).bit_length())]
+    for step in steps[::-1]:
         squares = squares + swap(squares, step)
-        step *= 2
+        if step == steps[-1]:
+            squares, rows_t, code_t, dec_t = together(squares, rows_t, code_t, dec_t)
     returned, squares = together(returned, squares)
     full, err_f, send_g = rebuild(select, select_t, returned, activations, dec_bias[None, :])
-    got_f, got_g, squares = deliver(err_f, send_g, beside(squares))
+    got_f, got_g, squares = deliver(err_f, send_g, lambda rows: rows, beside(squares))
     dec_grad, enc_grad, bias_grad = gradients(
         tok_rows * devices * feature_dim,
         squares,
         code_t,
         slopes,
-        dec_weight.T,
+        dec_t,
         rows_t,
         (got_f, got_g),
     )

time: 266 us -> 267 us (level)
  local copies, waits for them, and re-layouts: 33.2 us -> 36.9 us
    ppermute x35, starting transfers between devices: 44.8 us -> 40.8 us  [swap(): return lax.ppermute(rows, 'lat', [(i, i ^ step) for i in range(devices)])]
    dynamic_update_slice x28, local copies, waits for them, and re-layouts: 18.1 us -> 21.6 us  [the longest x14 12.6 us: deliver(): rows = lax.dynamic_update_index_in_dim(rows, part, me ^ k, 0)]
  transfers between devices with their start and end apart: 38 -> 38, of which waited for: 18 -> 21; matrix products, arithmetic and copies ran while one was open for 18% -> 19% of each run, Pallas kernels for 1% -> 1%
where the time goes in v8:
time: 267 us; the launch traced here: 264 us
  waiting for transfers between devices  119 us (45%)
  starting transfers between devices  62.9 us (24%)
  local copies, waits for them, and re-layouts  36.9 us (14%)
  Pallas kernels  24.2 us (9%)
  matrix products  13.3 us (5%)
  other arithmetic  6.44 us (2%)
    ppermute x35, waiting for transfers between devices, swap(): return lax.ppermute(rows, 'lat', [(i, i ^ step) for i in range(devices)])  119 us
    ppermute x35, starting transfers between devices, swap(): return lax.ppermute(rows, 'lat', [(i, i ^ step) for i in range(devices)])  40.8 us
    all_to_all x3, starting transfers between devices, exchange(): return lax.all_to_all(rows, 'lat', split_axis=0, concat_axis=0, tiled=True)  22.2 us
    dot_general x33, matrix products, dot(): return lax.dot_general(left, right, dims, preferred_element_type=F32)  13.3 us
    dynamic_update_slice x14, local copies, waits for them, and re-layouts, deliver(): rows = lax.dynamic_update_index_in_dim(rows, part, me ^ k, 0)  12.6 us
    pallas_call x1, Pallas kernels, gradients(): pl.pallas_call(lambda *refs: grads_kernel(count, *refs), out_shape=[pltpu...  9.26 us
    dynamic_update_slice x14, local copies, waits for them, and re-layouts, deliver(): rows = lax.dynamic_update_index_in_dim(rows, part, me ^ k + half, 0)  9.02 us
    pallas_call x1, Pallas kernels, encode(): pl.pallas_call(lambda *refs: encode_kernel(dev_slots, capacity, *refs), o...  7.48 us
  transfers between devices with their start and end apart: 38, of which 21 were waited for; matrix products, arithmetic and copies ran while one was open for 19% of the time, Pallas kernels for 1%

profile of v8, /device:TPU:13, one launch (start us, length us, event | category | flops | bytes accessed | tf_op | source)
XLA Modules:
  0.0 264.0 jit_solution(17073930359648288238)
XLA Ops:
  2.3 2.3 collective-permute-start.7
  6.1 2.2 squares.1
  10.2 2.7 %collective-permute-start.1 = (bf16[24,2048]{1,0:T(8,128)(2,1)S(1)}, bf16[24,2048]{1,0:T(8,128)(2,1)}, u32[]{:S(2)}, u32[]{:S(2)}) collective-permute-start(bf16[24,2048]{1,0:T(8,128)(2,1)S(1)} %convolution_convert_fusion.28), channel_id=1, source_target_pairs={{0,5},{1,4},{2,7},{3,6},{4,1},{5,0},{6,3},{7,2},{8,13},{9,12},{10,... | collective-permute-start | bytes 294920 | tf_op jit(solution)/shard_map/ppermute | solution.py:367
  16.1 7.1 %all-to-all-start = ((bf16[16,24,2048]{2,1,0:T(8,128)(2,1)}), bf16[16,24,2048]{2,1,0:T(8,128)(2,1)}, u32[]{:S(2)}, u32[]{:S(2)}) async-start(bf16[16,24,2048]{2,1,0:T(8,128)(2,1)} %bitcast.119), calls=%async_computation | async-start | bytes 3145728 | tf_op jit(solution)/shard_map/all_to_all | solution.py:364
  34.4 2.2 collective-permute-done.5
  37.2 2.6 collective-permute-done.6
  46.5 6.3 %collective-permute-done.9 = bf16[24,2048]{1,0:T(8,128)(2,1)S(1)} collective-permute-done((bf16[24,2048]{1,0:T(8,128)(2,1)S(1)}, bf16[24,2048]{1,0:T(8,128)(2,1)S(1)}, u32[]{:S(2)}, u32[]{:S(2)}) %collective-permute-start.9) | collective-permute-done | bytes 98336 | tf_op jit(solution)/shard_map/ppermute | solution.py:367
  54.5 3.7 %collective-permute-done.10 = bf16[24,2048]{1,0:T(8,128)(2,1)S(1)} collective-permute-done((bf16[24,2048]{1,0:T(8,128)(2,1)S(1)}, bf16[24,2048]{1,0:T(8,128)(2,1)S(1)}, u32[]{:S(2)}, u32[]{:S(2)}) %collective-permute-start.10) | collective-permute-done | bytes 98336 | tf_op jit(solution)/shard_map/ppermute | solution.py:367
  67.5 7.5 %encode.1 = (bf16[384,256]{1,0:T(8,128)(2,1)}, f32[384,256]{1,0:T(8,128)}, bf16[384,4096]{1,0:T(8,128)(2,1)}) custom-call(f32[1,256]{1,0:T(1,128)} %bitcast.127, bf16[384,2048]{1,0:T(8,128)(2,1)} %bitcast.20.refs_1_, bf16[384,2048]{1,0:T(8,128)(2,1)} %bitcast.22.refs_2_, bf16[4096,256]{1,0:T(8,128)(2,1)} %refs_3_.1, bf16[256,4096]{1,0:T(8,128)(2,1)} %refs_4_.1), custom_call_target="tpu_custom_call" | custom-call | flops 1610612736 | bytes 10485760 | tf_op jit(solution)/shard_map/encode/pallas_call | solution.py:171
  75.0 8.3 %all-to-all-start.1 = ((bf16[16,24,4096]{2,1,0:T(8,128)(2,1)}), bf16[16,24,4096]{2,1,0:T(8,128)(2,1)}, u32[]{:S(2)}, u32[]{:S(2)}) async-start(bf16[16,24,4096]{2,1,0:T(8,128)(2,1)} %bitcast.123), calls=%async_computation.1 | async-start | bytes 6291456 | tf_op jit(solution)/shard_map/all_to_all | solution.py:364
  85.5 4.1 %copy.27 = bf16[256,4096]{0,1:T(8,128)(2,1)} copy(bf16[256,4096]{1,0:T(8,128)(2,1)} %refs_4_.1) | data formatting | bytes 4194304 | tf_op args[4]
  89.5 61.7 %collective-permute-done.16 = f32[8,128]{1,0:T(8,128)S(1)} collective-permute-done((f32[8,128]{1,0:T(8,128)S(1)}, f32[8,128]{1,0:T(8,128)S(1)}, u32[]{:S(2)}, u32[]{:S(2)}) %collective-permute-start.16) | collective-permute-done | bytes 4128 | tf_op jit(solution)/shard_map/ppermute | solution.py:367
  151.2 2.6 copy.24
  153.8 2.6 copy.25
  157.2 3.8 %pad_maximum_fusion.refs_4_ = bf16[4096,384]{1,0:T(8,128)(2,1)} fusion(bf16[2048,384]{1,0:T(8,128)(2,1)} %bitcast.121, bf16[2048,384]{1,0:T(8,128)(2,1)} %bitcast.120), kind=kLoop, calls=%fused_computation | loop fusion | flops 6291456 | bytes 6291456 | tf_op jit(solution)/shard_map/concatenate | solution.py:422
  161.1 2.9 %collective-permute-start.17 = (f32[8,128]{1,0:T(8,128)S(1)}, f32[8,128]{1,0:T(8,128)S(1)}, u32[]{:S(2)}, u32[]{:S(2)}) collective-permute-start(f32[8,128]{1,0:T(8,128)S(1)} %add.113), channel_id=1, source_target_pairs={{0,4},{1,5},{2,6},{3,7},{4,0},{5,1},{6,2},{7,3},{8,12},{9,13},{10,... | collective-permute-start | bytes 12296 | tf_op jit(solution)/shard_map/ppermute | solution.py:367
  167.4 3.2 %collective-permute-start.19 = (f32[8,128]{1,0:T(8,128)S(1)}, f32[8,128]{1,0:T(8,128)S(1)}, u32[]{:S(2)}, u32[]{:S(2)}) collective-permute-start(f32[8,128]{1,0:T(8,128)S(1)} %add.115), channel_id=1, source_target_pairs={{0,1},{1,0},{2,3},{3,2},{4,5},{5,4},{6,7},{7,6},{8,9},{9,8},{10,11... | collective-permute-start | bytes 12296 | tf_op jit(solution)/shard_map/ppermute | solution.py:367
  172.0 4.0 %rebuild.1 = (bf16[128,4096]{1,0:T(8,128)(2,1)}, bf16[128,2048]{1,0:T(8,128)(2,1)}, bf16[384,2048]{1,0:T(8,128)(2,1)}) custom-call(bf16[384,128]{1,0:T(8,128)(2,1)S(1)} %convert_element_type.111.select_ref, bf16[128,384]{1,0:T(8,128)(2,1)S(1)} %convert_element_type.112.select_t_ref, f32[1,4096]{1,0:T(1,128)S(1)} %bitcast.117, bf16[128,4096]{1,0:T(8,128)(2,1)S(1)} %copy-done, ...), custom_call_target="tpu_custom_call" | custom-call | flops 805306368 | bytes 8388608 | tf_op jit(solution)/shard_map/rebuild/pallas_call | solution.py:238
  183.7 6.8 %all-to-all-start.2 = ((bf16[16,24,2048]{2,1,0:T(8,128)(2,1)}), bf16[16,24,2048]{2,1,0:T(8,128)(2,1)S(1)}, u32[]{:S(2)}, u32[]{:S(2)}) async-start(bf16[16,24,2048]{2,1,0:T(8,128)(2,1)} %bitcast.124), calls=%async_computation.2 | async-start | bytes 3145728 | tf_op jit(solution)/shard_map/all_to_all | solution.py:364
  193.7 2.8 %collective-permute-done.21 = bf16[24,2048]{1,0:T(8,128)(2,1)S(1)} collective-permute-done((bf16[24,2048]{1,0:T(8,128)(2,1)S(1)}, bf16[24,2048]{1,0:T(8,128)(2,1)S(1)}, u32[]{:S(2)}, u32[]{:S(2)}) %collective-permute-start.21) | collective-permute-done | bytes 98336 | tf_op jit(solution)/shard_map/ppermute | solution.py:367
  199.9 24.8 %collective-permute-done.22 = bf16[24,2048]{1,0:T(8,128)(2,1)S(1)} collective-permute-done((bf16[24,2048]{1,0:T(8,128)(2,1)S(1)}, bf16[24,2048]{1,0:T(8,128)(2,1)S(1)}, u32[]{:S(2)}, u32[]{:S(2)}) %collective-permute-start.22) | collective-permute-done | bytes 98336 | tf_op jit(solution)/shard_map/ppermute | solution.py:367
  226.3 2.5 collective-permute-start.27
  239.2 2.7 %collective-permute-start.30 = (bf16[24,2048]{1,0:T(8,128)(2,1)S(1)}, bf16[24,2048]{1,0:T(8,128)(2,1)S(1)}, u32[]{:S(2)}, u32[]{:S(2)}) collective-permute-start(bf16[24,2048]{1,0:T(8,128)(2,1)S(1)} %convolution_convert_fusion.6), channel_id=1, source_target_pairs={{0,6},{1,7},{2,4},{3,5},{4,2},{5,3},{6,0},{7,1},{8,14},{9,15},{10,... | collective-permute-start | bytes 294920 | tf_op jit(solution)/shard_map/ppermute | solution.py:367
  254.6 9.3 %gradients.1 = (bf16[256,4096]{1,0:T(8,128)(2,1)}, bf16[4096,256]{1,0:T(8,128)(2,1)}, f32[1,256]{1,0:T(1,128)}) custom-call(f32[8,128]{1,0:T(8,128)} %beside.1.refs_0_, bf16[256,384]{1,0:T(8,128)(2,1)} %bitcast.125, f32[384,256]{1,0:T(8,128)} %get-tuple-element.58.refs_2_, bf16[4096,256]{1,0:T(8,128)(2,1)} %bitcast.118, ...), custom_call_target="tpu_custom_call" | custom-call | flops 2415919104 | bytes 12582912 | tf_op jit(solution)/shard_map/gradients/pallas_call | solution.py:321
  (156 shorter events, 84.1 us)
Async XLA Ops:
  5.9 34.5 %collective-permute-start.8 = (bf16[128,2048]{1,0:T(8,128)(2,1)S(1)}, bf16[128,2048]{1,0:T(8,128)(2,1)S(1)}, u32[]{:S(2)}, u32[]{:S(2)}) collective-permute-start(bf16[128,2048]{1,0:T(8,128)(2,1)S(1)} %get-tuple-element.76), channel_id=1, source_target_pairs={{0,8},{1,9},{2,10},{3,11},{4,12},{5,13},{6,14},{7,15},{8,0},{9,1},... | collective-permute-start | bytes 1572872 | tf_op jit(solution)/shard_map/ppermute | solution.py:367
  9.9 13.3 %collective-permute-start = (bf16[24,2048]{1,0:T(8,128)(2,1)S(1)}, bf16[24,2048]{1,0:T(8,128)(2,1)}, u32[]{:S(2)}, u32[]{:S(2)}) collective-permute-start(bf16[24,2048]{1,0:T(8,128)(2,1)S(1)} %convolution_convert_fusion.29), channel_id=1, source_target_pairs={{0,4},{1,5},{2,6},{3,7},{4,0},{5,1},{6,2},{7,3},{8,12},{9,13},{10,... | collective-permute-start | bytes 294920 | tf_op jit(solution)/shard_map/ppermute | solution.py:367
  10.2 16.3 %collective-permute-start.1 = (bf16[24,2048]{1,0:T(8,128)(2,1)S(1)}, bf16[24,2048]{1,0:T(8,128)(2,1)}, u32[]{:S(2)}, u32[]{:S(2)}) collective-permute-start(bf16[24,2048]{1,0:T(8,128)(2,1)S(1)} %convolution_convert_fusion.28), channel_id=1, source_target_pairs={{0,5},{1,4},{2,7},{3,6},{4,1},{5,0},{6,3},{7,2},{8,13},{9,12},{10,... | collective-permute-start | bytes 294920 | tf_op jit(solution)/shard_map/ppermute | solution.py:367
  12.8 15.5 %collective-permute-start.2 = (bf16[24,2048]{1,0:T(8,128)(2,1)S(1)}, bf16[24,2048]{1,0:T(8,128)(2,1)}, u32[]{:S(2)}, u32[]{:S(2)}) collective-permute-start(bf16[24,2048]{1,0:T(8,128)(2,1)S(1)} %convolution_convert_fusion.27), channel_id=1, source_target_pairs={{0,6},{1,7},{2,4},{3,5},{4,2},{5,3},{6,0},{7,1},{8,14},{9,15},{10,... | collective-permute-start | bytes 294920 | tf_op jit(solution)/shard_map/ppermute | solution.py:367
  12.8 18.5 %collective-permute-start.3 = (bf16[24,2048]{1,0:T(8,128)(2,1)S(1)}, bf16[24,2048]{1,0:T(8,128)(2,1)}, u32[]{:S(2)}, u32[]{:S(2)}) collective-permute-start(bf16[24,2048]{1,0:T(8,128)(2,1)S(1)} %convolution_convert_fusion.26), channel_id=1, source_target_pairs={{0,7},{1,6},{2,5},{3,4},{4,3},{5,2},{6,1},{7,0},{8,15},{9,14},{10,... | collective-permute-start | bytes 294920 | tf_op jit(solution)/shard_map/ppermute | solution.py:367
  16.1 51.4 %all-to-all-start = ((bf16[16,24,2048]{2,1,0:T(8,128)(2,1)}), bf16[16,24,2048]{2,1,0:T(8,128)(2,1)}, u32[]{:S(2)}, u32[]{:S(2)}) async-start(bf16[16,24,2048]{2,1,0:T(8,128)(2,1)} %bitcast.119), calls=%async_computation | async-start | bytes 3145728 | tf_op jit(solution)/shard_map/all_to_all | solution.py:364
  23.2 10.6 %collective-permute-start.4 = (bf16[24,2048]{1,0:T(8,128)(2,1)S(1)}, bf16[24,2048]{1,0:T(8,128)(2,1)S(1)}, u32[]{:S(2)}, u32[]{:S(2)}) collective-permute-start(bf16[24,2048]{1,0:T(8,128)(2,1)S(1)} %convolution_convert_fusion.32), channel_id=1, source_target_pairs={{0,1},{1,0},{2,3},{3,2},{4,5},{5,4},{6,7},{7,6},{8,9},{9,8},{10,11... | collective-permute-start | bytes 294920 | tf_op jit(solution)/shard_map/ppermute | solution.py:367
  26.5 10.1 %collective-permute-start.5 = (bf16[24,2048]{1,0:T(8,128)(2,1)S(1)}, bf16[24,2048]{1,0:T(8,128)(2,1)S(1)}, u32[]{:S(2)}, u32[]{:S(2)}) collective-permute-start(bf16[24,2048]{1,0:T(8,128)(2,1)S(1)} %convolution_convert_fusion.31), channel_id=1, source_target_pairs={{0,2},{1,3},{2,0},{3,1},{4,6},{5,7},{6,4},{7,5},{8,10},{9,11},{10,... | collective-permute-start | bytes 294920 | tf_op jit(solution)/shard_map/ppermute | solution.py:367
  28.3 11.5 %collective-permute-start.6 = (bf16[24,2048]{1,0:T(8,128)(2,1)S(1)}, bf16[24,2048]{1,0:T(8,128)(2,1)S(1)}, u32[]{:S(2)}, u32[]{:S(2)}) collective-permute-start(bf16[24,2048]{1,0:T(8,128)(2,1)S(1)} %convolution_convert_fusion.30), channel_id=1, source_target_pairs={{0,3},{1,2},{2,1},{3,0},{4,7},{5,6},{6,5},{7,4},{8,11},{9,10},{10,... | collective-permute-start | bytes 294920 | tf_op jit(solution)/shard_map/ppermute | solution.py:367
  41.6 11.3 %collective-permute-start.9 = (bf16[24,2048]{1,0:T(8,128)(2,1)S(1)}, bf16[24,2048]{1,0:T(8,128)(2,1)S(1)}, u32[]{:S(2)}, u32[]{:S(2)}) collective-permute-start(bf16[24,2048]{1,0:T(8,128)(2,1)S(1)} %convolution_convert_fusion.24), channel_id=1, source_target_pairs={{0,4},{1,5},{2,6},{3,7},{4,0},{5,1},{6,2},{7,3},{8,12},{9,13},{10,... | collective-permute-start | bytes 294920 | tf_op jit(solution)/shard_map/ppermute | solution.py:367
  41.9 16.4 %collective-permute-start.10 = (bf16[24,2048]{1,0:T(8,128)(2,1)S(1)}, bf16[24,2048]{1,0:T(8,128)(2,1)S(1)}, u32[]{:S(2)}, u32[]{:S(2)}) collective-permute-start(bf16[24,2048]{1,0:T(8,128)(2,1)S(1)} %convolution_convert_fusion.23), channel_id=1, source_target_pairs={{0,5},{1,4},{2,7},{3,6},{4,1},{5,0},{6,3},{7,2},{8,13},{9,12},{10,... | collective-permute-start | bytes 294920 | tf_op jit(solution)/shard_map/ppermute | solution.py:367
  43.8 17.8 %collective-permute-start.11 = (bf16[24,2048]{1,0:T(8,128)(2,1)S(1)}, bf16[24,2048]{1,0:T(8,128)(2,1)S(1)}, u32[]{:S(2)}, u32[]{:S(2)}) collective-permute-start(bf16[24,2048]{1,0:T(8,128)(2,1)S(1)} %convolution_convert_fusion.22), channel_id=1, source_target_pairs={{0,6},{1,7},{2,4},{3,5},{4,2},{5,3},{6,0},{7,1},{8,14},{9,15},{10,... | collective-permute-start | bytes 294920 | tf_op jit(solution)/shard_map/ppermute | solution.py:367
  45.5 18.2 %collective-permute-start.12 = (bf16[24,2048]{1,0:T(8,128)(2,1)S(1)}, bf16[24,2048]{1,0:T(8,128)(2,1)S(1)}, u32[]{:S(2)}, u32[]{:S(2)}) collective-permute-start(bf16[24,2048]{1,0:T(8,128)(2,1)S(1)} %convolution_convert_fusion.21), channel_id=1, source_target_pairs={{0,7},{1,6},{2,5},{3,4},{4,3},{5,2},{6,1},{7,0},{8,15},{9,14},{10,... | collective-permute-start | bytes 294920 | tf_op jit(solution)/shard_map/ppermute | solution.py:367
  46.3 18.9 %collective-permute-start.13 = (bf16[24,2048]{1,0:T(8,128)(2,1)S(1)}, bf16[24,2048]{1,0:T(8,128)(2,1)S(1)}, u32[]{:S(2)}, u32[]{:S(2)}) collective-permute-start(bf16[24,2048]{1,0:T(8,128)(2,1)S(1)} %convolution_convert_fusion.19), channel_id=1, source_target_pairs={{0,1},{1,0},{2,3},{3,2},{4,5},{5,4},{6,7},{7,6},{8,9},{9,8},{10,11... | collective-permute-start | bytes 294920 | tf_op jit(solution)/shard_map/ppermute | solution.py:367
  52.9 13.0 %collective-permute-start.14 = (bf16[24,2048]{1,0:T(8,128)(2,1)S(1)}, bf16[24,2048]{1,0:T(8,128)(2,1)S(1)}, u32[]{:S(2)}, u32[]{:S(2)}) collective-permute-start(bf16[24,2048]{1,0:T(8,128)(2,1)S(1)} %convolution_convert_fusion.18), channel_id=1, source_target_pairs={{0,2},{1,3},{2,0},{3,1},{4,6},{5,7},{6,4},{7,5},{8,10},{9,11},{10,... | collective-permute-start | bytes 294920 | tf_op jit(solution)/shard_map/ppermute | solution.py:367
  75.0 97.0 %all-to-all-start.1 = ((bf16[16,24,4096]{2,1,0:T(8,128)(2,1)}), bf16[16,24,4096]{2,1,0:T(8,128)(2,1)}, u32[]{:S(2)}, u32[]{:S(2)}) async-start(bf16[16,24,4096]{2,1,0:T(8,128)(2,1)} %bitcast.123), calls=%async_computation.1 | async-start | bytes 6291456 | tf_op jit(solution)/shard_map/all_to_all | solution.py:364
  83.3 67.9 %collective-permute-start.16 = (f32[8,128]{1,0:T(8,128)S(1)}, f32[8,128]{1,0:T(8,128)S(1)}, u32[]{:S(2)}, u32[]{:S(2)}) collective-permute-start(f32[8,128]{1,0:T(8,128)S(1)} %copy-done.6), channel_id=1, source_target_pairs={{0,8},{1,9},{2,10},{3,11},{4,12},{5,13},{6,14},{7,15},{8,0},{9,1},... | collective-permute-start | bytes 12296 | tf_op jit(solution)/shard_map/ppermute | solution.py:367
  180.6 55.2 %collective-permute-start.20 = (bf16[128,2048]{1,0:T(8,128)(2,1)S(1)}, bf16[128,2048]{1,0:T(8,128)(2,1)S(1)}, u32[]{:S(2)}, u32[]{:S(2)}) collective-permute-start(bf16[128,2048]{1,0:T(8,128)(2,1)S(1)} %copy-done.2), channel_id=1, source_target_pairs={{0,8},{1,9},{2,10},{3,11},{4,12},{5,13},{6,14},{7,15},{8,0},{9,1},... | collective-permute-start | bytes 1572872 | tf_op jit(solution)/shard_map/ppermute | solution.py:367
  182.3 14.3 %collective-permute-start.21 = (bf16[24,2048]{1,0:T(8,128)(2,1)S(1)}, bf16[24,2048]{1,0:T(8,128)(2,1)S(1)}, u32[]{:S(2)}, u32[]{:S(2)}) collective-permute-start(bf16[24,2048]{1,0:T(8,128)(2,1)S(1)} %convolution_convert_fusion.13), channel_id=1, source_target_pairs={{0,4},{1,5},{2,6},{3,7},{4,0},{5,1},{6,2},{7,3},{8,12},{9,13},{10,... | collective-permute-start | bytes 294920 | tf_op jit(solution)/shard_map/ppermute | solution.py:367
  183.7 69.7 %all-to-all-start.2 = ((bf16[16,24,2048]{2,1,0:T(8,128)(2,1)}), bf16[16,24,2048]{2,1,0:T(8,128)(2,1)S(1)}, u32[]{:S(2)}, u32[]{:S(2)}) async-start(bf16[16,24,2048]{2,1,0:T(8,128)(2,1)} %bitcast.124), calls=%async_computation.2 | async-start | bytes 3145728 | tf_op jit(solution)/shard_map/all_to_all | solution.py:364
  190.5 34.2 %collective-permute-start.22 = (bf16[24,2048]{1,0:T(8,128)(2,1)S(1)}, bf16[24,2048]{1,0:T(8,128)(2,1)S(1)}, u32[]{:S(2)}, u32[]{:S(2)}) collective-permute-start(bf16[24,2048]{1,0:T(8,128)(2,1)S(1)} %convolution_convert_fusion.12), channel_id=1, source_target_pairs={{0,5},{1,4},{2,7},{3,6},{4,1},{5,0},{6,3},{7,2},{8,13},{9,12},{10,... | collective-permute-start | bytes 294920 | tf_op jit(solution)/shard_map/ppermute | solution.py:367
  191.0 35.2 %collective-permute-start.23 = (bf16[24,2048]{1,0:T(8,128)(2,1)S(1)}, bf16[24,2048]{1,0:T(8,128)(2,1)S(1)}, u32[]{:S(2)}, u32[]{:S(2)}) collective-permute-start(bf16[24,2048]{1,0:T(8,128)(2,1)S(1)} %convolution_convert_fusion.11), channel_id=1, source_target_pairs={{0,6},{1,7},{2,4},{3,5},{4,2},{5,3},{6,0},{7,1},{8,14},{9,15},{10,... | collective-permute-start | bytes 294920 | tf_op jit(solution)/shard_map/ppermute | solution.py:367
  192.2 37.1 %collective-permute-start.24 = (bf16[24,2048]{1,0:T(8,128)(2,1)S(1)}, bf16[24,2048]{1,0:T(8,128)(2,1)S(1)}, u32[]{:S(2)}, u32[]{:S(2)}) collective-permute-start(bf16[24,2048]{1,0:T(8,128)(2,1)S(1)} %convolution_convert_fusion.10), channel_id=1, source_target_pairs={{0,7},{1,6},{2,5},{3,4},{4,3},{5,2},{6,1},{7,0},{8,15},{9,14},{10,... | collective-permute-start | bytes 294920 | tf_op jit(solution)/shard_map/ppermute | solution.py:367
  196.5 34.3 %collective-permute-start.25 = (bf16[24,2048]{1,0:T(8,128)(2,1)S(1)}, bf16[24,2048]{1,0:T(8,128)(2,1)S(1)}, u32[]{:S(2)}, u32[]{:S(2)}) collective-permute-start(bf16[24,2048]{1,0:T(8,128)(2,1)S(1)} %convolution_convert_fusion.16), channel_id=1, source_target_pairs={{0,1},{1,0},{2,3},{3,2},{4,5},{5,4},{6,7},{7,6},{8,9},{9,8},{10,11... | collective-permute-start | bytes 294920 | tf_op jit(solution)/shard_map/ppermute | solution.py:367
  (21 other events, 134.5 us)

commit v9 on v8

--- a/solution.py
+++ b/solution.py
@@ -39,21 +39,6 @@
         part = rows_ref[:, i : i + 128].astype(F32)
         total = total + jnp.sum((part * part).reshape(rows // 8, 8, 128), axis=0)
     total_ref[...] = jnp.full((8, 128), jnp.sum(total), F32)
-
-
-def pass_kernel(value_ref, same_ref):
-    same_ref[...] = value_ref[...]
-
-
-def beside(value):
-    return pl.pallas_call(
-        pass_kernel,
-        out_shape=jax.ShapeDtypeStruct(value.shape, value.dtype),
-        in_specs=[VMEM_SPEC],
-        out_specs=VMEM_SPEC,
-        cost_estimate=pl.CostEstimate(flops=50_000_000_000, bytes_accessed=8192, transcendentals=0),
-        name="beside",
-    )(value)
 
 
 def sum_of_squares(rows):
@@ -203,12 +188,10 @@
     act_ref,
     returned_ref,
     full_ref,
-    errors_ref,
     send_ref,
     act_here,
     here_ref,
     full_out_ref,
-    errors_out_ref,
     send_out_ref,
     sems,
 ):
@@ -220,13 +203,8 @@
         finish(copies)
         full = dot(select_t_ref[...], columns(here_ref, i)[...], 1, 0) + columns(bias_ref, i)[...]
         errors = (full - columns(act_here, i)[...].astype(F32)).astype(BF16)
-        if i < PIECES // 2:
-            columns(errors_out_ref, i)[...] = errors
-            out, target = columns(errors_out_ref, i), two_parts((errors_ref, send_ref), i)
-        else:
-            columns(send_out_ref, i)[...] = dot(select_ref[...], errors, 1, 0).astype(BF16)
-            out, target = columns(send_out_ref, i), two_parts((errors_ref, send_ref), i)
-        store(stores, out, target, sems.at[1, i])
+        columns(send_out_ref, i)[...] = dot(select_ref[...], errors, 1, 0).astype(BF16)
+        store(stores, columns(send_out_ref, i), columns(send_ref, i), sems.at[1, i])
         columns(full_out_ref, i)[...] = full.astype(BF16)
         store(stores, columns(full_out_ref, i), columns(full_ref, i), sems.at[2, i])
     finish(stores)
@@ -239,15 +217,13 @@
         home_kernel,
         out_shape=[
             pltpu.HBM((tokens, features), BF16),
-            pltpu.HBM((tokens, features // 2), BF16),
-            pltpu.HBM((slots, features // 2), BF16),
+            pltpu.HBM((slots, features), BF16),
         ],
         in_specs=[VMEM_SPEC] * 3 + [HBM_SPEC] * 2,
-        out_specs=[HBM_SPEC] * 3,
+        out_specs=[HBM_SPEC, HBM_SPEC],
         scratch_shapes=[
             pltpu.VMEM((tokens, features), BF16),
             pltpu.VMEM((slots, features), BF16),
-            pltpu.VMEM((tokens, features), BF16),
             pltpu.VMEM((tokens, features), BF16),
             pltpu.VMEM((slots, features), BF16),
             pltpu.SemaphoreType.DMA((4, PIECES)),
@@ -269,8 +245,7 @@
     slopes_ref,
     dec_t_ref,
     rows_t_ref,
-    got_f_ref,
-    got_g_ref,
+    got_ref,
     dec_grad_ref,
     enc_grad_ref,
     bias_grad_ref,
@@ -286,7 +261,7 @@
     first = []
     store(first, code_t_ref, code_t_here, sems.at[5, 0])
     copies = fetch(
-        (columns, (got_f_ref, got_g_ref), got_here, sems.at[0]),
+        (columns, got_ref, got_here, sems.at[0]),
         (lines, dec_t_ref, dec_t_here, sems.at[1]),
     )
     second = []
@@ -325,7 +300,7 @@
             pltpu.HBM((features, latents), BF16),
             jax.ShapeDtypeStruct((1, latents), F32),
         ],
-        in_specs=[VMEM_SPEC] + [HBM_SPEC] * 6,
+        in_specs=[VMEM_SPEC] + [HBM_SPEC] * 5,
         out_specs=[HBM_SPEC, HBM_SPEC, VMEM_SPEC],
         scratch_shapes=[
             pltpu.VMEM((latents, slots), BF16),
@@ -344,7 +319,7 @@
         ),
         compiler_params=pltpu.CompilerParams(vmem_limit_bytes=60 * MIB),
         name="gradients",
-    )(squares, code_t, slopes, dec_t, rows_t, *got_errors)
+    )(squares, code_t, slopes, dec_t, rows_t, got_errors)
 
 
 def per_device(activations, block_ids, enc_weight, enc_bias, dec_weight, dec_bias):
@@ -418,26 +393,24 @@
         dev_slots, capacity, (rows_f, rows_g), enc_weight, enc_bias[None, :], dec_weight
     )
     returned = exchange(partial_value)
-    code_t = code_rows.T
-    rows_t = jnp.concatenate([rows_f.T, rows_g.T], axis=0)
-
-    dec_t = dec_weight.T
-    steps = [1 << i for i in range((devices - 1).bit_length())]
-    for step in steps[::-1]:
+    step = 1
+    while step < devices:
         squares = squares + swap(squares, step)
-        if step == steps[-1]:
-            squares, rows_t, code_t, dec_t = together(squares, rows_t, code_t, dec_t)
+        step *= 2
     returned, squares = together(returned, squares)
-    full, err_f, send_g = rebuild(select, select_t, returned, activations, dec_bias[None, :])
-    got_f, got_g, squares = deliver(err_f, send_g, lambda rows: rows, beside(squares))
+    full, send_errors = rebuild(select, select_t, returned, activations, dec_bias[None, :])
+    send_errors, code_rows, rows_f, rows_g, dec_rows = together(
+        send_errors, code_rows, rows_f, rows_g, dec_weight
+    )
+    got_errors = exchange(send_errors)
     dec_grad, enc_grad, bias_grad = gradients(
         tok_rows * devices * feature_dim,
         squares,
-        code_t,
+        code_rows.T,
         slopes,
-        dec_t,
-        rows_t,
-        (got_f, got_g),
+        dec_rows.T,
+        jnp.concatenate([rows_f.T, rows_g.T], axis=0),
+        got_errors,
     )
     return (full, enc_grad, dec_grad, bias_grad.reshape(local_latents))
 

time: 267 us -> 246 us (0.921)
  waiting for transfers between devices: 119 us -> 144 us
  starting transfers between devices: 62.9 us -> 38.1 us
  local copies, waits for them, and re-layouts: 36.9 us -> 26.2 us
  matrix products: 13.3 us -> 5.93 us
    all_to_all x3, waiting for transfers between devices: 0.01 us -> 57.6 us  [exchange(): return lax.all_to_all(rows, 'lat', split_axis=0, concat_axis=0, tiled=True)]
    ppermute x35 -> x20, waiting for transfers between devices: 119 us -> 86.3 us  [swap(): return lax.ppermute(rows, 'lat', [(i, i ^ step) for i in range(devices)])]
    ppermute x35 -> x20, starting transfers between devices: 40.8 us -> 16.6 us  [swap(): return lax.ppermute(rows, 'lat', [(i, i ^ step) for i in range(devices)])]
    optimization_barrier x0 -> x4, local copies, waits for them, and re-layouts: none -> 10.1 us  [together(): return lax.optimization_barrier(values)]
    dot_general x33 -> x17, matrix products: 13.3 us -> 5.93 us  [dot(): return lax.dot_general(left, right, dims, preferred_element_type=F32)]
    dynamic_update_slice x14 -> x7, local copies, waits for them, and re-layouts: 12.6 us -> 7.2 us  [deliver(): rows = lax.dynamic_update_index_in_dim(rows, part, me ^ k, 0)]
    dynamic_update_slice x14 -> x7, local copies, waits for them, and re-layouts: 9.02 us -> 4.53 us  [deliver(): rows = lax.dynamic_update_index_in_dim(rows, part, me ^ k + half, 0)]
    unnamed x15 -> x12, local copies, waits for them, and re-layouts: 5.24 us -> 1.72 us
  transfers between devices with their start and end apart: 38 -> 23, of which waited for: 21 -> 13; matrix products, arithmetic and copies ran while one was open for 19% -> 14% of each run, Pallas kernels for 1% -> 1%
where the time goes in v9:
time: 246 us; the launch traced here: 245 us
  waiting for transfers between devices  144 us (59%)
  starting transfers between devices  38.1 us (15%)
  local copies, waits for them, and re-layouts  26.2 us (11%)
  Pallas kernels  23.6 us (10%)
  other arithmetic  6.42 us (3%)
  matrix products  5.93 us (2%)
    ppermute x20, waiting for transfers between devices, swap(): return lax.ppermute(rows, 'lat', [(i, i ^ step) for i in range(devices)])  86.3 us
    all_to_all x3, waiting for transfers between devices, exchange(): return lax.all_to_all(rows, 'lat', split_axis=0, concat_axis=0, tiled=True)  57.6 us
    all_to_all x3, starting transfers between devices, exchange(): return lax.all_to_all(rows, 'lat', split_axis=0, concat_axis=0, tiled=True)  21.6 us
    ppermute x20, starting transfers between devices, swap(): return lax.ppermute(rows, 'lat', [(i, i ^ step) for i in range(devices)])  16.6 us
    optimization_barrier x4, local copies, waits for them, and re-layouts, together(): return lax.optimization_barrier(values)  10.1 us
    pallas_call x1, Pallas kernels, gradients(): pl.pallas_call(lambda *refs: grads_kernel(count, *refs), out_shape=[pltpu...  9.25 us
    pallas_call x1, Pallas kernels, encode(): pl.pallas_call(lambda *refs: encode_kernel(dev_slots, capacity, *refs), o...  7.49 us
    dynamic_update_slice x7, local copies, waits for them, and re-layouts, deliver(): rows = lax.dynamic_update_index_in_dim(rows, part, me ^ k, 0)  7.2 us
  transfers between devices with their start and end apart: 23, of which 13 were waited for; matrix products, arithmetic and copies ran while one was open for 14% of the time, Pallas kernels for 1%

profile of v9, /device:TPU:13, one launch (start us, length us, event | category | flops | bytes accessed | tf_op | source)
XLA Modules:
  0.0 245.3 jit_solution(8887780777596206455)
XLA Ops:
  2.3 2.3 collective-permute-start.7
  6.1 2.2 squares.1
  10.2 2.7 %collective-permute-start.1 = (bf16[24,2048]{1,0:T(8,128)(2,1)S(1)}, bf16[24,2048]{1,0:T(8,128)(2,1)}, u32[]{:S(2)}, u32[]{:S(2)}) collective-permute-start(bf16[24,2048]{1,0:T(8,128)(2,1)S(1)} %convolution_convert_fusion.12), channel_id=1, source_target_pairs={{0,5},{1,4},{2,7},{3,6},{4,1},{5,0},{6,3},{7,2},{8,13},{9,12},{10,... | collective-permute-start | bytes 294920 | tf_op jit(solution)/shard_map/ppermute | solution.py:342
  16.1 7.1 %all-to-all-start = ((bf16[16,24,2048]{2,1,0:T(8,128)(2,1)}), bf16[16,24,2048]{2,1,0:T(8,128)(2,1)}, u32[]{:S(2)}, u32[]{:S(2)}) async-start(bf16[16,24,2048]{2,1,0:T(8,128)(2,1)} %bitcast.67), calls=%async_computation | async-start | bytes 3145728 | tf_op jit(solution)/shard_map/all_to_all | solution.py:339
  33.5 3.1 %collective-permute-done.5 = bf16[24,2048]{1,0:T(8,128)(2,1)S(1)} collective-permute-done((bf16[24,2048]{1,0:T(8,128)(2,1)S(1)}, bf16[24,2048]{1,0:T(8,128)(2,1)S(1)}, u32[]{:S(2)}, u32[]{:S(2)}) %collective-permute-start.5) | collective-permute-done | bytes 98336 | tf_op jit(solution)/shard_map/ppermute | solution.py:342
  37.2 2.6 %collective-permute-done.6 = bf16[24,2048]{1,0:T(8,128)(2,1)S(1)} collective-permute-done((bf16[24,2048]{1,0:T(8,128)(2,1)S(1)}, bf16[24,2048]{1,0:T(8,128)(2,1)S(1)}, u32[]{:S(2)}, u32[]{:S(2)}) %collective-permute-start.6) | collective-permute-done | bytes 98336 | tf_op jit(solution)/shard_map/ppermute | solution.py:342
  41.9 1.9 collective-permute-start.10
  43.8 1.7 collective-permute-start.11
  46.5 6.3 %collective-permute-done.9 = bf16[24,2048]{1,0:T(8,128)(2,1)S(1)} collective-permute-done((bf16[24,2048]{1,0:T(8,128)(2,1)S(1)}, bf16[24,2048]{1,0:T(8,128)(2,1)S(1)}, u32[]{:S(2)}, u32[]{:S(2)}) %collective-permute-start.9) | collective-permute-done | bytes 98336 | tf_op jit(solution)/shard_map/ppermute | solution.py:342
  54.5 3.7 %collective-permute-done.10 = bf16[24,2048]{1,0:T(8,128)(2,1)S(1)} collective-permute-done((bf16[24,2048]{1,0:T(8,128)(2,1)S(1)}, bf16[24,2048]{1,0:T(8,128)(2,1)S(1)}, u32[]{:S(2)}, u32[]{:S(2)}) %collective-permute-start.10) | collective-permute-done | bytes 98336 | tf_op jit(solution)/shard_map/ppermute | solution.py:342
  59.4 2.2 collective-permute-done.11
  67.5 7.5 %encode.1 = (bf16[384,256]{1,0:T(8,128)(2,1)}, f32[384,256]{1,0:T(8,128)}, bf16[384,4096]{1,0:T(8,128)(2,1)}) custom-call(f32[1,256]{1,0:T(1,128)} %bitcast.74, bf16[384,2048]{1,0:T(8,128)(2,1)} %bitcast.20.refs_1_, bf16[384,2048]{1,0:T(8,128)(2,1)} %bitcast.22.refs_2_, bf16[4096,256]{1,0:T(8,128)(2,1)} %refs_3_.1, bf16[256,4096]{1,0:T(8,128)(2,1)} %refs_4_.1), custom_call_target="tpu_custom_call" | custom-call | flops 1610612736 | bytes 10485760 | tf_op jit(solution)/shard_map/encode/pallas_call | solution.py:156
  75.1 8.4 %all-to-all-start.1 = ((bf16[16,24,4096]{2,1,0:T(8,128)(2,1)}), bf16[16,24,4096]{2,1,0:T(8,128)(2,1)}, u32[]{:S(2)}, u32[]{:S(2)}) async-start(bf16[16,24,4096]{2,1,0:T(8,128)(2,1)} %bitcast.70), calls=%async_computation.1 | async-start | bytes 6291456 | tf_op jit(solution)/shard_map/all_to_all | solution.py:339
  85.1 12.5 %collective-permute-done.17 = f32[8,128]{1,0:T(8,128)S(1)} collective-permute-done((f32[8,128]{1,0:T(8,128)S(1)}, f32[8,128]{1,0:T(8,128)S(1)}, u32[]{:S(2)}, u32[]{:S(2)}) %collective-permute-start.17) | collective-permute-done | bytes 4128 | tf_op jit(solution)/shard_map/ppermute | solution.py:342
  97.9 38.7 %collective-permute-done.18 = f32[8,128]{1,0:T(8,128)S(1)} collective-permute-done((f32[8,128]{1,0:T(8,128)S(1)}, f32[8,128]{1,0:T(8,128)S(1)}, u32[]{:S(2)}, u32[]{:S(2)}) %collective-permute-start.18) | collective-permute-done | bytes 4128 | tf_op jit(solution)/shard_map/ppermute | solution.py:342
  136.9 14.5 %collective-permute-done.19 = f32[8,128]{1,0:T(8,128)S(1)} collective-permute-done((f32[8,128]{1,0:T(8,128)S(1)}, f32[8,128]{1,0:T(8,128)S(1)}, u32[]{:S(2)}, u32[]{:S(2)}) %collective-permute-start.19) | collective-permute-done | bytes 4128 | tf_op jit(solution)/shard_map/ppermute | solution.py:342
  153.6 4.6 %rebuild.1 = (bf16[128,4096]{1,0:T(8,128)(2,1)}, bf16[384,4096]{1,0:T(8,128)(2,1)}) custom-call(bf16[384,128]{1,0:T(8,128)(2,1)S(1)} %convert_element_type.63.select_ref, bf16[128,384]{1,0:T(8,128)(2,1)S(1)} %convert_element_type.64.select_t_ref, f32[1,4096]{1,0:T(1,128)S(1)} %bitcast.64, bf16[128,4096]{1,0:T(8,128)(2,1)S(1)} %copy-done, ...), custom_call_target="tpu_custom_call" | custom-call | flops 805306368 | bytes 8388608 | tf_op jit(solution)/shard_map/rebuild/pallas_call | solution.py:216
  158.2 6.0 %all-to-all-start.2 = ((bf16[16,24,4096]{2,1,0:T(8,128)(2,1)}), bf16[16,24,4096]{2,1,0:T(8,128)(2,1)S(1)}, u32[]{:S(2)}, u32[]{:S(2)}) async-start(bf16[16,24,4096]{2,1,0:T(8,128)(2,1)} %bitcast.71), calls=%async_computation.2 | async-start | bytes 6291456 | tf_op jit(solution)/shard_map/all_to_all | solution.py:339
  165.1 2.6 %copy.41 = bf16[384,2048]{0,1:T(8,128)(2,1)} copy(bf16[384,2048]{1,0:T(8,128)(2,1)} %bitcast.20.refs_1_) | data formatting | bytes 3145728 | tf_op jit(solution)/shard_map/optimization_barrier | solution.py:32
  167.7 2.6 %copy.42 = bf16[384,2048]{0,1:T(8,128)(2,1)} copy(bf16[384,2048]{1,0:T(8,128)(2,1)} %bitcast.22.refs_2_) | data formatting | bytes 3145728 | tf_op jit(solution)/shard_map/optimization_barrier | solution.py:32
  170.3 4.1 %copy.40 = bf16[256,4096]{0,1:T(8,128)(2,1)} copy(bf16[256,4096]{1,0:T(8,128)(2,1)} %refs_4_.1) | data formatting | bytes 4194304 | tf_op jit(solution)/shard_map/optimization_barrier | solution.py:32
  174.4 3.8 %pad_maximum_fusion.refs_4_ = bf16[4096,384]{1,0:T(8,128)(2,1)} fusion(bf16[2048,384]{1,0:T(8,128)(2,1)} %bitcast.69, bf16[2048,384]{1,0:T(8,128)(2,1)} %bitcast.68), kind=kLoop, calls=%fused_computation | loop fusion | flops 6291456 | bytes 6291456 | tf_op jit(solution)/shard_map/concatenate | solution.py:412
  178.2 56.0 %all-to-all-done.2 = bf16[16,24,4096]{2,1,0:T(8,128)(2,1)S(1)} async-done(((bf16[16,24,4096]{2,1,0:T(8,128)(2,1)}), bf16[16,24,4096]{2,1,0:T(8,128)(2,1)S(1)}, u32[]{:S(2)}, u32[]{:S(2)}) %all-to-all-start.2) | async-done | bytes 3145760 | tf_op jit(solution)/shard_map/all_to_all | solution.py:339
  235.9 9.3 %gradients.1 = (bf16[256,4096]{1,0:T(8,128)(2,1)}, bf16[4096,256]{1,0:T(8,128)(2,1)}, f32[1,256]{1,0:T(1,128)}) custom-call(f32[8,128]{1,0:T(8,128)} %add.100.refs_0_, bf16[256,384]{1,0:T(8,128)(2,1)} %bitcast.72, f32[384,256]{1,0:T(8,128)} %get-tuple-element.46.refs_2_, bf16[4096,256]{1,0:T(8,128)(2,1)} %bitcast.66, ...), custom_call_target="tpu_custom_call" | custom-call | flops 2415919104 | bytes 12582912 | tf_op jit(solution)/shard_map/gradients/pallas_call | solution.py:296
  (92 shorter events, 37.7 us)
Async XLA Ops:
  2.3 6.2 %collective-permute-start.7 = (s32[2,128]{1,0:T(2,128)S(1)}, s32[2,128]{1,0:T(2,128)S(1)}, u32[]{:S(2)}, u32[]{:S(2)}) collective-permute-start(s32[2,128]{1,0:T(2,128)S(1)} %multiply_add_fusion), channel_id=1, source_target_pairs={{0,8},{1,9},{2,10},{3,11},{4,12},{5,13},{6,14},{7,15},{8,0},{9,1},... | collective-permute-start | bytes 3080 | tf_op jit(solution)/shard_map/ppermute | solution.py:342
  5.9 34.5 %collective-permute-start.8 = (bf16[128,2048]{1,0:T(8,128)(2,1)S(1)}, bf16[128,2048]{1,0:T(8,128)(2,1)S(1)}, u32[]{:S(2)}, u32[]{:S(2)}) collective-permute-start(bf16[128,2048]{1,0:T(8,128)(2,1)S(1)} %get-tuple-element.56), channel_id=1, source_target_pairs={{0,8},{1,9},{2,10},{3,11},{4,12},{5,13},{6,14},{7,15},{8,0},{9,1},... | collective-permute-start | bytes 1572872 | tf_op jit(solution)/shard_map/ppermute | solution.py:342
  9.9 13.3 %collective-permute-start = (bf16[24,2048]{1,0:T(8,128)(2,1)S(1)}, bf16[24,2048]{1,0:T(8,128)(2,1)}, u32[]{:S(2)}, u32[]{:S(2)}) collective-permute-start(bf16[24,2048]{1,0:T(8,128)(2,1)S(1)} %convolution_convert_fusion.13), channel_id=1, source_target_pairs={{0,4},{1,5},{2,6},{3,7},{4,0},{5,1},{6,2},{7,3},{8,12},{9,13},{10,... | collective-permute-start | bytes 294920 | tf_op jit(solution)/shard_map/ppermute | solution.py:342
  10.2 16.3 %collective-permute-start.1 = (bf16[24,2048]{1,0:T(8,128)(2,1)S(1)}, bf16[24,2048]{1,0:T(8,128)(2,1)}, u32[]{:S(2)}, u32[]{:S(2)}) collective-permute-start(bf16[24,2048]{1,0:T(8,128)(2,1)S(1)} %convolution_convert_fusion.12), channel_id=1, source_target_pairs={{0,5},{1,4},{2,7},{3,6},{4,1},{5,0},{6,3},{7,2},{8,13},{9,12},{10,... | collective-permute-start | bytes 294920 | tf_op jit(solution)/shard_map/ppermute | solution.py:342
  12.8 15.5 %collective-permute-start.2 = (bf16[24,2048]{1,0:T(8,128)(2,1)S(1)}, bf16[24,2048]{1,0:T(8,128)(2,1)}, u32[]{:S(2)}, u32[]{:S(2)}) collective-permute-start(bf16[24,2048]{1,0:T(8,128)(2,1)S(1)} %convolution_convert_fusion.11), channel_id=1, source_target_pairs={{0,6},{1,7},{2,4},{3,5},{4,2},{5,3},{6,0},{7,1},{8,14},{9,15},{10,... | collective-permute-start | bytes 294920 | tf_op jit(solution)/shard_map/ppermute | solution.py:342
  12.8 18.5 %collective-permute-start.3 = (bf16[24,2048]{1,0:T(8,128)(2,1)S(1)}, bf16[24,2048]{1,0:T(8,128)(2,1)S(1)}, u32[]{:S(2)}, u32[]{:S(2)}) collective-permute-start(bf16[24,2048]{1,0:T(8,128)(2,1)S(1)} %convolution_convert_fusion.10), channel_id=1, source_target_pairs={{0,7},{1,6},{2,5},{3,4},{4,3},{5,2},{6,1},{7,0},{8,15},{9,14},{10,... | collective-permute-start | bytes 294920 | tf_op jit(solution)/shard_map/ppermute | solution.py:342
  16.1 51.4 %all-to-all-start = ((bf16[16,24,2048]{2,1,0:T(8,128)(2,1)}), bf16[16,24,2048]{2,1,0:T(8,128)(2,1)}, u32[]{:S(2)}, u32[]{:S(2)}) async-start(bf16[16,24,2048]{2,1,0:T(8,128)(2,1)} %bitcast.67), calls=%async_computation | async-start | bytes 3145728 | tf_op jit(solution)/shard_map/all_to_all | solution.py:339
  23.2 9.7 %collective-permute-start.4 = (bf16[24,2048]{1,0:T(8,128)(2,1)S(1)}, bf16[24,2048]{1,0:T(8,128)(2,1)S(1)}, u32[]{:S(2)}, u32[]{:S(2)}) collective-permute-start(bf16[24,2048]{1,0:T(8,128)(2,1)S(1)} %convolution_convert_fusion.16), channel_id=1, source_target_pairs={{0,1},{1,0},{2,3},{3,2},{4,5},{5,4},{6,7},{7,6},{8,9},{9,8},{10,11... | collective-permute-start | bytes 294920 | tf_op jit(solution)/shard_map/ppermute | solution.py:342
  26.5 10.1 %collective-permute-start.5 = (bf16[24,2048]{1,0:T(8,128)(2,1)S(1)}, bf16[24,2048]{1,0:T(8,128)(2,1)S(1)}, u32[]{:S(2)}, u32[]{:S(2)}) collective-permute-start(bf16[24,2048]{1,0:T(8,128)(2,1)S(1)} %convolution_convert_fusion.15), channel_id=1, source_target_pairs={{0,2},{1,3},{2,0},{3,1},{4,6},{5,7},{6,4},{7,5},{8,10},{9,11},{10,... | collective-permute-start | bytes 294920 | tf_op jit(solution)/shard_map/ppermute | solution.py:342
  28.3 11.5 %collective-permute-start.6 = (bf16[24,2048]{1,0:T(8,128)(2,1)S(1)}, bf16[24,2048]{1,0:T(8,128)(2,1)S(1)}, u32[]{:S(2)}, u32[]{:S(2)}) collective-permute-start(bf16[24,2048]{1,0:T(8,128)(2,1)S(1)} %convolution_convert_fusion.14), channel_id=1, source_target_pairs={{0,3},{1,2},{2,1},{3,0},{4,7},{5,6},{6,5},{7,4},{8,11},{9,10},{10,... | collective-permute-start | bytes 294920 | tf_op jit(solution)/shard_map/ppermute | solution.py:342
  41.6 11.3 %collective-permute-start.9 = (bf16[24,2048]{1,0:T(8,128)(2,1)S(1)}, bf16[24,2048]{1,0:T(8,128)(2,1)S(1)}, u32[]{:S(2)}, u32[]{:S(2)}) collective-permute-start(bf16[24,2048]{1,0:T(8,128)(2,1)S(1)} %convolution_convert_fusion.8), channel_id=1, source_target_pairs={{0,4},{1,5},{2,6},{3,7},{4,0},{5,1},{6,2},{7,3},{8,12},{9,13},{10,... | collective-permute-start | bytes 294920 | tf_op jit(solution)/shard_map/ppermute | solution.py:342
  41.9 16.4 %collective-permute-start.10 = (bf16[24,2048]{1,0:T(8,128)(2,1)S(1)}, bf16[24,2048]{1,0:T(8,128)(2,1)S(1)}, u32[]{:S(2)}, u32[]{:S(2)}) collective-permute-start(bf16[24,2048]{1,0:T(8,128)(2,1)S(1)} %convolution_convert_fusion.7), channel_id=1, source_target_pairs={{0,5},{1,4},{2,7},{3,6},{4,1},{5,0},{6,3},{7,2},{8,13},{9,12},{10,... | collective-permute-start | bytes 294920 | tf_op jit(solution)/shard_map/ppermute | solution.py:342
  43.8 17.8 %collective-permute-start.11 = (bf16[24,2048]{1,0:T(8,128)(2,1)S(1)}, bf16[24,2048]{1,0:T(8,128)(2,1)S(1)}, u32[]{:S(2)}, u32[]{:S(2)}) collective-permute-start(bf16[24,2048]{1,0:T(8,128)(2,1)S(1)} %convolution_convert_fusion.6), channel_id=1, source_target_pairs={{0,6},{1,7},{2,4},{3,5},{4,2},{5,3},{6,0},{7,1},{8,14},{9,15},{10,... | collective-permute-start | bytes 294920 | tf_op jit(solution)/shard_map/ppermute | solution.py:342
  45.5 18.2 %collective-permute-start.12 = (bf16[24,2048]{1,0:T(8,128)(2,1)S(1)}, bf16[24,2048]{1,0:T(8,128)(2,1)S(1)}, u32[]{:S(2)}, u32[]{:S(2)}) collective-permute-start(bf16[24,2048]{1,0:T(8,128)(2,1)S(1)} %convolution_convert_fusion.5), channel_id=1, source_target_pairs={{0,7},{1,6},{2,5},{3,4},{4,3},{5,2},{6,1},{7,0},{8,15},{9,14},{10,... | collective-permute-start | bytes 294920 | tf_op jit(solution)/shard_map/ppermute | solution.py:342
  46.3 18.9 %collective-permute-start.13 = (bf16[24,2048]{1,0:T(8,128)(2,1)S(1)}, bf16[24,2048]{1,0:T(8,128)(2,1)S(1)}, u32[]{:S(2)}, u32[]{:S(2)}) collective-permute-start(bf16[24,2048]{1,0:T(8,128)(2,1)S(1)} %convolution_convert_fusion.3), channel_id=1, source_target_pairs={{0,1},{1,0},{2,3},{3,2},{4,5},{5,4},{6,7},{7,6},{8,9},{9,8},{10,11... | collective-permute-start | bytes 294920 | tf_op jit(solution)/shard_map/ppermute | solution.py:342
  52.9 12.9 %collective-permute-start.14 = (bf16[24,2048]{1,0:T(8,128)(2,1)S(1)}, bf16[24,2048]{1,0:T(8,128)(2,1)S(1)}, u32[]{:S(2)}, u32[]{:S(2)}) collective-permute-start(bf16[24,2048]{1,0:T(8,128)(2,1)S(1)} %convolution_convert_fusion.2), channel_id=1, source_target_pairs={{0,2},{1,3},{2,0},{3,1},{4,6},{5,7},{6,4},{7,5},{8,10},{9,11},{10,... | collective-permute-start | bytes 294920 | tf_op jit(solution)/shard_map/ppermute | solution.py:342
  58.2 8.6 %collective-permute-start.15 = (bf16[24,2048]{1,0:T(8,128)(2,1)S(1)}, bf16[24,2048]{1,0:T(8,128)(2,1)S(1)}, u32[]{:S(2)}, u32[]{:S(2)}) collective-permute-start(bf16[24,2048]{1,0:T(8,128)(2,1)S(1)} %convolution_convert_fusion.1), channel_id=1, source_target_pairs={{0,3},{1,2},{2,1},{3,0},{4,7},{5,6},{6,5},{7,4},{8,11},{9,10},{10,... | collective-permute-start | bytes 294920 | tf_op jit(solution)/shard_map/ppermute | solution.py:342
  75.0 78.6 %copy-start.1 = (f32[4096]{0:T(1024)S(1)}, f32[4096]{0:T(1024)}, u32[]{:S(2)}) copy-start(f32[4096]{0:T(1024)} %param.11) | copy-start | bytes 49156
  75.1 78.6 %all-to-all-start.1 = ((bf16[16,24,4096]{2,1,0:T(8,128)(2,1)}), bf16[16,24,4096]{2,1,0:T(8,128)(2,1)}, u32[]{:S(2)}, u32[]{:S(2)}) async-start(bf16[16,24,4096]{2,1,0:T(8,128)(2,1)} %bitcast.70), calls=%async_computation.1 | async-start | bytes 6291456 | tf_op jit(solution)/shard_map/all_to_all | solution.py:339
  83.5 1.3 collective-permute-start.16
  84.8 12.8 %collective-permute-start.17 = (f32[8,128]{1,0:T(8,128)S(1)}, f32[8,128]{1,0:T(8,128)S(1)}, u32[]{:S(2)}, u32[]{:S(2)}) collective-permute-start(f32[8,128]{1,0:T(8,128)S(1)} %add.97), channel_id=1, source_target_pairs={{0,2},{1,3},{2,0},{3,1},{4,6},{5,7},{6,4},{7,5},{8,10},{9,11},{10,... | collective-permute-start | bytes 12296 | tf_op jit(solution)/shard_map/ppermute | solution.py:342
  97.6 39.0 %collective-permute-start.18 = (f32[8,128]{1,0:T(8,128)S(1)}, f32[8,128]{1,0:T(8,128)S(1)}, u32[]{:S(2)}, u32[]{:S(2)}) collective-permute-start(f32[8,128]{1,0:T(8,128)S(1)} %add.98), channel_id=1, source_target_pairs={{0,4},{1,5},{2,6},{3,7},{4,0},{5,1},{6,2},{7,3},{8,12},{9,13},{10,... | collective-permute-start | bytes 12296 | tf_op jit(solution)/shard_map/ppermute | solution.py:342
  136.6 14.7 %collective-permute-start.19 = (f32[8,128]{1,0:T(8,128)S(1)}, f32[8,128]{1,0:T(8,128)S(1)}, u32[]{:S(2)}, u32[]{:S(2)}) collective-permute-start(f32[8,128]{1,0:T(8,128)S(1)} %add.99), channel_id=1, source_target_pairs={{0,8},{1,9},{2,10},{3,11},{4,12},{5,13},{6,14},{7,15},{8,0},{9,1},... | collective-permute-start | bytes 12296 | tf_op jit(solution)/shard_map/ppermute | solution.py:342
  158.2 75.9 %all-to-all-start.2 = ((bf16[16,24,4096]{2,1,0:T(8,128)(2,1)}), bf16[16,24,4096]{2,1,0:T(8,128)(2,1)S(1)}, u32[]{:S(2)}, u32[]{:S(2)}) async-start(bf16[16,24,4096]{2,1,0:T(8,128)(2,1)} %bitcast.71), calls=%async_computation.2 | async-start | bytes 6291456 | tf_op jit(solution)/shard_map/all_to_all | solution.py:339
  (5 other events, 41.6 us)

commit v10 on v9

--- a/solution.py
+++ b/solution.py
@@ -317,7 +317,7 @@
             bytes_accessed=2 * features * (2 * slots + 3 * latents),
             transcendentals=0,
         ),
-        compiler_params=pltpu.CompilerParams(vmem_limit_bytes=60 * MIB),
+        compiler_params=pltpu.CompilerParams(vmem_limit_bytes=62 * MIB),
         name="gradients",
     )(squares, code_t, slopes, dec_t, rows_t, got_errors)
 
@@ -372,16 +372,20 @@
         by_slot_from = own.pop()
         held = swap(tokens)
         got = exchange(by_slot(by_slot_from))
-        held, value = together(held, value)
+        far = list(range(half // 2, half))
+        near = list(range(half // 2))
+        own = own[: half // 2] + [swap(own[k], k) for k in far]
+        held, value, *own[half // 2 :] = together(held, value, *own[half // 2 :])
         rows = jnp.zeros((devices, dev_slots, tokens.shape[1]), BF16)
-        far_first = list(range(half // 2, half)) + list(range(half // 2))
-        for k in far_first:
-            part = swap(own[k], k) if k else own[k]
-            rows = lax.dynamic_update_index_in_dim(rows, part, me ^ k, 0)
-        for k in far_first:
+        for k in far:
+            rows = lax.dynamic_update_index_in_dim(rows, own[k], me ^ k, 0)
+        for k in far + near:
             part = pick(select_held[cuts[k]], held)
             part = swap(part, k) if k else part
             rows = lax.dynamic_update_index_in_dim(rows, part, me ^ (k + half), 0)
+        for k in near:
+            part = swap(own[k], k) if k else own[k]
+            rows = lax.dynamic_update_index_in_dim(rows, part, me ^ k, 0)
         return rows.reshape(devices * dev_slots, tokens.shape[1]), got, value
 
     act_f, act_g = activations[:, :side], activations[:, side:]

time: 246 us -> 253 us (1.028)
  starting transfers between devices: 38.1 us -> 47.1 us
  local copies, waits for them, and re-layouts: 26.2 us -> 22.9 us
    ppermute x20, starting transfers between devices: 16.6 us -> 24.2 us  [swap(): return lax.ppermute(rows, 'lat', [(i, i ^ step) for i in range(devices)])]
    dynamic_update_slice x0 -> x4, local copies, waits for them, and re-layouts: none -> 5.26 us  [deliver(): rows = lax.dynamic_update_index_in_dim(rows, own[k], me ^ k, 0)]
    dynamic_update_slice x7 -> x3, local copies, waits for them, and re-layouts: 7.2 us -> 1.94 us  [deliver(): rows = lax.dynamic_update_index_in_dim(rows, part, me ^ k, 0)]
  transfers between devices with their start and end apart: 23 -> 23, of which waited for: 13 -> 14; matrix products, arithmetic and copies ran while one was open for 14% -> 13% of each run, Pallas kernels for 1% -> 1%
where the time goes in v10:
time: 253 us
  waiting for transfers between devices  145 us (57%)
  starting transfers between devices  47.1 us (19%)
  Pallas kernels  23.6 us (9%)
  local copies, waits for them, and re-layouts  22.9 us (9%)
  other arithmetic  6.49 us (3%)
  matrix products  5.93 us (2%)
    ppermute x20, waiting for transfers between devices, swap(): return lax.ppermute(rows, 'lat', [(i, i ^ step) for i in range(devices)])  86.2 us
    all_to_all x3, waiting for transfers between devices, exchange(): return lax.all_to_all(rows, 'lat', split_axis=0, concat_axis=0, tiled=True)  59.2 us
    ppermute x20, starting transfers between devices, swap(): return lax.ppermute(rows, 'lat', [(i, i ^ step) for i in range(devices)])  24.2 us
    all_to_all x3, starting transfers between devices, exchange(): return lax.all_to_all(rows, 'lat', split_axis=0, concat_axis=0, tiled=True)  22.9 us
    pallas_call x1, Pallas kernels, gradients(): pl.pallas_call(lambda *refs: grads_kernel(count, *refs), out_shape=[pltpu...  9.26 us
    optimization_barrier x4, local copies, waits for them, and re-layouts, together(): return lax.optimization_barrier(values)  8.54 us
    pallas_call x1, Pallas kernels, encode(): pl.pallas_call(lambda *refs: encode_kernel(dev_slots, capacity, *refs), o...  7.49 us
    dot_general x17, matrix products, dot(): return lax.dot_general(left, right, dims, preferred_element_type=F32)  5.93 us
  transfers between devices with their start and end apart: 23, of which 14 were waited for; matrix products, arithmetic and copies ran while one was open for 13% of the time, Pallas kernels for 1%

profile of v10, /device:TPU:13, one launch (start us, length us, event | category | flops | bytes accessed | tf_op | source)
XLA Modules:
  0.0 252.5 jit_solution(15798763325072895654)
XLA Ops:
  2.3 2.3 collective-permute-start.5
  6.1 2.2 squares.1
  10.2 2.7 %collective-permute-start.2 = (bf16[24,2048]{1,0:T(8,128)(2,1)S(1)}, bf16[24,2048]{1,0:T(8,128)(2,1)}, u32[]{:S(2)}, u32[]{:S(2)}) collective-permute-start(bf16[24,2048]{1,0:T(8,128)(2,1)S(1)} %convolution_convert_fusion.12), channel_id=1, source_target_pairs={{0,5},{1,4},{2,7},{3,6},{4,1},{5,0},{6,3},{7,2},{8,13},{9,12},{10,... | collective-permute-start | bytes 294920 | tf_op jit(solution)/shard_map/ppermute | solution.py:342
  16.1 7.1 %all-to-all-start = ((bf16[16,24,2048]{2,1,0:T(8,128)(2,1)}), bf16[16,24,2048]{2,1,0:T(8,128)(2,1)}, u32[]{:S(2)}, u32[]{:S(2)}) async-start(bf16[16,24,2048]{2,1,0:T(8,128)(2,1)} %bitcast.66), calls=%async_computation | async-start | bytes 3145728 | tf_op jit(solution)/shard_map/all_to_all | solution.py:339
  24.5 3.6 %collective-permute-start.15 = (bf16[24,2048]{1,0:T(8,128)(2,1)S(1)}, bf16[24,2048]{1,0:T(8,128)(2,1)S(1)}, u32[]{:S(2)}, u32[]{:S(2)}) collective-permute-start(bf16[24,2048]{1,0:T(8,128)(2,1)S(1)} %convolution_convert_fusion.14), channel_id=1, source_target_pairs={{0,3},{1,2},{2,1},{3,0},{4,7},{5,6},{6,5},{7,4},{8,11},{9,10},{10,... | collective-permute-start | bytes 294920 | tf_op jit(solution)/shard_map/ppermute | solution.py:342
  28.1 7.9 %collective-permute-done = bf16[128,2048]{1,0:T(8,128)(2,1)S(1)} collective-permute-done((bf16[128,2048]{1,0:T(8,128)(2,1)S(1)}, bf16[128,2048]{1,0:T(8,128)(2,1)S(1)}, u32[]{:S(2)}, u32[]{:S(2)}) %collective-permute-start) | collective-permute-done | bytes 524320 | tf_op jit(solution)/shard_map/ppermute | solution.py:342
  37.8 3.8 %collective-permute-start.7 = (bf16[24,2048]{1,0:T(8,128)(2,1)S(1)}, bf16[24,2048]{1,0:T(8,128)(2,1)S(1)}, u32[]{:S(2)}, u32[]{:S(2)}) collective-permute-start(bf16[24,2048]{1,0:T(8,128)(2,1)S(1)} %convolution_convert_fusion.8), channel_id=1, source_target_pairs={{0,5},{1,4},{2,7},{3,6},{4,1},{5,0},{6,3},{7,2},{8,13},{9,12},{10,... | collective-permute-start | bytes 294920 | tf_op jit(solution)/shard_map/ppermute | solution.py:342
  48.3 4.6 %collective-permute-done.6 = bf16[24,2048]{1,0:T(8,128)(2,1)S(1)} collective-permute-done((bf16[24,2048]{1,0:T(8,128)(2,1)S(1)}, bf16[24,2048]{1,0:T(8,128)(2,1)S(1)}, u32[]{:S(2)}, u32[]{:S(2)}) %collective-permute-start.6) | collective-permute-done | bytes 98336 | tf_op jit(solution)/shard_map/ppermute | solution.py:342
  52.9 2.4 collective-permute-start.8
  57.3 2.0 collective-permute-start.9
  69.1 2.5 %collective-permute-done.12 = bf16[24,2048]{1,0:T(8,128)(2,1)S(1)} collective-permute-done((bf16[24,2048]{1,0:T(8,128)(2,1)S(1)}, bf16[24,2048]{1,0:T(8,128)(2,1)S(1)}, u32[]{:S(2)}, u32[]{:S(2)}) %collective-permute-start.12) | collective-permute-done | bytes 98336 | tf_op jit(solution)/shard_map/ppermute | solution.py:342
  75.0 7.5 %encode.1 = (bf16[384,256]{1,0:T(8,128)(2,1)}, f32[384,256]{1,0:T(8,128)}, bf16[384,4096]{1,0:T(8,128)(2,1)}) custom-call(f32[1,256]{1,0:T(1,128)} %bitcast.73, bf16[384,2048]{1,0:T(8,128)(2,1)} %bitcast.20.refs_1_, bf16[384,2048]{1,0:T(8,128)(2,1)} %bitcast.22.refs_2_, bf16[4096,256]{1,0:T(8,128)(2,1)} %refs_3_.1, bf16[256,4096]{1,0:T(8,128)(2,1)} %refs_4_.1), custom_call_target="tpu_custom_call" | custom-call | flops 1610612736 | bytes 10485760 | tf_op jit(solution)/shard_map/encode/pallas_call | solution.py:156
  82.6 9.1 %all-to-all-start.1 = ((bf16[16,24,4096]{2,1,0:T(8,128)(2,1)}), bf16[16,24,4096]{2,1,0:T(8,128)(2,1)}, u32[]{:S(2)}, u32[]{:S(2)}) async-start(bf16[16,24,4096]{2,1,0:T(8,128)(2,1)} %bitcast.69), calls=%async_computation.1 | async-start | bytes 6291456 | tf_op jit(solution)/shard_map/all_to_all | solution.py:339
  93.2 12.5 %collective-permute-done.17 = f32[8,128]{1,0:T(8,128)S(1)} collective-permute-done((f32[8,128]{1,0:T(8,128)S(1)}, f32[8,128]{1,0:T(8,128)S(1)}, u32[]{:S(2)}, u32[]{:S(2)}) %collective-permute-start.17) | collective-permute-done | bytes 4128 | tf_op jit(solution)/shard_map/ppermute | solution.py:342
  106.1 38.7 %collective-permute-done.18 = f32[8,128]{1,0:T(8,128)S(1)} collective-permute-done((f32[8,128]{1,0:T(8,128)S(1)}, f32[8,128]{1,0:T(8,128)S(1)}, u32[]{:S(2)}, u32[]{:S(2)}) %collective-permute-start.18) | collective-permute-done | bytes 4128 | tf_op jit(solution)/shard_map/ppermute | solution.py:342
  145.1 14.5 %collective-permute-done.19 = f32[8,128]{1,0:T(8,128)S(1)} collective-permute-done((f32[8,128]{1,0:T(8,128)S(1)}, f32[8,128]{1,0:T(8,128)S(1)}, u32[]{:S(2)}, u32[]{:S(2)}) %collective-permute-start.19) | collective-permute-done | bytes 4128 | tf_op jit(solution)/shard_map/ppermute | solution.py:342
  161.8 4.6 %rebuild.1 = (bf16[128,4096]{1,0:T(8,128)(2,1)}, bf16[384,4096]{1,0:T(8,128)(2,1)}) custom-call(bf16[384,128]{1,0:T(8,128)(2,1)S(1)} %convert_element_type.63.select_ref, bf16[128,384]{1,0:T(8,128)(2,1)S(1)} %convert_element_type.64.select_t_ref, f32[1,4096]{1,0:T(1,128)S(1)} %bitcast.64, bf16[128,4096]{1,0:T(8,128)(2,1)S(1)} %copy-done, ...), custom_call_target="tpu_custom_call" | custom-call | flops 805306368 | bytes 8388608 | tf_op jit(solution)/shard_map/rebuild/pallas_call | solution.py:216
  166.4 6.7 %all-to-all-start.2 = ((bf16[16,24,4096]{2,1,0:T(8,128)(2,1)}), bf16[16,24,4096]{2,1,0:T(8,128)(2,1)}, u32[]{:S(2)}, u32[]{:S(2)}) async-start(bf16[16,24,4096]{2,1,0:T(8,128)(2,1)} %bitcast.70), calls=%async_computation.2 | async-start | bytes 6291456 | tf_op jit(solution)/shard_map/all_to_all | solution.py:339
  173.9 2.6 %copy.41 = bf16[384,2048]{0,1:T(8,128)(2,1)} copy(bf16[384,2048]{1,0:T(8,128)(2,1)} %bitcast.20.refs_1_) | data formatting | bytes 3145728 | tf_op jit(solution)/shard_map/optimization_barrier | solution.py:32
  176.5 2.7 %copy.42 = bf16[384,2048]{0,1:T(8,128)(2,1)} copy(bf16[384,2048]{1,0:T(8,128)(2,1)} %bitcast.22.refs_2_) | data formatting | bytes 3145728 | tf_op jit(solution)/shard_map/optimization_barrier | solution.py:32
  179.2 2.4 copy.40
  181.7 3.9 %pad_maximum_fusion.refs_4_ = bf16[4096,384]{1,0:T(8,128)(2,1)} fusion(bf16[2048,384]{1,0:T(8,128)(2,1)} %bitcast.68, bf16[2048,384]{1,0:T(8,128)(2,1)} %bitcast.67), kind=kLoop, calls=%fused_computation | loop fusion | flops 6291456 | bytes 6291456 | tf_op jit(solution)/shard_map/concatenate | solution.py:416
  185.6 57.6 %all-to-all-done.2 = bf16[16,24,4096]{2,1,0:T(8,128)(2,1)} async-done(((bf16[16,24,4096]{2,1,0:T(8,128)(2,1)}), bf16[16,24,4096]{2,1,0:T(8,128)(2,1)}, u32[]{:S(2)}, u32[]{:S(2)}) %all-to-all-start.2) | async-done | bytes 3145760 | tf_op jit(solution)/shard_map/all_to_all | solution.py:339
  243.1 9.3 %gradients.1 = (bf16[256,4096]{1,0:T(8,128)(2,1)}, bf16[4096,256]{1,0:T(8,128)(2,1)}, f32[1,256]{1,0:T(1,128)}) custom-call(f32[8,128]{1,0:T(8,128)} %add.100.refs_0_, bf16[256,384]{1,0:T(8,128)(2,1)} %bitcast.71, f32[384,256]{1,0:T(8,128)} %get-tuple-element.54.refs_2_, bf16[4096,256]{1,0:T(8,128)(2,1)} %bitcast.65, ...), custom_call_target="tpu_custom_call" | custom-call | flops 2415919104 | bytes 12582912 | tf_op jit(solution)/shard_map/gradients/pallas_call | solution.py:296
  (92 shorter events, 38.3 us)
Async XLA Ops:
  2.3 6.2 %collective-permute-start.5 = (s32[2,128]{1,0:T(2,128)S(1)}, s32[2,128]{1,0:T(2,128)S(1)}, u32[]{:S(2)}, u32[]{:S(2)}) collective-permute-start(s32[2,128]{1,0:T(2,128)S(1)} %multiply_add_fusion), channel_id=1, source_target_pairs={{0,8},{1,9},{2,10},{3,11},{4,12},{5,13},{6,14},{7,15},{8,0},{9,1},... | collective-permute-start | bytes 3080 | tf_op jit(solution)/shard_map/ppermute | solution.py:342
  5.9 30.0 %collective-permute-start = (bf16[128,2048]{1,0:T(8,128)(2,1)S(1)}, bf16[128,2048]{1,0:T(8,128)(2,1)S(1)}, u32[]{:S(2)}, u32[]{:S(2)}) collective-permute-start(bf16[128,2048]{1,0:T(8,128)(2,1)S(1)} %get-tuple-element.65), channel_id=1, source_target_pairs={{0,8},{1,9},{2,10},{3,11},{4,12},{5,13},{6,14},{7,15},{8,0},{9,1},... | collective-permute-start | bytes 1572872 | tf_op jit(solution)/shard_map/ppermute | solution.py:342
  9.9 13.3 %collective-permute-start.1 = (bf16[24,2048]{1,0:T(8,128)(2,1)S(1)}, bf16[24,2048]{1,0:T(8,128)(2,1)S(1)}, u32[]{:S(2)}, u32[]{:S(2)}) collective-permute-start(bf16[24,2048]{1,0:T(8,128)(2,1)S(1)} %convolution_convert_fusion.13), channel_id=1, source_target_pairs={{0,4},{1,5},{2,6},{3,7},{4,0},{5,1},{6,2},{7,3},{8,12},{9,13},{10,... | collective-permute-start | bytes 294920 | tf_op jit(solution)/shard_map/ppermute | solution.py:342
  10.2 14.4 %collective-permute-start.2 = (bf16[24,2048]{1,0:T(8,128)(2,1)S(1)}, bf16[24,2048]{1,0:T(8,128)(2,1)}, u32[]{:S(2)}, u32[]{:S(2)}) collective-permute-start(bf16[24,2048]{1,0:T(8,128)(2,1)S(1)} %convolution_convert_fusion.12), channel_id=1, source_target_pairs={{0,5},{1,4},{2,7},{3,6},{4,1},{5,0},{6,3},{7,2},{8,13},{9,12},{10,... | collective-permute-start | bytes 294920 | tf_op jit(solution)/shard_map/ppermute | solution.py:342
  12.8 11.7 %collective-permute-start.3 = (bf16[24,2048]{1,0:T(8,128)(2,1)S(1)}, bf16[24,2048]{1,0:T(8,128)(2,1)}, u32[]{:S(2)}, u32[]{:S(2)}) collective-permute-start(bf16[24,2048]{1,0:T(8,128)(2,1)S(1)} %convolution_convert_fusion.11), channel_id=1, source_target_pairs={{0,6},{1,7},{2,4},{3,5},{4,2},{5,3},{6,0},{7,1},{8,14},{9,15},{10,... | collective-permute-start | bytes 294920 | tf_op jit(solution)/shard_map/ppermute | solution.py:342
  12.8 15.3 %collective-permute-start.4 = (bf16[24,2048]{1,0:T(8,128)(2,1)S(1)}, bf16[24,2048]{1,0:T(8,128)(2,1)}, u32[]{:S(2)}, u32[]{:S(2)}) collective-permute-start(bf16[24,2048]{1,0:T(8,128)(2,1)S(1)} %convolution_convert_fusion.10), channel_id=1, source_target_pairs={{0,7},{1,6},{2,5},{3,4},{4,3},{5,2},{6,1},{7,0},{8,15},{9,14},{10,... | collective-permute-start | bytes 294920 | tf_op jit(solution)/shard_map/ppermute | solution.py:342
  16.1 58.9 %all-to-all-start = ((bf16[16,24,2048]{2,1,0:T(8,128)(2,1)}), bf16[16,24,2048]{2,1,0:T(8,128)(2,1)}, u32[]{:S(2)}, u32[]{:S(2)}) async-start(bf16[16,24,2048]{2,1,0:T(8,128)(2,1)} %bitcast.66), calls=%async_computation | async-start | bytes 3145728 | tf_op jit(solution)/shard_map/all_to_all | solution.py:339
  23.2 49.9 %collective-permute-start.13 = (bf16[24,2048]{1,0:T(8,128)(2,1)S(1)}, bf16[24,2048]{1,0:T(8,128)(2,1)S(1)}, u32[]{:S(2)}, u32[]{:S(2)}) collective-permute-start(bf16[24,2048]{1,0:T(8,128)(2,1)S(1)} %convolution_convert_fusion.16), channel_id=1, source_target_pairs={{0,1},{1,0},{2,3},{3,2},{4,5},{5,4},{6,7},{7,6},{8,9},{9,8},{10,11... | collective-permute-start | bytes 294920 | tf_op jit(solution)/shard_map/ppermute | solution.py:342
  24.5 49.2 %collective-permute-start.14 = (bf16[24,2048]{1,0:T(8,128)(2,1)S(1)}, bf16[24,2048]{1,0:T(8,128)(2,1)S(1)}, u32[]{:S(2)}, u32[]{:S(2)}) collective-permute-start(bf16[24,2048]{1,0:T(8,128)(2,1)S(1)} %convolution_convert_fusion.15), channel_id=1, source_target_pairs={{0,2},{1,3},{2,0},{3,1},{4,6},{5,7},{6,4},{7,5},{8,10},{9,11},{10,... | collective-permute-start | bytes 294920 | tf_op jit(solution)/shard_map/ppermute | solution.py:342
  24.5 49.9 %collective-permute-start.15 = (bf16[24,2048]{1,0:T(8,128)(2,1)S(1)}, bf16[24,2048]{1,0:T(8,128)(2,1)S(1)}, u32[]{:S(2)}, u32[]{:S(2)}) collective-permute-start(bf16[24,2048]{1,0:T(8,128)(2,1)S(1)} %convolution_convert_fusion.14), channel_id=1, source_target_pairs={{0,3},{1,2},{2,1},{3,0},{4,7},{5,6},{6,5},{7,4},{8,11},{9,10},{10,... | collective-permute-start | bytes 294920 | tf_op jit(solution)/shard_map/ppermute | solution.py:342
  37.1 15.8 %collective-permute-start.6 = (bf16[24,2048]{1,0:T(8,128)(2,1)S(1)}, bf16[24,2048]{1,0:T(8,128)(2,1)S(1)}, u32[]{:S(2)}, u32[]{:S(2)}) collective-permute-start(bf16[24,2048]{1,0:T(8,128)(2,1)S(1)} %convolution_convert_fusion.9), channel_id=1, source_target_pairs={{0,4},{1,5},{2,6},{3,7},{4,0},{5,1},{6,2},{7,3},{8,12},{9,13},{10,... | collective-permute-start | bytes 294920 | tf_op jit(solution)/shard_map/ppermute | solution.py:342
  37.8 19.5 %collective-permute-start.7 = (bf16[24,2048]{1,0:T(8,128)(2,1)S(1)}, bf16[24,2048]{1,0:T(8,128)(2,1)S(1)}, u32[]{:S(2)}, u32[]{:S(2)}) collective-permute-start(bf16[24,2048]{1,0:T(8,128)(2,1)S(1)} %convolution_convert_fusion.8), channel_id=1, source_target_pairs={{0,5},{1,4},{2,7},{3,6},{4,1},{5,0},{6,3},{7,2},{8,13},{9,12},{10,... | collective-permute-start | bytes 294920 | tf_op jit(solution)/shard_map/ppermute | solution.py:342
  52.9 8.5 %collective-permute-start.8 = (bf16[24,2048]{1,0:T(8,128)(2,1)S(1)}, bf16[24,2048]{1,0:T(8,128)(2,1)S(1)}, u32[]{:S(2)}, u32[]{:S(2)}) collective-permute-start(bf16[24,2048]{1,0:T(8,128)(2,1)S(1)} %convolution_convert_fusion.7), channel_id=1, source_target_pairs={{0,6},{1,7},{2,4},{3,5},{4,2},{5,3},{6,0},{7,1},{8,14},{9,15},{10,... | collective-permute-start | bytes 294920 | tf_op jit(solution)/shard_map/ppermute | solution.py:342
  57.3 6.8 %collective-permute-start.9 = (bf16[24,2048]{1,0:T(8,128)(2,1)S(1)}, bf16[24,2048]{1,0:T(8,128)(2,1)S(1)}, u32[]{:S(2)}, u32[]{:S(2)}) collective-permute-start(bf16[24,2048]{1,0:T(8,128)(2,1)S(1)} %convolution_convert_fusion.6), channel_id=1, source_target_pairs={{0,7},{1,6},{2,5},{3,4},{4,3},{5,2},{6,1},{7,0},{8,15},{9,14},{10,... | collective-permute-start | bytes 294920 | tf_op jit(solution)/shard_map/ppermute | solution.py:342
  61.3 5.3 %collective-permute-start.10 = (bf16[24,2048]{1,0:T(8,128)(2,1)S(1)}, bf16[24,2048]{1,0:T(8,128)(2,1)S(1)}, u32[]{:S(2)}, u32[]{:S(2)}) collective-permute-start(bf16[24,2048]{1,0:T(8,128)(2,1)S(1)} %convolution_convert_fusion.4), channel_id=1, source_target_pairs={{0,1},{1,0},{2,3},{3,2},{4,5},{5,4},{6,7},{7,6},{8,9},{9,8},{10,11... | collective-permute-start | bytes 294920 | tf_op jit(solution)/shard_map/ppermute | solution.py:342
  64.1 4.3 %collective-permute-start.11 = (bf16[24,2048]{1,0:T(8,128)(2,1)S(1)}, bf16[24,2048]{1,0:T(8,128)(2,1)S(1)}, u32[]{:S(2)}, u32[]{:S(2)}) collective-permute-start(bf16[24,2048]{1,0:T(8,128)(2,1)S(1)} %convolution_convert_fusion.3), channel_id=1, source_target_pairs={{0,2},{1,3},{2,0},{3,1},{4,6},{5,7},{6,4},{7,5},{8,10},{9,11},{10,... | collective-permute-start | bytes 294920 | tf_op jit(solution)/shard_map/ppermute | solution.py:342
  66.6 5.0 %collective-permute-start.12 = (bf16[24,2048]{1,0:T(8,128)(2,1)S(1)}, bf16[24,2048]{1,0:T(8,128)(2,1)S(1)}, u32[]{:S(2)}, u32[]{:S(2)}) collective-permute-start(bf16[24,2048]{1,0:T(8,128)(2,1)S(1)} %convolution_convert_fusion.2), channel_id=1, source_target_pairs={{0,3},{1,2},{2,1},{3,0},{4,7},{5,6},{6,5},{7,4},{8,11},{9,10},{10,... | collective-permute-start | bytes 294920 | tf_op jit(solution)/shard_map/ppermute | solution.py:342
  82.6 79.2 %copy-start.1 = (f32[4096]{0:T(1024)S(1)}, f32[4096]{0:T(1024)}, u32[]{:S(2)}) copy-start(f32[4096]{0:T(1024)} %param.11) | copy-start | bytes 49156
  82.6 79.2 %all-to-all-start.1 = ((bf16[16,24,4096]{2,1,0:T(8,128)(2,1)}), bf16[16,24,4096]{2,1,0:T(8,128)(2,1)}, u32[]{:S(2)}, u32[]{:S(2)}) async-start(bf16[16,24,4096]{2,1,0:T(8,128)(2,1)} %bitcast.69), calls=%async_computation.1 | async-start | bytes 6291456 | tf_op jit(solution)/shard_map/all_to_all | solution.py:339
  91.7 1.3 collective-permute-start.16
  92.9 12.8 %collective-permute-start.17 = (f32[8,128]{1,0:T(8,128)S(1)}, f32[8,128]{1,0:T(8,128)S(1)}, u32[]{:S(2)}, u32[]{:S(2)}) collective-permute-start(f32[8,128]{1,0:T(8,128)S(1)} %add.97), channel_id=1, source_target_pairs={{0,2},{1,3},{2,0},{3,1},{4,6},{5,7},{6,4},{7,5},{8,10},{9,11},{10,... | collective-permute-start | bytes 12296 | tf_op jit(solution)/shard_map/ppermute | solution.py:342
  105.7 39.0 %collective-permute-start.18 = (f32[8,128]{1,0:T(8,128)S(1)}, f32[8,128]{1,0:T(8,128)S(1)}, u32[]{:S(2)}, u32[]{:S(2)}) collective-permute-start(f32[8,128]{1,0:T(8,128)S(1)} %add.98), channel_id=1, source_target_pairs={{0,4},{1,5},{2,6},{3,7},{4,0},{5,1},{6,2},{7,3},{8,12},{9,13},{10,... | collective-permute-start | bytes 12296 | tf_op jit(solution)/shard_map/ppermute | solution.py:342
  144.8 14.7 %collective-permute-start.19 = (f32[8,128]{1,0:T(8,128)S(1)}, f32[8,128]{1,0:T(8,128)S(1)}, u32[]{:S(2)}, u32[]{:S(2)}) collective-permute-start(f32[8,128]{1,0:T(8,128)S(1)} %add.99), channel_id=1, source_target_pairs={{0,8},{1,9},{2,10},{3,11},{4,12},{5,13},{6,14},{7,15},{8,0},{9,1},... | collective-permute-start | bytes 12296 | tf_op jit(solution)/shard_map/ppermute | solution.py:342
  166.4 76.7 %all-to-all-start.2 = ((bf16[16,24,4096]{2,1,0:T(8,128)(2,1)}), bf16[16,24,4096]{2,1,0:T(8,128)(2,1)}, u32[]{:S(2)}, u32[]{:S(2)}) async-start(bf16[16,24,4096]{2,1,0:T(8,128)(2,1)} %bitcast.70), calls=%async_computation.2 | async-start | bytes 6291456 | tf_op jit(solution)/shard_map/all_to_all | solution.py:339
  (5 other events, 44.6 us)

commit v11 on v9

--- a/solution.py
+++ b/solution.py
@@ -317,7 +317,7 @@
             bytes_accessed=2 * features * (2 * slots + 3 * latents),
             transcendentals=0,
         ),
-        compiler_params=pltpu.CompilerParams(vmem_limit_bytes=60 * MIB),
+        compiler_params=pltpu.CompilerParams(vmem_limit_bytes=62 * MIB),
         name="gradients",
     )(squares, code_t, slopes, dec_t, rows_t, got_errors)
 

time: 246 us -> 245 us (level)
  local copies, waits for them, and re-layouts: 26.2 us -> 22.9 us
where the time goes in v11:
time: 245 us; the launch traced here: 244 us
  waiting for transfers between devices  145 us (59%)
  starting transfers between devices  38.8 us (16%)
  Pallas kernels  23.6 us (10%)
  local copies, waits for them, and re-layouts  22.9 us (9%)
  other arithmetic  6.49 us (3%)
  matrix products  5.93 us (2%)
    ppermute x20, waiting for transfers between devices, swap(): return lax.ppermute(rows, 'lat', [(i, i ^ step) for i in range(devices)])  86.3 us
    all_to_all x3, waiting for transfers between devices, exchange(): return lax.all_to_all(rows, 'lat', split_axis=0, concat_axis=0, tiled=True)  59.2 us
    all_to_all x3, starting transfers between devices, exchange(): return lax.all_to_all(rows, 'lat', split_axis=0, concat_axis=0, tiled=True)  22.2 us
    ppermute x20, starting transfers between devices, swap(): return lax.ppermute(rows, 'lat', [(i, i ^ step) for i in range(devices)])  16.6 us
    pallas_call x1, Pallas kernels, gradients(): pl.pallas_call(lambda *refs: grads_kernel(count, *refs), out_shape=[pltpu...  9.26 us
    optimization_barrier x4, local copies, waits for them, and re-layouts, together(): return lax.optimization_barrier(values)  8.54 us
    pallas_call x1, Pallas kernels, encode(): pl.pallas_call(lambda *refs: encode_kernel(dev_slots, capacity, *refs), o...  7.49 us
    dynamic_update_slice x7, local copies, waits for them, and re-layouts, deliver(): rows = lax.dynamic_update_index_in_dim(rows, part, me ^ k, 0)  7.2 us
  transfers between devices with their start and end apart: 23, of which 13 were waited for; matrix products, arithmetic and copies ran while one was open for 14% of the time, Pallas kernels for 1%

profile of v11, /device:TPU:13, one launch (start us, length us, event | category | flops | bytes accessed | tf_op | source)
XLA Modules:
  0.0 244.4 jit_solution(11813466470997782251)
XLA Ops:
  2.3 2.3 collective-permute-start.7
  6.1 2.2 squares.1
  10.2 2.7 %collective-permute-start.1 = (bf16[24,2048]{1,0:T(8,128)(2,1)S(1)}, bf16[24,2048]{1,0:T(8,128)(2,1)}, u32[]{:S(2)}, u32[]{:S(2)}) collective-permute-start(bf16[24,2048]{1,0:T(8,128)(2,1)S(1)} %convolution_convert_fusion.12), channel_id=1, source_target_pairs={{0,5},{1,4},{2,7},{3,6},{4,1},{5,0},{6,3},{7,2},{8,13},{9,12},{10,... | collective-permute-start | bytes 294920 | tf_op jit(solution)/shard_map/ppermute | solution.py:342
  16.1 7.1 %all-to-all-start = ((bf16[16,24,2048]{2,1,0:T(8,128)(2,1)}), bf16[16,24,2048]{2,1,0:T(8,128)(2,1)}, u32[]{:S(2)}, u32[]{:S(2)}) async-start(bf16[16,24,2048]{2,1,0:T(8,128)(2,1)} %bitcast.66), calls=%async_computation | async-start | bytes 3145728 | tf_op jit(solution)/shard_map/all_to_all | solution.py:339
  33.5 3.1 %collective-permute-done.5 = bf16[24,2048]{1,0:T(8,128)(2,1)S(1)} collective-permute-done((bf16[24,2048]{1,0:T(8,128)(2,1)S(1)}, bf16[24,2048]{1,0:T(8,128)(2,1)S(1)}, u32[]{:S(2)}, u32[]{:S(2)}) %collective-permute-start.5) | collective-permute-done | bytes 98336 | tf_op jit(solution)/shard_map/ppermute | solution.py:342
  37.2 2.6 %collective-permute-done.6 = bf16[24,2048]{1,0:T(8,128)(2,1)S(1)} collective-permute-done((bf16[24,2048]{1,0:T(8,128)(2,1)S(1)}, bf16[24,2048]{1,0:T(8,128)(2,1)S(1)}, u32[]{:S(2)}, u32[]{:S(2)}) %collective-permute-start.6) | collective-permute-done | bytes 98336 | tf_op jit(solution)/shard_map/ppermute | solution.py:342
  41.9 1.9 collective-permute-start.10
  43.8 1.7 collective-permute-start.11
  46.5 6.3 %collective-permute-done.9 = bf16[24,2048]{1,0:T(8,128)(2,1)S(1)} collective-permute-done((bf16[24,2048]{1,0:T(8,128)(2,1)S(1)}, bf16[24,2048]{1,0:T(8,128)(2,1)S(1)}, u32[]{:S(2)}, u32[]{:S(2)}) %collective-permute-start.9) | collective-permute-done | bytes 98336 | tf_op jit(solution)/shard_map/ppermute | solution.py:342
  54.5 3.7 %collective-permute-done.10 = bf16[24,2048]{1,0:T(8,128)(2,1)S(1)} collective-permute-done((bf16[24,2048]{1,0:T(8,128)(2,1)S(1)}, bf16[24,2048]{1,0:T(8,128)(2,1)S(1)}, u32[]{:S(2)}, u32[]{:S(2)}) %collective-permute-start.10) | collective-permute-done | bytes 98336 | tf_op jit(solution)/shard_map/ppermute | solution.py:342
  59.4 2.2 collective-permute-done.11
  67.5 7.5 %encode.1 = (bf16[384,256]{1,0:T(8,128)(2,1)}, f32[384,256]{1,0:T(8,128)}, bf16[384,4096]{1,0:T(8,128)(2,1)}) custom-call(f32[1,256]{1,0:T(1,128)} %bitcast.73, bf16[384,2048]{1,0:T(8,128)(2,1)} %bitcast.20.refs_1_, bf16[384,2048]{1,0:T(8,128)(2,1)} %bitcast.22.refs_2_, bf16[4096,256]{1,0:T(8,128)(2,1)} %refs_3_.1, bf16[256,4096]{1,0:T(8,128)(2,1)} %refs_4_.1), custom_call_target="tpu_custom_call" | custom-call | flops 1610612736 | bytes 10485760 | tf_op jit(solution)/shard_map/encode/pallas_call | solution.py:156
  75.1 8.4 %all-to-all-start.1 = ((bf16[16,24,4096]{2,1,0:T(8,128)(2,1)}), bf16[16,24,4096]{2,1,0:T(8,128)(2,1)}, u32[]{:S(2)}, u32[]{:S(2)}) async-start(bf16[16,24,4096]{2,1,0:T(8,128)(2,1)} %bitcast.69), calls=%async_computation.1 | async-start | bytes 6291456 | tf_op jit(solution)/shard_map/all_to_all | solution.py:339
  85.1 12.5 %collective-permute-done.17 = f32[8,128]{1,0:T(8,128)S(1)} collective-permute-done((f32[8,128]{1,0:T(8,128)S(1)}, f32[8,128]{1,0:T(8,128)S(1)}, u32[]{:S(2)}, u32[]{:S(2)}) %collective-permute-start.17) | collective-permute-done | bytes 4128 | tf_op jit(solution)/shard_map/ppermute | solution.py:342
  97.9 38.7 %collective-permute-done.18 = f32[8,128]{1,0:T(8,128)S(1)} collective-permute-done((f32[8,128]{1,0:T(8,128)S(1)}, f32[8,128]{1,0:T(8,128)S(1)}, u32[]{:S(2)}, u32[]{:S(2)}) %collective-permute-start.18) | collective-permute-done | bytes 4128 | tf_op jit(solution)/shard_map/ppermute | solution.py:342
  136.9 14.5 %collective-permute-done.19 = f32[8,128]{1,0:T(8,128)S(1)} collective-permute-done((f32[8,128]{1,0:T(8,128)S(1)}, f32[8,128]{1,0:T(8,128)S(1)}, u32[]{:S(2)}, u32[]{:S(2)}) %collective-permute-start.19) | collective-permute-done | bytes 4128 | tf_op jit(solution)/shard_map/ppermute | solution.py:342
  153.6 4.6 %rebuild.1 = (bf16[128,4096]{1,0:T(8,128)(2,1)}, bf16[384,4096]{1,0:T(8,128)(2,1)}) custom-call(bf16[384,128]{1,0:T(8,128)(2,1)S(1)} %convert_element_type.63.select_ref, bf16[128,384]{1,0:T(8,128)(2,1)S(1)} %convert_element_type.64.select_t_ref, f32[1,4096]{1,0:T(1,128)S(1)} %bitcast.64, bf16[128,4096]{1,0:T(8,128)(2,1)S(1)} %copy-done, ...), custom_call_target="tpu_custom_call" | custom-call | flops 805306368 | bytes 8388608 | tf_op jit(solution)/shard_map/rebuild/pallas_call | solution.py:216
  158.2 6.7 %all-to-all-start.2 = ((bf16[16,24,4096]{2,1,0:T(8,128)(2,1)}), bf16[16,24,4096]{2,1,0:T(8,128)(2,1)}, u32[]{:S(2)}, u32[]{:S(2)}) async-start(bf16[16,24,4096]{2,1,0:T(8,128)(2,1)} %bitcast.70), calls=%async_computation.2 | async-start | bytes 6291456 | tf_op jit(solution)/shard_map/all_to_all | solution.py:339
  165.8 2.6 %copy.41 = bf16[384,2048]{0,1:T(8,128)(2,1)} copy(bf16[384,2048]{1,0:T(8,128)(2,1)} %bitcast.20.refs_1_) | data formatting | bytes 3145728 | tf_op jit(solution)/shard_map/optimization_barrier | solution.py:32
  168.3 2.7 %copy.42 = bf16[384,2048]{0,1:T(8,128)(2,1)} copy(bf16[384,2048]{1,0:T(8,128)(2,1)} %bitcast.22.refs_2_) | data formatting | bytes 3145728 | tf_op jit(solution)/shard_map/optimization_barrier | solution.py:32
  171.1 2.4 copy.40
  173.5 3.9 %pad_maximum_fusion.refs_4_ = bf16[4096,384]{1,0:T(8,128)(2,1)} fusion(bf16[2048,384]{1,0:T(8,128)(2,1)} %bitcast.68, bf16[2048,384]{1,0:T(8,128)(2,1)} %bitcast.67), kind=kLoop, calls=%fused_computation | loop fusion | flops 6291456 | bytes 6291456 | tf_op jit(solution)/shard_map/concatenate | solution.py:412
  177.4 57.6 %all-to-all-done.2 = bf16[16,24,4096]{2,1,0:T(8,128)(2,1)} async-done(((bf16[16,24,4096]{2,1,0:T(8,128)(2,1)}), bf16[16,24,4096]{2,1,0:T(8,128)(2,1)}, u32[]{:S(2)}, u32[]{:S(2)}) %all-to-all-start.2) | async-done | bytes 3145760 | tf_op jit(solution)/shard_map/all_to_all | solution.py:339
  235.0 9.3 %gradients.1 = (bf16[256,4096]{1,0:T(8,128)(2,1)}, bf16[4096,256]{1,0:T(8,128)(2,1)}, f32[1,256]{1,0:T(1,128)}) custom-call(f32[8,128]{1,0:T(8,128)} %add.100.refs_0_, bf16[256,384]{1,0:T(8,128)(2,1)} %bitcast.71, f32[384,256]{1,0:T(8,128)} %get-tuple-element.46.refs_2_, bf16[4096,256]{1,0:T(8,128)(2,1)} %bitcast.65, ...), custom_call_target="tpu_custom_call" | custom-call | flops 2415919104 | bytes 12582912 | tf_op jit(solution)/shard_map/gradients/pallas_call | solution.py:296
  (92 shorter events, 36.0 us)
Async XLA Ops:
  2.3 6.2 %collective-permute-start.7 = (s32[2,128]{1,0:T(2,128)S(1)}, s32[2,128]{1,0:T(2,128)S(1)}, u32[]{:S(2)}, u32[]{:S(2)}) collective-permute-start(s32[2,128]{1,0:T(2,128)S(1)} %multiply_add_fusion), channel_id=1, source_target_pairs={{0,8},{1,9},{2,10},{3,11},{4,12},{5,13},{6,14},{7,15},{8,0},{9,1},... | collective-permute-start | bytes 3080 | tf_op jit(solution)/shard_map/ppermute | solution.py:342
  5.9 34.5 %collective-permute-start.8 = (bf16[128,2048]{1,0:T(8,128)(2,1)S(1)}, bf16[128,2048]{1,0:T(8,128)(2,1)S(1)}, u32[]{:S(2)}, u32[]{:S(2)}) collective-permute-start(bf16[128,2048]{1,0:T(8,128)(2,1)S(1)} %get-tuple-element.56), channel_id=1, source_target_pairs={{0,8},{1,9},{2,10},{3,11},{4,12},{5,13},{6,14},{7,15},{8,0},{9,1},... | collective-permute-start | bytes 1572872 | tf_op jit(solution)/shard_map/ppermute | solution.py:342
  9.9 13.3 %collective-permute-start = (bf16[24,2048]{1,0:T(8,128)(2,1)S(1)}, bf16[24,2048]{1,0:T(8,128)(2,1)}, u32[]{:S(2)}, u32[]{:S(2)}) collective-permute-start(bf16[24,2048]{1,0:T(8,128)(2,1)S(1)} %convolution_convert_fusion.13), channel_id=1, source_target_pairs={{0,4},{1,5},{2,6},{3,7},{4,0},{5,1},{6,2},{7,3},{8,12},{9,13},{10,... | collective-permute-start | bytes 294920 | tf_op jit(solution)/shard_map/ppermute | solution.py:342
  10.2 16.3 %collective-permute-start.1 = (bf16[24,2048]{1,0:T(8,128)(2,1)S(1)}, bf16[24,2048]{1,0:T(8,128)(2,1)}, u32[]{:S(2)}, u32[]{:S(2)}) collective-permute-start(bf16[24,2048]{1,0:T(8,128)(2,1)S(1)} %convolution_convert_fusion.12), channel_id=1, source_target_pairs={{0,5},{1,4},{2,7},{3,6},{4,1},{5,0},{6,3},{7,2},{8,13},{9,12},{10,... | collective-permute-start | bytes 294920 | tf_op jit(solution)/shard_map/ppermute | solution.py:342
  12.8 15.5 %collective-permute-start.2 = (bf16[24,2048]{1,0:T(8,128)(2,1)S(1)}, bf16[24,2048]{1,0:T(8,128)(2,1)}, u32[]{:S(2)}, u32[]{:S(2)}) collective-permute-start(bf16[24,2048]{1,0:T(8,128)(2,1)S(1)} %convolution_convert_fusion.11), channel_id=1, source_target_pairs={{0,6},{1,7},{2,4},{3,5},{4,2},{5,3},{6,0},{7,1},{8,14},{9,15},{10,... | collective-permute-start | bytes 294920 | tf_op jit(solution)/shard_map/ppermute | solution.py:342
  12.8 18.5 %collective-permute-start.3 = (bf16[24,2048]{1,0:T(8,128)(2,1)S(1)}, bf16[24,2048]{1,0:T(8,128)(2,1)S(1)}, u32[]{:S(2)}, u32[]{:S(2)}) collective-permute-start(bf16[24,2048]{1,0:T(8,128)(2,1)S(1)} %convolution_convert_fusion.10), channel_id=1, source_target_pairs={{0,7},{1,6},{2,5},{3,4},{4,3},{5,2},{6,1},{7,0},{8,15},{9,14},{10,... | collective-permute-start | bytes 294920 | tf_op jit(solution)/shard_map/ppermute | solution.py:342
  16.1 51.4 %all-to-all-start = ((bf16[16,24,2048]{2,1,0:T(8,128)(2,1)}), bf16[16,24,2048]{2,1,0:T(8,128)(2,1)}, u32[]{:S(2)}, u32[]{:S(2)}) async-start(bf16[16,24,2048]{2,1,0:T(8,128)(2,1)} %bitcast.66), calls=%async_computation | async-start | bytes 3145728 | tf_op jit(solution)/shard_map/all_to_all | solution.py:339
  23.2 9.7 %collective-permute-start.4 = (bf16[24,2048]{1,0:T(8,128)(2,1)S(1)}, bf16[24,2048]{1,0:T(8,128)(2,1)S(1)}, u32[]{:S(2)}, u32[]{:S(2)}) collective-permute-start(bf16[24,2048]{1,0:T(8,128)(2,1)S(1)} %convolution_convert_fusion.16), channel_id=1, source_target_pairs={{0,1},{1,0},{2,3},{3,2},{4,5},{5,4},{6,7},{7,6},{8,9},{9,8},{10,11... | collective-permute-start | bytes 294920 | tf_op jit(solution)/shard_map/ppermute | solution.py:342
  26.5 10.1 %collective-permute-start.5 = (bf16[24,2048]{1,0:T(8,128)(2,1)S(1)}, bf16[24,2048]{1,0:T(8,128)(2,1)S(1)}, u32[]{:S(2)}, u32[]{:S(2)}) collective-permute-start(bf16[24,2048]{1,0:T(8,128)(2,1)S(1)} %convolution_convert_fusion.15), channel_id=1, source_target_pairs={{0,2},{1,3},{2,0},{3,1},{4,6},{5,7},{6,4},{7,5},{8,10},{9,11},{10,... | collective-permute-start | bytes 294920 | tf_op jit(solution)/shard_map/ppermute | solution.py:342
  28.3 11.5 %collective-permute-start.6 = (bf16[24,2048]{1,0:T(8,128)(2,1)S(1)}, bf16[24,2048]{1,0:T(8,128)(2,1)S(1)}, u32[]{:S(2)}, u32[]{:S(2)}) collective-permute-start(bf16[24,2048]{1,0:T(8,128)(2,1)S(1)} %convolution_convert_fusion.14), channel_id=1, source_target_pairs={{0,3},{1,2},{2,1},{3,0},{4,7},{5,6},{6,5},{7,4},{8,11},{9,10},{10,... | collective-permute-start | bytes 294920 | tf_op jit(solution)/shard_map/ppermute | solution.py:342
  41.6 11.3 %collective-permute-start.9 = (bf16[24,2048]{1,0:T(8,128)(2,1)S(1)}, bf16[24,2048]{1,0:T(8,128)(2,1)S(1)}, u32[]{:S(2)}, u32[]{:S(2)}) collective-permute-start(bf16[24,2048]{1,0:T(8,128)(2,1)S(1)} %convolution_convert_fusion.8), channel_id=1, source_target_pairs={{0,4},{1,5},{2,6},{3,7},{4,0},{5,1},{6,2},{7,3},{8,12},{9,13},{10,... | collective-permute-start | bytes 294920 | tf_op jit(solution)/shard_map/ppermute | solution.py:342
  41.9 16.4 %collective-permute-start.10 = (bf16[24,2048]{1,0:T(8,128)(2,1)S(1)}, bf16[24,2048]{1,0:T(8,128)(2,1)S(1)}, u32[]{:S(2)}, u32[]{:S(2)}) collective-permute-start(bf16[24,2048]{1,0:T(8,128)(2,1)S(1)} %convolution_convert_fusion.7), channel_id=1, source_target_pairs={{0,5},{1,4},{2,7},{3,6},{4,1},{5,0},{6,3},{7,2},{8,13},{9,12},{10,... | collective-permute-start | bytes 294920 | tf_op jit(solution)/shard_map/ppermute | solution.py:342
  43.8 17.8 %collective-permute-start.11 = (bf16[24,2048]{1,0:T(8,128)(2,1)S(1)}, bf16[24,2048]{1,0:T(8,128)(2,1)S(1)}, u32[]{:S(2)}, u32[]{:S(2)}) collective-permute-start(bf16[24,2048]{1,0:T(8,128)(2,1)S(1)} %convolution_convert_fusion.6), channel_id=1, source_target_pairs={{0,6},{1,7},{2,4},{3,5},{4,2},{5,3},{6,0},{7,1},{8,14},{9,15},{10,... | collective-permute-start | bytes 294920 | tf_op jit(solution)/shard_map/ppermute | solution.py:342
  45.5 18.2 %collective-permute-start.12 = (bf16[24,2048]{1,0:T(8,128)(2,1)S(1)}, bf16[24,2048]{1,0:T(8,128)(2,1)S(1)}, u32[]{:S(2)}, u32[]{:S(2)}) collective-permute-start(bf16[24,2048]{1,0:T(8,128)(2,1)S(1)} %convolution_convert_fusion.5), channel_id=1, source_target_pairs={{0,7},{1,6},{2,5},{3,4},{4,3},{5,2},{6,1},{7,0},{8,15},{9,14},{10,... | collective-permute-start | bytes 294920 | tf_op jit(solution)/shard_map/ppermute | solution.py:342
  46.3 18.9 %collective-permute-start.13 = (bf16[24,2048]{1,0:T(8,128)(2,1)S(1)}, bf16[24,2048]{1,0:T(8,128)(2,1)S(1)}, u32[]{:S(2)}, u32[]{:S(2)}) collective-permute-start(bf16[24,2048]{1,0:T(8,128)(2,1)S(1)} %convolution_convert_fusion.3), channel_id=1, source_target_pairs={{0,1},{1,0},{2,3},{3,2},{4,5},{5,4},{6,7},{7,6},{8,9},{9,8},{10,11... | collective-permute-start | bytes 294920 | tf_op jit(solution)/shard_map/ppermute | solution.py:342
  52.9 12.9 %collective-permute-start.14 = (bf16[24,2048]{1,0:T(8,128)(2,1)S(1)}, bf16[24,2048]{1,0:T(8,128)(2,1)S(1)}, u32[]{:S(2)}, u32[]{:S(2)}) collective-permute-start(bf16[24,2048]{1,0:T(8,128)(2,1)S(1)} %convolution_convert_fusion.2), channel_id=1, source_target_pairs={{0,2},{1,3},{2,0},{3,1},{4,6},{5,7},{6,4},{7,5},{8,10},{9,11},{10,... | collective-permute-start | bytes 294920 | tf_op jit(solution)/shard_map/ppermute | solution.py:342
  58.2 8.6 %collective-permute-start.15 = (bf16[24,2048]{1,0:T(8,128)(2,1)S(1)}, bf16[24,2048]{1,0:T(8,128)(2,1)S(1)}, u32[]{:S(2)}, u32[]{:S(2)}) collective-permute-start(bf16[24,2048]{1,0:T(8,128)(2,1)S(1)} %convolution_convert_fusion.1), channel_id=1, source_target_pairs={{0,3},{1,2},{2,1},{3,0},{4,7},{5,6},{6,5},{7,4},{8,11},{9,10},{10,... | collective-permute-start | bytes 294920 | tf_op jit(solution)/shard_map/ppermute | solution.py:342
  75.0 78.6 %copy-start.1 = (f32[4096]{0:T(1024)S(1)}, f32[4096]{0:T(1024)}, u32[]{:S(2)}) copy-start(f32[4096]{0:T(1024)} %param.11) | copy-start | bytes 49156
  75.1 78.6 %all-to-all-start.1 = ((bf16[16,24,4096]{2,1,0:T(8,128)(2,1)}), bf16[16,24,4096]{2,1,0:T(8,128)(2,1)}, u32[]{:S(2)}, u32[]{:S(2)}) async-start(bf16[16,24,4096]{2,1,0:T(8,128)(2,1)} %bitcast.69), calls=%async_computation.1 | async-start | bytes 6291456 | tf_op jit(solution)/shard_map/all_to_all | solution.py:339
  83.5 1.3 collective-permute-start.16
  84.8 12.8 %collective-permute-start.17 = (f32[8,128]{1,0:T(8,128)S(1)}, f32[8,128]{1,0:T(8,128)S(1)}, u32[]{:S(2)}, u32[]{:S(2)}) collective-permute-start(f32[8,128]{1,0:T(8,128)S(1)} %add.97), channel_id=1, source_target_pairs={{0,2},{1,3},{2,0},{3,1},{4,6},{5,7},{6,4},{7,5},{8,10},{9,11},{10,... | collective-permute-start | bytes 12296 | tf_op jit(solution)/shard_map/ppermute | solution.py:342
  97.6 39.0 %collective-permute-start.18 = (f32[8,128]{1,0:T(8,128)S(1)}, f32[8,128]{1,0:T(8,128)S(1)}, u32[]{:S(2)}, u32[]{:S(2)}) collective-permute-start(f32[8,128]{1,0:T(8,128)S(1)} %add.98), channel_id=1, source_target_pairs={{0,4},{1,5},{2,6},{3,7},{4,0},{5,1},{6,2},{7,3},{8,12},{9,13},{10,... | collective-permute-start | bytes 12296 | tf_op jit(solution)/shard_map/ppermute | solution.py:342
  136.6 14.7 %collective-permute-start.19 = (f32[8,128]{1,0:T(8,128)S(1)}, f32[8,128]{1,0:T(8,128)S(1)}, u32[]{:S(2)}, u32[]{:S(2)}) collective-permute-start(f32[8,128]{1,0:T(8,128)S(1)} %add.99), channel_id=1, source_target_pairs={{0,8},{1,9},{2,10},{3,11},{4,12},{5,13},{6,14},{7,15},{8,0},{9,1},... | collective-permute-start | bytes 12296 | tf_op jit(solution)/shard_map/ppermute | solution.py:342
  158.2 76.7 %all-to-all-start.2 = ((bf16[16,24,4096]{2,1,0:T(8,128)(2,1)}), bf16[16,24,4096]{2,1,0:T(8,128)(2,1)}, u32[]{:S(2)}, u32[]{:S(2)}) async-start(bf16[16,24,4096]{2,1,0:T(8,128)(2,1)} %bitcast.70), calls=%async_computation.2 | async-start | bytes 6291456 | tf_op jit(solution)/shard_map/all_to_all | solution.py:339
  (5 other events, 43.3 us)

commit v12 on v11

--- a/solution.py
+++ b/solution.py
@@ -116,23 +116,17 @@
     slopes_ref,
     partial_ref,
     rows_here,
-    enc_here,
-    dec_here,
     code_here,
     slopes_here,
     out_here,
     sems,
 ):
     slots, latents = slopes_here.shape
-    copies = fetch(
-        (columns, (rows_f_ref, rows_g_ref), rows_here, sems.at[0]),
-        (lines, enc_ref, enc_here, sems.at[1]),
-    )
-    dec_copies = fetch((columns, dec_ref, dec_here, sems.at[2]))
+    copies = fetch((columns, (rows_f_ref, rows_g_ref), rows_here, sems.at[0]))
     preact = bias_ref[...]
     for i in range(PIECES):
         finish(copies[i])
-        preact = preact + dot(columns(rows_here, i)[...], lines(enc_here, i)[...], 1, 0)
+        preact = preact + dot(columns(rows_here, i)[...], lines(enc_ref, i)[...], 1, 0)
     output, slopes = activate(preact)
     row = lax.broadcasted_iota(jnp.int32, (slots, latents), 0)
     latent = lax.broadcasted_iota(jnp.int32, (slots, latents), 1)
@@ -144,8 +138,7 @@
     slopes_here[...] = jnp.where(own, slopes, 0.0)
     store(stores, slopes_here, slopes_ref, sems.at[3, 1])
     for i in range(PIECES):
-        finish(dec_copies[i])
-        columns(out_here, i)[...] = dot(code, columns(dec_here, i)[...], 1, 0).astype(BF16)
+        columns(out_here, i)[...] = dot(code, columns(dec_ref, i)[...], 1, 0).astype(BF16)
         store(stores, columns(out_here, i), columns(partial_ref, i), sems.at[4, i])
     finish(stores)
 
@@ -160,12 +153,10 @@
             pltpu.HBM((slots, latents), F32),
             pltpu.HBM((slots, features), BF16),
         ],
-        in_specs=[VMEM_SPEC] + [HBM_SPEC] * 4,
+        in_specs=[VMEM_SPEC] + [HBM_SPEC] * 2 + [VMEM_SPEC] * 2,
         out_specs=[HBM_SPEC] * 3,
         scratch_shapes=[
             pltpu.VMEM((slots, features), BF16),
-            pltpu.VMEM((features, latents), BF16),
-            pltpu.VMEM((latents, features), BF16),
             pltpu.VMEM((slots, latents), BF16),
             pltpu.VMEM((slots, latents), F32),
             pltpu.VMEM((slots, features), BF16),
@@ -176,7 +167,7 @@
             bytes_accessed=4 * features * (slots + latents),
             transcendentals=slots * latents,
         ),
-        compiler_params=pltpu.CompilerParams(vmem_limit_bytes=62 * MIB),
+        compiler_params=pltpu.CompilerParams(vmem_limit_bytes=40 * MIB),
         name="encode",
     )(enc_bias, *rows, enc_weight, dec_weight)
 

time: 245 us -> 253 us (1.033)
  waiting for transfers between devices: 145 us -> 154 us
  starting transfers between devices: 38.8 us -> 43.1 us
  local copies, waits for them, and re-layouts: 22.9 us -> 20.2 us
    ppermute x20, waiting for transfers between devices: 86.3 us -> 92.9 us  [swap(): return lax.ppermute(rows, 'lat', [(i, i ^ step) for i in range(devices)])]
    unnamed x12 -> x22, local copies, waits for them, and re-layouts: 0.04 us -> 5.77 us
    dynamic_update_slice x7, local copies, waits for them, and re-layouts: 4.53 us -> 0.08 us  [deliver(): rows = lax.dynamic_update_index_in_dim(rows, part, me ^ k + half, 0)]
    dynamic_update_slice x7, local copies, waits for them, and re-layouts: 7.2 us -> 3.64 us  [deliver(): rows = lax.dynamic_update_index_in_dim(rows, part, me ^ k, 0)]
    all_to_all x3, starting transfers between devices: 22.2 us -> 25.2 us  [exchange(): return lax.all_to_all(rows, 'lat', split_axis=0, concat_axis=0, tiled=True)]
  transfers between devices with their start and end apart: 23 -> 23, of which waited for: 13 -> 14; matrix products, arithmetic and copies ran while one was open for 14% -> 10% of each run, Pallas kernels for 1% -> 1%
where the time goes in v12:
time: 253 us; the launch traced here: 252 us
  waiting for transfers between devices  154 us (61%)
  starting transfers between devices  43.1 us (17%)
  Pallas kernels  21.3 us (8%)
  local copies, waits for them, and re-layouts  20.2 us (8%)
  matrix products  7.23 us (3%)
  other arithmetic  4.59 us (2%)
    ppermute x20, waiting for transfers between devices, swap(): return lax.ppermute(rows, 'lat', [(i, i ^ step) for i in range(devices)])  92.9 us
    all_to_all x3, waiting for transfers between devices, exchange(): return lax.all_to_all(rows, 'lat', split_axis=0, concat_axis=0, tiled=True)  61.2 us
    all_to_all x3, starting transfers between devices, exchange(): return lax.all_to_all(rows, 'lat', split_axis=0, concat_axis=0, tiled=True)  25.2 us
    ppermute x20, starting transfers between devices, swap(): return lax.ppermute(rows, 'lat', [(i, i ^ step) for i in range(devices)])  18 us
    pallas_call x1, Pallas kernels, gradients(): pl.pallas_call(lambda *refs: grads_kernel(count, *refs), out_shape=[pltpu...  9.26 us
    optimization_barrier x4, local copies, waits for them, and re-layouts, together(): return lax.optimization_barrier(values)  8.44 us
    dot_general x17, matrix products, dot(): return lax.dot_general(left, right, dims, preferred_element_type=F32)  7.23 us
    unnamed x22, local copies, waits for them, and re-layouts  5.77 us
  transfers between devices with their start and end apart: 23, of which 14 were waited for; matrix products, arithmetic and copies ran while one was open for 10% of the time, Pallas kernels for 1%

profile of v12, /device:TPU:13, one launch (start us, length us, event | category | flops | bytes accessed | tf_op | source)
XLA Modules:
  0.0 251.7 jit_solution(16906085059468430377)
XLA Ops:
  2.3 2.3 collective-permute-start.7
  4.6 2.1 fusion.40
  6.8 2.2 squares.1
  13.4 2.7 %collective-permute-start.1 = (bf16[24,2048]{1,0:T(8,128)(2,1)}, bf16[24,2048]{1,0:T(8,128)(2,1)}, u32[]{:S(2)}, u32[]{:S(2)}) collective-permute-start(bf16[24,2048]{1,0:T(8,128)(2,1)} %convolution_convert_fusion.12), channel_id=1, source_target_pairs={{0,5},{1,4},{2,7},{3,6},{4,1},{5,0},{6,3},{7,2},{8,13},{9,12},{10,... | collective-permute-start | bytes 294920 | tf_op jit(solution)/shard_map/ppermute | solution.py:333
  19.4 7.1 %all-to-all-start = ((bf16[16,24,2048]{2,1,0:T(8,128)(2,1)}), bf16[16,24,2048]{2,1,0:T(8,128)(2,1)S(1)}, u32[]{:S(2)}, u32[]{:S(2)}) async-start(bf16[16,24,2048]{2,1,0:T(8,128)(2,1)} %bitcast.71), calls=%async_computation | async-start | bytes 3145728 | tf_op jit(solution)/shard_map/all_to_all | solution.py:330
  31.7 2.1 collective-permute-done.3
  36.2 4.7 %collective-permute-done.6 = bf16[24,2048]{1,0:T(8,128)(2,1)S(1)} collective-permute-done((bf16[24,2048]{1,0:T(8,128)(2,1)S(1)}, bf16[24,2048]{1,0:T(8,128)(2,1)S(1)}, u32[]{:S(2)}, u32[]{:S(2)}) %collective-permute-start.6) | collective-permute-done | bytes 98336 | tf_op jit(solution)/shard_map/ppermute | solution.py:333
  42.7 3.1 %collective-permute-start.10 = (bf16[24,2048]{1,0:T(8,128)(2,1)S(1)}, bf16[24,2048]{1,0:T(8,128)(2,1)S(1)}, u32[]{:S(2)}, u32[]{:S(2)}) collective-permute-start(bf16[24,2048]{1,0:T(8,128)(2,1)S(1)} %convolution_convert_fusion.7), channel_id=1, source_target_pairs={{0,5},{1,4},{2,7},{3,6},{4,1},{5,0},{6,3},{7,2},{8,13},{9,12},{10,... | collective-permute-start | bytes 294920 | tf_op jit(solution)/shard_map/ppermute | solution.py:333
  45.9 3.0 %collective-permute-start.11 = (bf16[24,2048]{1,0:T(8,128)(2,1)S(1)}, bf16[24,2048]{1,0:T(8,128)(2,1)S(1)}, u32[]{:S(2)}, u32[]{:S(2)}) collective-permute-start(bf16[24,2048]{1,0:T(8,128)(2,1)S(1)} %convolution_convert_fusion.6), channel_id=1, source_target_pairs={{0,6},{1,7},{2,4},{3,5},{4,2},{5,3},{6,0},{7,1},{8,14},{9,15},{10,... | collective-permute-start | bytes 294920 | tf_op jit(solution)/shard_map/ppermute | solution.py:333
  49.6 7.6 %collective-permute-done.9 = bf16[24,2048]{1,0:T(8,128)(2,1)S(1)} collective-permute-done((bf16[24,2048]{1,0:T(8,128)(2,1)S(1)}, bf16[24,2048]{1,0:T(8,128)(2,1)S(1)}, u32[]{:S(2)}, u32[]{:S(2)}) %collective-permute-start.9) | collective-permute-done | bytes 98336 | tf_op jit(solution)/shard_map/ppermute | solution.py:333
  57.5 5.3 %collective-permute-done.10 = bf16[24,2048]{1,0:T(8,128)(2,1)S(1)} collective-permute-done((bf16[24,2048]{1,0:T(8,128)(2,1)S(1)}, bf16[24,2048]{1,0:T(8,128)(2,1)S(1)}, u32[]{:S(2)}, u32[]{:S(2)}) %collective-permute-start.10) | collective-permute-done | bytes 98336 | tf_op jit(solution)/shard_map/ppermute | solution.py:333
  62.8 2.1 collective-permute-done.11
  64.9 2.1 collective-permute-done.12
  74.2 5.2 %encode.1 = (bf16[384,256]{1,0:T(8,128)(2,1)}, f32[384,256]{1,0:T(8,128)}, bf16[384,4096]{1,0:T(8,128)(2,1)}) custom-call(f32[1,256]{1,0:T(1,128)S(1)} %bitcast.69, bf16[384,2048]{1,0:T(8,128)(2,1)S(1)} %bitcast.67, bf16[384,2048]{1,0:T(8,128)(2,1)S(1)} %bitcast.64, bf16[4096,256]{1,0:T(8,128)(2,1)S(1)} %copy-done.4, bf16[256,4096]{1,0:T(8,128)(2,1)S(1)} %copy-done.3), custom_call_target="tpu_custom_call" | custom-call | flops 1610612736 | bytes 10485760 | tf_op jit(solution)/shard_map/encode/pallas_call | solution.py:149
  79.5 11.3 %all-to-all-start.1 = ((bf16[16,24,4096]{2,1,0:T(8,128)(2,1)}), bf16[16,24,4096]{2,1,0:T(8,128)(2,1)}, u32[]{:S(2)}, u32[]{:S(2)}) async-start(bf16[16,24,4096]{2,1,0:T(8,128)(2,1)} %bitcast.74), calls=%async_computation.1 | async-start | bytes 6291456 | tf_op jit(solution)/shard_map/all_to_all | solution.py:330
  92.4 12.5 %collective-permute-done.17 = f32[8,128]{1,0:T(8,128)S(1)} collective-permute-done((f32[8,128]{1,0:T(8,128)S(1)}, f32[8,128]{1,0:T(8,128)S(1)}, u32[]{:S(2)}, u32[]{:S(2)}) %collective-permute-start.17) | collective-permute-done | bytes 4128 | tf_op jit(solution)/shard_map/ppermute | solution.py:333
  105.2 38.7 %collective-permute-done.18 = f32[8,128]{1,0:T(8,128)S(1)} collective-permute-done((f32[8,128]{1,0:T(8,128)S(1)}, f32[8,128]{1,0:T(8,128)S(1)}, u32[]{:S(2)}, u32[]{:S(2)}) %collective-permute-start.18) | collective-permute-done | bytes 4128 | tf_op jit(solution)/shard_map/ppermute | solution.py:333
  144.3 14.5 %collective-permute-done.19 = f32[8,128]{1,0:T(8,128)S(1)} collective-permute-done((f32[8,128]{1,0:T(8,128)S(1)}, f32[8,128]{1,0:T(8,128)S(1)}, u32[]{:S(2)}, u32[]{:S(2)}) %collective-permute-start.19) | collective-permute-done | bytes 4128 | tf_op jit(solution)/shard_map/ppermute | solution.py:333
  161.0 4.6 %rebuild.1 = (bf16[128,4096]{1,0:T(8,128)(2,1)}, bf16[384,4096]{1,0:T(8,128)(2,1)}) custom-call(bf16[384,128]{1,0:T(8,128)(2,1)S(1)} %convert_element_type.63.select_ref, bf16[128,384]{1,0:T(8,128)(2,1)S(1)} %convert_element_type.64.select_t_ref, f32[1,4096]{1,0:T(1,128)S(1)} %bitcast.68, bf16[128,4096]{1,0:T(8,128)(2,1)S(1)} %copy-done, ...), custom_call_target="tpu_custom_call" | custom-call | flops 805306368 | bytes 8388608 | tf_op jit(solution)/shard_map/rebuild/pallas_call | solution.py:207
  165.5 6.8 %all-to-all-start.2 = ((bf16[16,24,4096]{2,1,0:T(8,128)(2,1)}), bf16[16,24,4096]{2,1,0:T(8,128)(2,1)}, u32[]{:S(2)}, u32[]{:S(2)}) async-start(bf16[16,24,4096]{2,1,0:T(8,128)(2,1)} %bitcast.75), calls=%async_computation.2 | async-start | bytes 6291456 | tf_op jit(solution)/shard_map/all_to_all | solution.py:330
  176.6 4.2 %copy.40 = bf16[256,4096]{0,1:T(8,128)(2,1)} copy(bf16[256,4096]{1,0:T(8,128)(2,1)} %refs_4_.1) | data formatting | bytes 4194304 | tf_op jit(solution)/shard_map/optimization_barrier | solution.py:32
  180.8 2.0 pad_maximum_fusion.refs_4_
  182.8 59.5 %all-to-all-done.2 = bf16[16,24,4096]{2,1,0:T(8,128)(2,1)} async-done(((bf16[16,24,4096]{2,1,0:T(8,128)(2,1)}), bf16[16,24,4096]{2,1,0:T(8,128)(2,1)}, u32[]{:S(2)}, u32[]{:S(2)}) %all-to-all-start.2) | async-done | bytes 3145760 | tf_op jit(solution)/shard_map/all_to_all | solution.py:330
  242.3 9.3 %gradients.1 = (bf16[256,4096]{1,0:T(8,128)(2,1)}, bf16[4096,256]{1,0:T(8,128)(2,1)}, f32[1,256]{1,0:T(1,128)}) custom-call(f32[8,128]{1,0:T(8,128)} %add.100.refs_0_, bf16[256,384]{1,0:T(8,128)(2,1)} %bitcast.76, f32[384,256]{1,0:T(8,128)} %get-tuple-element.46.refs_2_, bf16[4096,256]{1,0:T(8,128)(2,1)} %bitcast.70, ...), custom_call_target="tpu_custom_call" | custom-call | flops 2415919104 | bytes 12582912 | tf_op jit(solution)/shard_map/gradients/pallas_call | solution.py:287
  (102 shorter events, 35.4 us)
Async XLA Ops:
  2.3 6.8 %collective-permute-start.7 = (s32[2,128]{1,0:T(2,128)S(1)}, s32[2,128]{1,0:T(2,128)S(1)}, u32[]{:S(2)}, u32[]{:S(2)}) collective-permute-start(s32[2,128]{1,0:T(2,128)S(1)} %multiply_add_fusion), channel_id=1, source_target_pairs={{0,8},{1,9},{2,10},{3,11},{4,12},{5,13},{6,14},{7,15},{8,0},{9,1},... | collective-permute-start | bytes 3080 | tf_op jit(solution)/shard_map/ppermute | solution.py:333
  6.7 34.1 %collective-permute-start.8 = (bf16[128,2048]{1,0:T(8,128)(2,1)}, bf16[128,2048]{1,0:T(8,128)(2,1)S(1)}, u32[]{:S(2)}, u32[]{:S(2)}) collective-permute-start(bf16[128,2048]{1,0:T(8,128)(2,1)} %get-tuple-element.56), channel_id=1, source_target_pairs={{0,8},{1,9},{2,10},{3,11},{4,12},{5,13},{6,14},{7,15},{8,0},{9,1},... | collective-permute-start | bytes 1572872 | tf_op jit(solution)/shard_map/ppermute | solution.py:333
  13.2 13.3 %collective-permute-start = (bf16[24,2048]{1,0:T(8,128)(2,1)}, bf16[24,2048]{1,0:T(8,128)(2,1)}, u32[]{:S(2)}, u32[]{:S(2)}) collective-permute-start(bf16[24,2048]{1,0:T(8,128)(2,1)} %convolution_convert_fusion.13), channel_id=1, source_target_pairs={{0,4},{1,5},{2,6},{3,7},{4,0},{5,1},{6,2},{7,3},{8,12},{9,13},{10,... | collective-permute-start | bytes 294920 | tf_op jit(solution)/shard_map/ppermute | solution.py:333
  13.4 14.6 %collective-permute-start.1 = (bf16[24,2048]{1,0:T(8,128)(2,1)}, bf16[24,2048]{1,0:T(8,128)(2,1)}, u32[]{:S(2)}, u32[]{:S(2)}) collective-permute-start(bf16[24,2048]{1,0:T(8,128)(2,1)} %convolution_convert_fusion.12), channel_id=1, source_target_pairs={{0,5},{1,4},{2,7},{3,6},{4,1},{5,0},{6,3},{7,2},{8,13},{9,12},{10,... | collective-permute-start | bytes 294920 | tf_op jit(solution)/shard_map/ppermute | solution.py:333
  16.1 13.1 %collective-permute-start.2 = (bf16[24,2048]{1,0:T(8,128)(2,1)}, bf16[24,2048]{1,0:T(8,128)(2,1)}, u32[]{:S(2)}, u32[]{:S(2)}) collective-permute-start(bf16[24,2048]{1,0:T(8,128)(2,1)} %convolution_convert_fusion.11), channel_id=1, source_target_pairs={{0,6},{1,7},{2,4},{3,5},{4,2},{5,3},{6,0},{7,1},{8,14},{9,15},{10,... | collective-permute-start | bytes 294920 | tf_op jit(solution)/shard_map/ppermute | solution.py:333
  16.1 17.7 %collective-permute-start.3 = (bf16[24,2048]{1,0:T(8,128)(2,1)}, bf16[24,2048]{1,0:T(8,128)(2,1)}, u32[]{:S(2)}, u32[]{:S(2)}) collective-permute-start(bf16[24,2048]{1,0:T(8,128)(2,1)} %convolution_convert_fusion.10), channel_id=1, source_target_pairs={{0,7},{1,6},{2,5},{3,4},{4,3},{5,2},{6,1},{7,0},{8,15},{9,14},{10,... | collective-permute-start | bytes 294920 | tf_op jit(solution)/shard_map/ppermute | solution.py:333
  19.4 50.3 %all-to-all-start = ((bf16[16,24,2048]{2,1,0:T(8,128)(2,1)}), bf16[16,24,2048]{2,1,0:T(8,128)(2,1)S(1)}, u32[]{:S(2)}, u32[]{:S(2)}) async-start(bf16[16,24,2048]{2,1,0:T(8,128)(2,1)} %bitcast.71), calls=%async_computation | async-start | bytes 3145728 | tf_op jit(solution)/shard_map/all_to_all | solution.py:330
  26.5 8.5 %collective-permute-start.4 = (bf16[24,2048]{1,0:T(8,128)(2,1)S(1)}, bf16[24,2048]{1,0:T(8,128)(2,1)S(1)}, u32[]{:S(2)}, u32[]{:S(2)}) collective-permute-start(bf16[24,2048]{1,0:T(8,128)(2,1)S(1)} %convolution_convert_fusion.16), channel_id=1, source_target_pairs={{0,1},{1,0},{2,3},{3,2},{4,5},{5,4},{6,7},{7,6},{8,9},{9,8},{10,11... | collective-permute-start | bytes 294920 | tf_op jit(solution)/shard_map/ppermute | solution.py:333
  28.0 8.2 %collective-permute-start.5 = (bf16[24,2048]{1,0:T(8,128)(2,1)S(1)}, bf16[24,2048]{1,0:T(8,128)(2,1)S(1)}, u32[]{:S(2)}, u32[]{:S(2)}) collective-permute-start(bf16[24,2048]{1,0:T(8,128)(2,1)S(1)} %convolution_convert_fusion.15), channel_id=1, source_target_pairs={{0,2},{1,3},{2,0},{3,1},{4,6},{5,7},{6,4},{7,5},{8,10},{9,11},{10,... | collective-permute-start | bytes 294920 | tf_op jit(solution)/shard_map/ppermute | solution.py:333
  29.3 11.6 %collective-permute-start.6 = (bf16[24,2048]{1,0:T(8,128)(2,1)S(1)}, bf16[24,2048]{1,0:T(8,128)(2,1)S(1)}, u32[]{:S(2)}, u32[]{:S(2)}) collective-permute-start(bf16[24,2048]{1,0:T(8,128)(2,1)S(1)} %convolution_convert_fusion.14), channel_id=1, source_target_pairs={{0,3},{1,2},{2,1},{3,0},{4,7},{5,6},{6,5},{7,4},{8,11},{9,10},{10,... | collective-permute-start | bytes 294920 | tf_op jit(solution)/shard_map/ppermute | solution.py:333
  42.0 15.2 %collective-permute-start.9 = (bf16[24,2048]{1,0:T(8,128)(2,1)S(1)}, bf16[24,2048]{1,0:T(8,128)(2,1)S(1)}, u32[]{:S(2)}, u32[]{:S(2)}) collective-permute-start(bf16[24,2048]{1,0:T(8,128)(2,1)S(1)} %convolution_convert_fusion.8), channel_id=1, source_target_pairs={{0,4},{1,5},{2,6},{3,7},{4,0},{5,1},{6,2},{7,3},{8,12},{9,13},{10,... | collective-permute-start | bytes 294920 | tf_op jit(solution)/shard_map/ppermute | solution.py:333
  42.7 20.1 %collective-permute-start.10 = (bf16[24,2048]{1,0:T(8,128)(2,1)S(1)}, bf16[24,2048]{1,0:T(8,128)(2,1)S(1)}, u32[]{:S(2)}, u32[]{:S(2)}) collective-permute-start(bf16[24,2048]{1,0:T(8,128)(2,1)S(1)} %convolution_convert_fusion.7), channel_id=1, source_target_pairs={{0,5},{1,4},{2,7},{3,6},{4,1},{5,0},{6,3},{7,2},{8,13},{9,12},{10,... | collective-permute-start | bytes 294920 | tf_op jit(solution)/shard_map/ppermute | solution.py:333
  45.9 19.1 %collective-permute-start.11 = (bf16[24,2048]{1,0:T(8,128)(2,1)S(1)}, bf16[24,2048]{1,0:T(8,128)(2,1)S(1)}, u32[]{:S(2)}, u32[]{:S(2)}) collective-permute-start(bf16[24,2048]{1,0:T(8,128)(2,1)S(1)} %convolution_convert_fusion.6), channel_id=1, source_target_pairs={{0,6},{1,7},{2,4},{3,5},{4,2},{5,3},{6,0},{7,1},{8,14},{9,15},{10,... | collective-permute-start | bytes 294920 | tf_op jit(solution)/shard_map/ppermute | solution.py:333
  48.9 18.1 %collective-permute-start.12 = (bf16[24,2048]{1,0:T(8,128)(2,1)S(1)}, bf16[24,2048]{1,0:T(8,128)(2,1)S(1)}, u32[]{:S(2)}, u32[]{:S(2)}) collective-permute-start(bf16[24,2048]{1,0:T(8,128)(2,1)S(1)} %convolution_convert_fusion.5), channel_id=1, source_target_pairs={{0,7},{1,6},{2,5},{3,4},{4,3},{5,2},{6,1},{7,0},{8,15},{9,14},{10,... | collective-permute-start | bytes 294920 | tf_op jit(solution)/shard_map/ppermute | solution.py:333
  49.3 18.0 %collective-permute-start.13 = (bf16[24,2048]{1,0:T(8,128)(2,1)S(1)}, bf16[24,2048]{1,0:T(8,128)(2,1)S(1)}, u32[]{:S(2)}, u32[]{:S(2)}) collective-permute-start(bf16[24,2048]{1,0:T(8,128)(2,1)S(1)} %convolution_convert_fusion.3), channel_id=1, source_target_pairs={{0,1},{1,0},{2,3},{3,2},{4,5},{5,4},{6,7},{7,6},{8,9},{9,8},{10,11... | collective-permute-start | bytes 294920 | tf_op jit(solution)/shard_map/ppermute | solution.py:333
  57.2 10.0 %collective-permute-start.14 = (bf16[24,2048]{1,0:T(8,128)(2,1)S(1)}, bf16[24,2048]{1,0:T(8,128)(2,1)S(1)}, u32[]{:S(2)}, u32[]{:S(2)}) collective-permute-start(bf16[24,2048]{1,0:T(8,128)(2,1)S(1)} %convolution_convert_fusion.2), channel_id=1, source_target_pairs={{0,2},{1,3},{2,0},{3,1},{4,6},{5,7},{6,4},{7,5},{8,10},{9,11},{10,... | collective-permute-start | bytes 294920 | tf_op jit(solution)/shard_map/ppermute | solution.py:333
  62.8 5.7 %collective-permute-start.15 = (bf16[24,2048]{1,0:T(8,128)(2,1)S(1)}, bf16[24,2048]{1,0:T(8,128)(2,1)S(1)}, u32[]{:S(2)}, u32[]{:S(2)}) collective-permute-start(bf16[24,2048]{1,0:T(8,128)(2,1)S(1)} %convolution_convert_fusion.1), channel_id=1, source_target_pairs={{0,3},{1,2},{2,1},{3,0},{4,7},{5,6},{6,5},{7,4},{8,11},{9,10},{10,... | collective-permute-start | bytes 294920 | tf_op jit(solution)/shard_map/ppermute | solution.py:333
  79.5 81.5 %copy-start.5 = (f32[4096]{0:T(1024)S(1)}, f32[4096]{0:T(1024)}, u32[]{:S(2)}) copy-start(f32[4096]{0:T(1024)} %param.11) | copy-start | bytes 49156
  79.5 81.4 %all-to-all-start.1 = ((bf16[16,24,4096]{2,1,0:T(8,128)(2,1)}), bf16[16,24,4096]{2,1,0:T(8,128)(2,1)}, u32[]{:S(2)}, u32[]{:S(2)}) async-start(bf16[16,24,4096]{2,1,0:T(8,128)(2,1)} %bitcast.74), calls=%async_computation.1 | async-start | bytes 6291456 | tf_op jit(solution)/shard_map/all_to_all | solution.py:330
  90.8 1.3 collective-permute-start.16
  92.1 12.8 %collective-permute-start.17 = (f32[8,128]{1,0:T(8,128)S(1)}, f32[8,128]{1,0:T(8,128)S(1)}, u32[]{:S(2)}, u32[]{:S(2)}) collective-permute-start(f32[8,128]{1,0:T(8,128)S(1)} %add.97), channel_id=1, source_target_pairs={{0,2},{1,3},{2,0},{3,1},{4,6},{5,7},{6,4},{7,5},{8,10},{9,11},{10,... | collective-permute-start | bytes 12296 | tf_op jit(solution)/shard_map/ppermute | solution.py:333
  104.9 39.0 %collective-permute-start.18 = (f32[8,128]{1,0:T(8,128)S(1)}, f32[8,128]{1,0:T(8,128)S(1)}, u32[]{:S(2)}, u32[]{:S(2)}) collective-permute-start(f32[8,128]{1,0:T(8,128)S(1)} %add.98), channel_id=1, source_target_pairs={{0,4},{1,5},{2,6},{3,7},{4,0},{5,1},{6,2},{7,3},{8,12},{9,13},{10,... | collective-permute-start | bytes 12296 | tf_op jit(solution)/shard_map/ppermute | solution.py:333
  144.0 14.7 %collective-permute-start.19 = (f32[8,128]{1,0:T(8,128)S(1)}, f32[8,128]{1,0:T(8,128)S(1)}, u32[]{:S(2)}, u32[]{:S(2)}) collective-permute-start(f32[8,128]{1,0:T(8,128)S(1)} %add.99), channel_id=1, source_target_pairs={{0,8},{1,9},{2,10},{3,11},{4,12},{5,13},{6,14},{7,15},{8,0},{9,1},... | collective-permute-start | bytes 12296 | tf_op jit(solution)/shard_map/ppermute | solution.py:333
  165.5 76.8 %all-to-all-start.2 = ((bf16[16,24,4096]{2,1,0:T(8,128)(2,1)}), bf16[16,24,4096]{2,1,0:T(8,128)(2,1)}, u32[]{:S(2)}, u32[]{:S(2)}) async-start(bf16[16,24,4096]{2,1,0:T(8,128)(2,1)} %bitcast.75), calls=%async_computation.2 | async-start | bytes 6291456 | tf_op jit(solution)/shard_map/all_to_all | solution.py:330
  (10 other events, 84.1 us)
